TPU v7x, 32 devices: a whole 2x2x4 slice. The times are simulated.
32 devices in a mesh: region: 2 (over y), row: 2 (over core), col: 8 (over z, x).
Axes of the slice: x: 2, y: 2, z: 4, core: 2. Of those that a mesh axis runs over, the one named last changes fastest.
Arguments:
- blocks: bfloat16 [4, 8, 128, 128, 128], P(('region', 'row'), 'col'), parts along dimension 0, may hold values from -0.125 to 0.125
- block_rows: int32 [4, 8, 128], P(('region', 'row'), 'col'), parts along dimension 0, may hold values from 0 to 63, as said below
- block_cols: int32 [4, 8, 128], P(('region', 'row'), 'col'), parts along dimension 0, may hold values from 0 to 7, as said below
- counts: int32 [4, 8], P(('region', 'row'), 'col'), parts along dimension 0, may hold values from 42 to 128, as said below
- u_rays: float32 [8, 32768], P(None, ('region', 'row', 'col')), parts along dimension 1, may hold values from -6 to 6
- v_cells: float32 [8, 16384], P(None, ('region', 'col', 'row')), parts along dimension 1, may hold values from -6 to 6
- x_cells: float32 [8, 16384], P(None, ('region', 'col', 'row')), parts along dimension 1, may hold values from -6 to 6
- w_cells: float32 [8, 16384], P(None, ('region', 'col', 'row')), parts along dimension 1, may hold values from -6 to 6
- alpha: float32 [16], P('region'), parts along dimension 0, may hold values from 0.5 to 2
- phibar: float32 [16], P('region'), parts along dimension 0, may hold values from 0.5 to 2
- rhobar: float32 [16], P('region'), parts along dimension 0, may hold values from 0.5 to 2
Outputs:
- u_next: float32 [8, 32768], P(None, ('region', 'row', 'col')), parts along dimension 1
- v_next: float32 [8, 16384], P(None, ('region', 'col', 'row')), parts along dimension 1
- x_next: float32 [8, 16384], P(None, ('region', 'col', 'row')), parts along dimension 1
- w_next: float32 [8, 16384], P(None, ('region', 'col', 'row')), parts along dimension 1
- scalars: float32 [3, 16], P(None, 'region'), parts along dimension 1
There are 2 independent parts, one for each index of `region`. A program takes and returns all parts, laid end to end along the dimension named above; each array names one. Nothing has to cross between parts.
Inputs may be any that keep to these rules, and one draw needn't show every extreme that they name: Block row within the row group, below 64; the pairs (block_rows, block_cols) of one device's slots are all different. `block_cols`: block column within the column group, below 8. Only slots k < counts of a device hold blocks of A; the values in the other slots are not part of A.
All inputs are finite; a program needn't handle non-finite values.
Results may differ from a plain program's by a relative error of at most 0.015.
Values may be sent and summed in bfloat16 or wider, within the bound.
No kernel may reach another device: no remote copies, remote signals or barrier semaphores. Data moves between devices by JAX's collectives and lax.ppermute only.
A program may use at most 64 MiB of HBM per device.

v0:
```python
import jax
import jax.numpy as jnp
from jax import lax
from jax.sharding import PartitionSpec as P

ITERS = 2


def local_forward(blk, rws, cls, cnt, vg3, br_dev):
    sel = jnp.take(vg3, cls, axis=1)
    prod = jnp.einsum("skj,kij->ski", sel, blk, preferred_element_type=jnp.float32)
    mask = (jnp.arange(blk.shape[0]) < cnt).astype(jnp.float32)
    onehot = (rws[:, None] == jnp.arange(br_dev)[None, :]).astype(jnp.float32) * mask[:, None]
    out = jnp.einsum("kb,ski->sbi", onehot, prod, precision=lax.Precision.HIGHEST)
    return out.reshape(vg3.shape[0], br_dev * blk.shape[1])


def local_backward(blk, rws, cls, cnt, ug3, bc_dev):
    sel = jnp.take(ug3, rws, axis=1)
    prod = jnp.einsum("ski,kij->skj", sel, blk, preferred_element_type=jnp.float32)
    mask = (jnp.arange(blk.shape[0]) < cnt).astype(jnp.float32)
    onehot = (cls[:, None] == jnp.arange(bc_dev)[None, :]).astype(jnp.float32) * mask[:, None]
    out = jnp.einsum("kb,skj->sbj", onehot, prod, precision=lax.Precision.HIGHEST)
    return out.reshape(ug3.shape[0], bc_dev * blk.shape[2])


def body(
    blocks, block_rows, block_cols, counts, u_rays, v_cells, x_cells, w_cells, alpha, phibar, rhobar
):
    blk = blocks[0, 0]
    rws = block_rows[0, 0]
    cls = block_cols[0, 0]
    cnt = counts[0, 0]
    width = blk.shape[1]
    n_row = lax.axis_size("row")
    n_col = lax.axis_size("col")
    ray_piece = u_rays.shape[1]
    cell_piece = v_cells.shape[1]
    br_dev = ray_piece * n_col // width
    bc_dev = cell_piece * n_row // width
    total_rays = ray_piece * n_row * n_col
    total_cells = cell_piece * n_row * n_col
    u, v, x, w = (u_rays, v_cells, x_cells, w_cells)
    u_group = lax.all_gather(u_rays, "col", axis=1, tiled=True)
    for step in range(ITERS):
        vg = lax.all_gather(v.astype(jnp.bfloat16), "row", axis=1, tiled=True)
        partial_rays = local_forward(
            blk, rws, cls, cnt, vg.reshape(vg.shape[0], bc_dev, width), br_dev
        )
        ray_sum = lax.psum(partial_rays, "col")
        upd = ray_sum - alpha[:, None] * u_group
        squares = lax.psum(jnp.sum(upd * upd, axis=1), "row")
        beta = jnp.sqrt(squares / total_rays + 1e-06)
        u_group = upd / beta[:, None]
        ug = u_group.astype(jnp.bfloat16)
        partial_cells = local_backward(
            blk, rws, cls, cnt, ug.reshape(ug.shape[0], br_dev, width), bc_dev
        )
        cell_sum = lax.psum_scatter(
            partial_cells.astype(jnp.bfloat16), "row", scatter_dimension=1, tiled=True
        ).astype(jnp.float32)
        vupd = cell_sum - beta[:, None] * v
        vsquares = lax.psum(jnp.sum(vupd * vupd, axis=1), ("row", "col"))
        alpha = jnp.sqrt(vsquares / total_cells + 1e-06)
        v = vupd / alpha[:, None]
        rho = jnp.sqrt(rhobar * rhobar + beta * beta)
        cosine = rhobar / rho
        sine = beta / rho
        theta = sine * alpha
        phi = cosine * phibar
        rhobar = -cosine * alpha
        phibar = sine * phibar
        x = x + (phi / rho)[:, None] * w
        w = v - (theta / rho)[:, None] * w
    u = lax.dynamic_slice_in_dim(u_group, lax.axis_index("col") * ray_piece, ray_piece, 1)
    return (u, v, x, w, jnp.stack([alpha, phibar, rhobar]))


def solution(mesh):
    placed = (
        P(("region", "row"), "col", None, None, None),
        P(("region", "row"), "col", None),
        P(("region", "row"), "col", None),
        P(("region", "row"), "col"),
        P(None, ("region", "row", "col")),
        P(None, ("region", "col", "row")),
        P(None, ("region", "col", "row")),
        P(None, ("region", "col", "row")),
        P("region"),
        P("region"),
        P("region"),
    )
    return jax.shard_map(
        body,
        mesh=mesh,
        in_specs=placed,
        out_specs=(
            P(None, ("region", "row", "col")),
            P(None, ("region", "col", "row")),
            P(None, ("region", "col", "row")),
            P(None, ("region", "col", "row")),
            P(None, "region"),
        ),
        check_vma=False,
    )
```

profile of v0, /device:TPU:0, one launch (start us, length us, event | category | flops | bytes accessed | tf_op | source)
XLA Modules:
  0.0 279.4 jit_solution(11426050431257514057)
XLA Ops:
  7.2 0.0 all-reduce.3.cloned.1.call-start
  7.2 0.7 compare_select_fusion
  7.9 0.7 compare_and_fusion
  9.2 0.7 convert_element_type.50
  10.0 1.9 all_gather.9
  11.9 0.7 gather_fusion
  12.6 4.5 %fusion.6 = f32[128,8,128]{2,1,0:T(8,128)S(1)} fusion(bf16[1,1,128,128,128]{4,3,2,1,0:T(8,128)(2,1)} %param.15, bf16[128,8,128]{2,1,0:T(8,128)(2,1)S(1)} %gather_fusion, pred[128]{0:T(512)(128)(4,1)S(1)} %compare_and_fusion), kind=kOutput, calls=%fused_computation.10 | convolution fusion | flops 33685504 | bytes 4980864 | tf_op jit(solution)/shard_map/skj,kij->ski/dot_general | solution.py:11
  17.1 0.5 convolution_bitcast_fusion.1
  17.6 0.9 copy.45
  18.4 0.0 all-reduce.3.cloned.1.call-update
  18.5 0.0 reduce-scatter.3.cloned.1.call-start
  18.5 32.5 %all_gather.10 = f32[8,8192]{1,0:T(8,128)S(1)} all-gather(f32[8,1024]{1,0:T(8,128)S(1)} %copy-done.1), channel_id=1, replica_groups=mesh['region'=2,'row'=2,'col'=8] {'col'}, dimensions={1}, use_global_device_ids=true | all-gather | bytes 294912 | tf_op jit(solution)/shard_map/all_gather | solution.py:44
  51.1 40.9 %all-reduce.3.cloned.1.call-done = f32[8,8192]{1,0:T(8,128)} async-done(((f32[8,8192]{1,0:T(8,128)}), f32[8,8192]{1,0:T(8,128)}) %all-reduce.3.cloned.1.call-update) | async-done | bytes 262160 | tf_op jit(solution)/shard_map/psum | solution.py:50
  92.0 1.2 multiply_reduce_fusion.1
  93.2 2.5 psum.43
  95.7 0.1 convert_bitcast_fusion.1
  95.8 0.7 gather_fusion.1
  96.5 3.4 %fusion.4 = f32[128,8,128]{2,1,0:T(8,128)S(1)} fusion(bf16[1,1,128,128,128]{4,3,2,1,0:T(8,128)(2,1)} %param.15, bf16[128,8,128]{2,1,0:T(8,128)(2,1)S(1)} %gather_fusion.1, pred[128]{0:T(512)(128)(4,1)S(1)} %compare_and_fusion.1), kind=kOutput, calls=%fused_computation.8 | convolution fusion | flops 33685504 | bytes 4980864 | tf_op jit(solution)/shard_map/ski,kij->skj/dot_general | solution.py:20
  99.9 0.4 fusion.8
  100.3 0.6 copy.47
  101.0 0.0 reduce-scatter.3.cloned.1.call-update
  101.0 0.0 all-reduce.5.cloned.1.call-start
  101.0 6.8 %reduce-scatter.3.cloned.1.call-done = bf16[8,512]{1,0:T(8,128)(2,1)} async-done(((bf16[8,1024]{1,0:T(8,128)(2,1)}), bf16[8,512]{1,0:T(8,128)(2,1)}) %reduce-scatter.3.cloned.1.call-update) | async-done | bytes 8208 | tf_op jit(solution)/shard_map/reduce_scatter | solution.py:59
  107.8 0.9 multiply_reduce_fusion.3
  108.7 33.9 %psum.44 = f32[8]{0:T(128)S(1)} all-reduce(f32[8]{0:T(128)S(1)} %multiply_reduce_fusion.3), channel_id=1, replica_groups=mesh['region'=2,'row'=2,'col'=8] {'row','col'}, use_global_device_ids=true, to_apply=%region_5.8 | all-reduce | flops 8 | bytes 64 | tf_op jit(solution)/shard_map/psum | solution.py:63
  142.6 0.8 fusion.72
  143.4 1.8 all_gather.11
  145.2 0.7 gather_fusion.2
  145.9 4.5 %fusion.2 = f32[128,8,128]{2,1,0:T(8,128)S(1)} fusion(bf16[1,1,128,128,128]{4,3,2,1,0:T(8,128)(2,1)} %param.15, bf16[128,8,128]{2,1,0:T(8,128)(2,1)S(1)} %gather_fusion.2, pred[128]{0:T(512)(128)(4,1)S(1)} %compare_and_fusion), kind=kOutput, calls=%fused_computation.6 | convolution fusion | flops 33685504 | bytes 4980864 | tf_op jit(solution)/shard_map/skj,kij->ski/dot_general | solution.py:11
  150.4 0.5 convolution_bitcast_fusion
  150.9 0.9 copy.44
  151.7 0.0 all-reduce.5.cloned.1.call-update
  151.7 0.0 reduce-scatter.5.cloned.1.call-start
  151.8 67.9 %all-reduce.5.cloned.1.call-done = f32[8,8192]{1,0:T(8,128)} async-done(((f32[8,8192]{1,0:T(8,128)}), f32[8,8192]{1,0:T(8,128)}) %all-reduce.5.cloned.1.call-update) | async-done | bytes 262160 | tf_op jit(solution)/shard_map/psum | solution.py:50
  219.7 1.2 multiply_reduce_fusion
  220.9 2.5 psum.46
  223.4 0.1 convert_bitcast_fusion
  223.5 0.7 gather_fusion.3
  224.2 3.4 %fusion = f32[128,8,128]{2,1,0:T(8,128)S(1)} fusion(bf16[1,1,128,128,128]{4,3,2,1,0:T(8,128)(2,1)} %param.15, bf16[128,8,128]{2,1,0:T(8,128)(2,1)S(1)} %gather_fusion.3, pred[128]{0:T(512)(128)(4,1)S(1)} %compare_and_fusion.1), kind=kOutput, calls=%fused_computation.4 | convolution fusion | flops 33685504 | bytes 4980864 | tf_op jit(solution)/shard_map/ski,kij->skj/dot_general | solution.py:20
  227.6 0.4 fusion.9
  228.1 0.6 copy.46
  228.7 0.0 reduce-scatter.5.cloned.1.call-update
  228.7 6.8 %reduce-scatter.5.cloned.1.call-done = bf16[8,512]{1,0:T(8,128)(2,1)} async-done(((bf16[8,1024]{1,0:T(8,128)(2,1)}), bf16[8,512]{1,0:T(8,128)(2,1)}) %reduce-scatter.5.cloned.1.call-update) | async-done | bytes 8208 | tf_op jit(solution)/shard_map/reduce_scatter | solution.py:59
  235.5 0.9 multiply_reduce_fusion.2
  236.4 0.6 constant_dynamic-slice_fusion
  237.1 33.8 %psum.47 = f32[8]{0:T(128)S(1)} all-reduce(f32[8]{0:T(128)S(1)} %multiply_reduce_fusion.2), channel_id=1, replica_groups=mesh['region'=2,'row'=2,'col'=8] {'row','col'}, use_global_device_ids=true, to_apply=%region_11.14 | all-reduce | flops 8 | bytes 64 | tf_op jit(solution)/shard_map/psum | solution.py:63
  270.9 0.6 pad_maximum_fusion
  271.5 1.4 multiply_subtract_fusion.2
  (28 shorter events, 0.1 us)
Async XLA Ops:
  7.2 9.9 %copy-start.5 = (s32[1,1,128]{2,1,0:T(1,128)S(1)}, s32[1,1,128]{2,1,0:T(1,128)}, u32[]{:S(2)}) copy-start(s32[1,1,128]{2,1,0:T(1,128)} %param.16) | copy-start | bytes 1540
  7.2 11.3 %copy-start.1 = (f32[8,1024]{1,0:T(8,128)S(1)}, f32[8,1024]{1,0:T(8,128)}, u32[]{:S(2)}) copy-start(f32[8,1024]{1,0:T(8,128)} %param.19) | copy-start | bytes 98308
  7.2 84.8 %copy-start.7 = (f32[8]{0:T(128)S(1)}, f32[8]{0:T(128)}, u32[]{:S(2)}) copy-start(f32[8]{0:T(128)} %param.23) | copy-start | bytes 100
  7.2 84.8 %all-reduce.3.cloned.1.call-start = ((), (), s32[]{:S(2)}) async-start(), calls=%async_computation.2 | async-start | bytes 524288 | tf_op jit(solution)/shard_map/psum | solution.py:50
  17.1 82.8 %copy-start.6 = (s32[1,1,128]{2,1,0:T(1,128)S(1)}, s32[1,1,128]{2,1,0:T(1,128)}, u32[]{:S(2)}) copy-start(s32[1,1,128]{2,1,0:T(1,128)} %param.17) | copy-start | bytes 1540
  17.6 90.3 %copy-start = (f32[8,512]{1,0:T(8,128)S(1)}, f32[8,512]{1,0:T(8,128)}, u32[]{:S(2)}) copy-start(f32[8,512]{1,0:T(8,128)} %param.20) | copy-start | bytes 49156
  18.5 89.4 %reduce-scatter.3.cloned.1.call-start = ((), (), s32[]{:S(2)}) async-start(), calls=%async_computation.3 | async-start | bytes 24576 | tf_op jit(solution)/shard_map/reduce_scatter | solution.py:59
  99.9 123.4 %copy-start.4 = (f32[8]{0:T(128)S(1)}, f32[8]{0:T(128)}, u32[]{:S(2)}) copy-start(f32[8]{0:T(128)} %param.24) | copy-start | bytes 100
  99.9 123.4 %copy-start.8 = (f32[8]{0:T(128)S(1)}, f32[8]{0:T(128)}, u32[]{:S(2)}) copy-start(f32[8]{0:T(128)} %param.25) | copy-start | bytes 100
  101.0 118.7 %all-reduce.5.cloned.1.call-start = ((), (), s32[]{:S(2)}) async-start(), calls=%async_computation.4 | async-start | bytes 524288 | tf_op jit(solution)/shard_map/psum | solution.py:50
  150.8 120.7 %copy-start.2 = (f32[8,512]{1,0:T(8,128)S(1)}, f32[8,512]{1,0:T(8,128)}, u32[]{:S(2)}) copy-start(f32[8,512]{1,0:T(8,128)} %param.22) | copy-start | bytes 49156
  150.9 120.7 %copy-start.3 = (f32[8,512]{1,0:T(8,128)S(1)}, f32[8,512]{1,0:T(8,128)}, u32[]{:S(2)}) copy-start(f32[8,512]{1,0:T(8,128)} %param.21) | copy-start | bytes 49156
  151.7 83.8 %reduce-scatter.5.cloned.1.call-start = ((), (), s32[]{:S(2)}) async-start(), calls=%async_computation.5 | async-start | bytes 24576 | tf_op jit(solution)/shard_map/reduce_scatter | solution.py:59
Sparse Core Ops, SparseCore 0:
  18.6 73.3 all-reduce.2
  101.1 6.6 reduce-scatter.2
  151.9 67.7 all-reduce.4
  228.8 6.6 reduce-scatter.4
where the time goes:
time: 280 us; the launch traced here: 279 us
  waiting for transfers between devices  122 us (44%)
  blocking collectives  109 us (39%)
  matrix products  17.7 us (6%)
  between operations  14.6 us (5%)
  other arithmetic  9.28 us (3%)
  local copies, waits for them, and re-layouts  6.37 us (2%)
    psum x2, waiting for transfers between devices, body(): ray_sum = lax.psum(partial_rays, 'col')  109 us
    psum x2, blocking collectives, body(): vsquares = lax.psum(jnp.sum(vupd * vupd, axis=1), ('row', 'col'))  67.7 us
    all_gather x1, blocking collectives, body(): u_group = lax.all_gather(u_rays, 'col', axis=1, tiled=True)  32.5 us
    reduce_scatter x2, waiting for transfers between devices, body(): lax.psum_scatter(partial_cells.astype(jnp.bfloat16), 'row', scatter_dimen...  13.7 us
    dot_general x2, matrix products, local_forward(): jnp.einsum('skj,kij->ski', sel, blk, preferred_element_type=jnp.float32)  8.97 us
    dot_general x2, matrix products, local_backward(): jnp.einsum('ski,kij->skj', sel, blk, preferred_element_type=jnp.float32)  6.86 us
  transfers between devices with their start and end apart: 4, of which 4 were waited for; matrix products, arithmetic and copies ran while one was open for 0% of the time, Pallas kernels for 0%

commit v1 on v0

v1 whole, which is shorter than its diff:
```python
import functools

import jax
import jax.numpy as jnp
from jax import lax
from jax.experimental import pallas as pl
from jax.experimental.pallas import tpu as pltpu
from jax.sharding import PartitionSpec as P

ITERS = 2
EPS = 1e-6
UNROLL = 4
F32 = jnp.float32
BF16 = jnp.bfloat16
SMEM = pl.BlockSpec(memory_space=pltpu.SMEM)
VMEM = pl.BlockSpec(memory_space=pltpu.VMEM)


def call(kernel, out_shape, in_specs, scratch=()):
    return pl.pallas_call(
        kernel,
        out_shape=out_shape,
        in_specs=in_specs,
        out_specs=jax.tree.map(lambda _: VMEM, out_shape),
        scratch_shapes=list(scratch),
        compiler_params=pltpu.CompilerParams(vmem_limit_bytes=48 * 1024 * 1024),
    )


def shape(*dims, dtype=F32):
    return jax.ShapeDtypeStruct(dims, dtype)


def forward(blk, rws, cls, cnt, v_ref, acc_ref):
    spare = acc_ref.shape[0] - 1
    count = cnt[0, 0]
    acc_ref[...] = jnp.zeros_like(acc_ref)

    def group(g, carry):
        prods = []
        for p in range(UNROLL):
            k = (g * UNROLL + p) * 2
            pair = jnp.concatenate([v_ref[cls[0, 0, k]], v_ref[cls[0, 0, k + 1]]], axis=0)
            a = blk[0, 0, pl.ds(k, 2)].reshape(256, 128)
            prods.append(
                lax.dot_general(
                    pair.astype(BF16), a, (((1,), (1,)), ((), ())), preferred_element_type=F32
                )
            )
        for p in range(UNROLL):
            k = (g * UNROLL + p) * 2
            r0 = jnp.where(k < count, rws[0, 0, k], spare)
            acc_ref[r0] += prods[p][:8, :128]
            r1 = jnp.where(k + 1 < count, rws[0, 0, k + 1], spare)
            acc_ref[r1] += prods[p][8:, 128:]
        return carry

    step = 2 * UNROLL
    lax.fori_loop(0, (count + step - 1) // step, group, 0)


def backward(blk, rws, cls, cnt, u_ref, acc_ref):
    spare = acc_ref.shape[0] - 1
    count = cnt[0, 0]
    acc_ref[...] = jnp.zeros_like(acc_ref)
    zero = jnp.zeros((8, 128), F32)

    def group(g, carry):
        prods = []
        for p in range(UNROLL):
            k = (g * UNROLL + p) * 2
            u0 = jnp.concatenate([u_ref[rws[0, 0, k]], zero], axis=0).astype(BF16)
            u1 = jnp.concatenate([zero, u_ref[rws[0, 0, k + 1]]], axis=0).astype(BF16)
            pair = jnp.concatenate([u0, u1], axis=1)
            a = blk[0, 0, pl.ds(k, 2)].reshape(256, 128)
            prods.append(jnp.dot(pair, a, preferred_element_type=F32))
        for p in range(UNROLL):
            k = (g * UNROLL + p) * 2
            c0 = jnp.where(k < count, cls[0, 0, k], spare)
            acc_ref[c0] += prods[p][:8]
            c1 = jnp.where(k + 1 < count, cls[0, 0, k + 1], spare)
            acc_ref[c1] += prods[p][8:]
        return carry

    step = 2 * UNROLL
    lax.fori_loop(0, (count + step - 1) // step, group, 0)


def column(ref):
    rows = lax.broadcasted_iota(jnp.int32, (8, 128), 0)
    out = jnp.zeros((8, 128), F32)
    for s in range(8):
        out = jnp.where(rows == s, ref[s], out)
    return out


def lane_sum(x):
    return jnp.broadcast_to(jnp.sum(x, axis=1, keepdims=True), (8, 128))


def squares(ref, blocks):
    total = jnp.zeros((8, 128), F32)
    for b in range(blocks):
        total = total + ref[b] * ref[b]
    return lane_sum(total)


def store_pairs(acc_ref, out_ref, blocks):
    for b in range(0, blocks, 2):
        pair = jnp.concatenate([acc_ref[b], acc_ref[b + 1]], axis=0)
        out_ref[b // 2] = pair.astype(BF16)


def place_halves(own, other, out_ref):
    half = own.shape[1] // 128
    row = lax.axis_index("row")
    for b in range(half):
        out_ref[row * half + b] = own[:, b * 128 : (b + 1) * 128]
        out_ref[(1 - row) * half + b] = other[:, b * 128 : (b + 1) * 128]


def first_forward(rws, cls, cnt, alpha, blk, own, other, u_piece, out, v_out, acc):
    place_halves(own, other, v_out)
    forward(blk, rws, cls, cnt, v_out, acc)
    pieces = u_piece.shape[1] // 128
    base = lax.axis_index("col") * pieces
    a = column(alpha)
    for b in range(pieces):
        acc[base + b] -= a * u_piece[:, b * 128 : (b + 1) * 128]
    store_pairs(acc, out, acc.shape[0] - 1)


def first_backward(rws, cls, cnt, blk, sum0, sum1, upd, message, acc):
    blocks = upd.shape[0]
    for b in range(blocks // 2):
        s = sum0[b].astype(F32) + sum1[b].astype(F32)
        upd[2 * b] = s[:8]
        upd[2 * b + 1] = s[8:]
    backward(blk, rws, cls, cnt, upd, acc)
    cells = acc.shape[0] - 1
    message[:cells] = acc[:cells]
    message[cells] = squares(upd, blocks)


def next_forward(total_rays, rws, cls, cnt, blk, own, other, v_old, out, vupd, beta_out, acc):
    cells = v_old.shape[0]
    beta = jnp.sqrt((own[cells] + other[cells]) / total_rays + EPS)
    beta_out[...] = beta
    inv = 1.0 / beta
    for b in range(cells):
        vupd[b] = (own[b] + other[b]) * inv - beta * v_old[b]
    forward(blk, rws, cls, cnt, vupd, acc)
    rays = acc.shape[0] - 1
    store_pairs(acc, out, rays)
    sq = squares(vupd, cells)
    lanes = lax.broadcasted_iota(jnp.int32, (8, 128), 1)
    sq = jnp.where(lanes == lax.axis_index("col"), sq, 0.0)
    high = sq.astype(BF16).astype(F32)
    out[rays // 2] = jnp.concatenate([high, sq - high], axis=0).astype(BF16)


def next_backward(
    total_cells, pieces, rws, cls, cnt, blk, sum0, sum1, old, beta, message, u_piece, alpha_out, upd, acc
):
    blocks = upd.shape[0]
    tail = sum0[blocks // 2].astype(F32) + sum1[blocks // 2].astype(F32)
    alpha = jnp.sqrt(lane_sum(tail[:8] + tail[8:]) / total_cells + EPS)
    alpha_out[...] = alpha
    inv = 1.0 / alpha
    ratio = alpha / beta[...]
    for b in range(blocks // 2):
        s = sum0[b].astype(F32) + sum1[b].astype(F32)
        upd[2 * b] = s[:8] * inv - ratio * old[2 * b]
        upd[2 * b + 1] = s[8:] * inv - ratio * old[2 * b + 1]
    backward(blk, rws, cls, cnt, upd, acc)
    cells = acc.shape[0] - 1
    message[:cells] = acc[:cells]
    message[cells] = squares(upd, blocks)
    base = lax.axis_index("col") * pieces
    for b in range(pieces):
        u_piece[b] = upd[base + b]


def last_cells(total_rays, own, other, v_old, alpha, sq_out, vupd, beta_out):
    cells = v_old.shape[0]
    beta = jnp.sqrt((own[cells] + other[cells]) / total_rays + EPS)
    beta_out[...] = beta
    inv = 1.0 / beta
    scale = beta / alpha[...]
    for b in range(cells):
        vupd[b] = (own[b] + other[b]) * inv - scale * v_old[b]
    sq = squares(vupd, cells)
    for c in range(sq_out.shape[0]):
        sq_out[c] = sq


def finish(
    total_cells,
    phibar_in,
    rhobar_in,
    sq,
    v1,
    v2,
    u_piece,
    x_in,
    w_in,
    beta1,
    alpha1,
    beta2,
    u_out,
    v_out,
    x_out,
    w_out,
    scalars,
):
    total = sq[0]
    for c in range(1, sq.shape[0]):
        total = total + sq[c]
    alpha2 = jnp.sqrt(total / total_cells + EPS)
    phibar, rhobar = column(phibar_in), column(rhobar_in)
    steps = []
    for beta, alpha in ((beta1[...], alpha1[...]), (beta2[...], alpha2)):
        rho = jnp.sqrt(rhobar * rhobar + beta * beta)
        cosine, sine = rhobar / rho, beta / rho
        steps.append((cosine * phibar / rho, sine * alpha / rho, 1.0 / alpha))
        rhobar = -cosine * alpha
        phibar = sine * phibar
    half = x_in.shape[1] // 128
    base = lax.axis_index("row") * half
    for b in range(half):
        at = slice(b * 128, (b + 1) * 128)
        x, w = x_in[:, at], w_in[:, at]
        for (along, back, inv), vupd in zip(steps, (v1, v2)):
            v = vupd[base + b] * inv
            x = x + along * w
            w = v - back * w
        v_out[:, at], x_out[:, at], w_out[:, at] = v, x, w
    inv = 1.0 / beta2[...]
    for b in range(u_piece.shape[0]):
        u_out[:, b * 128 : (b + 1) * 128] = u_piece[b] * inv
    rows = lax.broadcasted_iota(jnp.int32, (8, 128), 0)
    lanes = lax.broadcasted_iota(jnp.int32, (8, 128), 1)
    for i, value in enumerate((alpha2, phibar, rhobar)):
        line = jnp.sum(jnp.where(rows == lanes, value, 0.0), axis=0, keepdims=True)
        scalars[i : i + 1, :] = line[:, :8]


def other_core(x):
    return lax.ppermute(x, "row", [(0, 1), (1, 0)])


def column_sum(x):
    n = lax.axis_size("col")
    m = 1
    while True:
        y = lax.ppermute(x, "col", [(i, i ^ m) for i in range(n)])
        m *= 2
        if m >= n:
            return x, y
        x = (x.astype(F32) + y.astype(F32)).astype(BF16)


def body(
    blocks, block_rows, block_cols, counts, u_rays, v_cells, x_cells, w_cells, alpha, phibar, rhobar
):
    n_row = lax.axis_size("row")
    n_col = lax.axis_size("col")
    pieces = u_rays.shape[1] // 128
    half = v_cells.shape[1] // 128
    rays = pieces * n_col
    cells = half * n_row
    total_rays = float(rays * 128 * n_row)
    total_cells = float(cells * 128 * n_col)
    where = (block_rows, block_cols, counts)
    listed = [SMEM] * 3
    ray_acc = pltpu.VMEM((rays + 1, 8, 128), F32)
    cell_acc = pltpu.VMEM((cells + 1, 8, 128), F32)

    part, v0 = call(
        first_forward,
        (shape(rays // 2, 16, 128, dtype=BF16), shape(cells, 8, 128)),
        listed + [SMEM] + [VMEM] * 4,
        [ray_acc],
    )(*where, alpha, blocks, v_cells, other_core(v_cells), u_rays)
    sum0, sum1 = column_sum(part)
    upd1, message = call(
        first_backward,
        (shape(rays, 8, 128), shape(cells + 1, 8, 128)),
        listed + [VMEM] * 3,
        [cell_acc],
    )(*where, blocks, sum0, sum1)
    part, v1, beta1 = call(
        functools.partial(next_forward, total_rays),
        (shape(rays // 2 + 1, 16, 128, dtype=BF16), shape(cells, 8, 128), shape(8, 128)),
        listed + [VMEM] * 4,
        [ray_acc],
    )(*where, blocks, message, other_core(message), v0)
    sum0, sum1 = column_sum(part)
    message, u_piece, alpha1 = call(
        functools.partial(next_backward, total_cells, pieces),
        (shape(cells + 1, 8, 128), shape(pieces, 8, 128), shape(8, 128)),
        listed + [VMEM] * 5,
        [pltpu.VMEM((rays, 8, 128), F32), cell_acc],
    )(*where, blocks, sum0, sum1, upd1, beta1)
    sq, v2, beta2 = call(
        functools.partial(last_cells, total_rays),
        (shape(n_col, 8, 128), shape(cells, 8, 128), shape(8, 128)),
        [VMEM] * 4,
    )(message, other_core(message), v1, alpha1)
    sq = lax.all_to_all(sq, "col", 0, 0, tiled=True)
    flat = shape(*v_cells.shape)
    return call(
        functools.partial(finish, total_cells),
        (shape(*u_rays.shape), flat, flat, flat, shape(3, 8)),
        [SMEM] * 2 + [VMEM] * 9,
    )(phibar, rhobar, sq, v1, v2, u_piece, x_cells, w_cells, beta1, alpha1, beta2)


def solution(mesh):
    placed = (
        P(("region", "row"), "col", None, None, None),
        P(("region", "row"), "col", None),
        P(("region", "row"), "col", None),
        P(("region", "row"), "col"),
        P(None, ("region", "row", "col")),
        P(None, ("region", "col", "row")),
        P(None, ("region", "col", "row")),
        P(None, ("region", "col", "row")),
        P("region"),
        P("region"),
        P("region"),
    )
    return jax.shard_map(
        body,
        mesh=mesh,
        in_specs=placed,
        out_specs=(
            P(None, ("region", "row", "col")),
            P(None, ("region", "col", "row")),
            P(None, ("region", "col", "row")),
            P(None, ("region", "col", "row")),
            P(None, "region"),
        ),
        check_vma=False,
    )
```

time: 280 us -> 76.1 us (0.27)
  blocking collectives: 109 us -> 12.8 us
  waiting for transfers between devices: 122 us -> 26.7 us
  matrix products: 17.7 us -> 0 us
  starting transfers between devices: 0.16 us -> 15.8 us
  Pallas kernels: 0 us -> 13.4 us
  between operations: 14.6 us -> 1.35 us
  other arithmetic: 9.28 us -> 0.16 us
    psum x2 -> x0, waiting for transfers between devices: 109 us -> none  [body(): ray_sum = lax.psum(partial_rays, 'col')]
    psum x4 -> x0, blocking collectives: 72.6 us -> none  [the longest x2 67.7 us: body(): vsquares = lax.psum(jnp.sum(vupd * vupd, axis=1), ('row', 'col'))]
    all_gather x3 -> x0, blocking collectives: 36.3 us -> none  [the longest x1 32.5 us: body(): u_group = lax.all_gather(u_rays, 'col', axis=1, tiled=True)]
    ppermute x0 -> x9, waiting for transfers between devices: none -> 26.7 us  [the longest x6 23.8 us: column_sum(): y = lax.ppermute(x, 'col', [(i, i ^ m) for i in range(n)])]
    dot_general x8 -> x0, matrix products: 17.7 us -> none  [the longest x2 8.97 us: local_forward(): jnp.einsum('skj,kij->ski', sel, blk, preferred_element_type=jnp.float32)]
    ppermute x0 -> x9, starting transfers between devices: none -> 15.8 us  [the longest x6 15.3 us: column_sum(): y = lax.ppermute(x, 'col', [(i, i ^ m) for i in range(n)])]
    reduce_scatter x2 -> x0, waiting for transfers between devices: 13.7 us -> none  [body(): lax.psum_scatter(partial_cells.astype(jnp.bfloat16), 'row', scatter_dimen...]
    pallas_call x0 -> x6, Pallas kernels: none -> 13.4 us  [the longest x1 3.17 us: body(): call(functools.partial(next_forward, total_rays), (shape(rays // 2 + 1, 1...]
  transfers between devices with their start and end apart: 4 -> 9, of which waited for: 4 -> 9; matrix products, arithmetic and copies ran while one was open for 0% -> 0% of each run, Pallas kernels for 0% -> 0%
where the time goes in v1:
time: 76.1 us; the launch traced here: 75.8 us
  waiting for transfers between devices  26.7 us (35%)
  starting transfers between devices  15.8 us (21%)
  Pallas kernels  13.4 us (18%)
  blocking collectives  12.8 us (17%)
  local copies, waits for them, and re-layouts  5.64 us (7%)
  between operations  1.35 us (2%)
    ppermute x6, waiting for transfers between devices, column_sum(): y = lax.ppermute(x, 'col', [(i, i ^ m) for i in range(n)])  23.8 us
    ppermute x6, starting transfers between devices, column_sum(): y = lax.ppermute(x, 'col', [(i, i ^ m) for i in range(n)])  15.3 us
    all_to_all x1, blocking collectives, body(): sq = lax.all_to_all(sq, 'col', 0, 0, tiled=True)  12.8 us
    unnamed x22, local copies, waits for them, and re-layouts  5.64 us
    pallas_call x1, Pallas kernels, body(): call(functools.partial(next_forward, total_rays), (shape(rays // 2 + 1, 1...  3.17 us
    pallas_call x1, Pallas kernels, body(): call(first_forward, (shape(rays // 2, 16, 128, dtype=BF16), shape(cells,...  3.1 us
    pallas_call x1, Pallas kernels, body(): call(functools.partial(next_backward, total_cells, pieces), (shape(cells...  2.94 us
    pallas_call x1, Pallas kernels, body(): call(first_backward, (shape(rays, 8, 128), shape(cells + 1, 8, 128)), lis...  2.85 us
  transfers between devices with their start and end apart: 9, of which 9 were waited for; matrix products, arithmetic and copies ran while one was open for 0% of the time, Pallas kernels for 0%

profile of v1, /device:TPU:0, one launch (start us, length us, event | category | flops | bytes accessed | tf_op | source)
XLA Modules:
  0.0 75.8 jit_solution(149021310776706550)
XLA Ops:
  0.6 0.5 collective-permute-start
  1.8 0.4 collective-permute-done.other
  2.2 0.0 copy-start
  2.2 2.2 %copy-done = bf16[1,1,128,128,128]{4,3,2,1,0:T(8,128)(2,1)S(1)} copy-done((bf16[1,1,128,128,128]{4,3,2,1,0:T(8,128)(2,1)S(1)}, bf16[1,1,128,128,128]{4,3,2,1,0:T(8,128)(2,1)}, u32[]{:S(2)}) %copy-start) | copy-done | bytes 4194328
  4.4 0.0 copy-start.2
  4.4 0.8 copy-done.2
  5.1 0.0 copy-start.3
  5.2 0.7 copy-done.3
  5.9 0.0 copy-start.6
  5.9 0.7 copy-done.6
  6.5 0.0 copy-start.7
  6.5 0.7 copy-done.7
  7.2 0.0 copy-start.10
  7.2 0.7 copy-done.10
  7.8 0.0 copy-start.1
  7.8 3.1 %shard_map.146 = (bf16[32,16,128]{2,1,0:T(8,128)(2,1)S(1)}, f32[8,8,128]{2,1,0:T(8,128)S(1)}) custom-call(s32[1,1,128]{2,1,0:T(1,128)S(1)} %copy-done.6, s32[1,1,128]{2,1,0:T(1,128)S(1)} %copy-done.7, s32[1,1]{1,0:T(1,128)S(6)} %copy.16.cnt, f32[8]{0:T(128)S(1)} %copy-done.10, bf16[1,1,128,128,128]{4,3,2,1,0:T(8,128)(2,1)S(1)} %copy-done, ...), custom_call_target="tpu_custom_call" | custom-call | tf_op jit(solution)/shard_map/pallas_call | solution.py:279
  10.9 2.7 %collective-permute-start.1 = (bf16[32,16,128]{2,1,0:T(8,128)(2,1)S(1)}, bf16[32,16,128]{2,1,0:T(8,128)(2,1)S(1)}, u32[]{:S(2)}, u32[]{:S(2)}) collective-permute-start(bf16[32,16,128]{2,1,0:T(8,128)(2,1)S(1)} %get-tuple-element.18), channel_id=1, source_target_pairs={{0,1},{1,0},{2,3},{3,2},{4,5},{5,4},{6,7},{7,6},{8,9},{9,8},{10,11... | collective-permute-start | bytes 393224 | tf_op jit(solution)/shard_map/ppermute | solution.py:256
  13.6 3.6 %collective-permute-done.1 = bf16[32,16,128]{2,1,0:T(8,128)(2,1)S(1)} collective-permute-done((bf16[32,16,128]{2,1,0:T(8,128)(2,1)S(1)}, bf16[32,16,128]{2,1,0:T(8,128)(2,1)S(1)}, u32[]{:S(2)}, u32[]{:S(2)}) %collective-permute-start.1) | collective-permute-done | bytes 131104 | tf_op jit(solution)/shard_map/ppermute | solution.py:256
  17.3 2.5 %collective-permute-start.2 = (bf16[32,16,128]{2,1,0:T(8,128)(2,1)S(1)}, bf16[32,16,128]{2,1,0:T(8,128)(2,1)S(1)}, u32[]{:S(2)}, u32[]{:S(2)}) collective-permute-start(bf16[32,16,128]{2,1,0:T(8,128)(2,1)S(1)} %add_convert_fusion.3), channel_id=1, source_target_pairs={{0,2},{1,3},{2,0},{3,1},{4,6},{5,7},{6,4},{7,5},{8,10},{9,11},{10,... | collective-permute-start | bytes 393224 | tf_op jit(solution)/shard_map/ppermute | solution.py:256
  19.8 3.0 %collective-permute-done.2 = bf16[32,16,128]{2,1,0:T(8,128)(2,1)S(1)} collective-permute-done((bf16[32,16,128]{2,1,0:T(8,128)(2,1)S(1)}, bf16[32,16,128]{2,1,0:T(8,128)(2,1)S(1)}, u32[]{:S(2)}, u32[]{:S(2)}) %collective-permute-start.2) | collective-permute-done | bytes 131104 | tf_op jit(solution)/shard_map/ppermute | solution.py:256
  22.9 3.2 %collective-permute-start.3 = (bf16[32,16,128]{2,1,0:T(8,128)(2,1)S(1)}, bf16[32,16,128]{2,1,0:T(8,128)(2,1)S(1)}, u32[]{:S(2)}, u32[]{:S(2)}) collective-permute-start(bf16[32,16,128]{2,1,0:T(8,128)(2,1)S(1)} %add_convert_fusion.2.sum0), channel_id=1, source_target_pairs={{0,4},{1,5},{2,6},{3,7},{4,0},{5,1},{6,2},{7,3},{8,12},{9,13},{10,... | collective-permute-start | bytes 393224 | tf_op jit(solution)/shard_map/ppermute | solution.py:256
  26.0 4.8 %collective-permute-done.3.sum1 = bf16[32,16,128]{2,1,0:T(8,128)(2,1)S(1)} collective-permute-done((bf16[32,16,128]{2,1,0:T(8,128)(2,1)S(1)}, bf16[32,16,128]{2,1,0:T(8,128)(2,1)S(1)}, u32[]{:S(2)}, u32[]{:S(2)}) %collective-permute-start.3) | collective-permute-done | bytes 131104 | tf_op jit(solution)/shard_map/ppermute | solution.py:256
  30.8 0.0 copy-done.1
  30.8 2.9 %shard_map.147 = (f32[64,8,128]{2,1,0:T(8,128)S(1)}, f32[9,8,128]{2,1,0:T(8,128)S(1)}) custom-call(s32[1,1,128]{2,1,0:T(1,128)S(1)} %copy-done.6, s32[1,1,128]{2,1,0:T(1,128)S(1)} %copy-done.7, s32[1,1]{1,0:T(1,128)S(6)} %copy.16.cnt, bf16[1,1,128,128,128]{4,3,2,1,0:T(8,128)(2,1)S(1)} %copy-done.1, bf16[32,16,128]{2,1,0:T(8,128)(2,1)S(1)} %add_convert_fusion.2.sum0, ...), custom_call_target="tpu_custom_call" | custom-call | tf_op jit(solution)/shard_map/pallas_call | solution.py:286
  33.7 0.0 collective-permute-start.4
  33.7 1.2 %collective-permute-done.4.other = f32[9,8,128]{2,1,0:T(8,128)S(1)} collective-permute-done((f32[9,8,128]{2,1,0:T(8,128)S(1)}, f32[9,8,128]{2,1,0:T(8,128)S(1)}, u32[]{:S(2)}, u32[]{:S(2)}) %collective-permute-start.4) | collective-permute-done | bytes 36896 | tf_op jit(solution)/shard_map/ppermute | solution.py:249
  34.9 0.0 copy-start.4
  34.9 0.0 copy-start.5
  34.9 0.0 copy-start.8
  34.9 0.0 copy-start.9
  34.9 3.2 %shard_map.148 = (bf16[33,16,128]{2,1,0:T(8,128)(2,1)S(1)}, f32[8,8,128]{2,1,0:T(8,128)S(1)}, f32[8,128]{1,0:T(8,128)S(1)}) custom-call(s32[1,1,128]{2,1,0:T(1,128)S(1)} %copy-done.6, s32[1,1,128]{2,1,0:T(1,128)S(1)} %copy-done.7, s32[1,1]{1,0:T(1,128)S(6)} %copy.16.cnt, bf16[1,1,128,128,128]{4,3,2,1,0:T(8,128)(2,1)S(1)} %copy-done.1, ...), custom_call_target="tpu_custom_call" | custom-call | tf_op jit(solution)/shard_map/pallas_call | solution.py:292
  38.1 1.3 %collective-permute-start.5 = (bf16[33,16,128]{2,1,0:T(8,128)(2,1)S(1)}, bf16[33,16,128]{2,1,0:T(8,128)(2,1)S(1)}, u32[]{:S(2)}, u32[]{:S(2)}) collective-permute-start(bf16[33,16,128]{2,1,0:T(8,128)(2,1)S(1)} %get-tuple-element.21), channel_id=1, source_target_pairs={{0,1},{1,0},{2,3},{3,2},{4,5},{5,4},{6,7},{7,6},{8,9},{9,8},{10,11... | collective-permute-start | bytes 405512 | tf_op jit(solution)/shard_map/ppermute | solution.py:256
  39.3 3.7 %collective-permute-done.5 = bf16[33,16,128]{2,1,0:T(8,128)(2,1)S(1)} collective-permute-done((bf16[33,16,128]{2,1,0:T(8,128)(2,1)S(1)}, bf16[33,16,128]{2,1,0:T(8,128)(2,1)S(1)}, u32[]{:S(2)}, u32[]{:S(2)}) %collective-permute-start.5) | collective-permute-done | bytes 135200 | tf_op jit(solution)/shard_map/ppermute | solution.py:256
  43.1 1.8 %collective-permute-start.6 = (bf16[33,16,128]{2,1,0:T(8,128)(2,1)S(1)}, bf16[33,16,128]{2,1,0:T(8,128)(2,1)S(1)}, u32[]{:S(2)}, u32[]{:S(2)}) collective-permute-start(bf16[33,16,128]{2,1,0:T(8,128)(2,1)S(1)} %add_convert_fusion.1), channel_id=1, source_target_pairs={{0,2},{1,3},{2,0},{3,1},{4,6},{5,7},{6,4},{7,5},{8,10},{9,11},{10,... | collective-permute-start | bytes 405512 | tf_op jit(solution)/shard_map/ppermute | solution.py:256
  44.9 3.3 %collective-permute-done.6 = bf16[33,16,128]{2,1,0:T(8,128)(2,1)S(1)} collective-permute-done((bf16[33,16,128]{2,1,0:T(8,128)(2,1)S(1)}, bf16[33,16,128]{2,1,0:T(8,128)(2,1)S(1)}, u32[]{:S(2)}, u32[]{:S(2)}) %collective-permute-start.6) | collective-permute-done | bytes 135200 | tf_op jit(solution)/shard_map/ppermute | solution.py:256
  48.3 3.9 %collective-permute-start.7 = (bf16[33,16,128]{2,1,0:T(8,128)(2,1)S(1)}, bf16[33,16,128]{2,1,0:T(8,128)(2,1)S(1)}, u32[]{:S(2)}, u32[]{:S(2)}) collective-permute-start(bf16[33,16,128]{2,1,0:T(8,128)(2,1)S(1)} %add_convert_fusion.sum0), channel_id=1, source_target_pairs={{0,4},{1,5},{2,6},{3,7},{4,0},{5,1},{6,2},{7,3},{8,12},{9,13},{10,... | collective-permute-start | bytes 405512 | tf_op jit(solution)/shard_map/ppermute | solution.py:256
  52.2 5.3 %collective-permute-done.7.sum1 = bf16[33,16,128]{2,1,0:T(8,128)(2,1)S(1)} collective-permute-done((bf16[33,16,128]{2,1,0:T(8,128)(2,1)S(1)}, bf16[33,16,128]{2,1,0:T(8,128)(2,1)S(1)}, u32[]{:S(2)}, u32[]{:S(2)}) %collective-permute-start.7) | collective-permute-done | bytes 135200 | tf_op jit(solution)/shard_map/ppermute | solution.py:256
  57.5 2.9 %shard_map.149 = (f32[9,8,128]{2,1,0:T(8,128)S(1)}, f32[8,8,128]{2,1,0:T(8,128)S(1)}, f32[8,128]{1,0:T(8,128)S(1)}) custom-call(s32[1,1,128]{2,1,0:T(1,128)S(1)} %copy-done.6, s32[1,1,128]{2,1,0:T(1,128)S(1)} %copy-done.7, s32[1,1]{1,0:T(1,128)S(6)} %copy.16.cnt, bf16[1,1,128,128,128]{4,3,2,1,0:T(8,128)(2,1)S(1)} %copy-done.1, ...), custom_call_target="tpu_custom_call" | custom-call | tf_op jit(solution)/shard_map/pallas_call | solution.py:299
  60.4 0.0 collective-permute-start.8
  60.4 1.2 %collective-permute-done.8.other = f32[9,8,128]{2,1,0:T(8,128)S(1)} collective-permute-done((f32[9,8,128]{2,1,0:T(8,128)S(1)}, f32[9,8,128]{2,1,0:T(8,128)S(1)}, u32[]{:S(2)}, u32[]{:S(2)}) %collective-permute-start.8) | collective-permute-done | bytes 36896 | tf_op jit(solution)/shard_map/ppermute | solution.py:249
  61.7 0.1 shard_map.150
  61.8 12.8 %all_to_all.5.sq = f32[8,8,128]{2,1,0:T(8,128)S(1)} all-to-all(f32[8,8,128]{2,1,0:T(8,128)S(1)} %get-tuple-element.27), channel_id=1, replica_groups=mesh['region'=2,'row'=2,'col'=8] {'col'}, dimensions={0} | all-to-all | bytes 65536 | tf_op jit(solution)/shard_map/all_to_all | solution.py:310
  74.6 0.0 copy-done.4
  74.6 0.0 copy-done.5
  74.6 0.0 copy-done.8
  74.6 0.0 copy-done.9
  74.6 1.2 %shard_map.151 = (f32[8,1024]{1,0:T(8,128)}, f32[8,512]{1,0:T(8,128)}, f32[8,512]{1,0:T(8,128)}, f32[8,512]{1,0:T(8,128)}, f32[3,8]{1,0:T(4,128)}) custom-call(f32[8]{0:T(128)S(1)} %copy-done.8, f32[8]{0:T(128)S(1)} %copy-done.9, f32[8,8,128]{2,1,0:T(8,128)S(1)} %all_to_all.5.sq, f32[8,8,128]{2,1,0:T(8,128)S(1)} %get-tuple-element.25.v_old.v1, ...), custom_call_target="tpu_custom_call" | custom-call | tf_op jit(solution)/shard_map/pallas_call | solution.py:312
  (4 shorter events, 0.2 us)
Async XLA Ops:
  0.6 1.6 %collective-permute-start = (f32[8,512]{1,0:T(8,128)}, f32[8,512]{1,0:T(8,128)S(1)}, u32[]{:S(2)}, u32[]{:S(2)}) collective-permute-start(f32[8,512]{1,0:T(8,128)} %own.1), channel_id=1, source_target_pairs={{0,8},{8,0},{1,9},{9,1},{2,10},{10,2},{3,11},{11,3},{4,12},{12,4},... | collective-permute-start | bytes 49160 | tf_op jit(solution)/shard_map/ppermute | solution.py:249
  2.2 2.2 %copy-start = (bf16[1,1,128,128,128]{4,3,2,1,0:T(8,128)(2,1)S(1)}, bf16[1,1,128,128,128]{4,3,2,1,0:T(8,128)(2,1)}, u32[]{:S(2)}) copy-start(bf16[1,1,128,128,128]{4,3,2,1,0:T(8,128)(2,1)} %blk.7) | copy-start | bytes 12582916
  4.4 0.8 copy-start.2
  5.1 0.7 copy-start.3
  5.9 0.7 copy-start.6
  6.5 0.7 copy-start.7
  7.2 0.7 copy-start.10
  7.8 23.0 %copy-start.1 = (bf16[1,1,128,128,128]{4,3,2,1,0:T(8,128)(2,1)S(1)}, bf16[1,1,128,128,128]{4,3,2,1,0:T(8,128)(2,1)}, u32[]{:S(2)}) copy-start(bf16[1,1,128,128,128]{4,3,2,1,0:T(8,128)(2,1)} %blk.7) | copy-start | bytes 12582916
  10.9 6.3 %collective-permute-start.1 = (bf16[32,16,128]{2,1,0:T(8,128)(2,1)S(1)}, bf16[32,16,128]{2,1,0:T(8,128)(2,1)S(1)}, u32[]{:S(2)}, u32[]{:S(2)}) collective-permute-start(bf16[32,16,128]{2,1,0:T(8,128)(2,1)S(1)} %get-tuple-element.18), channel_id=1, source_target_pairs={{0,1},{1,0},{2,3},{3,2},{4,5},{5,4},{6,7},{7,6},{8,9},{9,8},{10,11... | collective-permute-start | bytes 393224 | tf_op jit(solution)/shard_map/ppermute | solution.py:256
  17.3 5.5 %collective-permute-start.2 = (bf16[32,16,128]{2,1,0:T(8,128)(2,1)S(1)}, bf16[32,16,128]{2,1,0:T(8,128)(2,1)S(1)}, u32[]{:S(2)}, u32[]{:S(2)}) collective-permute-start(bf16[32,16,128]{2,1,0:T(8,128)(2,1)S(1)} %add_convert_fusion.3), channel_id=1, source_target_pairs={{0,2},{1,3},{2,0},{3,1},{4,6},{5,7},{6,4},{7,5},{8,10},{9,11},{10,... | collective-permute-start | bytes 393224 | tf_op jit(solution)/shard_map/ppermute | solution.py:256
  22.9 8.0 %collective-permute-start.3 = (bf16[32,16,128]{2,1,0:T(8,128)(2,1)S(1)}, bf16[32,16,128]{2,1,0:T(8,128)(2,1)S(1)}, u32[]{:S(2)}, u32[]{:S(2)}) collective-permute-start(bf16[32,16,128]{2,1,0:T(8,128)(2,1)S(1)} %add_convert_fusion.2.sum0), channel_id=1, source_target_pairs={{0,4},{1,5},{2,6},{3,7},{4,0},{5,1},{6,2},{7,3},{8,12},{9,13},{10,... | collective-permute-start | bytes 393224 | tf_op jit(solution)/shard_map/ppermute | solution.py:256
  33.7 1.2 %collective-permute-start.4 = (f32[9,8,128]{2,1,0:T(8,128)S(1)}, f32[9,8,128]{2,1,0:T(8,128)S(1)}, u32[]{:S(2)}, u32[]{:S(2)}) collective-permute-start(f32[9,8,128]{2,1,0:T(8,128)S(1)} %get-tuple-element.19.own), channel_id=1, source_target_pairs={{0,8},{8,0},{1,9},{9,1},{2,10},{10,2},{3,11},{11,3},{4,12},{12,4},... | collective-permute-start | bytes 110600 | tf_op jit(solution)/shard_map/ppermute | solution.py:249
  34.9 39.7 %copy-start.4 = (f32[8,512]{1,0:T(8,128)S(1)}, f32[8,512]{1,0:T(8,128)}, u32[]{:S(2)}) copy-start(f32[8,512]{1,0:T(8,128)} %x_in.1) | copy-start | bytes 49156
  34.9 39.7 %copy-start.5 = (f32[8,512]{1,0:T(8,128)S(1)}, f32[8,512]{1,0:T(8,128)}, u32[]{:S(2)}) copy-start(f32[8,512]{1,0:T(8,128)} %w_in.1) | copy-start | bytes 49156
  34.9 39.7 %copy-start.8 = (f32[8]{0:T(128)S(1)}, f32[8]{0:T(128)}, u32[]{:S(2)}) copy-start(f32[8]{0:T(128)} %phibar_in.1) | copy-start | bytes 100
  34.9 39.7 %copy-start.9 = (f32[8]{0:T(128)S(1)}, f32[8]{0:T(128)}, u32[]{:S(2)}) copy-start(f32[8]{0:T(128)} %rhobar_in.1) | copy-start | bytes 100
  38.1 5.0 %collective-permute-start.5 = (bf16[33,16,128]{2,1,0:T(8,128)(2,1)S(1)}, bf16[33,16,128]{2,1,0:T(8,128)(2,1)S(1)}, u32[]{:S(2)}, u32[]{:S(2)}) collective-permute-start(bf16[33,16,128]{2,1,0:T(8,128)(2,1)S(1)} %get-tuple-element.21), channel_id=1, source_target_pairs={{0,1},{1,0},{2,3},{3,2},{4,5},{5,4},{6,7},{7,6},{8,9},{9,8},{10,11... | collective-permute-start | bytes 405512 | tf_op jit(solution)/shard_map/ppermute | solution.py:256
  43.1 5.1 %collective-permute-start.6 = (bf16[33,16,128]{2,1,0:T(8,128)(2,1)S(1)}, bf16[33,16,128]{2,1,0:T(8,128)(2,1)S(1)}, u32[]{:S(2)}, u32[]{:S(2)}) collective-permute-start(bf16[33,16,128]{2,1,0:T(8,128)(2,1)S(1)} %add_convert_fusion.1), channel_id=1, source_target_pairs={{0,2},{1,3},{2,0},{3,1},{4,6},{5,7},{6,4},{7,5},{8,10},{9,11},{10,... | collective-permute-start | bytes 405512 | tf_op jit(solution)/shard_map/ppermute | solution.py:256
  48.3 9.2 %collective-permute-start.7 = (bf16[33,16,128]{2,1,0:T(8,128)(2,1)S(1)}, bf16[33,16,128]{2,1,0:T(8,128)(2,1)S(1)}, u32[]{:S(2)}, u32[]{:S(2)}) collective-permute-start(bf16[33,16,128]{2,1,0:T(8,128)(2,1)S(1)} %add_convert_fusion.sum0), channel_id=1, source_target_pairs={{0,4},{1,5},{2,6},{3,7},{4,0},{5,1},{6,2},{7,3},{8,12},{9,13},{10,... | collective-permute-start | bytes 405512 | tf_op jit(solution)/shard_map/ppermute | solution.py:256
  60.4 1.2 %collective-permute-start.8 = (f32[9,8,128]{2,1,0:T(8,128)S(1)}, f32[9,8,128]{2,1,0:T(8,128)S(1)}, u32[]{:S(2)}, u32[]{:S(2)}) collective-permute-start(f32[9,8,128]{2,1,0:T(8,128)S(1)} %get-tuple-element.24.own), channel_id=1, source_target_pairs={{0,8},{8,0},{1,9},{9,1},{2,10},{10,2},{3,11},{11,3},{4,12},{12,4},... | collective-permute-start | bytes 110600 | tf_op jit(solution)/shard_map/ppermute | solution.py:249

commit v2 on v1

--- a/solution.py
+++ b/solution.py
@@ -9,10 +9,10 @@
 
 ITERS = 2
 EPS = 1e-6
-UNROLL = 4
 F32 = jnp.float32
 BF16 = jnp.bfloat16
 SMEM = pl.BlockSpec(memory_space=pltpu.SMEM)
+HBM = pl.BlockSpec(memory_space=pltpu.HBM)
 VMEM = pl.BlockSpec(memory_space=pltpu.VMEM)
 
 
@@ -31,32 +31,20 @@
     return jax.ShapeDtypeStruct(dims, dtype)
 
 
-def forward(blk, rws, cls, cnt, v_ref, acc_ref):
+def forward(blk, rws, cls, cnt, v_ref, acc_ref, ready=None):
     spare = acc_ref.shape[0] - 1
     count = cnt[0, 0]
     acc_ref[...] = jnp.zeros_like(acc_ref)
-
-    def group(g, carry):
-        prods = []
-        for p in range(UNROLL):
-            k = (g * UNROLL + p) * 2
-            pair = jnp.concatenate([v_ref[cls[0, 0, k]], v_ref[cls[0, 0, k + 1]]], axis=0)
-            a = blk[0, 0, pl.ds(k, 2)].reshape(256, 128)
-            prods.append(
-                lax.dot_general(
-                    pair.astype(BF16), a, (((1,), (1,)), ((), ())), preferred_element_type=F32
-                )
-            )
-        for p in range(UNROLL):
-            k = (g * UNROLL + p) * 2
-            r0 = jnp.where(k < count, rws[0, 0, k], spare)
-            acc_ref[r0] += prods[p][:8, :128]
-            r1 = jnp.where(k + 1 < count, rws[0, 0, k + 1], spare)
-            acc_ref[r1] += prods[p][8:, 128:]
-        return carry
-
-    step = 2 * UNROLL
-    lax.fori_loop(0, (count + step - 1) // step, group, 0)
+    for k in range(0, blk.shape[0], 2):
+        if ready is not None:
+            ready(k)
+        pair = jnp.concatenate([v_ref[cls[0, 0, k]], v_ref[cls[0, 0, k + 1]]], axis=0)
+        a = blk[k : k + 2].reshape(256, 128)
+        prod = lax.dot_general(
+            pair.astype(BF16), a, (((1,), (1,)), ((), ())), preferred_element_type=F32
+        )
+        acc_ref[jnp.where(k < count, rws[0, 0, k], spare)] += prod[:8, :128]
+        acc_ref[jnp.where(k + 1 < count, rws[0, 0, k + 1], spare)] += prod[8:, 128:]
 
 
 def backward(blk, rws, cls, cnt, u_ref, acc_ref):
@@ -64,26 +52,13 @@
     count = cnt[0, 0]
     acc_ref[...] = jnp.zeros_like(acc_ref)
     zero = jnp.zeros((8, 128), F32)
-
-    def group(g, carry):
-        prods = []
-        for p in range(UNROLL):
-            k = (g * UNROLL + p) * 2
-            u0 = jnp.concatenate([u_ref[rws[0, 0, k]], zero], axis=0).astype(BF16)
-            u1 = jnp.concatenate([zero, u_ref[rws[0, 0, k + 1]]], axis=0).astype(BF16)
-            pair = jnp.concatenate([u0, u1], axis=1)
-            a = blk[0, 0, pl.ds(k, 2)].reshape(256, 128)
-            prods.append(jnp.dot(pair, a, preferred_element_type=F32))
-        for p in range(UNROLL):
-            k = (g * UNROLL + p) * 2
-            c0 = jnp.where(k < count, cls[0, 0, k], spare)
-            acc_ref[c0] += prods[p][:8]
-            c1 = jnp.where(k + 1 < count, cls[0, 0, k + 1], spare)
-            acc_ref[c1] += prods[p][8:]
-        return carry
-
-    step = 2 * UNROLL
-    lax.fori_loop(0, (count + step - 1) // step, group, 0)
+    for k in range(0, blk.shape[0], 2):
+        u0 = jnp.concatenate([u_ref[rws[0, 0, k]], zero], axis=0).astype(BF16)
+        u1 = jnp.concatenate([zero, u_ref[rws[0, 0, k + 1]]], axis=0).astype(BF16)
+        a = blk[k : k + 2].reshape(256, 128)
+        prod = jnp.dot(jnp.concatenate([u0, u1], axis=1), a, preferred_element_type=F32)
+        acc_ref[jnp.where(k < count, cls[0, 0, k], spare)] += prod[:8]
+        acc_ref[jnp.where(k + 1 < count, cls[0, 0, k + 1], spare)] += prod[8:]
 
 
 def column(ref):
@@ -119,9 +94,43 @@
         out_ref[(1 - row) * half + b] = other[:, b * 128 : (b + 1) * 128]
 
 
-def first_forward(rws, cls, cnt, alpha, blk, own, other, u_piece, out, v_out, acc):
+def first_forward(
+    alpha_hbm, rws_hbm, cls_hbm, cnt_hbm, blk_hbm, own_hbm, other_hbm, u_hbm,
+    out, v_out, blk,
+    alpha, rws, cls, cnt, own, other, u_piece, acc, small_sems, sems,
+):
+    small = [
+        pltpu.make_async_copy(src, dst, small_sems.at[i])
+        for i, (src, dst) in enumerate(
+            (
+                (rws_hbm, rws),
+                (cls_hbm, cls),
+                (cnt_hbm, cnt),
+                (own_hbm, own),
+                (other_hbm, other),
+                (alpha_hbm, alpha),
+                (u_hbm, u_piece),
+            )
+        )
+    ]
+    chunk = blk.shape[0] // sems.shape[0]
+    large = [
+        pltpu.make_async_copy(
+            blk_hbm.at[0, 0, pl.ds(i * chunk, chunk)], blk.at[pl.ds(i * chunk, chunk)], sems.at[i]
+        )
+        for i in range(sems.shape[0])
+    ]
+    for copy in small + large:
+        copy.start()
+    for copy in small:
+        copy.wait()
     place_halves(own, other, v_out)
-    forward(blk, rws, cls, cnt, v_out, acc)
+
+    def ready(k):
+        if k % chunk == 0:
+            large[k // chunk].wait()
+
+    forward(blk, rws, cls, cnt, v_out, acc, ready)
     pieces = u_piece.shape[1] // 128
     base = lax.axis_index("col") * pieces
     a = column(alpha)
@@ -181,7 +190,7 @@
         u_piece[b] = upd[base + b]
 
 
-def last_cells(total_rays, own, other, v_old, alpha, sq_out, vupd, beta_out):
+def last_cells(total_rays, own, other, v_old, alpha, sq, vupd, beta_out):
     cells = v_old.shape[0]
     beta = jnp.sqrt((own[cells] + other[cells]) / total_rays + EPS)
     beta_out[...] = beta
@@ -189,9 +198,7 @@
     scale = beta / alpha[...]
     for b in range(cells):
         vupd[b] = (own[b] + other[b]) * inv - scale * v_old[b]
-    sq = squares(vupd, cells)
-    for c in range(sq_out.shape[0]):
-        sq_out[c] = sq
+    sq[...] = squares(vupd, cells)
 
 
 def finish(
@@ -199,6 +206,7 @@
     phibar_in,
     rhobar_in,
     sq,
+    sq_other,
     v1,
     v2,
     u_piece,
@@ -213,9 +221,7 @@
     w_out,
     scalars,
 ):
-    total = sq[0]
-    for c in range(1, sq.shape[0]):
-        total = total + sq[c]
+    total = jnp.where(lax.axis_index("row") == 1, sq[...], sq_other[...])
     alpha2 = jnp.sqrt(total / total_cells + EPS)
     phibar, rhobar = column(phibar_in), column(rhobar_in)
     steps = []
@@ -260,6 +266,15 @@
         x = (x.astype(F32) + y.astype(F32)).astype(BF16)
 
 
+def last_sum(x):
+    n = lax.axis_size("col")
+    m = 1
+    while m < n:
+        x = x + lax.ppermute(x, ("row", "col"), [(n + i, n + (i ^ m)) for i in range(n)])
+        m *= 2
+    return x, lax.ppermute(x, "row", [(1, 0)])
+
+
 def body(
     blocks, block_rows, block_cols, counts, u_rays, v_cells, x_cells, w_cells, alpha, phibar, rhobar
 ):
@@ -276,44 +291,60 @@
     ray_acc = pltpu.VMEM((rays + 1, 8, 128), F32)
     cell_acc = pltpu.VMEM((cells + 1, 8, 128), F32)
 
-    part, v0 = call(
+    slots = blocks.shape[2]
+    part, v0, blk = call(
         first_forward,
-        (shape(rays // 2, 16, 128, dtype=BF16), shape(cells, 8, 128)),
-        listed + [SMEM] + [VMEM] * 4,
-        [ray_acc],
-    )(*where, alpha, blocks, v_cells, other_core(v_cells), u_rays)
+        (
+            shape(rays // 2, 16, 128, dtype=BF16),
+            shape(cells, 8, 128),
+            shape(slots, 128, 128, dtype=BF16),
+        ),
+        [HBM] * 8,
+        [
+            pltpu.SMEM(alpha.shape, F32),
+            pltpu.SMEM(block_rows.shape, jnp.int32),
+            pltpu.SMEM(block_cols.shape, jnp.int32),
+            pltpu.SMEM(counts.shape, jnp.int32),
+            pltpu.VMEM(v_cells.shape, F32),
+            pltpu.VMEM(v_cells.shape, F32),
+            pltpu.VMEM(u_rays.shape, F32),
+            ray_acc,
+            pltpu.SemaphoreType.DMA((7,)),
+            pltpu.SemaphoreType.DMA((8,)),
+        ],
+    )(alpha, *where, blocks, v_cells, other_core(v_cells), u_rays)
     sum0, sum1 = column_sum(part)
     upd1, message = call(
         first_backward,
         (shape(rays, 8, 128), shape(cells + 1, 8, 128)),
         listed + [VMEM] * 3,
         [cell_acc],
-    )(*where, blocks, sum0, sum1)
+    )(*where, blk, sum0, sum1)
     part, v1, beta1 = call(
         functools.partial(next_forward, total_rays),
         (shape(rays // 2 + 1, 16, 128, dtype=BF16), shape(cells, 8, 128), shape(8, 128)),
         listed + [VMEM] * 4,
         [ray_acc],
-    )(*where, blocks, message, other_core(message), v0)
+    )(*where, blk, message, other_core(message), v0)
     sum0, sum1 = column_sum(part)
     message, u_piece, alpha1 = call(
         functools.partial(next_backward, total_cells, pieces),
         (shape(cells + 1, 8, 128), shape(pieces, 8, 128), shape(8, 128)),
         listed + [VMEM] * 5,
         [pltpu.VMEM((rays, 8, 128), F32), cell_acc],
-    )(*where, blocks, sum0, sum1, upd1, beta1)
+    )(*where, blk, sum0, sum1, upd1, beta1)
     sq, v2, beta2 = call(
         functools.partial(last_cells, total_rays),
-        (shape(n_col, 8, 128), shape(cells, 8, 128), shape(8, 128)),
+        (shape(8, 128), shape(cells, 8, 128), shape(8, 128)),
         [VMEM] * 4,
     )(message, other_core(message), v1, alpha1)
-    sq = lax.all_to_all(sq, "col", 0, 0, tiled=True)
+    sq, sq_other = last_sum(sq)
     flat = shape(*v_cells.shape)
     return call(
         functools.partial(finish, total_cells),
         (shape(*u_rays.shape), flat, flat, flat, shape(3, 8)),
-        [SMEM] * 2 + [VMEM] * 9,
-    )(phibar, rhobar, sq, v1, v2, u_piece, x_cells, w_cells, beta1, alpha1, beta2)
+        [SMEM] * 2 + [VMEM] * 10,
+    )(phibar, rhobar, sq, sq_other, v1, v2, u_piece, x_cells, w_cells, beta1, alpha1, beta2)
 
 
 def solution(mesh):

time: 76.1 us -> 72.4 us (0.951)
  waiting for transfers between devices: 26.7 us -> 43 us
  blocking collectives: 12.8 us -> 0 us
  Pallas kernels: 13.4 us -> 9.35 us
  local copies, waits for them, and re-layouts: 5.64 us -> 3.46 us
  starting transfers between devices: 15.8 us -> 14.6 us
    all_to_all x1 -> x0, blocking collectives: 12.8 us -> none  [body(): sq = lax.all_to_all(sq, 'col', 0, 0, tiled=True)]
    ppermute x0 -> x4, waiting for transfers between devices: none -> 12.7 us  [the longest x1 12.7 us: last_sum(): return (x, lax.ppermute(x, 'row', [(1, 0)]))]
    ppermute x6, starting transfers between devices: 15.3 us -> 10.7 us  [column_sum(): y = lax.ppermute(x, 'col', [(i, i ^ m) for i in range(n)])]
    ppermute x6, waiting for transfers between devices: 23.8 us -> 27.5 us  [column_sum(): y = lax.ppermute(x, 'col', [(i, i ^ m) for i in range(n)])]
    ppermute x0 -> x4, starting transfers between devices: none -> 3.27 us  [the longest x3 1.98 us: last_sum(): lax.ppermute(x, ('row', 'col'), [(n + i, n + (i ^ m)) for i in range(n)])]
    unnamed x22, local copies, waits for them, and re-layouts: 5.64 us -> 3.46 us
    pallas_call x1, Pallas kernels: 2.94 us -> 1.48 us  [body(): call(functools.partial(next_backward, total_cells, pieces), (shape(cells...]
    pallas_call x1, Pallas kernels: 2.85 us -> 1.4 us  [body(): call(first_backward, (shape(rays, 8, 128), shape(cells + 1, 8, 128)), lis...]
  transfers between devices with their start and end apart: 9 -> 13, of which waited for: 9 -> 10; matrix products, arithmetic and copies ran while one was open for 0% -> 0% of each run, Pallas kernels for 0% -> 0%
where the time goes in v2:
time: 72.4 us; the launch traced here: 72 us
  waiting for transfers between devices  43 us (59%)
  starting transfers between devices  14.6 us (20%)
  Pallas kernels  9.35 us (13%)
  local copies, waits for them, and re-layouts  3.46 us (5%)
  between operations  1.46 us (2%)
    ppermute x6, waiting for transfers between devices, column_sum(): y = lax.ppermute(x, 'col', [(i, i ^ m) for i in range(n)])  27.5 us
    ppermute x1, waiting for transfers between devices, last_sum(): return (x, lax.ppermute(x, 'row', [(1, 0)]))  12.7 us
    ppermute x6, starting transfers between devices, column_sum(): y = lax.ppermute(x, 'col', [(i, i ^ m) for i in range(n)])  10.7 us
    unnamed x22, local copies, waits for them, and re-layouts  3.46 us
    pallas_call x1, Pallas kernels, body(): call(first_forward, (shape(rays // 2, 16, 128, dtype=BF16), shape(cells,...  3.36 us
    ppermute x3, waiting for transfers between devices, other_core(): return lax.ppermute(x, 'row', [(0, 1), (1, 0)])  2.8 us
    ppermute x3, starting transfers between devices, last_sum(): lax.ppermute(x, ('row', 'col'), [(n + i, n + (i ^ m)) for i in range(n)])  1.98 us
    pallas_call x1, Pallas kernels, body(): call(functools.partial(next_forward, total_rays), (shape(rays // 2 + 1, 1...  1.79 us
  transfers between devices with their start and end apart: 13, of which 10 were waited for; matrix products, arithmetic and copies ran while one was open for 0% of the time, Pallas kernels for 0%

profile of v2, /device:TPU:0, one launch (start us, length us, event | category | flops | bytes accessed | tf_op | source)
XLA Modules:
  0.0 72.0 jit_solution(3768852996528635640)
XLA Ops:
  0.6 0.0 copy-start.7
  0.6 0.0 copy-start.5
  0.7 0.5 collective-permute-start
  1.8 0.4 collective-permute-done.other_hbm
  2.2 0.0 copy-start
  2.2 0.8 %copy-done = f32[8,1024]{1,0:T(8,128)S(1)} copy-done((f32[8,1024]{1,0:T(8,128)S(1)}, f32[8,1024]{1,0:T(8,128)}, u32[]{:S(2)}) %copy-start) | copy-done | bytes 32792
  3.0 0.0 copy-start.1
  3.0 0.7 copy-done.1
  3.7 0.0 copy-start.4
  3.7 0.7 copy-done.4
  4.4 0.7 copy-done.6
  5.0 0.7 copy-done.10
  5.7 3.4 %shard_map.146 = (bf16[32,16,128]{2,1,0:T(8,128)(2,1)S(1)}, f32[8,8,128]{2,1,0:T(8,128)S(1)}, bf16[128,128,128]{2,1,0:T(8,128)(2,1)S(1)}) custom-call(f32[8]{0:T(128)S(1)} %copy-done.10, s32[1,1,128]{2,1,0:T(1,128)S(1)} %copy-done.4, s32[1,1,128]{2,1,0:T(1,128)S(1)} %copy-done.6, s32[1,1]{1,0:T(1,128)S(6)} %copy.16.cnt_hbm.cnt, ...), custom_call_target="tpu_custom_call" | custom-call | tf_op jit(solution)/shard_map/pallas_call | solution.py:295
  9.0 2.9 %collective-permute-start.1 = (bf16[32,16,128]{2,1,0:T(8,128)(2,1)S(1)}, bf16[32,16,128]{2,1,0:T(8,128)(2,1)S(1)}, u32[]{:S(2)}, u32[]{:S(2)}) collective-permute-start(bf16[32,16,128]{2,1,0:T(8,128)(2,1)S(1)} %get-tuple-element.20), channel_id=1, source_target_pairs={{0,1},{1,0},{2,3},{3,2},{4,5},{5,4},{6,7},{7,6},{8,9},{9,8},{10,11... | collective-permute-start | bytes 393224 | tf_op jit(solution)/shard_map/ppermute | solution.py:262
  11.9 3.8 %collective-permute-done.1 = bf16[32,16,128]{2,1,0:T(8,128)(2,1)S(1)} collective-permute-done((bf16[32,16,128]{2,1,0:T(8,128)(2,1)S(1)}, bf16[32,16,128]{2,1,0:T(8,128)(2,1)S(1)}, u32[]{:S(2)}, u32[]{:S(2)}) %collective-permute-start.1) | collective-permute-done | bytes 131104 | tf_op jit(solution)/shard_map/ppermute | solution.py:262
  15.8 1.9 %collective-permute-start.2 = (bf16[32,16,128]{2,1,0:T(8,128)(2,1)S(1)}, bf16[32,16,128]{2,1,0:T(8,128)(2,1)S(1)}, u32[]{:S(2)}, u32[]{:S(2)}) collective-permute-start(bf16[32,16,128]{2,1,0:T(8,128)(2,1)S(1)} %add_convert_fusion.3), channel_id=1, source_target_pairs={{0,2},{1,3},{2,0},{3,1},{4,6},{5,7},{6,4},{7,5},{8,10},{9,11},{10,... | collective-permute-start | bytes 393224 | tf_op jit(solution)/shard_map/ppermute | solution.py:262
  17.7 3.3 %collective-permute-done.2 = bf16[32,16,128]{2,1,0:T(8,128)(2,1)S(1)} collective-permute-done((bf16[32,16,128]{2,1,0:T(8,128)(2,1)S(1)}, bf16[32,16,128]{2,1,0:T(8,128)(2,1)S(1)}, u32[]{:S(2)}, u32[]{:S(2)}) %collective-permute-start.2) | collective-permute-done | bytes 131104 | tf_op jit(solution)/shard_map/ppermute | solution.py:262
  21.0 2.8 %collective-permute-start.3 = (bf16[32,16,128]{2,1,0:T(8,128)(2,1)S(1)}, bf16[32,16,128]{2,1,0:T(8,128)(2,1)S(1)}, u32[]{:S(2)}, u32[]{:S(2)}) collective-permute-start(bf16[32,16,128]{2,1,0:T(8,128)(2,1)S(1)} %add_convert_fusion.2.sum0), channel_id=1, source_target_pairs={{0,4},{1,5},{2,6},{3,7},{4,0},{5,1},{6,2},{7,3},{8,12},{9,13},{10,... | collective-permute-start | bytes 393224 | tf_op jit(solution)/shard_map/ppermute | solution.py:262
  23.8 5.2 %collective-permute-done.3.sum1 = bf16[32,16,128]{2,1,0:T(8,128)(2,1)S(1)} collective-permute-done((bf16[32,16,128]{2,1,0:T(8,128)(2,1)S(1)}, bf16[32,16,128]{2,1,0:T(8,128)(2,1)S(1)}, u32[]{:S(2)}, u32[]{:S(2)}) %collective-permute-start.3) | collective-permute-done | bytes 131104 | tf_op jit(solution)/shard_map/ppermute | solution.py:262
  29.0 0.0 copy-done.7
  29.0 0.0 copy-done.5
  29.0 1.4 %shard_map.147 = (f32[64,8,128]{2,1,0:T(8,128)S(1)}, f32[9,8,128]{2,1,0:T(8,128)S(1)}) custom-call(s32[1,1,128]{2,1,0:T(1,128)S(1)} %copy-done.5, s32[1,1,128]{2,1,0:T(1,128)S(1)} %copy-done.7, s32[1,1]{1,0:T(1,128)S(6)} %copy.16.cnt_hbm.cnt, bf16[128,128,128]{2,1,0:T(8,128)(2,1)S(1)} %get-tuple-element.19.blk, ...), custom_call_target="tpu_custom_call" | custom-call | tf_op jit(solution)/shard_map/pallas_call | solution.py:317
  30.4 0.1 collective-permute-start.4
  30.5 1.2 %collective-permute-done.4.other = f32[9,8,128]{2,1,0:T(8,128)S(1)} collective-permute-done((f32[9,8,128]{2,1,0:T(8,128)S(1)}, f32[9,8,128]{2,1,0:T(8,128)S(1)}, u32[]{:S(2)}, u32[]{:S(2)}) %collective-permute-start.4) | collective-permute-done | bytes 36896 | tf_op jit(solution)/shard_map/ppermute | solution.py:255
  31.7 1.8 %shard_map.148 = (bf16[33,16,128]{2,1,0:T(8,128)(2,1)S(1)}, f32[8,8,128]{2,1,0:T(8,128)S(1)}, f32[8,128]{1,0:T(8,128)S(1)}) custom-call(s32[1,1,128]{2,1,0:T(1,128)S(1)} %copy-done.5, s32[1,1,128]{2,1,0:T(1,128)S(1)} %copy-done.7, s32[1,1]{1,0:T(1,128)S(6)} %copy.16.cnt_hbm.cnt, bf16[128,128,128]{2,1,0:T(8,128)(2,1)S(1)} %get-tuple-element.19.blk, ...), custom_call_target="tpu_custom_call" | custom-call | tf_op jit(solution)/shard_map/pallas_call | solution.py:323
  33.5 1.1 %collective-permute-start.5 = (bf16[33,16,128]{2,1,0:T(8,128)(2,1)S(1)}, bf16[33,16,128]{2,1,0:T(8,128)(2,1)S(1)}, u32[]{:S(2)}, u32[]{:S(2)}) collective-permute-start(bf16[33,16,128]{2,1,0:T(8,128)(2,1)S(1)} %get-tuple-element.23), channel_id=1, source_target_pairs={{0,1},{1,0},{2,3},{3,2},{4,5},{5,4},{6,7},{7,6},{8,9},{9,8},{10,11... | collective-permute-start | bytes 405512 | tf_op jit(solution)/shard_map/ppermute | solution.py:262
  34.6 4.6 %collective-permute-done.5 = bf16[33,16,128]{2,1,0:T(8,128)(2,1)S(1)} collective-permute-done((bf16[33,16,128]{2,1,0:T(8,128)(2,1)S(1)}, bf16[33,16,128]{2,1,0:T(8,128)(2,1)S(1)}, u32[]{:S(2)}, u32[]{:S(2)}) %collective-permute-start.5) | collective-permute-done | bytes 135200 | tf_op jit(solution)/shard_map/ppermute | solution.py:262
  39.3 0.3 collective-permute-start.6
  39.6 4.7 %collective-permute-done.6 = bf16[33,16,128]{2,1,0:T(8,128)(2,1)S(1)} collective-permute-done((bf16[33,16,128]{2,1,0:T(8,128)(2,1)S(1)}, bf16[33,16,128]{2,1,0:T(8,128)(2,1)S(1)}, u32[]{:S(2)}, u32[]{:S(2)}) %collective-permute-start.6) | collective-permute-done | bytes 135200 | tf_op jit(solution)/shard_map/ppermute | solution.py:262
  44.4 1.7 %collective-permute-start.7 = (bf16[33,16,128]{2,1,0:T(8,128)(2,1)S(1)}, bf16[33,16,128]{2,1,0:T(8,128)(2,1)S(1)}, u32[]{:S(2)}, u32[]{:S(2)}) collective-permute-start(bf16[33,16,128]{2,1,0:T(8,128)(2,1)S(1)} %add_convert_fusion.sum0), channel_id=1, source_target_pairs={{0,4},{1,5},{2,6},{3,7},{4,0},{5,1},{6,2},{7,3},{8,12},{9,13},{10,... | collective-permute-start | bytes 405512 | tf_op jit(solution)/shard_map/ppermute | solution.py:262
  46.0 5.9 %collective-permute-done.7.sum1 = bf16[33,16,128]{2,1,0:T(8,128)(2,1)S(1)} collective-permute-done((bf16[33,16,128]{2,1,0:T(8,128)(2,1)S(1)}, bf16[33,16,128]{2,1,0:T(8,128)(2,1)S(1)}, u32[]{:S(2)}, u32[]{:S(2)}) %collective-permute-start.7) | collective-permute-done | bytes 135200 | tf_op jit(solution)/shard_map/ppermute | solution.py:262
  51.9 1.5 %shard_map.149 = (f32[9,8,128]{2,1,0:T(8,128)S(1)}, f32[8,8,128]{2,1,0:T(8,128)S(1)}, f32[8,128]{1,0:T(8,128)S(1)}) custom-call(s32[1,1,128]{2,1,0:T(1,128)S(1)} %copy-done.5, s32[1,1,128]{2,1,0:T(1,128)S(1)} %copy-done.7, s32[1,1]{1,0:T(1,128)S(6)} %copy.16.cnt_hbm.cnt, bf16[128,128,128]{2,1,0:T(8,128)(2,1)S(1)} %get-tuple-element.19.blk, ...), custom_call_target="tpu_custom_call" | custom-call | tf_op jit(solution)/shard_map/pallas_call | solution.py:330
  53.4 0.1 collective-permute-start.8
  53.5 1.2 %collective-permute-done.8.other = f32[9,8,128]{2,1,0:T(8,128)S(1)} collective-permute-done((f32[9,8,128]{2,1,0:T(8,128)S(1)}, f32[9,8,128]{2,1,0:T(8,128)S(1)}, u32[]{:S(2)}, u32[]{:S(2)}) %collective-permute-start.8) | collective-permute-done | bytes 36896 | tf_op jit(solution)/shard_map/ppermute | solution.py:255
  54.7 0.1 shard_map.150
  54.8 0.7 collective-permute-start.9
  55.5 0.0 collective-permute-done.9
  55.5 0.7 collective-permute-start.10
  56.1 0.0 collective-permute-done.10
  56.2 0.7 collective-permute-start.11
  56.8 0.0 collective-permute-done.11
  56.9 1.3 %collective-permute-start.12 = (f32[8,128]{1,0:T(8,128)S(1)}, f32[8,128]{1,0:T(8,128)S(1)}, u32[]{:S(2)}, u32[]{:S(2)}) collective-permute-start(f32[8,128]{1,0:T(8,128)S(1)} %add.27.sq), channel_id=1, source_target_pairs={{8,0},{9,1},{10,2},{11,3},{12,4},{13,5},{14,6},{15,7},{24,16},{25,... | collective-permute-start | bytes 12296 | tf_op jit(solution)/shard_map/ppermute | solution.py:275
  58.2 12.7 %collective-permute-done.12.sq_other = f32[8,128]{1,0:T(8,128)S(1)} collective-permute-done((f32[8,128]{1,0:T(8,128)S(1)}, f32[8,128]{1,0:T(8,128)S(1)}, u32[]{:S(2)}, u32[]{:S(2)}) %collective-permute-start.12) | collective-permute-done | bytes 4128 | tf_op jit(solution)/shard_map/ppermute | solution.py:275
  70.8 0.0 copy-done.2
  70.8 0.0 copy-done.3
  70.8 0.0 copy-done.8
  70.8 0.0 copy-done.9
  70.8 1.2 %shard_map.151 = (f32[8,1024]{1,0:T(8,128)}, f32[8,512]{1,0:T(8,128)}, f32[8,512]{1,0:T(8,128)}, f32[8,512]{1,0:T(8,128)}, f32[3,8]{1,0:T(4,128)}) custom-call(f32[8]{0:T(128)S(1)} %copy-done.8, f32[8]{0:T(128)S(1)} %copy-done.9, f32[8,128]{1,0:T(8,128)S(1)} %add.27.sq, f32[8,128]{1,0:T(8,128)S(1)} %collective-permute-done.12.sq_other, ...), custom_call_target="tpu_custom_call" | custom-call | tf_op jit(solution)/shard_map/pallas_call | solution.py:343
  (13 shorter events, 0.2 us)
Async XLA Ops:
  0.6 28.3 %copy-start.7 = (s32[1,1,128]{2,1,0:T(1,128)S(1)}, s32[1,1,128]{2,1,0:T(1,128)}, u32[]{:S(2)}) copy-start(s32[1,1,128]{2,1,0:T(1,128)} %cls.5) | copy-start | bytes 1540
  0.6 28.3 %copy-start.5 = (s32[1,1,128]{2,1,0:T(1,128)S(1)}, s32[1,1,128]{2,1,0:T(1,128)}, u32[]{:S(2)}) copy-start(s32[1,1,128]{2,1,0:T(1,128)} %rws.5) | copy-start | bytes 1540
  0.7 1.6 %collective-permute-start = (f32[8,512]{1,0:T(8,128)}, f32[8,512]{1,0:T(8,128)S(1)}, u32[]{:S(2)}, u32[]{:S(2)}) collective-permute-start(f32[8,512]{1,0:T(8,128)} %own_hbm.1), channel_id=1, source_target_pairs={{0,8},{8,0},{1,9},{9,1},{2,10},{10,2},{3,11},{11,3},{4,12},{12,4},... | collective-permute-start | bytes 49160 | tf_op jit(solution)/shard_map/ppermute | solution.py:255
  2.2 0.8 %copy-start = (f32[8,1024]{1,0:T(8,128)S(1)}, f32[8,1024]{1,0:T(8,128)}, u32[]{:S(2)}) copy-start(f32[8,1024]{1,0:T(8,128)} %u_hbm.1) | copy-start | bytes 98308
  3.0 0.7 copy-start.1
  3.7 0.7 copy-start.4
  4.4 0.7 copy-start.6
  5.0 0.7 copy-start.10
  9.0 6.7 %collective-permute-start.1 = (bf16[32,16,128]{2,1,0:T(8,128)(2,1)S(1)}, bf16[32,16,128]{2,1,0:T(8,128)(2,1)S(1)}, u32[]{:S(2)}, u32[]{:S(2)}) collective-permute-start(bf16[32,16,128]{2,1,0:T(8,128)(2,1)S(1)} %get-tuple-element.20), channel_id=1, source_target_pairs={{0,1},{1,0},{2,3},{3,2},{4,5},{5,4},{6,7},{7,6},{8,9},{9,8},{10,11... | collective-permute-start | bytes 393224 | tf_op jit(solution)/shard_map/ppermute | solution.py:262
  15.8 5.1 %collective-permute-start.2 = (bf16[32,16,128]{2,1,0:T(8,128)(2,1)S(1)}, bf16[32,16,128]{2,1,0:T(8,128)(2,1)S(1)}, u32[]{:S(2)}, u32[]{:S(2)}) collective-permute-start(bf16[32,16,128]{2,1,0:T(8,128)(2,1)S(1)} %add_convert_fusion.3), channel_id=1, source_target_pairs={{0,2},{1,3},{2,0},{3,1},{4,6},{5,7},{6,4},{7,5},{8,10},{9,11},{10,... | collective-permute-start | bytes 393224 | tf_op jit(solution)/shard_map/ppermute | solution.py:262
  21.0 8.0 %collective-permute-start.3 = (bf16[32,16,128]{2,1,0:T(8,128)(2,1)S(1)}, bf16[32,16,128]{2,1,0:T(8,128)(2,1)S(1)}, u32[]{:S(2)}, u32[]{:S(2)}) collective-permute-start(bf16[32,16,128]{2,1,0:T(8,128)(2,1)S(1)} %add_convert_fusion.2.sum0), channel_id=1, source_target_pairs={{0,4},{1,5},{2,6},{3,7},{4,0},{5,1},{6,2},{7,3},{8,12},{9,13},{10,... | collective-permute-start | bytes 393224 | tf_op jit(solution)/shard_map/ppermute | solution.py:262
  30.4 1.3 %collective-permute-start.4 = (f32[9,8,128]{2,1,0:T(8,128)S(1)}, f32[9,8,128]{2,1,0:T(8,128)S(1)}, u32[]{:S(2)}, u32[]{:S(2)}) collective-permute-start(f32[9,8,128]{2,1,0:T(8,128)S(1)} %get-tuple-element.21.own), channel_id=1, source_target_pairs={{0,8},{8,0},{1,9},{9,1},{2,10},{10,2},{3,11},{11,3},{4,12},{12,4},... | collective-permute-start | bytes 110600 | tf_op jit(solution)/shard_map/ppermute | solution.py:255
  31.7 39.2 %copy-start.2 = (f32[8,512]{1,0:T(8,128)S(1)}, f32[8,512]{1,0:T(8,128)}, u32[]{:S(2)}) copy-start(f32[8,512]{1,0:T(8,128)} %x_in.1) | copy-start | bytes 49156
  31.7 39.2 %copy-start.3 = (f32[8,512]{1,0:T(8,128)S(1)}, f32[8,512]{1,0:T(8,128)}, u32[]{:S(2)}) copy-start(f32[8,512]{1,0:T(8,128)} %w_in.1) | copy-start | bytes 49156
  31.7 39.2 %copy-start.8 = (f32[8]{0:T(128)S(1)}, f32[8]{0:T(128)}, u32[]{:S(2)}) copy-start(f32[8]{0:T(128)} %phibar_in.1) | copy-start | bytes 100
  31.7 39.2 %copy-start.9 = (f32[8]{0:T(128)S(1)}, f32[8]{0:T(128)}, u32[]{:S(2)}) copy-start(f32[8]{0:T(128)} %rhobar_in.1) | copy-start | bytes 100
  33.5 5.7 %collective-permute-start.5 = (bf16[33,16,128]{2,1,0:T(8,128)(2,1)S(1)}, bf16[33,16,128]{2,1,0:T(8,128)(2,1)S(1)}, u32[]{:S(2)}, u32[]{:S(2)}) collective-permute-start(bf16[33,16,128]{2,1,0:T(8,128)(2,1)S(1)} %get-tuple-element.23), channel_id=1, source_target_pairs={{0,1},{1,0},{2,3},{3,2},{4,5},{5,4},{6,7},{7,6},{8,9},{9,8},{10,11... | collective-permute-start | bytes 405512 | tf_op jit(solution)/shard_map/ppermute | solution.py:262
  39.3 5.1 %collective-permute-start.6 = (bf16[33,16,128]{2,1,0:T(8,128)(2,1)S(1)}, bf16[33,16,128]{2,1,0:T(8,128)(2,1)S(1)}, u32[]{:S(2)}, u32[]{:S(2)}) collective-permute-start(bf16[33,16,128]{2,1,0:T(8,128)(2,1)S(1)} %add_convert_fusion.1), channel_id=1, source_target_pairs={{0,2},{1,3},{2,0},{3,1},{4,6},{5,7},{6,4},{7,5},{8,10},{9,11},{10,... | collective-permute-start | bytes 405512 | tf_op jit(solution)/shard_map/ppermute | solution.py:262
  44.4 7.6 %collective-permute-start.7 = (bf16[33,16,128]{2,1,0:T(8,128)(2,1)S(1)}, bf16[33,16,128]{2,1,0:T(8,128)(2,1)S(1)}, u32[]{:S(2)}, u32[]{:S(2)}) collective-permute-start(bf16[33,16,128]{2,1,0:T(8,128)(2,1)S(1)} %add_convert_fusion.sum0), channel_id=1, source_target_pairs={{0,4},{1,5},{2,6},{3,7},{4,0},{5,1},{6,2},{7,3},{8,12},{9,13},{10,... | collective-permute-start | bytes 405512 | tf_op jit(solution)/shard_map/ppermute | solution.py:262
  53.4 1.3 %collective-permute-start.8 = (f32[9,8,128]{2,1,0:T(8,128)S(1)}, f32[9,8,128]{2,1,0:T(8,128)S(1)}, u32[]{:S(2)}, u32[]{:S(2)}) collective-permute-start(f32[9,8,128]{2,1,0:T(8,128)S(1)} %get-tuple-element.26.own), channel_id=1, source_target_pairs={{0,8},{8,0},{1,9},{9,1},{2,10},{10,2},{3,11},{11,3},{4,12},{12,4},... | collective-permute-start | bytes 110600 | tf_op jit(solution)/shard_map/ppermute | solution.py:255
  54.8 0.7 collective-permute-start.9
  55.5 0.7 collective-permute-start.10
  56.2 0.7 collective-permute-start.11
  56.9 14.0 %collective-permute-start.12 = (f32[8,128]{1,0:T(8,128)S(1)}, f32[8,128]{1,0:T(8,128)S(1)}, u32[]{:S(2)}, u32[]{:S(2)}) collective-permute-start(f32[8,128]{1,0:T(8,128)S(1)} %add.27.sq), channel_id=1, source_target_pairs={{8,0},{9,1},{10,2},{11,3},{12,4},{13,5},{14,6},{15,7},{24,16},{25,... | collective-permute-start | bytes 12296 | tf_op jit(solution)/shard_map/ppermute | solution.py:275

commit v3 on v2

--- a/solution.py
+++ b/solution.py
@@ -33,7 +33,7 @@
 
 def forward(blk, rws, cls, cnt, v_ref, acc_ref, ready=None):
     spare = acc_ref.shape[0] - 1
-    count = cnt[0, 0]
+    count = cnt[0]
     acc_ref[...] = jnp.zeros_like(acc_ref)
     for k in range(0, blk.shape[0], 2):
         if ready is not None:
@@ -49,7 +49,7 @@
 
 def backward(blk, rws, cls, cnt, u_ref, acc_ref):
     spare = acc_ref.shape[0] - 1
-    count = cnt[0, 0]
+    count = cnt[0]
     acc_ref[...] = jnp.zeros_like(acc_ref)
     zero = jnp.zeros((8, 128), F32)
     for k in range(0, blk.shape[0], 2):
@@ -94,43 +94,15 @@
         out_ref[(1 - row) * half + b] = other[:, b * 128 : (b + 1) * 128]
 
 
-def first_forward(
-    alpha_hbm, rws_hbm, cls_hbm, cnt_hbm, blk_hbm, own_hbm, other_hbm, u_hbm,
-    out, v_out, blk,
-    alpha, rws, cls, cnt, own, other, u_piece, acc, small_sems, sems,
-):
-    small = [
-        pltpu.make_async_copy(src, dst, small_sems.at[i])
-        for i, (src, dst) in enumerate(
-            (
-                (rws_hbm, rws),
-                (cls_hbm, cls),
-                (cnt_hbm, cnt),
-                (own_hbm, own),
-                (other_hbm, other),
-                (alpha_hbm, alpha),
-                (u_hbm, u_piece),
-            )
-        )
-    ]
-    chunk = blk.shape[0] // sems.shape[0]
-    large = [
-        pltpu.make_async_copy(
-            blk_hbm.at[0, 0, pl.ds(i * chunk, chunk)], blk.at[pl.ds(i * chunk, chunk)], sems.at[i]
-        )
-        for i in range(sems.shape[0])
-    ]
-    for copy in small + large:
-        copy.start()
-    for copy in small:
-        copy.wait()
+def load(blk_hbm, blk, sem):
+    copy = pltpu.make_async_copy(blk_hbm.at[0, 0], blk, sem)
+    copy.start()
+    copy.wait()
+
+
+def first_forward(rws, cls, cnt, alpha, blk, own, other, u_piece, out, v_out, acc):
     place_halves(own, other, v_out)
-
-    def ready(k):
-        if k % chunk == 0:
-            large[k // chunk].wait()
-
-    forward(blk, rws, cls, cnt, v_out, acc, ready)
+    forward(blk, rws, cls, cnt, v_out, acc)
     pieces = u_piece.shape[1] // 128
     base = lax.axis_index("col") * pieces
     a = column(alpha)
@@ -206,7 +178,6 @@
     phibar_in,
     rhobar_in,
     sq,
-    sq_other,
     v1,
     v2,
     u_piece,
@@ -221,8 +192,7 @@
     w_out,
     scalars,
 ):
-    total = jnp.where(lax.axis_index("row") == 1, sq[...], sq_other[...])
-    alpha2 = jnp.sqrt(total / total_cells + EPS)
+    alpha2 = jnp.sqrt(sq[...] / total_cells + EPS)
     phibar, rhobar = column(phibar_in), column(rhobar_in)
     steps = []
     for beta, alpha in ((beta1[...], alpha1[...]), (beta2[...], alpha2)):
@@ -270,9 +240,10 @@
     n = lax.axis_size("col")
     m = 1
     while m < n:
-        x = x + lax.ppermute(x, ("row", "col"), [(n + i, n + (i ^ m)) for i in range(n)])
+        pairs = [(i + n * r, (i ^ m) + n * (1 - r)) for r in (0, 1) for i in range(n)]
+        x = x + lax.ppermute(x, ("row", "col"), pairs)
         m *= 2
-    return x, lax.ppermute(x, "row", [(1, 0)])
+    return x
 
 
 def body(
@@ -286,33 +257,24 @@
     cells = half * n_row
     total_rays = float(rays * 128 * n_row)
     total_cells = float(cells * 128 * n_col)
-    where = (block_rows, block_cols, counts)
+    where = (block_rows, block_cols, counts.reshape(1))
     listed = [SMEM] * 3
     ray_acc = pltpu.VMEM((rays + 1, 8, 128), F32)
     cell_acc = pltpu.VMEM((cells + 1, 8, 128), F32)
 
-    slots = blocks.shape[2]
-    part, v0, blk = call(
+    v_other = other_core(v_cells)
+    blk = call(
+        load,
+        shape(*blocks.shape[2:], dtype=BF16),
+        [HBM],
+        [pltpu.SemaphoreType.DMA],
+    )(blocks)
+    part, v0 = call(
         first_forward,
-        (
-            shape(rays // 2, 16, 128, dtype=BF16),
-            shape(cells, 8, 128),
-            shape(slots, 128, 128, dtype=BF16),
-        ),
-        [HBM] * 8,
-        [
-            pltpu.SMEM(alpha.shape, F32),
-            pltpu.SMEM(block_rows.shape, jnp.int32),
-            pltpu.SMEM(block_cols.shape, jnp.int32),
-            pltpu.SMEM(counts.shape, jnp.int32),
-            pltpu.VMEM(v_cells.shape, F32),
-            pltpu.VMEM(v_cells.shape, F32),
-            pltpu.VMEM(u_rays.shape, F32),
-            ray_acc,
-            pltpu.SemaphoreType.DMA((7,)),
-            pltpu.SemaphoreType.DMA((8,)),
-        ],
-    )(alpha, *where, blocks, v_cells, other_core(v_cells), u_rays)
+        (shape(rays // 2, 16, 128, dtype=BF16), shape(cells, 8, 128)),
+        listed + [SMEM] + [VMEM] * 4,
+        [ray_acc],
+    )(*where, alpha, blk, v_cells, v_other, u_rays)
     sum0, sum1 = column_sum(part)
     upd1, message = call(
         first_backward,
@@ -338,13 +300,13 @@
         (shape(8, 128), shape(cells, 8, 128), shape(8, 128)),
         [VMEM] * 4,
     )(message, other_core(message), v1, alpha1)
-    sq, sq_other = last_sum(sq)
+    sq = last_sum(sq)
     flat = shape(*v_cells.shape)
     return call(
         functools.partial(finish, total_cells),
         (shape(*u_rays.shape), flat, flat, flat, shape(3, 8)),
-        [SMEM] * 2 + [VMEM] * 10,
-    )(phibar, rhobar, sq, sq_other, v1, v2, u_piece, x_cells, w_cells, beta1, alpha1, beta2)
+        [SMEM] * 2 + [VMEM] * 9,
+    )(phibar, rhobar, sq, v1, v2, u_piece, x_cells, w_cells, beta1, alpha1, beta2)
 
 
 def solution(mesh):

time: 72.4 us -> 63.7 us (0.88)
  waiting for transfers between devices: 43 us -> 37.6 us
  local copies, waits for them, and re-layouts: 3.46 us -> 0.04 us
  Pallas kernels: 9.35 us -> 10.3 us
    ppermute x4 -> x3, waiting for transfers between devices: 12.7 us -> 7.46 us  [last_sum(): x = x + lax.ppermute(x, ('row', 'col'), pairs)]
    unnamed x22 -> x18, local copies, waits for them, and re-layouts: 3.46 us -> 0.04 us
    pallas_call x0 -> x1, Pallas kernels: none -> 2.23 us  [body(): call(load, shape(*blocks.shape[2:], dtype=BF16), [HBM], [pltpu.SemaphoreT...]
    pallas_call x1, Pallas kernels: 3.36 us -> 1.85 us  [body(): call(first_forward, (shape(rays // 2, 16, 128, dtype=BF16), shape(cells,...]
    ppermute x4 -> x3, starting transfers between devices: 3.27 us -> 2.54 us  [last_sum(): x = x + lax.ppermute(x, ('row', 'col'), pairs)]
  transfers between devices with their start and end apart: 13 -> 12, of which waited for: 10 -> 11; matrix products, arithmetic and copies ran while one was open for 0% -> 0% of each run, Pallas kernels for 0% -> 3%
where the time goes in v3:
time: 63.7 us; the launch traced here: 63.6 us
  waiting for transfers between devices  37.6 us (59%)
  starting transfers between devices  14 us (22%)
  Pallas kernels  10.3 us (16%)
  between operations  1.46 us (2%)
    ppermute x6, waiting for transfers between devices, column_sum(): y = lax.ppermute(x, 'col', [(i, i ^ m) for i in range(n)])  27.8 us
    ppermute x6, starting transfers between devices, column_sum(): y = lax.ppermute(x, 'col', [(i, i ^ m) for i in range(n)])  10.9 us
    ppermute x3, waiting for transfers between devices, last_sum(): x = x + lax.ppermute(x, ('row', 'col'), pairs)  7.46 us
    ppermute x3, starting transfers between devices, last_sum(): x = x + lax.ppermute(x, ('row', 'col'), pairs)  2.54 us
    ppermute x3, waiting for transfers between devices, other_core(): return lax.ppermute(x, 'row', [(0, 1), (1, 0)])  2.4 us
    pallas_call x1, Pallas kernels, body(): call(load, shape(*blocks.shape[2:], dtype=BF16), [HBM], [pltpu.SemaphoreT...  2.23 us
    pallas_call x1, Pallas kernels, body(): call(first_forward, (shape(rays // 2, 16, 128, dtype=BF16), shape(cells,...  1.85 us
    pallas_call x1, Pallas kernels, body(): call(functools.partial(next_forward, total_rays), (shape(rays // 2 + 1, 1...  1.83 us
  transfers between devices with their start and end apart: 12, of which 11 were waited for; matrix products, arithmetic and copies ran while one was open for 0% of the time, Pallas kernels for 3%

profile of v3, /device:TPU:0, one launch (start us, length us, event | category | flops | bytes accessed | tf_op | source)
XLA Modules:
  0.0 63.6 jit_solution(13799127292751172909)
XLA Ops:
  0.6 0.5 collective-permute-start
  1.8 0.0 copy-start
  1.8 0.0 copy-start.1
  1.8 0.0 copy-start.4
  1.8 0.0 copy-start.5
  1.8 0.0 copy-start.8
  1.9 2.2 %shard_map.146.blk = bf16[128,128,128]{2,1,0:T(8,128)(2,1)S(1)} custom-call(bf16[1,1,128,128,128]{4,3,2,1,0:T(8,128)(2,1)} %blk_hbm.1), custom_call_target="tpu_custom_call" | custom-call | tf_op jit(solution)/shard_map/pallas_call | solution.py:266
  4.1 0.0 collective-permute-done.other
  4.1 0.0 copy-done
  4.1 0.0 copy-done.1
  4.1 0.0 copy-done.4
  4.1 0.0 copy-done.5
  4.1 0.0 copy-done.8
  4.1 1.8 %shard_map.147 = (bf16[32,16,128]{2,1,0:T(8,128)(2,1)S(1)}, f32[8,8,128]{2,1,0:T(8,128)S(1)}) custom-call(s32[1,1,128]{2,1,0:T(1,128)S(1)} %copy-done.4, s32[1,1,128]{2,1,0:T(1,128)S(1)} %copy-done.5, s32[1]{0:T(128)} %bitcast.1.cnt, f32[8]{0:T(128)S(1)} %copy-done.8, bf16[128,128,128]{2,1,0:T(8,128)(2,1)S(1)} %shard_map.146.blk, f32[8,512]{1,0:T(8,128)S(1)} %copy-done.1, ...), custom_call_target="tpu_custom_call" | custom-call | tf_op jit(solution)/shard_map/pallas_call | solution.py:272
  6.0 2.6 %collective-permute-start.1 = (bf16[32,16,128]{2,1,0:T(8,128)(2,1)S(1)}, bf16[32,16,128]{2,1,0:T(8,128)(2,1)S(1)}, u32[]{:S(2)}, u32[]{:S(2)}) collective-permute-start(bf16[32,16,128]{2,1,0:T(8,128)(2,1)S(1)} %get-tuple-element.18), channel_id=1, source_target_pairs={{0,1},{1,0},{2,3},{3,2},{4,5},{5,4},{6,7},{7,6},{8,9},{9,8},{10,11... | collective-permute-start | bytes 393224 | tf_op jit(solution)/shard_map/ppermute | solution.py:232
  8.6 4.1 %collective-permute-done.1 = bf16[32,16,128]{2,1,0:T(8,128)(2,1)S(1)} collective-permute-done((bf16[32,16,128]{2,1,0:T(8,128)(2,1)S(1)}, bf16[32,16,128]{2,1,0:T(8,128)(2,1)S(1)}, u32[]{:S(2)}, u32[]{:S(2)}) %collective-permute-start.1) | collective-permute-done | bytes 131104 | tf_op jit(solution)/shard_map/ppermute | solution.py:232
  12.7 1.9 %collective-permute-start.2 = (bf16[32,16,128]{2,1,0:T(8,128)(2,1)S(1)}, bf16[32,16,128]{2,1,0:T(8,128)(2,1)S(1)}, u32[]{:S(2)}, u32[]{:S(2)}) collective-permute-start(bf16[32,16,128]{2,1,0:T(8,128)(2,1)S(1)} %add_convert_fusion.3), channel_id=1, source_target_pairs={{0,2},{1,3},{2,0},{3,1},{4,6},{5,7},{6,4},{7,5},{8,10},{9,11},{10,... | collective-permute-start | bytes 393224 | tf_op jit(solution)/shard_map/ppermute | solution.py:232
  14.6 3.4 %collective-permute-done.2 = bf16[32,16,128]{2,1,0:T(8,128)(2,1)S(1)} collective-permute-done((bf16[32,16,128]{2,1,0:T(8,128)(2,1)S(1)}, bf16[32,16,128]{2,1,0:T(8,128)(2,1)S(1)}, u32[]{:S(2)}, u32[]{:S(2)}) %collective-permute-start.2) | collective-permute-done | bytes 131104 | tf_op jit(solution)/shard_map/ppermute | solution.py:232
  18.1 2.7 %collective-permute-start.3 = (bf16[32,16,128]{2,1,0:T(8,128)(2,1)S(1)}, bf16[32,16,128]{2,1,0:T(8,128)(2,1)S(1)}, u32[]{:S(2)}, u32[]{:S(2)}) collective-permute-start(bf16[32,16,128]{2,1,0:T(8,128)(2,1)S(1)} %add_convert_fusion.2.sum0), channel_id=1, source_target_pairs={{0,4},{1,5},{2,6},{3,7},{4,0},{5,1},{6,2},{7,3},{8,12},{9,13},{10,... | collective-permute-start | bytes 393224 | tf_op jit(solution)/shard_map/ppermute | solution.py:232
  20.8 5.5 %collective-permute-done.3.sum1 = bf16[32,16,128]{2,1,0:T(8,128)(2,1)S(1)} collective-permute-done((bf16[32,16,128]{2,1,0:T(8,128)(2,1)S(1)}, bf16[32,16,128]{2,1,0:T(8,128)(2,1)S(1)}, u32[]{:S(2)}, u32[]{:S(2)}) %collective-permute-start.3) | collective-permute-done | bytes 131104 | tf_op jit(solution)/shard_map/ppermute | solution.py:232
  26.3 1.5 %shard_map.148 = (f32[64,8,128]{2,1,0:T(8,128)S(1)}, f32[9,8,128]{2,1,0:T(8,128)S(1)}) custom-call(s32[1,1,128]{2,1,0:T(1,128)S(1)} %copy-done.4, s32[1,1,128]{2,1,0:T(1,128)S(1)} %copy-done.5, s32[1]{0:T(128)} %bitcast.2.cnt, bf16[128,128,128]{2,1,0:T(8,128)(2,1)S(1)} %shard_map.146.blk, bf16[32,16,128]{2,1,0:T(8,128)(2,1)S(1)} %add_convert_fusion.2.sum0, ...), custom_call_target="tpu_custom_call" | custom-call | tf_op jit(solution)/shard_map/pallas_call | solution.py:279
  27.8 0.1 collective-permute-start.4
  27.9 1.2 %collective-permute-done.4.other = f32[9,8,128]{2,1,0:T(8,128)S(1)} collective-permute-done((f32[9,8,128]{2,1,0:T(8,128)S(1)}, f32[9,8,128]{2,1,0:T(8,128)S(1)}, u32[]{:S(2)}, u32[]{:S(2)}) %collective-permute-start.4) | collective-permute-done | bytes 36896 | tf_op jit(solution)/shard_map/ppermute | solution.py:225
  29.1 0.0 copy-start.2
  29.1 0.0 copy-start.3
  29.1 0.0 copy-start.6
  29.1 1.8 %shard_map.149 = (bf16[33,16,128]{2,1,0:T(8,128)(2,1)S(1)}, f32[8,8,128]{2,1,0:T(8,128)S(1)}, f32[8,128]{1,0:T(8,128)S(1)}) custom-call(s32[1,1,128]{2,1,0:T(1,128)S(1)} %copy-done.4, s32[1,1,128]{2,1,0:T(1,128)S(1)} %copy-done.5, s32[1]{0:T(128)} %bitcast.3.cnt, bf16[128,128,128]{2,1,0:T(8,128)(2,1)S(1)} %shard_map.146.blk, ...), custom_call_target="tpu_custom_call" | custom-call | tf_op jit(solution)/shard_map/pallas_call | solution.py:285
  30.9 1.4 %collective-permute-start.5 = (bf16[33,16,128]{2,1,0:T(8,128)(2,1)S(1)}, bf16[33,16,128]{2,1,0:T(8,128)(2,1)S(1)}, u32[]{:S(2)}, u32[]{:S(2)}) collective-permute-start(bf16[33,16,128]{2,1,0:T(8,128)(2,1)S(1)} %get-tuple-element.21), channel_id=1, source_target_pairs={{0,1},{1,0},{2,3},{3,2},{4,5},{5,4},{6,7},{7,6},{8,9},{9,8},{10,11... | collective-permute-start | bytes 405512 | tf_op jit(solution)/shard_map/ppermute | solution.py:232
  32.3 4.3 %collective-permute-done.5 = bf16[33,16,128]{2,1,0:T(8,128)(2,1)S(1)} collective-permute-done((bf16[33,16,128]{2,1,0:T(8,128)(2,1)S(1)}, bf16[33,16,128]{2,1,0:T(8,128)(2,1)S(1)}, u32[]{:S(2)}, u32[]{:S(2)}) %collective-permute-start.5) | collective-permute-done | bytes 135200 | tf_op jit(solution)/shard_map/ppermute | solution.py:232
  36.7 0.5 collective-permute-start.6
  37.2 4.6 %collective-permute-done.6 = bf16[33,16,128]{2,1,0:T(8,128)(2,1)S(1)} collective-permute-done((bf16[33,16,128]{2,1,0:T(8,128)(2,1)S(1)}, bf16[33,16,128]{2,1,0:T(8,128)(2,1)S(1)}, u32[]{:S(2)}, u32[]{:S(2)}) %collective-permute-start.6) | collective-permute-done | bytes 135200 | tf_op jit(solution)/shard_map/ppermute | solution.py:232
  41.8 1.8 %collective-permute-start.7 = (bf16[33,16,128]{2,1,0:T(8,128)(2,1)S(1)}, bf16[33,16,128]{2,1,0:T(8,128)(2,1)S(1)}, u32[]{:S(2)}, u32[]{:S(2)}) collective-permute-start(bf16[33,16,128]{2,1,0:T(8,128)(2,1)S(1)} %add_convert_fusion.sum0), channel_id=1, source_target_pairs={{0,4},{1,5},{2,6},{3,7},{4,0},{5,1},{6,2},{7,3},{8,12},{9,13},{10,... | collective-permute-start | bytes 405512 | tf_op jit(solution)/shard_map/ppermute | solution.py:232
  43.7 5.7 %collective-permute-done.7.sum1 = bf16[33,16,128]{2,1,0:T(8,128)(2,1)S(1)} collective-permute-done((bf16[33,16,128]{2,1,0:T(8,128)(2,1)S(1)}, bf16[33,16,128]{2,1,0:T(8,128)(2,1)S(1)}, u32[]{:S(2)}, u32[]{:S(2)}) %collective-permute-start.7) | collective-permute-done | bytes 135200 | tf_op jit(solution)/shard_map/ppermute | solution.py:232
  49.4 1.6 %shard_map.150 = (f32[9,8,128]{2,1,0:T(8,128)S(1)}, f32[8,8,128]{2,1,0:T(8,128)S(1)}, f32[8,128]{1,0:T(8,128)S(1)}) custom-call(s32[1,1,128]{2,1,0:T(1,128)S(1)} %copy-done.4, s32[1,1,128]{2,1,0:T(1,128)S(1)} %copy-done.5, s32[1]{0:T(128)} %bitcast.4.cnt, bf16[128,128,128]{2,1,0:T(8,128)(2,1)S(1)} %shard_map.146.blk, ...), custom_call_target="tpu_custom_call" | custom-call | tf_op jit(solution)/shard_map/pallas_call | solution.py:292
  51.0 0.1 collective-permute-start.8
  51.1 1.2 %collective-permute-done.8.other = f32[9,8,128]{2,1,0:T(8,128)S(1)} collective-permute-done((f32[9,8,128]{2,1,0:T(8,128)S(1)}, f32[9,8,128]{2,1,0:T(8,128)S(1)}, u32[]{:S(2)}, u32[]{:S(2)}) %collective-permute-start.8) | collective-permute-done | bytes 36896 | tf_op jit(solution)/shard_map/ppermute | solution.py:225
  52.3 0.1 shard_map.151
  52.4 1.0 %collective-permute-start.9 = (f32[8,128]{1,0:T(8,128)S(1)}, f32[8,128]{1,0:T(8,128)S(1)}, u32[]{:S(2)}, u32[]{:S(2)}) collective-permute-start(f32[8,128]{1,0:T(8,128)S(1)} %get-tuple-element.27), channel_id=1, source_target_pairs={{0,9},{1,8},{2,11},{3,10},{4,13},{5,12},{6,15},{7,14},{8,1},{9,0},... | collective-permute-start | bytes 12296 | tf_op jit(solution)/shard_map/ppermute | solution.py:244
  53.3 2.1 %collective-permute-done.9 = f32[8,128]{1,0:T(8,128)S(1)} collective-permute-done((f32[8,128]{1,0:T(8,128)S(1)}, f32[8,128]{1,0:T(8,128)S(1)}, u32[]{:S(2)}, u32[]{:S(2)}) %collective-permute-start.9) | collective-permute-done | bytes 4128 | tf_op jit(solution)/shard_map/ppermute | solution.py:244
  55.4 0.0 collective-permute-start.10
  55.4 3.0 %collective-permute-done.10 = f32[8,128]{1,0:T(8,128)S(1)} collective-permute-done((f32[8,128]{1,0:T(8,128)S(1)}, f32[8,128]{1,0:T(8,128)S(1)}, u32[]{:S(2)}, u32[]{:S(2)}) %collective-permute-start.10) | collective-permute-done | bytes 4128 | tf_op jit(solution)/shard_map/ppermute | solution.py:244
  58.4 1.5 %collective-permute-start.11 = (f32[8,128]{1,0:T(8,128)S(1)}, f32[8,128]{1,0:T(8,128)S(1)}, u32[]{:S(2)}, u32[]{:S(2)}) collective-permute-start(f32[8,128]{1,0:T(8,128)S(1)} %add.26), channel_id=1, source_target_pairs={{0,12},{1,13},{2,14},{3,15},{4,8},{5,9},{6,10},{7,11},{8,4},{9,5},... | collective-permute-start | bytes 12296 | tf_op jit(solution)/shard_map/ppermute | solution.py:244
  60.0 2.4 %collective-permute-done.11 = f32[8,128]{1,0:T(8,128)S(1)} collective-permute-done((f32[8,128]{1,0:T(8,128)S(1)}, f32[8,128]{1,0:T(8,128)S(1)}, u32[]{:S(2)}, u32[]{:S(2)}) %collective-permute-start.11) | collective-permute-done | bytes 4128 | tf_op jit(solution)/shard_map/ppermute | solution.py:244
  62.4 0.0 copy-done.2
  62.4 0.0 copy-done.3
  62.4 0.0 copy-done.6
  62.4 0.0 copy-done.7
  62.4 1.2 %shard_map.152 = (f32[8,1024]{1,0:T(8,128)}, f32[8,512]{1,0:T(8,128)}, f32[8,512]{1,0:T(8,128)}, f32[8,512]{1,0:T(8,128)}, f32[3,8]{1,0:T(4,128)}) custom-call(f32[8]{0:T(128)S(1)} %copy-done.6, f32[8]{0:T(128)S(1)} %copy-done.7, f32[8,128]{1,0:T(8,128)S(1)} %add.27.sq, f32[8,8,128]{2,1,0:T(8,128)S(1)} %get-tuple-element.25.v_old.v1, ...), custom_call_target="tpu_custom_call" | custom-call | tf_op jit(solution)/shard_map/pallas_call | solution.py:305
  (8 shorter events, 0.2 us)
Async XLA Ops:
  0.6 3.5 %collective-permute-start = (f32[8,512]{1,0:T(8,128)}, f32[8,512]{1,0:T(8,128)S(1)}, u32[]{:S(2)}, u32[]{:S(2)}) collective-permute-start(f32[8,512]{1,0:T(8,128)} %own.1), channel_id=1, source_target_pairs={{0,8},{8,0},{1,9},{9,1},{2,10},{10,2},{3,11},{11,3},{4,12},{12,4},... | collective-permute-start | bytes 49160 | tf_op jit(solution)/shard_map/ppermute | solution.py:225
  1.8 2.3 %copy-start = (f32[8,1024]{1,0:T(8,128)S(1)}, f32[8,1024]{1,0:T(8,128)}, u32[]{:S(2)}) copy-start(f32[8,1024]{1,0:T(8,128)} %u_piece.1) | copy-start | bytes 98308
  1.8 2.3 %copy-start.1 = (f32[8,512]{1,0:T(8,128)S(1)}, f32[8,512]{1,0:T(8,128)}, u32[]{:S(2)}) copy-start(f32[8,512]{1,0:T(8,128)} %own.1) | copy-start | bytes 49156
  1.8 2.3 %copy-start.4 = (s32[1,1,128]{2,1,0:T(1,128)S(1)}, s32[1,1,128]{2,1,0:T(1,128)}, u32[]{:S(2)}) copy-start(s32[1,1,128]{2,1,0:T(1,128)} %rws.7) | copy-start | bytes 1540
  1.8 2.3 %copy-start.5 = (s32[1,1,128]{2,1,0:T(1,128)S(1)}, s32[1,1,128]{2,1,0:T(1,128)}, u32[]{:S(2)}) copy-start(s32[1,1,128]{2,1,0:T(1,128)} %cls.7) | copy-start | bytes 1540
  1.8 2.3 %copy-start.8 = (f32[8]{0:T(128)S(1)}, f32[8]{0:T(128)}, u32[]{:S(2)}) copy-start(f32[8]{0:T(128)} %alpha.1) | copy-start | bytes 100
  6.0 6.7 %collective-permute-start.1 = (bf16[32,16,128]{2,1,0:T(8,128)(2,1)S(1)}, bf16[32,16,128]{2,1,0:T(8,128)(2,1)S(1)}, u32[]{:S(2)}, u32[]{:S(2)}) collective-permute-start(bf16[32,16,128]{2,1,0:T(8,128)(2,1)S(1)} %get-tuple-element.18), channel_id=1, source_target_pairs={{0,1},{1,0},{2,3},{3,2},{4,5},{5,4},{6,7},{7,6},{8,9},{9,8},{10,11... | collective-permute-start | bytes 393224 | tf_op jit(solution)/shard_map/ppermute | solution.py:232
  12.7 5.4 %collective-permute-start.2 = (bf16[32,16,128]{2,1,0:T(8,128)(2,1)S(1)}, bf16[32,16,128]{2,1,0:T(8,128)(2,1)S(1)}, u32[]{:S(2)}, u32[]{:S(2)}) collective-permute-start(bf16[32,16,128]{2,1,0:T(8,128)(2,1)S(1)} %add_convert_fusion.3), channel_id=1, source_target_pairs={{0,2},{1,3},{2,0},{3,1},{4,6},{5,7},{6,4},{7,5},{8,10},{9,11},{10,... | collective-permute-start | bytes 393224 | tf_op jit(solution)/shard_map/ppermute | solution.py:232
  18.1 8.2 %collective-permute-start.3 = (bf16[32,16,128]{2,1,0:T(8,128)(2,1)S(1)}, bf16[32,16,128]{2,1,0:T(8,128)(2,1)S(1)}, u32[]{:S(2)}, u32[]{:S(2)}) collective-permute-start(bf16[32,16,128]{2,1,0:T(8,128)(2,1)S(1)} %add_convert_fusion.2.sum0), channel_id=1, source_target_pairs={{0,4},{1,5},{2,6},{3,7},{4,0},{5,1},{6,2},{7,3},{8,12},{9,13},{10,... | collective-permute-start | bytes 393224 | tf_op jit(solution)/shard_map/ppermute | solution.py:232
  27.8 1.3 %collective-permute-start.4 = (f32[9,8,128]{2,1,0:T(8,128)S(1)}, f32[9,8,128]{2,1,0:T(8,128)S(1)}, u32[]{:S(2)}, u32[]{:S(2)}) collective-permute-start(f32[9,8,128]{2,1,0:T(8,128)S(1)} %get-tuple-element.19.own), channel_id=1, source_target_pairs={{0,8},{8,0},{1,9},{9,1},{2,10},{10,2},{3,11},{11,3},{4,12},{12,4},... | collective-permute-start | bytes 110600 | tf_op jit(solution)/shard_map/ppermute | solution.py:225
  29.1 33.3 %copy-start.2 = (f32[8,512]{1,0:T(8,128)S(1)}, f32[8,512]{1,0:T(8,128)}, u32[]{:S(2)}) copy-start(f32[8,512]{1,0:T(8,128)} %x_in.1) | copy-start | bytes 49156
  29.1 33.3 %copy-start.3 = (f32[8,512]{1,0:T(8,128)S(1)}, f32[8,512]{1,0:T(8,128)}, u32[]{:S(2)}) copy-start(f32[8,512]{1,0:T(8,128)} %w_in.1) | copy-start | bytes 49156
  29.1 33.3 %copy-start.6 = (f32[8]{0:T(128)S(1)}, f32[8]{0:T(128)}, u32[]{:S(2)}) copy-start(f32[8]{0:T(128)} %phibar_in.1) | copy-start | bytes 100
  29.1 33.3 %copy-start.7 = (f32[8]{0:T(128)S(1)}, f32[8]{0:T(128)}, u32[]{:S(2)}) copy-start(f32[8]{0:T(128)} %rhobar_in.1) | copy-start | bytes 100
  30.9 5.7 %collective-permute-start.5 = (bf16[33,16,128]{2,1,0:T(8,128)(2,1)S(1)}, bf16[33,16,128]{2,1,0:T(8,128)(2,1)S(1)}, u32[]{:S(2)}, u32[]{:S(2)}) collective-permute-start(bf16[33,16,128]{2,1,0:T(8,128)(2,1)S(1)} %get-tuple-element.21), channel_id=1, source_target_pairs={{0,1},{1,0},{2,3},{3,2},{4,5},{5,4},{6,7},{7,6},{8,9},{9,8},{10,11... | collective-permute-start | bytes 405512 | tf_op jit(solution)/shard_map/ppermute | solution.py:232
  36.7 5.1 %collective-permute-start.6 = (bf16[33,16,128]{2,1,0:T(8,128)(2,1)S(1)}, bf16[33,16,128]{2,1,0:T(8,128)(2,1)S(1)}, u32[]{:S(2)}, u32[]{:S(2)}) collective-permute-start(bf16[33,16,128]{2,1,0:T(8,128)(2,1)S(1)} %add_convert_fusion.1), channel_id=1, source_target_pairs={{0,2},{1,3},{2,0},{3,1},{4,6},{5,7},{6,4},{7,5},{8,10},{9,11},{10,... | collective-permute-start | bytes 405512 | tf_op jit(solution)/shard_map/ppermute | solution.py:232
  41.8 7.6 %collective-permute-start.7 = (bf16[33,16,128]{2,1,0:T(8,128)(2,1)S(1)}, bf16[33,16,128]{2,1,0:T(8,128)(2,1)S(1)}, u32[]{:S(2)}, u32[]{:S(2)}) collective-permute-start(bf16[33,16,128]{2,1,0:T(8,128)(2,1)S(1)} %add_convert_fusion.sum0), channel_id=1, source_target_pairs={{0,4},{1,5},{2,6},{3,7},{4,0},{5,1},{6,2},{7,3},{8,12},{9,13},{10,... | collective-permute-start | bytes 405512 | tf_op jit(solution)/shard_map/ppermute | solution.py:232
  51.0 1.3 %collective-permute-start.8 = (f32[9,8,128]{2,1,0:T(8,128)S(1)}, f32[9,8,128]{2,1,0:T(8,128)S(1)}, u32[]{:S(2)}, u32[]{:S(2)}) collective-permute-start(f32[9,8,128]{2,1,0:T(8,128)S(1)} %get-tuple-element.24.own), channel_id=1, source_target_pairs={{0,8},{8,0},{1,9},{9,1},{2,10},{10,2},{3,11},{11,3},{4,12},{12,4},... | collective-permute-start | bytes 110600 | tf_op jit(solution)/shard_map/ppermute | solution.py:225
  52.4 3.0 %collective-permute-start.9 = (f32[8,128]{1,0:T(8,128)S(1)}, f32[8,128]{1,0:T(8,128)S(1)}, u32[]{:S(2)}, u32[]{:S(2)}) collective-permute-start(f32[8,128]{1,0:T(8,128)S(1)} %get-tuple-element.27), channel_id=1, source_target_pairs={{0,9},{1,8},{2,11},{3,10},{4,13},{5,12},{6,15},{7,14},{8,1},{9,0},... | collective-permute-start | bytes 12296 | tf_op jit(solution)/shard_map/ppermute | solution.py:244
  55.4 3.0 %collective-permute-start.10 = (f32[8,128]{1,0:T(8,128)S(1)}, f32[8,128]{1,0:T(8,128)S(1)}, u32[]{:S(2)}, u32[]{:S(2)}) collective-permute-start(f32[8,128]{1,0:T(8,128)S(1)} %add.25), channel_id=1, source_target_pairs={{0,10},{1,11},{2,8},{3,9},{4,14},{5,15},{6,12},{7,13},{8,2},{9,3},... | collective-permute-start | bytes 12296 | tf_op jit(solution)/shard_map/ppermute | solution.py:244
  58.4 3.9 %collective-permute-start.11 = (f32[8,128]{1,0:T(8,128)S(1)}, f32[8,128]{1,0:T(8,128)S(1)}, u32[]{:S(2)}, u32[]{:S(2)}) collective-permute-start(f32[8,128]{1,0:T(8,128)S(1)} %add.26), channel_id=1, source_target_pairs={{0,12},{1,13},{2,14},{3,15},{4,8},{5,9},{6,10},{7,11},{8,4},{9,5},... | collective-permute-start | bytes 12296 | tf_op jit(solution)/shard_map/ppermute | solution.py:244

commit v4 on v3

--- a/solution.py
+++ b/solution.py
@@ -31,34 +31,52 @@
     return jax.ShapeDtypeStruct(dims, dtype)
 
 
-def forward(blk, rws, cls, cnt, v_ref, acc_ref, ready=None):
-    spare = acc_ref.shape[0] - 1
-    count = cnt[0]
+def lists(rws_ref, cls_ref, rws, cls, sems):
+    copies = [
+        pltpu.make_async_copy(rws_ref, rws, sems.at[0]),
+        pltpu.make_async_copy(cls_ref, cls, sems.at[1]),
+    ]
+    for copy in copies:
+        copy.start()
+    return copies
+
+
+def used(count, k, prod):
+    return jnp.where(count > k, prod, 0.0)
+
+
+def forward(blks, rws, cls, cnt, v_ref, acc_ref, between=None):
+    count = jnp.broadcast_to(cnt[...], (8, 128))
     acc_ref[...] = jnp.zeros_like(acc_ref)
-    for k in range(0, blk.shape[0], 2):
-        if ready is not None:
-            ready(k)
-        pair = jnp.concatenate([v_ref[cls[0, 0, k]], v_ref[cls[0, 0, k + 1]]], axis=0)
-        a = blk[k : k + 2].reshape(256, 128)
-        prod = lax.dot_general(
-            pair.astype(BF16), a, (((1,), (1,)), ((), ())), preferred_element_type=F32
-        )
-        acc_ref[jnp.where(k < count, rws[0, 0, k], spare)] += prod[:8, :128]
-        acc_ref[jnp.where(k + 1 < count, rws[0, 0, k + 1], spare)] += prod[8:, 128:]
-
-
-def backward(blk, rws, cls, cnt, u_ref, acc_ref):
-    spare = acc_ref.shape[0] - 1
-    count = cnt[0]
+    k = 0
+    for blk in blks:
+        if between is not None and k > 0:
+            between()
+        for at in range(0, blk.shape[0], 2):
+            pair = jnp.concatenate([v_ref[cls[0, 0, k]], v_ref[cls[0, 0, k + 1]]], axis=0)
+            a = blk[at : at + 2].reshape(256, 128)
+            prod = lax.dot_general(
+                pair.astype(BF16), a, (((1,), (1,)), ((), ())), preferred_element_type=F32
+            )
+            acc_ref[rws[0, 0, k]] += used(count, k, prod[:8, :128])
+            acc_ref[rws[0, 0, k + 1]] += used(count, k + 1, prod[8:, 128:])
+            k += 2
+
+
+def backward(blks, rws, cls, cnt, u_ref, acc_ref):
+    count = jnp.broadcast_to(cnt[...], (8, 128))
     acc_ref[...] = jnp.zeros_like(acc_ref)
     zero = jnp.zeros((8, 128), F32)
-    for k in range(0, blk.shape[0], 2):
-        u0 = jnp.concatenate([u_ref[rws[0, 0, k]], zero], axis=0).astype(BF16)
-        u1 = jnp.concatenate([zero, u_ref[rws[0, 0, k + 1]]], axis=0).astype(BF16)
-        a = blk[k : k + 2].reshape(256, 128)
-        prod = jnp.dot(jnp.concatenate([u0, u1], axis=1), a, preferred_element_type=F32)
-        acc_ref[jnp.where(k < count, cls[0, 0, k], spare)] += prod[:8]
-        acc_ref[jnp.where(k + 1 < count, cls[0, 0, k + 1], spare)] += prod[8:]
+    k = 0
+    for blk in blks:
+        for at in range(0, blk.shape[0], 2):
+            u0 = jnp.concatenate([u_ref[rws[0, 0, k]], zero], axis=0).astype(BF16)
+            u1 = jnp.concatenate([zero, u_ref[rws[0, 0, k + 1]]], axis=0).astype(BF16)
+            a = blk[at : at + 2].reshape(256, 128)
+            prod = jnp.dot(jnp.concatenate([u0, u1], axis=1), a, preferred_element_type=F32)
+            acc_ref[cls[0, 0, k]] += used(count, k, prod[:8])
+            acc_ref[cls[0, 0, k + 1]] += used(count, k + 1, prod[8:])
+            k += 2
 
 
 def column(ref):
@@ -95,54 +113,79 @@
 
 
 def load(blk_hbm, blk, sem):
-    copy = pltpu.make_async_copy(blk_hbm.at[0, 0], blk, sem)
+    copy = pltpu.make_async_copy(blk_hbm.at[0, 0, pl.ds(0, blk.shape[0])], blk, sem)
     copy.start()
     copy.wait()
 
 
-def first_forward(rws, cls, cnt, alpha, blk, own, other, u_piece, out, v_out, acc):
+def first_forward(
+    rws_ref, cls_ref, cnt, alpha, blk0, blk_hbm, own, other, u_piece,
+    out, v_out, blk1,
+    rws, cls, sems, sem, acc,
+):
+    rest = blk1.shape[0]
+    copy = pltpu.make_async_copy(blk_hbm.at[0, 0, pl.ds(blk0.shape[0], rest)], blk1, sem)
+    copy.start()
+    copies = lists(rws_ref, cls_ref, rws, cls, sems)
     place_halves(own, other, v_out)
-    forward(blk, rws, cls, cnt, v_out, acc)
+    for c in copies:
+        c.wait()
+    forward((blk0, blk1), rws, cls, cnt, v_out, acc, copy.wait)
     pieces = u_piece.shape[1] // 128
     base = lax.axis_index("col") * pieces
     a = column(alpha)
     for b in range(pieces):
         acc[base + b] -= a * u_piece[:, b * 128 : (b + 1) * 128]
-    store_pairs(acc, out, acc.shape[0] - 1)
-
-
-def first_backward(rws, cls, cnt, blk, sum0, sum1, upd, message, acc):
+    store_pairs(acc, out, acc.shape[0])
+
+
+def first_backward(rws_ref, cls_ref, cnt, blk0, blk1, sum0, sum1, upd, message, rws, cls, sems, acc):
+    copies = lists(rws_ref, cls_ref, rws, cls, sems)
     blocks = upd.shape[0]
     for b in range(blocks // 2):
         s = sum0[b].astype(F32) + sum1[b].astype(F32)
         upd[2 * b] = s[:8]
         upd[2 * b + 1] = s[8:]
-    backward(blk, rws, cls, cnt, upd, acc)
-    cells = acc.shape[0] - 1
-    message[:cells] = acc[:cells]
+    cells = acc.shape[0]
     message[cells] = squares(upd, blocks)
-
-
-def next_forward(total_rays, rws, cls, cnt, blk, own, other, v_old, out, vupd, beta_out, acc):
+    for c in copies:
+        c.wait()
+    backward((blk0, blk1), rws, cls, cnt, upd, acc)
+    message[:cells] = acc[...]
+
+
+def next_forward(
+    total_rays,
+    rws_ref, cls_ref, cnt, blk0, blk1, own, other, v_old,
+    out, vupd, beta_out,
+    rws, cls, sems, acc,
+):
+    copies = lists(rws_ref, cls_ref, rws, cls, sems)
     cells = v_old.shape[0]
     beta = jnp.sqrt((own[cells] + other[cells]) / total_rays + EPS)
     beta_out[...] = beta
     inv = 1.0 / beta
     for b in range(cells):
         vupd[b] = (own[b] + other[b]) * inv - beta * v_old[b]
-    forward(blk, rws, cls, cnt, vupd, acc)
-    rays = acc.shape[0] - 1
-    store_pairs(acc, out, rays)
+    rays = acc.shape[0]
     sq = squares(vupd, cells)
     lanes = lax.broadcasted_iota(jnp.int32, (8, 128), 1)
     sq = jnp.where(lanes == lax.axis_index("col"), sq, 0.0)
     high = sq.astype(BF16).astype(F32)
     out[rays // 2] = jnp.concatenate([high, sq - high], axis=0).astype(BF16)
+    for c in copies:
+        c.wait()
+    forward((blk0, blk1), rws, cls, cnt, vupd, acc)
+    store_pairs(acc, out, rays)
 
 
 def next_backward(
-    total_cells, pieces, rws, cls, cnt, blk, sum0, sum1, old, beta, message, u_piece, alpha_out, upd, acc
-):
+    total_cells, pieces,
+    rws_ref, cls_ref, cnt, blk0, blk1, sum0, sum1, old, beta,
+    message, u_piece, alpha_out,
+    rws, cls, sems, upd, acc,
+):
+    copies = lists(rws_ref, cls_ref, rws, cls, sems)
     blocks = upd.shape[0]
     tail = sum0[blocks // 2].astype(F32) + sum1[blocks // 2].astype(F32)
     alpha = jnp.sqrt(lane_sum(tail[:8] + tail[8:]) / total_cells + EPS)
@@ -153,13 +196,15 @@
         s = sum0[b].astype(F32) + sum1[b].astype(F32)
         upd[2 * b] = s[:8] * inv - ratio * old[2 * b]
         upd[2 * b + 1] = s[8:] * inv - ratio * old[2 * b + 1]
-    backward(blk, rws, cls, cnt, upd, acc)
-    cells = acc.shape[0] - 1
-    message[:cells] = acc[:cells]
+    cells = acc.shape[0]
     message[cells] = squares(upd, blocks)
     base = lax.axis_index("col") * pieces
     for b in range(pieces):
         u_piece[b] = upd[base + b]
+    for c in copies:
+        c.wait()
+    backward((blk0, blk1), rws, cls, cnt, upd, acc)
+    message[:cells] = acc[...]
 
 
 def last_cells(total_rays, own, other, v_old, alpha, sq, vupd, beta_out):
@@ -257,44 +302,46 @@
     cells = half * n_row
     total_rays = float(rays * 128 * n_row)
     total_cells = float(cells * 128 * n_col)
-    where = (block_rows, block_cols, counts.reshape(1))
-    listed = [SMEM] * 3
-    ray_acc = pltpu.VMEM((rays + 1, 8, 128), F32)
-    cell_acc = pltpu.VMEM((cells + 1, 8, 128), F32)
+    where = (block_rows, block_cols, counts)
+    listed = [
+        pltpu.SMEM(block_rows.shape, jnp.int32),
+        pltpu.SMEM(block_cols.shape, jnp.int32),
+        pltpu.SemaphoreType.DMA((2,)),
+    ]
+    ray_acc = pltpu.VMEM((rays, 8, 128), F32)
+    cell_acc = pltpu.VMEM((cells, 8, 128), F32)
+    slots = blocks.shape[2]
+    half_blk = shape(slots // 2, 128, 128, dtype=BF16)
 
     v_other = other_core(v_cells)
-    blk = call(
-        load,
-        shape(*blocks.shape[2:], dtype=BF16),
-        [HBM],
-        [pltpu.SemaphoreType.DMA],
-    )(blocks)
-    part, v0 = call(
+    blk0 = call(load, half_blk, [HBM], [pltpu.SemaphoreType.DMA])(blocks)
+    part, v0, blk1 = call(
         first_forward,
-        (shape(rays // 2, 16, 128, dtype=BF16), shape(cells, 8, 128)),
-        listed + [SMEM] + [VMEM] * 4,
-        [ray_acc],
-    )(*where, alpha, blk, v_cells, v_other, u_rays)
+        (shape(rays // 2, 16, 128, dtype=BF16), shape(cells, 8, 128), half_blk),
+        [VMEM] * 3 + [SMEM, VMEM, HBM] + [VMEM] * 3,
+        listed + [pltpu.SemaphoreType.DMA, ray_acc],
+    )(*where, alpha, blk0, blocks, v_cells, v_other, u_rays)
+    operator = (*where, blk0, blk1)
     sum0, sum1 = column_sum(part)
     upd1, message = call(
         first_backward,
         (shape(rays, 8, 128), shape(cells + 1, 8, 128)),
-        listed + [VMEM] * 3,
-        [cell_acc],
-    )(*where, blk, sum0, sum1)
+        [VMEM] * 7,
+        listed + [cell_acc],
+    )(*operator, sum0, sum1)
     part, v1, beta1 = call(
         functools.partial(next_forward, total_rays),
         (shape(rays // 2 + 1, 16, 128, dtype=BF16), shape(cells, 8, 128), shape(8, 128)),
-        listed + [VMEM] * 4,
-        [ray_acc],
-    )(*where, blk, message, other_core(message), v0)
+        [VMEM] * 8,
+        listed + [ray_acc],
+    )(*operator, message, other_core(message), v0)
     sum0, sum1 = column_sum(part)
     message, u_piece, alpha1 = call(
         functools.partial(next_backward, total_cells, pieces),
         (shape(cells + 1, 8, 128), shape(pieces, 8, 128), shape(8, 128)),
-        listed + [VMEM] * 5,
-        [pltpu.VMEM((rays, 8, 128), F32), cell_acc],
-    )(*where, blk, sum0, sum1, upd1, beta1)
+        [VMEM] * 9,
+        listed + [pltpu.VMEM((rays, 8, 128), F32), cell_acc],
+    )(*operator, sum0, sum1, upd1, beta1)
     sq, v2, beta2 = call(
         functools.partial(last_cells, total_rays),
         (shape(8, 128), shape(cells, 8, 128), shape(8, 128)),

time: 63.7 us -> 64.1 us (level)
  starting transfers between devices: 14 us -> 15.1 us
  waiting for transfers between devices: 37.6 us -> 36.6 us
    pallas_call x1, Pallas kernels: 1.85 us -> 2.85 us  [body(): call(first_forward, (shape(rays // 2, 16, 128, dtype=BF16), shape(cells,...]
    ppermute x3, waiting for transfers between devices: 7.46 us -> 6.72 us  [last_sum(): x = x + lax.ppermute(x, ('row', 'col'), pairs)]
    ppermute x3, starting transfers between devices: 2.54 us -> 3.28 us  [last_sum(): x = x + lax.ppermute(x, ('row', 'col'), pairs)]
    pallas_call x2, Pallas kernels: 3.71 us -> 3 us  [the longest x1 1.63 us: body(): blk0 = call(load, half_blk, [HBM], [pltpu.SemaphoreType.DMA])(blocks)]
where the time goes in v4:
time: 64.1 us; the launch traced here: 63.9 us
  waiting for transfers between devices  36.6 us (57%)
  starting transfers between devices  15.1 us (24%)
  Pallas kernels  10.5 us (16%)
  between operations  1.48 us (2%)
    ppermute x6, waiting for transfers between devices, column_sum(): y = lax.ppermute(x, 'col', [(i, i ^ m) for i in range(n)])  27.5 us
    ppermute x6, starting transfers between devices, column_sum(): y = lax.ppermute(x, 'col', [(i, i ^ m) for i in range(n)])  11.2 us
    ppermute x3, waiting for transfers between devices, last_sum(): x = x + lax.ppermute(x, ('row', 'col'), pairs)  6.72 us
    ppermute x3, starting transfers between devices, last_sum(): x = x + lax.ppermute(x, ('row', 'col'), pairs)  3.28 us
    pallas_call x1, Pallas kernels, body(): call(first_forward, (shape(rays // 2, 16, 128, dtype=BF16), shape(cells,...  2.85 us
    ppermute x3, waiting for transfers between devices, other_core(): return lax.ppermute(x, 'row', [(0, 1), (1, 0)])  2.4 us
    pallas_call x1, Pallas kernels, body(): call(functools.partial(next_forward, total_rays), (shape(rays // 2 + 1, 1...  1.8 us
    pallas_call x1, Pallas kernels, body(): blk0 = call(load, half_blk, [HBM], [pltpu.SemaphoreType.DMA])(blocks)  1.63 us
  transfers between devices with their start and end apart: 12, of which 11 were waited for; matrix products, arithmetic and copies ran while one was open for 0% of the time, Pallas kernels for 3%

profile of v4, /device:TPU:0, one launch (start us, length us, event | category | flops | bytes accessed | tf_op | source)
XLA Modules:
  0.0 63.9 jit_solution(5590448424222650312)
XLA Ops:
  0.6 0.5 collective-permute-start
  1.8 0.0 copy-start
  1.8 0.0 copy-start.1
  1.8 0.0 copy-start.4
  1.8 0.0 copy-start.5
  1.8 0.0 copy-start.6
  1.9 1.6 %shard_map.146.blk0 = bf16[64,128,128]{2,1,0:T(8,128)(2,1)S(1)} custom-call(bf16[1,1,128,128,128]{4,3,2,1,0:T(8,128)(2,1)} %blk_hbm.3), custom_call_target="tpu_custom_call" | custom-call | tf_op jit(solution)/shard_map/pallas_call | solution.py:317
  3.5 0.0 collective-permute-done.other
  3.5 0.0 copy-done
  3.5 0.0 copy-done.1
  3.5 0.0 copy-done.4
  3.5 0.0 copy-done.5
  3.5 0.0 copy-done.6
  3.6 2.9 %shard_map.147 = (bf16[32,16,128]{2,1,0:T(8,128)(2,1)S(1)}, f32[8,8,128]{2,1,0:T(8,128)S(1)}, bf16[64,128,128]{2,1,0:T(8,128)(2,1)S(1)}) custom-call(s32[1,1,128]{2,1,0:T(1,128)S(1)} %copy-done.4, s32[1,1,128]{2,1,0:T(1,128)S(1)} %copy-done.5, s32[1,1]{1,0:T(1,128)S(6)} %copy.16.cnt, f32[8]{0:T(128)S(1)} %copy-done.6, ...), custom_call_target="tpu_custom_call" | custom-call | tf_op jit(solution)/shard_map/pallas_call | solution.py:318
  6.4 2.6 %collective-permute-start.1 = (bf16[32,16,128]{2,1,0:T(8,128)(2,1)S(1)}, bf16[32,16,128]{2,1,0:T(8,128)(2,1)S(1)}, u32[]{:S(2)}, u32[]{:S(2)}) collective-permute-start(bf16[32,16,128]{2,1,0:T(8,128)(2,1)S(1)} %get-tuple-element.20), channel_id=1, source_target_pairs={{0,1},{1,0},{2,3},{3,2},{4,5},{5,4},{6,7},{7,6},{8,9},{9,8},{10,11... | collective-permute-start | bytes 393224 | tf_op jit(solution)/shard_map/ppermute | solution.py:277
  9.0 4.2 %collective-permute-done.1 = bf16[32,16,128]{2,1,0:T(8,128)(2,1)S(1)} collective-permute-done((bf16[32,16,128]{2,1,0:T(8,128)(2,1)S(1)}, bf16[32,16,128]{2,1,0:T(8,128)(2,1)S(1)}, u32[]{:S(2)}, u32[]{:S(2)}) %collective-permute-start.1) | collective-permute-done | bytes 131104 | tf_op jit(solution)/shard_map/ppermute | solution.py:277
  13.2 1.9 %collective-permute-start.2 = (bf16[32,16,128]{2,1,0:T(8,128)(2,1)S(1)}, bf16[32,16,128]{2,1,0:T(8,128)(2,1)S(1)}, u32[]{:S(2)}, u32[]{:S(2)}) collective-permute-start(bf16[32,16,128]{2,1,0:T(8,128)(2,1)S(1)} %add_convert_fusion.3), channel_id=1, source_target_pairs={{0,2},{1,3},{2,0},{3,1},{4,6},{5,7},{6,4},{7,5},{8,10},{9,11},{10,... | collective-permute-start | bytes 393224 | tf_op jit(solution)/shard_map/ppermute | solution.py:277
  15.1 3.5 %collective-permute-done.2 = bf16[32,16,128]{2,1,0:T(8,128)(2,1)S(1)} collective-permute-done((bf16[32,16,128]{2,1,0:T(8,128)(2,1)S(1)}, bf16[32,16,128]{2,1,0:T(8,128)(2,1)S(1)}, u32[]{:S(2)}, u32[]{:S(2)}) %collective-permute-start.2) | collective-permute-done | bytes 131104 | tf_op jit(solution)/shard_map/ppermute | solution.py:277
  18.6 2.7 %collective-permute-start.3 = (bf16[32,16,128]{2,1,0:T(8,128)(2,1)S(1)}, bf16[32,16,128]{2,1,0:T(8,128)(2,1)S(1)}, u32[]{:S(2)}, u32[]{:S(2)}) collective-permute-start(bf16[32,16,128]{2,1,0:T(8,128)(2,1)S(1)} %add_convert_fusion.2.sum0), channel_id=1, source_target_pairs={{0,4},{1,5},{2,6},{3,7},{4,0},{5,1},{6,2},{7,3},{8,12},{9,13},{10,... | collective-permute-start | bytes 393224 | tf_op jit(solution)/shard_map/ppermute | solution.py:277
  21.3 5.5 %collective-permute-done.3.sum1 = bf16[32,16,128]{2,1,0:T(8,128)(2,1)S(1)} collective-permute-done((bf16[32,16,128]{2,1,0:T(8,128)(2,1)S(1)}, bf16[32,16,128]{2,1,0:T(8,128)(2,1)S(1)}, u32[]{:S(2)}, u32[]{:S(2)}) %collective-permute-start.3) | collective-permute-done | bytes 131104 | tf_op jit(solution)/shard_map/ppermute | solution.py:277
  26.8 1.4 %shard_map.148 = (f32[64,8,128]{2,1,0:T(8,128)S(1)}, f32[9,8,128]{2,1,0:T(8,128)S(1)}) custom-call(s32[1,1,128]{2,1,0:T(1,128)S(1)} %copy-done.4, s32[1,1,128]{2,1,0:T(1,128)S(1)} %copy-done.5, s32[1,1]{1,0:T(1,128)S(6)} %copy.16.cnt, bf16[64,128,128]{2,1,0:T(8,128)(2,1)S(1)} %shard_map.146.blk0, bf16[64,128,128]{2,1,0:T(8,128)(2,1)S(1)} %get-tuple-element.19.blk1, ...), custom_call_target="tpu_custom_call" | custom-call | tf_op jit(solution)/shard_map/pallas_call | solution.py:326
  28.2 0.1 collective-permute-start.4
  28.3 1.2 %collective-permute-done.4.other = f32[9,8,128]{2,1,0:T(8,128)S(1)} collective-permute-done((f32[9,8,128]{2,1,0:T(8,128)S(1)}, f32[9,8,128]{2,1,0:T(8,128)S(1)}, u32[]{:S(2)}, u32[]{:S(2)}) %collective-permute-start.4) | collective-permute-done | bytes 36896 | tf_op jit(solution)/shard_map/ppermute | solution.py:270
  29.5 1.8 %shard_map.149 = (bf16[33,16,128]{2,1,0:T(8,128)(2,1)S(1)}, f32[8,8,128]{2,1,0:T(8,128)S(1)}, f32[8,128]{1,0:T(8,128)S(1)}) custom-call(s32[1,1,128]{2,1,0:T(1,128)S(1)} %copy-done.4, s32[1,1,128]{2,1,0:T(1,128)S(1)} %copy-done.5, s32[1,1]{1,0:T(1,128)S(6)} %copy.16.cnt, bf16[64,128,128]{2,1,0:T(8,128)(2,1)S(1)} %shard_map.146.blk0, ...), custom_call_target="tpu_custom_call" | custom-call | tf_op jit(solution)/shard_map/pallas_call | solution.py:332
  31.3 1.4 %collective-permute-start.5 = (bf16[33,16,128]{2,1,0:T(8,128)(2,1)S(1)}, bf16[33,16,128]{2,1,0:T(8,128)(2,1)S(1)}, u32[]{:S(2)}, u32[]{:S(2)}) collective-permute-start(bf16[33,16,128]{2,1,0:T(8,128)(2,1)S(1)} %get-tuple-element.23), channel_id=1, source_target_pairs={{0,1},{1,0},{2,3},{3,2},{4,5},{5,4},{6,7},{7,6},{8,9},{9,8},{10,11... | collective-permute-start | bytes 405512 | tf_op jit(solution)/shard_map/ppermute | solution.py:277
  32.7 4.3 %collective-permute-done.5 = bf16[33,16,128]{2,1,0:T(8,128)(2,1)S(1)} collective-permute-done((bf16[33,16,128]{2,1,0:T(8,128)(2,1)S(1)}, bf16[33,16,128]{2,1,0:T(8,128)(2,1)S(1)}, u32[]{:S(2)}, u32[]{:S(2)}) %collective-permute-start.5) | collective-permute-done | bytes 135200 | tf_op jit(solution)/shard_map/ppermute | solution.py:277
  37.1 0.6 collective-permute-start.6
  37.7 4.5 %collective-permute-done.6 = bf16[33,16,128]{2,1,0:T(8,128)(2,1)S(1)} collective-permute-done((bf16[33,16,128]{2,1,0:T(8,128)(2,1)S(1)}, bf16[33,16,128]{2,1,0:T(8,128)(2,1)S(1)}, u32[]{:S(2)}, u32[]{:S(2)}) %collective-permute-start.6) | collective-permute-done | bytes 135200 | tf_op jit(solution)/shard_map/ppermute | solution.py:277
  42.2 2.0 %collective-permute-start.7 = (bf16[33,16,128]{2,1,0:T(8,128)(2,1)S(1)}, bf16[33,16,128]{2,1,0:T(8,128)(2,1)S(1)}, u32[]{:S(2)}, u32[]{:S(2)}) collective-permute-start(bf16[33,16,128]{2,1,0:T(8,128)(2,1)S(1)} %add_convert_fusion.sum0), channel_id=1, source_target_pairs={{0,4},{1,5},{2,6},{3,7},{4,0},{5,1},{6,2},{7,3},{8,12},{9,13},{10,... | collective-permute-start | bytes 405512 | tf_op jit(solution)/shard_map/ppermute | solution.py:277
  44.2 5.5 %collective-permute-done.7.sum1 = bf16[33,16,128]{2,1,0:T(8,128)(2,1)S(1)} collective-permute-done((bf16[33,16,128]{2,1,0:T(8,128)(2,1)S(1)}, bf16[33,16,128]{2,1,0:T(8,128)(2,1)S(1)}, u32[]{:S(2)}, u32[]{:S(2)}) %collective-permute-start.7) | collective-permute-done | bytes 135200 | tf_op jit(solution)/shard_map/ppermute | solution.py:277
  49.7 0.0 copy-start.2
  49.7 0.0 copy-start.3
  49.7 0.0 copy-start.8
  49.7 1.5 %shard_map.150 = (f32[9,8,128]{2,1,0:T(8,128)S(1)}, f32[8,8,128]{2,1,0:T(8,128)S(1)}, f32[8,128]{1,0:T(8,128)S(1)}) custom-call(s32[1,1,128]{2,1,0:T(1,128)S(1)} %copy-done.4, s32[1,1,128]{2,1,0:T(1,128)S(1)} %copy-done.5, s32[1,1]{1,0:T(1,128)S(6)} %copy.16.cnt, bf16[64,128,128]{2,1,0:T(8,128)(2,1)S(1)} %shard_map.146.blk0, ...), custom_call_target="tpu_custom_call" | custom-call | tf_op jit(solution)/shard_map/pallas_call | solution.py:339
  51.3 0.1 collective-permute-start.8
  51.3 1.2 %collective-permute-done.8.other = f32[9,8,128]{2,1,0:T(8,128)S(1)} collective-permute-done((f32[9,8,128]{2,1,0:T(8,128)S(1)}, f32[9,8,128]{2,1,0:T(8,128)S(1)}, u32[]{:S(2)}, u32[]{:S(2)}) %collective-permute-start.8) | collective-permute-done | bytes 36896 | tf_op jit(solution)/shard_map/ppermute | solution.py:270
  52.5 0.1 shard_map.151
  52.6 1.1 %collective-permute-start.9 = (f32[8,128]{1,0:T(8,128)S(1)}, f32[8,128]{1,0:T(8,128)S(1)}, u32[]{:S(2)}, u32[]{:S(2)}) collective-permute-start(f32[8,128]{1,0:T(8,128)S(1)} %get-tuple-element.29), channel_id=1, source_target_pairs={{0,9},{1,8},{2,11},{3,10},{4,13},{5,12},{6,15},{7,14},{8,1},{9,0},... | collective-permute-start | bytes 12296 | tf_op jit(solution)/shard_map/ppermute | solution.py:289
  53.7 1.9 %collective-permute-done.9 = f32[8,128]{1,0:T(8,128)S(1)} collective-permute-done((f32[8,128]{1,0:T(8,128)S(1)}, f32[8,128]{1,0:T(8,128)S(1)}, u32[]{:S(2)}, u32[]{:S(2)}) %collective-permute-start.9) | collective-permute-done | bytes 4128 | tf_op jit(solution)/shard_map/ppermute | solution.py:289
  55.7 0.3 collective-permute-start.10
  56.0 2.7 %collective-permute-done.10 = f32[8,128]{1,0:T(8,128)S(1)} collective-permute-done((f32[8,128]{1,0:T(8,128)S(1)}, f32[8,128]{1,0:T(8,128)S(1)}, u32[]{:S(2)}, u32[]{:S(2)}) %collective-permute-start.10) | collective-permute-done | bytes 4128 | tf_op jit(solution)/shard_map/ppermute | solution.py:289
  58.7 1.9 %collective-permute-start.11 = (f32[8,128]{1,0:T(8,128)S(1)}, f32[8,128]{1,0:T(8,128)S(1)}, u32[]{:S(2)}, u32[]{:S(2)}) collective-permute-start(f32[8,128]{1,0:T(8,128)S(1)} %add.26), channel_id=1, source_target_pairs={{0,12},{1,13},{2,14},{3,15},{4,8},{5,9},{6,10},{7,11},{8,4},{9,5},... | collective-permute-start | bytes 12296 | tf_op jit(solution)/shard_map/ppermute | solution.py:289
  60.6 2.0 %collective-permute-done.11 = f32[8,128]{1,0:T(8,128)S(1)} collective-permute-done((f32[8,128]{1,0:T(8,128)S(1)}, f32[8,128]{1,0:T(8,128)S(1)}, u32[]{:S(2)}, u32[]{:S(2)}) %collective-permute-start.11) | collective-permute-done | bytes 4128 | tf_op jit(solution)/shard_map/ppermute | solution.py:289
  62.7 0.0 copy-done.2
  62.7 0.0 copy-done.3
  62.7 0.0 copy-done.7
  62.7 0.0 copy-done.8
  62.7 1.2 %shard_map.152 = (f32[8,1024]{1,0:T(8,128)}, f32[8,512]{1,0:T(8,128)}, f32[8,512]{1,0:T(8,128)}, f32[8,512]{1,0:T(8,128)}, f32[3,8]{1,0:T(4,128)}) custom-call(f32[8]{0:T(128)S(1)} %copy-done.7, f32[8]{0:T(128)S(1)} %copy-done.8, f32[8,128]{1,0:T(8,128)S(1)} %add.27.sq, f32[8,8,128]{2,1,0:T(8,128)S(1)} %get-tuple-element.27.v_old.v1, ...), custom_call_target="tpu_custom_call" | custom-call | tf_op jit(solution)/shard_map/pallas_call | solution.py:352
  (8 shorter events, 0.2 us)
Async XLA Ops:
  0.6 2.9 %collective-permute-start = (f32[8,512]{1,0:T(8,128)}, f32[8,512]{1,0:T(8,128)S(1)}, u32[]{:S(2)}, u32[]{:S(2)}) collective-permute-start(f32[8,512]{1,0:T(8,128)} %own.1), channel_id=1, source_target_pairs={{0,8},{8,0},{1,9},{9,1},{2,10},{10,2},{3,11},{11,3},{4,12},{12,4},... | collective-permute-start | bytes 49160 | tf_op jit(solution)/shard_map/ppermute | solution.py:270
  1.8 1.7 %copy-start = (f32[8,1024]{1,0:T(8,128)S(1)}, f32[8,1024]{1,0:T(8,128)}, u32[]{:S(2)}) copy-start(f32[8,1024]{1,0:T(8,128)} %u_piece.1) | copy-start | bytes 98308
  1.8 1.7 %copy-start.1 = (f32[8,512]{1,0:T(8,128)S(1)}, f32[8,512]{1,0:T(8,128)}, u32[]{:S(2)}) copy-start(f32[8,512]{1,0:T(8,128)} %own.1) | copy-start | bytes 49156
  1.8 1.7 %copy-start.4 = (s32[1,1,128]{2,1,0:T(1,128)S(1)}, s32[1,1,128]{2,1,0:T(1,128)}, u32[]{:S(2)}) copy-start(s32[1,1,128]{2,1,0:T(1,128)} %rws_ref.7) | copy-start | bytes 1540
  1.8 1.7 %copy-start.5 = (s32[1,1,128]{2,1,0:T(1,128)S(1)}, s32[1,1,128]{2,1,0:T(1,128)}, u32[]{:S(2)}) copy-start(s32[1,1,128]{2,1,0:T(1,128)} %cls_ref.7) | copy-start | bytes 1540
  1.8 1.7 %copy-start.6 = (f32[8]{0:T(128)S(1)}, f32[8]{0:T(128)}, u32[]{:S(2)}) copy-start(f32[8]{0:T(128)} %alpha.1) | copy-start | bytes 100
  6.4 6.7 %collective-permute-start.1 = (bf16[32,16,128]{2,1,0:T(8,128)(2,1)S(1)}, bf16[32,16,128]{2,1,0:T(8,128)(2,1)S(1)}, u32[]{:S(2)}, u32[]{:S(2)}) collective-permute-start(bf16[32,16,128]{2,1,0:T(8,128)(2,1)S(1)} %get-tuple-element.20), channel_id=1, source_target_pairs={{0,1},{1,0},{2,3},{3,2},{4,5},{5,4},{6,7},{7,6},{8,9},{9,8},{10,11... | collective-permute-start | bytes 393224 | tf_op jit(solution)/shard_map/ppermute | solution.py:277
  13.2 5.4 %collective-permute-start.2 = (bf16[32,16,128]{2,1,0:T(8,128)(2,1)S(1)}, bf16[32,16,128]{2,1,0:T(8,128)(2,1)S(1)}, u32[]{:S(2)}, u32[]{:S(2)}) collective-permute-start(bf16[32,16,128]{2,1,0:T(8,128)(2,1)S(1)} %add_convert_fusion.3), channel_id=1, source_target_pairs={{0,2},{1,3},{2,0},{3,1},{4,6},{5,7},{6,4},{7,5},{8,10},{9,11},{10,... | collective-permute-start | bytes 393224 | tf_op jit(solution)/shard_map/ppermute | solution.py:277
  18.6 8.2 %collective-permute-start.3 = (bf16[32,16,128]{2,1,0:T(8,128)(2,1)S(1)}, bf16[32,16,128]{2,1,0:T(8,128)(2,1)S(1)}, u32[]{:S(2)}, u32[]{:S(2)}) collective-permute-start(bf16[32,16,128]{2,1,0:T(8,128)(2,1)S(1)} %add_convert_fusion.2.sum0), channel_id=1, source_target_pairs={{0,4},{1,5},{2,6},{3,7},{4,0},{5,1},{6,2},{7,3},{8,12},{9,13},{10,... | collective-permute-start | bytes 393224 | tf_op jit(solution)/shard_map/ppermute | solution.py:277
  28.2 1.3 %collective-permute-start.4 = (f32[9,8,128]{2,1,0:T(8,128)S(1)}, f32[9,8,128]{2,1,0:T(8,128)S(1)}, u32[]{:S(2)}, u32[]{:S(2)}) collective-permute-start(f32[9,8,128]{2,1,0:T(8,128)S(1)} %get-tuple-element.21.own), channel_id=1, source_target_pairs={{0,8},{8,0},{1,9},{9,1},{2,10},{10,2},{3,11},{11,3},{4,12},{12,4},... | collective-permute-start | bytes 110600 | tf_op jit(solution)/shard_map/ppermute | solution.py:270
  31.3 5.7 %collective-permute-start.5 = (bf16[33,16,128]{2,1,0:T(8,128)(2,1)S(1)}, bf16[33,16,128]{2,1,0:T(8,128)(2,1)S(1)}, u32[]{:S(2)}, u32[]{:S(2)}) collective-permute-start(bf16[33,16,128]{2,1,0:T(8,128)(2,1)S(1)} %get-tuple-element.23), channel_id=1, source_target_pairs={{0,1},{1,0},{2,3},{3,2},{4,5},{5,4},{6,7},{7,6},{8,9},{9,8},{10,11... | collective-permute-start | bytes 405512 | tf_op jit(solution)/shard_map/ppermute | solution.py:277
  37.1 5.1 %collective-permute-start.6 = (bf16[33,16,128]{2,1,0:T(8,128)(2,1)S(1)}, bf16[33,16,128]{2,1,0:T(8,128)(2,1)S(1)}, u32[]{:S(2)}, u32[]{:S(2)}) collective-permute-start(bf16[33,16,128]{2,1,0:T(8,128)(2,1)S(1)} %add_convert_fusion.1), channel_id=1, source_target_pairs={{0,2},{1,3},{2,0},{3,1},{4,6},{5,7},{6,4},{7,5},{8,10},{9,11},{10,... | collective-permute-start | bytes 405512 | tf_op jit(solution)/shard_map/ppermute | solution.py:277
  42.2 7.5 %collective-permute-start.7 = (bf16[33,16,128]{2,1,0:T(8,128)(2,1)S(1)}, bf16[33,16,128]{2,1,0:T(8,128)(2,1)S(1)}, u32[]{:S(2)}, u32[]{:S(2)}) collective-permute-start(bf16[33,16,128]{2,1,0:T(8,128)(2,1)S(1)} %add_convert_fusion.sum0), channel_id=1, source_target_pairs={{0,4},{1,5},{2,6},{3,7},{4,0},{5,1},{6,2},{7,3},{8,12},{9,13},{10,... | collective-permute-start | bytes 405512 | tf_op jit(solution)/shard_map/ppermute | solution.py:277
  49.7 12.9 %copy-start.2 = (f32[8,512]{1,0:T(8,128)S(1)}, f32[8,512]{1,0:T(8,128)}, u32[]{:S(2)}) copy-start(f32[8,512]{1,0:T(8,128)} %x_in.1) | copy-start | bytes 49156
  49.7 12.9 %copy-start.3 = (f32[8,512]{1,0:T(8,128)S(1)}, f32[8,512]{1,0:T(8,128)}, u32[]{:S(2)}) copy-start(f32[8,512]{1,0:T(8,128)} %w_in.1) | copy-start | bytes 49156
  49.7 12.9 %copy-start.7 = (f32[8]{0:T(128)S(1)}, f32[8]{0:T(128)}, u32[]{:S(2)}) copy-start(f32[8]{0:T(128)} %phibar_in.1) | copy-start | bytes 100
  49.7 12.9 %copy-start.8 = (f32[8]{0:T(128)S(1)}, f32[8]{0:T(128)}, u32[]{:S(2)}) copy-start(f32[8]{0:T(128)} %rhobar_in.1) | copy-start | bytes 100
  51.3 1.3 %collective-permute-start.8 = (f32[9,8,128]{2,1,0:T(8,128)S(1)}, f32[9,8,128]{2,1,0:T(8,128)S(1)}, u32[]{:S(2)}, u32[]{:S(2)}) collective-permute-start(f32[9,8,128]{2,1,0:T(8,128)S(1)} %get-tuple-element.26.own), channel_id=1, source_target_pairs={{0,8},{8,0},{1,9},{9,1},{2,10},{10,2},{3,11},{11,3},{4,12},{12,4},... | collective-permute-start | bytes 110600 | tf_op jit(solution)/shard_map/ppermute | solution.py:270
  52.6 3.0 %collective-permute-start.9 = (f32[8,128]{1,0:T(8,128)S(1)}, f32[8,128]{1,0:T(8,128)S(1)}, u32[]{:S(2)}, u32[]{:S(2)}) collective-permute-start(f32[8,128]{1,0:T(8,128)S(1)} %get-tuple-element.29), channel_id=1, source_target_pairs={{0,9},{1,8},{2,11},{3,10},{4,13},{5,12},{6,15},{7,14},{8,1},{9,0},... | collective-permute-start | bytes 12296 | tf_op jit(solution)/shard_map/ppermute | solution.py:289
  55.7 3.0 %collective-permute-start.10 = (f32[8,128]{1,0:T(8,128)S(1)}, f32[8,128]{1,0:T(8,128)S(1)}, u32[]{:S(2)}, u32[]{:S(2)}) collective-permute-start(f32[8,128]{1,0:T(8,128)S(1)} %add.25), channel_id=1, source_target_pairs={{0,10},{1,11},{2,8},{3,9},{4,14},{5,15},{6,12},{7,13},{8,2},{9,3},... | collective-permute-start | bytes 12296 | tf_op jit(solution)/shard_map/ppermute | solution.py:289
  58.7 3.9 %collective-permute-start.11 = (f32[8,128]{1,0:T(8,128)S(1)}, f32[8,128]{1,0:T(8,128)S(1)}, u32[]{:S(2)}, u32[]{:S(2)}) collective-permute-start(f32[8,128]{1,0:T(8,128)S(1)} %add.26), channel_id=1, source_target_pairs={{0,12},{1,13},{2,14},{3,15},{4,8},{5,9},{6,10},{7,11},{8,4},{9,5},... | collective-permute-start | bytes 12296 | tf_op jit(solution)/shard_map/ppermute | solution.py:289

commit v5 on v4

--- a/solution.py
+++ b/solution.py
@@ -16,13 +16,14 @@
 VMEM = pl.BlockSpec(memory_space=pltpu.VMEM)
 
 
-def call(kernel, out_shape, in_specs, scratch=()):
+def call(kernel, out_shape, in_specs, scratch=(), cost=None):
     return pl.pallas_call(
         kernel,
         out_shape=out_shape,
         in_specs=in_specs,
         out_specs=jax.tree.map(lambda _: VMEM, out_shape),
         scratch_shapes=list(scratch),
+        cost_estimate=cost,
         compiler_params=pltpu.CompilerParams(vmem_limit_bytes=48 * 1024 * 1024),
     )
 
@@ -45,38 +46,30 @@
     return jnp.where(count > k, prod, 0.0)
 
 
-def forward(blks, rws, cls, cnt, v_ref, acc_ref, between=None):
+def forward(blk, rws, cls, cnt, v_ref, acc_ref):
     count = jnp.broadcast_to(cnt[...], (8, 128))
     acc_ref[...] = jnp.zeros_like(acc_ref)
-    k = 0
-    for blk in blks:
-        if between is not None and k > 0:
-            between()
-        for at in range(0, blk.shape[0], 2):
-            pair = jnp.concatenate([v_ref[cls[0, 0, k]], v_ref[cls[0, 0, k + 1]]], axis=0)
-            a = blk[at : at + 2].reshape(256, 128)
-            prod = lax.dot_general(
-                pair.astype(BF16), a, (((1,), (1,)), ((), ())), preferred_element_type=F32
-            )
-            acc_ref[rws[0, 0, k]] += used(count, k, prod[:8, :128])
-            acc_ref[rws[0, 0, k + 1]] += used(count, k + 1, prod[8:, 128:])
-            k += 2
-
-
-def backward(blks, rws, cls, cnt, u_ref, acc_ref):
+    for k in range(0, blk.shape[0], 2):
+        pair = jnp.concatenate([v_ref[cls[0, 0, k]], v_ref[cls[0, 0, k + 1]]], axis=0)
+        a = blk[k : k + 2].reshape(256, 128)
+        prod = lax.dot_general(
+            pair.astype(BF16), a, (((1,), (1,)), ((), ())), preferred_element_type=F32
+        )
+        acc_ref[rws[0, 0, k]] += used(count, k, prod[:8, :128])
+        acc_ref[rws[0, 0, k + 1]] += used(count, k + 1, prod[8:, 128:])
+
+
+def backward(blk, rws, cls, cnt, u_ref, acc_ref):
     count = jnp.broadcast_to(cnt[...], (8, 128))
     acc_ref[...] = jnp.zeros_like(acc_ref)
     zero = jnp.zeros((8, 128), F32)
-    k = 0
-    for blk in blks:
-        for at in range(0, blk.shape[0], 2):
-            u0 = jnp.concatenate([u_ref[rws[0, 0, k]], zero], axis=0).astype(BF16)
-            u1 = jnp.concatenate([zero, u_ref[rws[0, 0, k + 1]]], axis=0).astype(BF16)
-            a = blk[at : at + 2].reshape(256, 128)
-            prod = jnp.dot(jnp.concatenate([u0, u1], axis=1), a, preferred_element_type=F32)
-            acc_ref[cls[0, 0, k]] += used(count, k, prod[:8])
-            acc_ref[cls[0, 0, k + 1]] += used(count, k + 1, prod[8:])
-            k += 2
+    for k in range(0, blk.shape[0], 2):
+        u0 = jnp.concatenate([u_ref[rws[0, 0, k]], zero], axis=0).astype(BF16)
+        u1 = jnp.concatenate([zero, u_ref[rws[0, 0, k + 1]]], axis=0).astype(BF16)
+        a = blk[k : k + 2].reshape(256, 128)
+        prod = jnp.dot(jnp.concatenate([u0, u1], axis=1), a, preferred_element_type=F32)
+        acc_ref[cls[0, 0, k]] += used(count, k, prod[:8])
+        acc_ref[cls[0, 0, k + 1]] += used(count, k + 1, prod[8:])
 
 
 def column(ref):
@@ -112,25 +105,22 @@
         out_ref[(1 - row) * half + b] = other[:, b * 128 : (b + 1) * 128]
 
 
-def load(blk_hbm, blk, sem):
-    copy = pltpu.make_async_copy(blk_hbm.at[0, 0, pl.ds(0, blk.shape[0])], blk, sem)
+def load(own_hbm, own, sem):
+    copy = pltpu.make_async_copy(own_hbm, own, sem)
     copy.start()
     copy.wait()
 
 
 def first_forward(
-    rws_ref, cls_ref, cnt, alpha, blk0, blk_hbm, own, other, u_piece,
-    out, v_out, blk1,
-    rws, cls, sems, sem, acc,
-):
-    rest = blk1.shape[0]
-    copy = pltpu.make_async_copy(blk_hbm.at[0, 0, pl.ds(blk0.shape[0], rest)], blk1, sem)
-    copy.start()
+    rws_ref, cls_ref, cnt, alpha, blk, own, other, u_piece,
+    out, v_out,
+    rws, cls, sems, acc,
+):
     copies = lists(rws_ref, cls_ref, rws, cls, sems)
     place_halves(own, other, v_out)
     for c in copies:
         c.wait()
-    forward((blk0, blk1), rws, cls, cnt, v_out, acc, copy.wait)
+    forward(blk, rws, cls, cnt, v_out, acc)
     pieces = u_piece.shape[1] // 128
     base = lax.axis_index("col") * pieces
     a = column(alpha)
@@ -139,7 +129,7 @@
     store_pairs(acc, out, acc.shape[0])
 
 
-def first_backward(rws_ref, cls_ref, cnt, blk0, blk1, sum0, sum1, upd, message, rws, cls, sems, acc):
+def first_backward(rws_ref, cls_ref, cnt, blk, sum0, sum1, upd, message, rws, cls, sems, acc):
     copies = lists(rws_ref, cls_ref, rws, cls, sems)
     blocks = upd.shape[0]
     for b in range(blocks // 2):
@@ -150,13 +140,13 @@
     message[cells] = squares(upd, blocks)
     for c in copies:
         c.wait()
-    backward((blk0, blk1), rws, cls, cnt, upd, acc)
+    backward(blk, rws, cls, cnt, upd, acc)
     message[:cells] = acc[...]
 
 
 def next_forward(
     total_rays,
-    rws_ref, cls_ref, cnt, blk0, blk1, own, other, v_old,
+    rws_ref, cls_ref, cnt, blk, own, other, v_old,
     out, vupd, beta_out,
     rws, cls, sems, acc,
 ):
@@ -175,13 +165,13 @@
     out[rays // 2] = jnp.concatenate([high, sq - high], axis=0).astype(BF16)
     for c in copies:
         c.wait()
-    forward((blk0, blk1), rws, cls, cnt, vupd, acc)
+    forward(blk, rws, cls, cnt, vupd, acc)
     store_pairs(acc, out, rays)
 
 
 def next_backward(
     total_cells, pieces,
-    rws_ref, cls_ref, cnt, blk0, blk1, sum0, sum1, old, beta,
+    rws_ref, cls_ref, cnt, blk, sum0, sum1, old, beta,
     message, u_piece, alpha_out,
     rws, cls, sems, upd, acc,
 ):
@@ -203,7 +193,7 @@
         u_piece[b] = upd[base + b]
     for c in copies:
         c.wait()
-    backward((blk0, blk1), rws, cls, cnt, upd, acc)
+    backward(blk, rws, cls, cnt, upd, acc)
     message[:cells] = acc[...]
 
 
@@ -272,11 +262,11 @@
 
 def column_sum(x):
     n = lax.axis_size("col")
-    m = 1
-    while True:
-        y = lax.ppermute(x, "col", [(i, i ^ m) for i in range(n)])
-        m *= 2
-        if m >= n:
+    steps = [1 << i for i in range((n - 1).bit_length())]
+    for first, second in zip(steps, steps[-1:] + steps[:-1]):
+        pairs = [(i, i ^ first) for i in range(n)] + [(n + i, n + (i ^ second)) for i in range(n)]
+        y = lax.ppermute(x, ("row", "col"), pairs)
+        if first == steps[-1]:
             return x, y
         x = (x.astype(F32) + y.astype(F32)).astype(BF16)
 
@@ -310,36 +300,40 @@
     ]
     ray_acc = pltpu.VMEM((rays, 8, 128), F32)
     cell_acc = pltpu.VMEM((cells, 8, 128), F32)
-    slots = blocks.shape[2]
-    half_blk = shape(slots // 2, 128, 128, dtype=BF16)
-
-    v_other = other_core(v_cells)
-    blk0 = call(load, half_blk, [HBM], [pltpu.SemaphoreType.DMA])(blocks)
-    part, v0, blk1 = call(
+    own = call(
+        load,
+        shape(*v_cells.shape),
+        [HBM],
+        [pltpu.SemaphoreType.DMA],
+        pl.CostEstimate(flops=5 * 10**9, bytes_accessed=1, transcendentals=0),
+    )(v_cells)
+    v_other = other_core(own)
+    blk = blocks.reshape(blocks.shape[2:])
+    part, v0 = call(
         first_forward,
-        (shape(rays // 2, 16, 128, dtype=BF16), shape(cells, 8, 128), half_blk),
-        [VMEM] * 3 + [SMEM, VMEM, HBM] + [VMEM] * 3,
-        listed + [pltpu.SemaphoreType.DMA, ray_acc],
-    )(*where, alpha, blk0, blocks, v_cells, v_other, u_rays)
-    operator = (*where, blk0, blk1)
+        (shape(rays // 2, 16, 128, dtype=BF16), shape(cells, 8, 128)),
+        [VMEM] * 3 + [SMEM] + [VMEM] * 4,
+        listed + [ray_acc],
+    )(*where, alpha, blk, own, v_other, u_rays)
+    operator = (*where, blk)
     sum0, sum1 = column_sum(part)
     upd1, message = call(
         first_backward,
         (shape(rays, 8, 128), shape(cells + 1, 8, 128)),
-        [VMEM] * 7,
+        [VMEM] * 6,
         listed + [cell_acc],
     )(*operator, sum0, sum1)
     part, v1, beta1 = call(
         functools.partial(next_forward, total_rays),
         (shape(rays // 2 + 1, 16, 128, dtype=BF16), shape(cells, 8, 128), shape(8, 128)),
-        [VMEM] * 8,
+        [VMEM] * 7,
         listed + [ray_acc],
     )(*operator, message, other_core(message), v0)
     sum0, sum1 = column_sum(part)
     message, u_piece, alpha1 = call(
         functools.partial(next_backward, total_cells, pieces),
         (shape(cells + 1, 8, 128), shape(pieces, 8, 128), shape(8, 128)),
-        [VMEM] * 9,
+        [VMEM] * 8,
         listed + [pltpu.VMEM((rays, 8, 128), F32), cell_acc],
     )(*operator, sum0, sum1, upd1, beta1)
     sq, v2, beta2 = call(

time: 64.1 us -> 59.6 us (0.930)
  waiting for transfers between devices: 36.6 us -> 24.9 us
  starting transfers between devices: 15.1 us -> 23.6 us
  Pallas kernels: 10.5 us -> 8.37 us
  local copies, waits for them, and re-layouts: 0.04 us -> 0.9 us
    ppermute x6, waiting for transfers between devices: 27.5 us -> 17.8 us  [column_sum(): y = lax.ppermute(x, ('row', 'col'), pairs)]
    ppermute x6, starting transfers between devices: 11.2 us -> 16.2 us  [column_sum(): y = lax.ppermute(x, ('row', 'col'), pairs)]
    ppermute x3, starting transfers between devices: 3.28 us -> 6.75 us  [last_sum(): x = x + lax.ppermute(x, ('row', 'col'), pairs)]
    ppermute x3, waiting for transfers between devices: 6.72 us -> 4.45 us  [last_sum(): x = x + lax.ppermute(x, ('row', 'col'), pairs)]
    pallas_call x1, Pallas kernels: 1.63 us -> 0.02 us  [body(): call(load, shape(*v_cells.shape), [HBM], [pltpu.SemaphoreType.DMA], pl.Co...]
    unnamed x18 -> x20, local copies, waits for them, and re-layouts: 0.04 us -> 0.9 us
  transfers between devices with their start and end apart: 12 -> 12, of which waited for: 11 -> 12; matrix products, arithmetic and copies ran while one was open for 0% -> 0% of each run, Pallas kernels for 3% -> 0%
where the time goes in v5:
time: 59.6 us; the launch traced here: 59.3 us
  waiting for transfers between devices  24.9 us (42%)
  starting transfers between devices  23.6 us (40%)
  Pallas kernels  8.37 us (14%)
  between operations  1.45 us (2%)
  local copies, waits for them, and re-layouts  0.9 us (2%)
    ppermute x6, waiting for transfers between devices, column_sum(): y = lax.ppermute(x, ('row', 'col'), pairs)  17.8 us
    ppermute x6, starting transfers between devices, column_sum(): y = lax.ppermute(x, ('row', 'col'), pairs)  16.2 us
    ppermute x3, starting transfers between devices, last_sum(): x = x + lax.ppermute(x, ('row', 'col'), pairs)  6.75 us
    ppermute x3, waiting for transfers between devices, last_sum(): x = x + lax.ppermute(x, ('row', 'col'), pairs)  4.45 us
    ppermute x3, waiting for transfers between devices, other_core(): return lax.ppermute(x, 'row', [(0, 1), (1, 0)])  2.59 us
    pallas_call x1, Pallas kernels, body(): call(first_forward, (shape(rays // 2, 16, 128, dtype=BF16), shape(cells,...  2.35 us
    pallas_call x1, Pallas kernels, body(): call(functools.partial(next_forward, total_rays), (shape(rays // 2 + 1, 1...  1.81 us
    pallas_call x1, Pallas kernels, body(): call(functools.partial(next_backward, total_cells, pieces), (shape(cells...  1.51 us
  transfers between devices with their start and end apart: 12, of which 12 were waited for; matrix products, arithmetic and copies ran while one was open for 0% of the time, Pallas kernels for 0%

profile of v5, /device:TPU:0, one launch (start us, length us, event | category | flops | bytes accessed | tf_op | source)
XLA Modules:
  0.0 59.3 jit_solution(10610679835253897557)
XLA Ops:
  0.6 0.0 copy-start.5
  0.6 0.0 copy-start.4
  0.7 0.0 copy-start.8
  0.7 0.0 copy-start.1
  0.7 0.0 copy-start
  0.7 0.0 copy-start.9
  0.7 0.9 %copy-done.9 = f32[8,512]{1,0:T(8,128)S(1)} copy-done((f32[8,512]{1,0:T(8,128)S(1)}, f32[8,512]{1,0:T(8,128)}, u32[]{:S(2)}) %copy-start.9) | copy-done | bytes 16408
  1.6 0.5 collective-permute-start
  2.7 0.2 collective-permute-done.other
  2.9 0.0 copy-done.5
  2.9 0.0 copy-done.4
  2.9 0.0 copy-done.8
  2.9 0.0 copy-done.1
  2.9 0.0 copy-done
  3.0 2.4 %shard_map.147 = (bf16[32,16,128]{2,1,0:T(8,128)(2,1)S(1)}, f32[8,8,128]{2,1,0:T(8,128)S(1)}) custom-call(s32[1,1,128]{2,1,0:T(1,128)S(1)} %copy-done.4, s32[1,1,128]{2,1,0:T(1,128)S(1)} %copy-done.5, s32[1,1]{1,0:T(1,128)S(6)} %copy.16.cnt, f32[8]{0:T(128)S(1)} %copy-done.8, bf16[128,128,128]{2,1,0:T(8,128)(2,1)S(1)} %bitcast.1, ...), custom_call_target="tpu_custom_call" | custom-call | tf_op jit(solution)/shard_map/pallas_call | solution.py:312
  5.3 2.9 %collective-permute-start.1 = (bf16[32,16,128]{2,1,0:T(8,128)(2,1)S(1)}, bf16[32,16,128]{2,1,0:T(8,128)(2,1)S(1)}, u32[]{:S(2)}, u32[]{:S(2)}) collective-permute-start(bf16[32,16,128]{2,1,0:T(8,128)(2,1)S(1)} %get-tuple-element.18), channel_id=1, source_target_pairs={{0,1},{1,0},{2,3},{3,2},{4,5},{5,4},{6,7},{7,6},{8,12},{9,13},{10,... | collective-permute-start | bytes 393224 | tf_op jit(solution)/shard_map/ppermute | solution.py:268
  8.3 2.9 %collective-permute-done.1 = bf16[32,16,128]{2,1,0:T(8,128)(2,1)S(1)} collective-permute-done((bf16[32,16,128]{2,1,0:T(8,128)(2,1)S(1)}, bf16[32,16,128]{2,1,0:T(8,128)(2,1)S(1)}, u32[]{:S(2)}, u32[]{:S(2)}) %collective-permute-start.1) | collective-permute-done | bytes 131104 | tf_op jit(solution)/shard_map/ppermute | solution.py:268
  11.3 2.2 %collective-permute-start.2 = (bf16[32,16,128]{2,1,0:T(8,128)(2,1)S(1)}, bf16[32,16,128]{2,1,0:T(8,128)(2,1)S(1)}, u32[]{:S(2)}, u32[]{:S(2)}) collective-permute-start(bf16[32,16,128]{2,1,0:T(8,128)(2,1)S(1)} %add_convert_fusion.3), channel_id=1, source_target_pairs={{0,2},{1,3},{2,0},{3,1},{4,6},{5,7},{6,4},{7,5},{8,9},{9,8},{10,11... | collective-permute-start | bytes 393224 | tf_op jit(solution)/shard_map/ppermute | solution.py:268
  13.4 2.9 %collective-permute-done.2 = bf16[32,16,128]{2,1,0:T(8,128)(2,1)S(1)} collective-permute-done((bf16[32,16,128]{2,1,0:T(8,128)(2,1)S(1)}, bf16[32,16,128]{2,1,0:T(8,128)(2,1)S(1)}, u32[]{:S(2)}, u32[]{:S(2)}) %collective-permute-start.2) | collective-permute-done | bytes 131104 | tf_op jit(solution)/shard_map/ppermute | solution.py:268
  16.4 3.1 %collective-permute-start.3 = (bf16[32,16,128]{2,1,0:T(8,128)(2,1)S(1)}, bf16[32,16,128]{2,1,0:T(8,128)(2,1)S(1)}, u32[]{:S(2)}, u32[]{:S(2)}) collective-permute-start(bf16[32,16,128]{2,1,0:T(8,128)(2,1)S(1)} %add_convert_fusion.2.sum0), channel_id=1, source_target_pairs={{0,4},{1,5},{2,6},{3,7},{4,0},{5,1},{6,2},{7,3},{8,10},{9,11},{10,... | collective-permute-start | bytes 393224 | tf_op jit(solution)/shard_map/ppermute | solution.py:268
  19.5 3.0 %collective-permute-done.3.sum1 = bf16[32,16,128]{2,1,0:T(8,128)(2,1)S(1)} collective-permute-done((bf16[32,16,128]{2,1,0:T(8,128)(2,1)S(1)}, bf16[32,16,128]{2,1,0:T(8,128)(2,1)S(1)}, u32[]{:S(2)}, u32[]{:S(2)}) %collective-permute-start.3) | collective-permute-done | bytes 131104 | tf_op jit(solution)/shard_map/ppermute | solution.py:268
  22.5 1.4 %shard_map.148 = (f32[64,8,128]{2,1,0:T(8,128)S(1)}, f32[9,8,128]{2,1,0:T(8,128)S(1)}) custom-call(s32[1,1,128]{2,1,0:T(1,128)S(1)} %copy-done.4, s32[1,1,128]{2,1,0:T(1,128)S(1)} %copy-done.5, s32[1,1]{1,0:T(1,128)S(6)} %copy.16.cnt, bf16[128,128,128]{2,1,0:T(8,128)(2,1)S(1)} %bitcast.2, bf16[32,16,128]{2,1,0:T(8,128)(2,1)S(1)} %add_convert_fusion.2.sum0, ...), custom_call_target="tpu_custom_call" | custom-call | tf_op jit(solution)/shard_map/pallas_call | solution.py:320
  23.9 0.1 collective-permute-start.4
  23.9 1.2 %collective-permute-done.4.other = f32[9,8,128]{2,1,0:T(8,128)S(1)} collective-permute-done((f32[9,8,128]{2,1,0:T(8,128)S(1)}, f32[9,8,128]{2,1,0:T(8,128)S(1)}, u32[]{:S(2)}, u32[]{:S(2)}) %collective-permute-start.4) | collective-permute-done | bytes 36896 | tf_op jit(solution)/shard_map/ppermute | solution.py:260
  25.1 0.0 copy-start.2
  25.1 0.0 copy-start.3
  25.1 1.8 %shard_map.149 = (bf16[33,16,128]{2,1,0:T(8,128)(2,1)S(1)}, f32[8,8,128]{2,1,0:T(8,128)S(1)}, f32[8,128]{1,0:T(8,128)S(1)}) custom-call(s32[1,1,128]{2,1,0:T(1,128)S(1)} %copy-done.4, s32[1,1,128]{2,1,0:T(1,128)S(1)} %copy-done.5, s32[1,1]{1,0:T(1,128)S(6)} %copy.16.cnt, bf16[128,128,128]{2,1,0:T(8,128)(2,1)S(1)} %bitcast.3, ...), custom_call_target="tpu_custom_call" | custom-call | tf_op jit(solution)/shard_map/pallas_call | solution.py:326
  27.0 2.3 %collective-permute-start.5 = (bf16[33,16,128]{2,1,0:T(8,128)(2,1)S(1)}, bf16[33,16,128]{2,1,0:T(8,128)(2,1)S(1)}, u32[]{:S(2)}, u32[]{:S(2)}) collective-permute-start(bf16[33,16,128]{2,1,0:T(8,128)(2,1)S(1)} %get-tuple-element.21), channel_id=1, source_target_pairs={{0,1},{1,0},{2,3},{3,2},{4,5},{5,4},{6,7},{7,6},{8,12},{9,13},{10,... | collective-permute-start | bytes 405512 | tf_op jit(solution)/shard_map/ppermute | solution.py:268
  29.2 3.0 %collective-permute-done.5 = bf16[33,16,128]{2,1,0:T(8,128)(2,1)S(1)} collective-permute-done((bf16[33,16,128]{2,1,0:T(8,128)(2,1)S(1)}, bf16[33,16,128]{2,1,0:T(8,128)(2,1)S(1)}, u32[]{:S(2)}, u32[]{:S(2)}) %collective-permute-start.5) | collective-permute-done | bytes 135200 | tf_op jit(solution)/shard_map/ppermute | solution.py:268
  32.3 2.3 %collective-permute-start.6 = (bf16[33,16,128]{2,1,0:T(8,128)(2,1)S(1)}, bf16[33,16,128]{2,1,0:T(8,128)(2,1)S(1)}, u32[]{:S(2)}, u32[]{:S(2)}) collective-permute-start(bf16[33,16,128]{2,1,0:T(8,128)(2,1)S(1)} %add_convert_fusion.1), channel_id=1, source_target_pairs={{0,2},{1,3},{2,0},{3,1},{4,6},{5,7},{6,4},{7,5},{8,9},{9,8},{10,11... | collective-permute-start | bytes 405512 | tf_op jit(solution)/shard_map/ppermute | solution.py:268
  34.5 3.0 %collective-permute-done.6 = bf16[33,16,128]{2,1,0:T(8,128)(2,1)S(1)} collective-permute-done((bf16[33,16,128]{2,1,0:T(8,128)(2,1)S(1)}, bf16[33,16,128]{2,1,0:T(8,128)(2,1)S(1)}, u32[]{:S(2)}, u32[]{:S(2)}) %collective-permute-start.6) | collective-permute-done | bytes 135200 | tf_op jit(solution)/shard_map/ppermute | solution.py:268
  37.6 3.4 %collective-permute-start.7 = (bf16[33,16,128]{2,1,0:T(8,128)(2,1)S(1)}, bf16[33,16,128]{2,1,0:T(8,128)(2,1)S(1)}, u32[]{:S(2)}, u32[]{:S(2)}) collective-permute-start(bf16[33,16,128]{2,1,0:T(8,128)(2,1)S(1)} %add_convert_fusion.sum0), channel_id=1, source_target_pairs={{0,4},{1,5},{2,6},{3,7},{4,0},{5,1},{6,2},{7,3},{8,10},{9,11},{10,... | collective-permute-start | bytes 405512 | tf_op jit(solution)/shard_map/ppermute | solution.py:268
  41.0 3.0 %collective-permute-done.7.sum1 = bf16[33,16,128]{2,1,0:T(8,128)(2,1)S(1)} collective-permute-done((bf16[33,16,128]{2,1,0:T(8,128)(2,1)S(1)}, bf16[33,16,128]{2,1,0:T(8,128)(2,1)S(1)}, u32[]{:S(2)}, u32[]{:S(2)}) %collective-permute-start.7) | collective-permute-done | bytes 135200 | tf_op jit(solution)/shard_map/ppermute | solution.py:268
  44.0 1.5 %shard_map.150 = (f32[9,8,128]{2,1,0:T(8,128)S(1)}, f32[8,8,128]{2,1,0:T(8,128)S(1)}, f32[8,128]{1,0:T(8,128)S(1)}) custom-call(s32[1,1,128]{2,1,0:T(1,128)S(1)} %copy-done.4, s32[1,1,128]{2,1,0:T(1,128)S(1)} %copy-done.5, s32[1,1]{1,0:T(1,128)S(6)} %copy.16.cnt, bf16[128,128,128]{2,1,0:T(8,128)(2,1)S(1)} %bitcast.4, ...), custom_call_target="tpu_custom_call" | custom-call | tf_op jit(solution)/shard_map/pallas_call | solution.py:333
  45.5 0.1 collective-permute-start.8
  45.6 1.2 %collective-permute-done.8.other = f32[9,8,128]{2,1,0:T(8,128)S(1)} collective-permute-done((f32[9,8,128]{2,1,0:T(8,128)S(1)}, f32[9,8,128]{2,1,0:T(8,128)S(1)}, u32[]{:S(2)}, u32[]{:S(2)}) %collective-permute-start.8) | collective-permute-done | bytes 36896 | tf_op jit(solution)/shard_map/ppermute | solution.py:260
  46.8 0.1 shard_map.151
  46.9 1.2 %collective-permute-start.9 = (f32[8,128]{1,0:T(8,128)S(1)}, f32[8,128]{1,0:T(8,128)S(1)}, u32[]{:S(2)}, u32[]{:S(2)}) collective-permute-start(f32[8,128]{1,0:T(8,128)S(1)} %get-tuple-element.27), channel_id=1, source_target_pairs={{0,9},{1,8},{2,11},{3,10},{4,13},{5,12},{6,15},{7,14},{8,1},{9,0},... | collective-permute-start | bytes 12296 | tf_op jit(solution)/shard_map/ppermute | solution.py:279
  48.2 1.8 %collective-permute-done.9 = f32[8,128]{1,0:T(8,128)S(1)} collective-permute-done((f32[8,128]{1,0:T(8,128)S(1)}, f32[8,128]{1,0:T(8,128)S(1)}, u32[]{:S(2)}, u32[]{:S(2)}) %collective-permute-start.9) | collective-permute-done | bytes 4128 | tf_op jit(solution)/shard_map/ppermute | solution.py:279
  49.9 2.2 %collective-permute-start.10 = (f32[8,128]{1,0:T(8,128)S(1)}, f32[8,128]{1,0:T(8,128)S(1)}, u32[]{:S(2)}, u32[]{:S(2)}) collective-permute-start(f32[8,128]{1,0:T(8,128)S(1)} %add.25), channel_id=1, source_target_pairs={{0,10},{1,11},{2,8},{3,9},{4,14},{5,15},{6,12},{7,13},{8,2},{9,3},... | collective-permute-start | bytes 12296 | tf_op jit(solution)/shard_map/ppermute | solution.py:279
  52.2 1.3 %collective-permute-done.10 = f32[8,128]{1,0:T(8,128)S(1)} collective-permute-done((f32[8,128]{1,0:T(8,128)S(1)}, f32[8,128]{1,0:T(8,128)S(1)}, u32[]{:S(2)}, u32[]{:S(2)}) %collective-permute-start.10) | collective-permute-done | bytes 4128 | tf_op jit(solution)/shard_map/ppermute | solution.py:279
  53.5 3.3 %collective-permute-start.11 = (f32[8,128]{1,0:T(8,128)S(1)}, f32[8,128]{1,0:T(8,128)S(1)}, u32[]{:S(2)}, u32[]{:S(2)}) collective-permute-start(f32[8,128]{1,0:T(8,128)S(1)} %add.26), channel_id=1, source_target_pairs={{0,12},{1,13},{2,14},{3,15},{4,8},{5,9},{6,10},{7,11},{8,4},{9,5},... | collective-permute-start | bytes 12296 | tf_op jit(solution)/shard_map/ppermute | solution.py:279
  56.8 1.3 %collective-permute-done.11 = f32[8,128]{1,0:T(8,128)S(1)} collective-permute-done((f32[8,128]{1,0:T(8,128)S(1)}, f32[8,128]{1,0:T(8,128)S(1)}, u32[]{:S(2)}, u32[]{:S(2)}) %collective-permute-start.11) | collective-permute-done | bytes 4128 | tf_op jit(solution)/shard_map/ppermute | solution.py:279
  58.1 0.0 copy-done.2
  58.1 0.0 copy-done.3
  58.1 0.0 copy-done.6
  58.1 0.0 copy-done.7
  58.1 1.2 %shard_map.152 = (f32[8,1024]{1,0:T(8,128)}, f32[8,512]{1,0:T(8,128)}, f32[8,512]{1,0:T(8,128)}, f32[8,512]{1,0:T(8,128)}, f32[3,8]{1,0:T(4,128)}) custom-call(f32[8]{0:T(128)S(1)} %copy-done.6, f32[8]{0:T(128)S(1)} %copy-done.7, f32[8,128]{1,0:T(8,128)S(1)} %add.27.sq, f32[8,8,128]{2,1,0:T(8,128)S(1)} %get-tuple-element.25.v_old.v1, ...), custom_call_target="tpu_custom_call" | custom-call | tf_op jit(solution)/shard_map/pallas_call | solution.py:346
  (10 shorter events, 0.2 us)
Async XLA Ops:
  0.6 2.3 %copy-start.5 = (s32[1,1,128]{2,1,0:T(1,128)S(1)}, s32[1,1,128]{2,1,0:T(1,128)}, u32[]{:S(2)}) copy-start(s32[1,1,128]{2,1,0:T(1,128)} %cls_ref.7) | copy-start | bytes 1540
  0.6 2.3 %copy-start.4 = (s32[1,1,128]{2,1,0:T(1,128)S(1)}, s32[1,1,128]{2,1,0:T(1,128)}, u32[]{:S(2)}) copy-start(s32[1,1,128]{2,1,0:T(1,128)} %rws_ref.7) | copy-start | bytes 1540
  0.7 2.3 %copy-start.8 = (f32[8]{0:T(128)S(1)}, f32[8]{0:T(128)}, u32[]{:S(2)}) copy-start(f32[8]{0:T(128)} %alpha.1) | copy-start | bytes 100
  0.7 2.3 %copy-start.1 = (f32[8,1024]{1,0:T(8,128)S(1)}, f32[8,1024]{1,0:T(8,128)}, u32[]{:S(2)}) copy-start(f32[8,1024]{1,0:T(8,128)} %u_piece.1) | copy-start | bytes 98308
  0.7 2.3 %copy-start = (bf16[1,1,128,128,128]{4,3,2,1,0:T(8,128)(2,1)S(1)}, bf16[1,1,128,128,128]{4,3,2,1,0:T(8,128)(2,1)}, u32[]{:S(2)}) copy-start(bf16[1,1,128,128,128]{4,3,2,1,0:T(8,128)(2,1)} %param.11) | copy-start | bytes 12582916
  0.7 0.9 %copy-start.9 = (f32[8,512]{1,0:T(8,128)S(1)}, f32[8,512]{1,0:T(8,128)}, u32[]{:S(2)}) copy-start(f32[8,512]{1,0:T(8,128)} %own_hbm.1) | copy-start | bytes 49156
  1.6 1.4 %collective-permute-start = (f32[8,512]{1,0:T(8,128)S(1)}, f32[8,512]{1,0:T(8,128)S(1)}, u32[]{:S(2)}, u32[]{:S(2)}) collective-permute-start(f32[8,512]{1,0:T(8,128)S(1)} %shard_map.146.own), channel_id=1, source_target_pairs={{0,8},{8,0},{1,9},{9,1},{2,10},{10,2},{3,11},{11,3},{4,12},{12,4},... | collective-permute-start | bytes 49160 | tf_op jit(solution)/shard_map/ppermute | solution.py:260
  5.3 5.9 %collective-permute-start.1 = (bf16[32,16,128]{2,1,0:T(8,128)(2,1)S(1)}, bf16[32,16,128]{2,1,0:T(8,128)(2,1)S(1)}, u32[]{:S(2)}, u32[]{:S(2)}) collective-permute-start(bf16[32,16,128]{2,1,0:T(8,128)(2,1)S(1)} %get-tuple-element.18), channel_id=1, source_target_pairs={{0,1},{1,0},{2,3},{3,2},{4,5},{5,4},{6,7},{7,6},{8,12},{9,13},{10,... | collective-permute-start | bytes 393224 | tf_op jit(solution)/shard_map/ppermute | solution.py:268
  11.3 5.1 %collective-permute-start.2 = (bf16[32,16,128]{2,1,0:T(8,128)(2,1)S(1)}, bf16[32,16,128]{2,1,0:T(8,128)(2,1)S(1)}, u32[]{:S(2)}, u32[]{:S(2)}) collective-permute-start(bf16[32,16,128]{2,1,0:T(8,128)(2,1)S(1)} %add_convert_fusion.3), channel_id=1, source_target_pairs={{0,2},{1,3},{2,0},{3,1},{4,6},{5,7},{6,4},{7,5},{8,9},{9,8},{10,11... | collective-permute-start | bytes 393224 | tf_op jit(solution)/shard_map/ppermute | solution.py:268
  16.4 6.1 %collective-permute-start.3 = (bf16[32,16,128]{2,1,0:T(8,128)(2,1)S(1)}, bf16[32,16,128]{2,1,0:T(8,128)(2,1)S(1)}, u32[]{:S(2)}, u32[]{:S(2)}) collective-permute-start(bf16[32,16,128]{2,1,0:T(8,128)(2,1)S(1)} %add_convert_fusion.2.sum0), channel_id=1, source_target_pairs={{0,4},{1,5},{2,6},{3,7},{4,0},{5,1},{6,2},{7,3},{8,10},{9,11},{10,... | collective-permute-start | bytes 393224 | tf_op jit(solution)/shard_map/ppermute | solution.py:268
  23.9 1.3 %collective-permute-start.4 = (f32[9,8,128]{2,1,0:T(8,128)S(1)}, f32[9,8,128]{2,1,0:T(8,128)S(1)}, u32[]{:S(2)}, u32[]{:S(2)}) collective-permute-start(f32[9,8,128]{2,1,0:T(8,128)S(1)} %get-tuple-element.19.own), channel_id=1, source_target_pairs={{0,8},{8,0},{1,9},{9,1},{2,10},{10,2},{3,11},{11,3},{4,12},{12,4},... | collective-permute-start | bytes 110600 | tf_op jit(solution)/shard_map/ppermute | solution.py:260
  25.1 33.0 %copy-start.2 = (f32[8,512]{1,0:T(8,128)S(1)}, f32[8,512]{1,0:T(8,128)}, u32[]{:S(2)}) copy-start(f32[8,512]{1,0:T(8,128)} %x_in.1) | copy-start | bytes 49156
  25.1 33.0 %copy-start.3 = (f32[8,512]{1,0:T(8,128)S(1)}, f32[8,512]{1,0:T(8,128)}, u32[]{:S(2)}) copy-start(f32[8,512]{1,0:T(8,128)} %w_in.1) | copy-start | bytes 49156
  25.1 33.0 %copy-start.6 = (f32[8]{0:T(128)S(1)}, f32[8]{0:T(128)}, u32[]{:S(2)}) copy-start(f32[8]{0:T(128)} %phibar_in.1) | copy-start | bytes 100
  25.1 33.0 %copy-start.7 = (f32[8]{0:T(128)S(1)}, f32[8]{0:T(128)}, u32[]{:S(2)}) copy-start(f32[8]{0:T(128)} %rhobar_in.1) | copy-start | bytes 100
  27.0 5.3 %collective-permute-start.5 = (bf16[33,16,128]{2,1,0:T(8,128)(2,1)S(1)}, bf16[33,16,128]{2,1,0:T(8,128)(2,1)S(1)}, u32[]{:S(2)}, u32[]{:S(2)}) collective-permute-start(bf16[33,16,128]{2,1,0:T(8,128)(2,1)S(1)} %get-tuple-element.21), channel_id=1, source_target_pairs={{0,1},{1,0},{2,3},{3,2},{4,5},{5,4},{6,7},{7,6},{8,12},{9,13},{10,... | collective-permute-start | bytes 405512 | tf_op jit(solution)/shard_map/ppermute | solution.py:268
  32.3 5.3 %collective-permute-start.6 = (bf16[33,16,128]{2,1,0:T(8,128)(2,1)S(1)}, bf16[33,16,128]{2,1,0:T(8,128)(2,1)S(1)}, u32[]{:S(2)}, u32[]{:S(2)}) collective-permute-start(bf16[33,16,128]{2,1,0:T(8,128)(2,1)S(1)} %add_convert_fusion.1), channel_id=1, source_target_pairs={{0,2},{1,3},{2,0},{3,1},{4,6},{5,7},{6,4},{7,5},{8,9},{9,8},{10,11... | collective-permute-start | bytes 405512 | tf_op jit(solution)/shard_map/ppermute | solution.py:268
  37.6 6.4 %collective-permute-start.7 = (bf16[33,16,128]{2,1,0:T(8,128)(2,1)S(1)}, bf16[33,16,128]{2,1,0:T(8,128)(2,1)S(1)}, u32[]{:S(2)}, u32[]{:S(2)}) collective-permute-start(bf16[33,16,128]{2,1,0:T(8,128)(2,1)S(1)} %add_convert_fusion.sum0), channel_id=1, source_target_pairs={{0,4},{1,5},{2,6},{3,7},{4,0},{5,1},{6,2},{7,3},{8,10},{9,11},{10,... | collective-permute-start | bytes 405512 | tf_op jit(solution)/shard_map/ppermute | solution.py:268
  45.5 1.3 %collective-permute-start.8 = (f32[9,8,128]{2,1,0:T(8,128)S(1)}, f32[9,8,128]{2,1,0:T(8,128)S(1)}, u32[]{:S(2)}, u32[]{:S(2)}) collective-permute-start(f32[9,8,128]{2,1,0:T(8,128)S(1)} %get-tuple-element.24.own), channel_id=1, source_target_pairs={{0,8},{8,0},{1,9},{9,1},{2,10},{10,2},{3,11},{11,3},{4,12},{12,4},... | collective-permute-start | bytes 110600 | tf_op jit(solution)/shard_map/ppermute | solution.py:260
  46.9 3.0 %collective-permute-start.9 = (f32[8,128]{1,0:T(8,128)S(1)}, f32[8,128]{1,0:T(8,128)S(1)}, u32[]{:S(2)}, u32[]{:S(2)}) collective-permute-start(f32[8,128]{1,0:T(8,128)S(1)} %get-tuple-element.27), channel_id=1, source_target_pairs={{0,9},{1,8},{2,11},{3,10},{4,13},{5,12},{6,15},{7,14},{8,1},{9,0},... | collective-permute-start | bytes 12296 | tf_op jit(solution)/shard_map/ppermute | solution.py:279
  49.9 3.5 %collective-permute-start.10 = (f32[8,128]{1,0:T(8,128)S(1)}, f32[8,128]{1,0:T(8,128)S(1)}, u32[]{:S(2)}, u32[]{:S(2)}) collective-permute-start(f32[8,128]{1,0:T(8,128)S(1)} %add.25), channel_id=1, source_target_pairs={{0,10},{1,11},{2,8},{3,9},{4,14},{5,15},{6,12},{7,13},{8,2},{9,3},... | collective-permute-start | bytes 12296 | tf_op jit(solution)/shard_map/ppermute | solution.py:279
  53.5 4.6 %collective-permute-start.11 = (f32[8,128]{1,0:T(8,128)S(1)}, f32[8,128]{1,0:T(8,128)S(1)}, u32[]{:S(2)}, u32[]{:S(2)}) collective-permute-start(f32[8,128]{1,0:T(8,128)S(1)} %add.26), channel_id=1, source_target_pairs={{0,12},{1,13},{2,14},{3,15},{4,8},{5,9},{6,10},{7,11},{8,4},{9,5},... | collective-permute-start | bytes 12296 | tf_op jit(solution)/shard_map/ppermute | solution.py:279

commit v6 on v5

--- a/solution.py
+++ b/solution.py
@@ -32,11 +32,8 @@
     return jax.ShapeDtypeStruct(dims, dtype)
 
 
-def lists(rws_ref, cls_ref, rws, cls, sems):
-    copies = [
-        pltpu.make_async_copy(rws_ref, rws, sems.at[0]),
-        pltpu.make_async_copy(cls_ref, cls, sems.at[1]),
-    ]
+def lists(*pairs, sems):
+    copies = [pltpu.make_async_copy(*pair, sems.at[i]) for i, pair in enumerate(pairs)]
     for copy in copies:
         copy.start()
     return copies
@@ -91,10 +88,11 @@
     return lane_sum(total)
 
 
-def store_pairs(acc_ref, out_ref, blocks):
-    for b in range(0, blocks, 2):
-        pair = jnp.concatenate([acc_ref[b], acc_ref[b + 1]], axis=0)
-        out_ref[b // 2] = pair.astype(BF16)
+def store_pairs(acc_ref, outs):
+    half = acc_ref.shape[0] // 4
+    for b in range(2 * half):
+        pair = jnp.concatenate([acc_ref[2 * b], acc_ref[2 * b + 1]], axis=0)
+        outs[b // half][b % half] = pair.astype(BF16)
 
 
 def place_halves(own, other, out_ref):
@@ -112,11 +110,11 @@
 
 
 def first_forward(
-    rws_ref, cls_ref, cnt, alpha, blk, own, other, u_piece,
-    out, v_out,
-    rws, cls, sems, acc,
-):
-    copies = lists(rws_ref, cls_ref, rws, cls, sems)
+    rws_ref, cls_ref, cnt, blk, alpha_ref, own, other, u_piece,
+    out0, out1, v_out,
+    rws, cls, sems, alpha, acc,
+):
+    copies = lists((rws_ref, rws), (cls_ref, cls), (alpha_ref, alpha), sems=sems)
     place_halves(own, other, v_out)
     for c in copies:
         c.wait()
@@ -126,14 +124,20 @@
     a = column(alpha)
     for b in range(pieces):
         acc[base + b] -= a * u_piece[:, b * 128 : (b + 1) * 128]
-    store_pairs(acc, out, acc.shape[0])
-
-
-def first_backward(rws_ref, cls_ref, cnt, blk, sum0, sum1, upd, message, rws, cls, sems, acc):
-    copies = lists(rws_ref, cls_ref, rws, cls, sems)
+    store_pairs(acc, (out0, out1))
+
+
+def pair_sums(pairs, a0, a1, b0, b1):
+    half = pairs // 2
+    for b in range(pairs):
+        one, two = (a0, a1) if b < half else (b0, b1)
+        yield one[b % half].astype(F32) + two[b % half].astype(F32)
+
+
+def first_backward(rws_ref, cls_ref, cnt, blk, sums0, sums1, sums2, sums3, upd, message, rws, cls, sems, acc):
+    copies = lists((rws_ref, rws), (cls_ref, cls), sems=sems)
     blocks = upd.shape[0]
-    for b in range(blocks // 2):
-        s = sum0[b].astype(F32) + sum1[b].astype(F32)
+    for b, s in enumerate(pair_sums(blocks // 2, sums0, sums1, sums2, sums3)):
         upd[2 * b] = s[:8]
         upd[2 * b + 1] = s[8:]
     cells = acc.shape[0]
@@ -147,10 +151,10 @@
 def next_forward(
     total_rays,
     rws_ref, cls_ref, cnt, blk, own, other, v_old,
-    out, vupd, beta_out,
+    out0, out1, vupd, beta_out,
     rws, cls, sems, acc,
 ):
-    copies = lists(rws_ref, cls_ref, rws, cls, sems)
+    copies = lists((rws_ref, rws), (cls_ref, cls), sems=sems)
     cells = v_old.shape[0]
     beta = jnp.sqrt((own[cells] + other[cells]) / total_rays + EPS)
     beta_out[...] = beta
@@ -162,28 +166,27 @@
     lanes = lax.broadcasted_iota(jnp.int32, (8, 128), 1)
     sq = jnp.where(lanes == lax.axis_index("col"), sq, 0.0)
     high = sq.astype(BF16).astype(F32)
-    out[rays // 2] = jnp.concatenate([high, sq - high], axis=0).astype(BF16)
+    out0[rays // 4] = jnp.concatenate([high, sq - high], axis=0).astype(BF16)
     for c in copies:
         c.wait()
     forward(blk, rws, cls, cnt, vupd, acc)
-    store_pairs(acc, out, rays)
+    store_pairs(acc, (out0, out1))
 
 
 def next_backward(
     total_cells, pieces,
-    rws_ref, cls_ref, cnt, blk, sum0, sum1, old, beta,
+    rws_ref, cls_ref, cnt, blk, sums0, sums1, sums2, sums3, old, beta,
     message, u_piece, alpha_out,
     rws, cls, sems, upd, acc,
 ):
-    copies = lists(rws_ref, cls_ref, rws, cls, sems)
+    copies = lists((rws_ref, rws), (cls_ref, cls), sems=sems)
     blocks = upd.shape[0]
-    tail = sum0[blocks // 2].astype(F32) + sum1[blocks // 2].astype(F32)
+    tail = sums0[blocks // 4].astype(F32) + sums1[blocks // 4].astype(F32)
     alpha = jnp.sqrt(lane_sum(tail[:8] + tail[8:]) / total_cells + EPS)
     alpha_out[...] = alpha
     inv = 1.0 / alpha
     ratio = alpha / beta[...]
-    for b in range(blocks // 2):
-        s = sum0[b].astype(F32) + sum1[b].astype(F32)
+    for b, s in enumerate(pair_sums(blocks // 2, sums0, sums1, sums2, sums3)):
         upd[2 * b] = s[:8] * inv - ratio * old[2 * b]
         upd[2 * b + 1] = s[8:] * inv - ratio * old[2 * b + 1]
     cells = acc.shape[0]
@@ -260,15 +263,24 @@
     return lax.ppermute(x, "row", [(0, 1), (1, 0)])
 
 
-def column_sum(x):
+def column_sum(halves):
     n = lax.axis_size("col")
     steps = [1 << i for i in range((n - 1).bit_length())]
-    for first, second in zip(steps, steps[-1:] + steps[:-1]):
-        pairs = [(i, i ^ first) for i in range(n)] + [(n + i, n + (i ^ second)) for i in range(n)]
-        y = lax.ppermute(x, ("row", "col"), pairs)
-        if first == steps[-1]:
-            return x, y
-        x = (x.astype(F32) + y.astype(F32)).astype(BF16)
+    turned = steps[-1:] + steps[:-1]
+    orders = ((steps, turned), (steps, turned))
+    xs = list(halves)
+    for i in range(len(steps)):
+        ys = [
+            lax.ppermute(
+                x,
+                ("row", "col"),
+                [(j, j ^ first[i]) for j in range(n)] + [(n + j, n + (j ^ second[i])) for j in range(n)],
+            )
+            for x, (first, second) in zip(xs, orders)
+        ]
+        if i == len(steps) - 1:
+            return xs[0], ys[0], xs[1], ys[1]
+        xs = [(x.astype(F32) + y.astype(F32)).astype(BF16) for x, y in zip(xs, ys)]
 
 
 def last_sum(x):
@@ -296,7 +308,7 @@
     listed = [
         pltpu.SMEM(block_rows.shape, jnp.int32),
         pltpu.SMEM(block_cols.shape, jnp.int32),
-        pltpu.SemaphoreType.DMA((2,)),
+        pltpu.SemaphoreType.DMA((3,)),
     ]
     ray_acc = pltpu.VMEM((rays, 8, 128), F32)
     cell_acc = pltpu.VMEM((cells, 8, 128), F32)
@@ -309,33 +321,34 @@
     )(v_cells)
     v_other = other_core(own)
     blk = blocks.reshape(blocks.shape[2:])
-    part, v0 = call(
+    operator = (*where, blk)
+    half_rays = shape(rays // 4, 16, 128, dtype=BF16)
+    *part, v0 = call(
         first_forward,
-        (shape(rays // 2, 16, 128, dtype=BF16), shape(cells, 8, 128)),
-        [VMEM] * 3 + [SMEM] + [VMEM] * 4,
-        listed + [ray_acc],
-    )(*where, alpha, blk, own, v_other, u_rays)
-    operator = (*where, blk)
-    sum0, sum1 = column_sum(part)
+        (half_rays, half_rays, shape(cells, 8, 128)),
+        [VMEM] * 8,
+        listed + [pltpu.SMEM(alpha.shape, F32), ray_acc],
+    )(*operator, alpha, own, v_other, u_rays)
+    sums = column_sum(part)
     upd1, message = call(
         first_backward,
         (shape(rays, 8, 128), shape(cells + 1, 8, 128)),
-        [VMEM] * 6,
+        [VMEM] * 8,
         listed + [cell_acc],
-    )(*operator, sum0, sum1)
-    part, v1, beta1 = call(
+    )(*operator, *sums)
+    *part, v1, beta1 = call(
         functools.partial(next_forward, total_rays),
-        (shape(rays // 2 + 1, 16, 128, dtype=BF16), shape(cells, 8, 128), shape(8, 128)),
+        (shape(rays // 4 + 1, 16, 128, dtype=BF16), half_rays, shape(cells, 8, 128), shape(8, 128)),
         [VMEM] * 7,
         listed + [ray_acc],
     )(*operator, message, other_core(message), v0)
-    sum0, sum1 = column_sum(part)
+    sums = column_sum(part)
     message, u_piece, alpha1 = call(
         functools.partial(next_backward, total_cells, pieces),
         (shape(cells + 1, 8, 128), shape(pieces, 8, 128), shape(8, 128)),
-        [VMEM] * 8,
+        [VMEM] * 10,
         listed + [pltpu.VMEM((rays, 8, 128), F32), cell_acc],
-    )(*operator, sum0, sum1, upd1, beta1)
+    )(*operator, *sums, upd1, beta1)
     sq, v2, beta2 = call(
         functools.partial(last_cells, total_rays),
         (shape(8, 128), shape(cells, 8, 128), shape(8, 128)),

time: 59.6 us -> 57.9 us (0.971)
  waiting for transfers between devices: 24.9 us -> 22.2 us
  starting transfers between devices: 23.6 us -> 25 us
    ppermute x6 -> x12, waiting for transfers between devices: 17.8 us -> 13.7 us  [column_sum(): lax.ppermute(x, ('row', 'col'), [(j, j ^ first[i]) for j in range(n)] + [...]
    ppermute x6 -> x12, starting transfers between devices: 16.2 us -> 20.2 us  [column_sum(): lax.ppermute(x, ('row', 'col'), [(j, j ^ first[i]) for j in range(n)] + [...]
    ppermute x3, starting transfers between devices: 6.75 us -> 4.09 us  [last_sum(): x = x + lax.ppermute(x, ('row', 'col'), pairs)]
    ppermute x3, waiting for transfers between devices: 4.45 us -> 5.91 us  [last_sum(): x = x + lax.ppermute(x, ('row', 'col'), pairs)]
  transfers between devices with their start and end apart: 12 -> 18, of which waited for: 12 -> 14; matrix products, arithmetic and copies ran while one was open for 0% -> 0% of each run, Pallas kernels for 0% -> 0%
where the time goes in v6:
time: 57.9 us; the launch traced here: 57.7 us
  starting transfers between devices  25 us (43%)
  waiting for transfers between devices  22.2 us (38%)
  Pallas kernels  7.88 us (14%)
  between operations  1.48 us (3%)
  local copies, waits for them, and re-layouts  0.9 us (2%)
    ppermute x12, starting transfers between devices, column_sum(): lax.ppermute(x, ('row', 'col'), [(j, j ^ first[i]) for j in range(n)] + [...  20.2 us
    ppermute x12, waiting for transfers between devices, column_sum(): lax.ppermute(x, ('row', 'col'), [(j, j ^ first[i]) for j in range(n)] + [...  13.7 us
    ppermute x3, waiting for transfers between devices, last_sum(): x = x + lax.ppermute(x, ('row', 'col'), pairs)  5.91 us
    ppermute x3, starting transfers between devices, last_sum(): x = x + lax.ppermute(x, ('row', 'col'), pairs)  4.09 us
    ppermute x3, waiting for transfers between devices, other_core(): return lax.ppermute(x, 'row', [(0, 1), (1, 0)])  2.59 us
    pallas_call x1, Pallas kernels, body(): call(first_forward, (half_rays, half_rays, shape(cells, 8, 128)), [VMEM]...  1.83 us
    pallas_call x1, Pallas kernels, body(): call(functools.partial(next_forward, total_rays), (shape(rays // 4 + 1, 1...  1.81 us
    pallas_call x1, Pallas kernels, body(): call(functools.partial(next_backward, total_cells, pieces), (shape(cells...  1.52 us
  transfers between devices with their start and end apart: 18, of which 14 were waited for; matrix products, arithmetic and copies ran while one was open for 0% of the time, Pallas kernels for 0%

profile of v6, /device:TPU:0, one launch (start us, length us, event | category | flops | bytes accessed | tf_op | source)
XLA Modules:
  0.0 57.7 jit_solution(16220332567475977851)
XLA Ops:
  0.6 0.0 copy-start.5
  0.6 0.0 copy-start.4
  0.7 0.0 copy-start.8
  0.7 0.9 %copy-done.9 = f32[8,512]{1,0:T(8,128)S(1)} copy-done((f32[8,512]{1,0:T(8,128)S(1)}, f32[8,512]{1,0:T(8,128)}, u32[]{:S(2)}) %copy-start.9) | copy-done | bytes 16408
  1.6 0.5 collective-permute-start
  2.7 0.2 collective-permute-done.other
  2.9 0.0 copy-done.4
  3.0 1.8 %shard_map.147 = (bf16[16,16,128]{2,1,0:T(8,128)(2,1)S(1)}, bf16[16,16,128]{2,1,0:T(8,128)(2,1)S(1)}, f32[8,8,128]{2,1,0:T(8,128)S(1)}) custom-call(s32[1,1,128]{2,1,0:T(1,128)S(1)} %copy-done.4, s32[1,1,128]{2,1,0:T(1,128)S(1)} %copy-done.5, s32[1,1]{1,0:T(1,128)S(6)} %copy.16.cnt, bf16[128,128,128]{2,1,0:T(8,128)(2,1)S(1)} %bitcast.1, f32[8]{0:T(128)S(1)} %copy-done.8, ...), custom_call_target="tpu_custom_call" | custom-call | tf_op jit(solution)/shard_map/pallas_call | solution.py:326
  4.8 2.9 %collective-permute-start.1 = (bf16[16,16,128]{2,1,0:T(8,128)(2,1)S(1)}, bf16[16,16,128]{2,1,0:T(8,128)(2,1)S(1)}, u32[]{:S(2)}, u32[]{:S(2)}) collective-permute-start(bf16[16,16,128]{2,1,0:T(8,128)(2,1)S(1)} %get-tuple-element.20), channel_id=1, source_target_pairs={{0,1},{1,0},{2,3},{3,2},{4,5},{5,4},{6,7},{7,6},{8,12},{9,13},{10,... | collective-permute-start | bytes 196616 | tf_op jit(solution)/shard_map/ppermute | solution.py:274
  7.7 0.1 collective-permute-start.4
  7.8 2.2 %collective-permute-done.1 = bf16[16,16,128]{2,1,0:T(8,128)(2,1)S(1)} collective-permute-done((bf16[16,16,128]{2,1,0:T(8,128)(2,1)S(1)}, bf16[16,16,128]{2,1,0:T(8,128)(2,1)S(1)}, u32[]{:S(2)}, u32[]{:S(2)}) %collective-permute-start.1) | collective-permute-done | bytes 65568 | tf_op jit(solution)/shard_map/ppermute | solution.py:274
  10.0 2.2 %collective-permute-start.2 = (bf16[16,16,128]{2,1,0:T(8,128)(2,1)S(1)}, bf16[16,16,128]{2,1,0:T(8,128)(2,1)S(1)}, u32[]{:S(2)}, u32[]{:S(2)}) collective-permute-start(bf16[16,16,128]{2,1,0:T(8,128)(2,1)S(1)} %add_convert_fusion.7), channel_id=1, source_target_pairs={{0,2},{1,3},{2,0},{3,1},{4,6},{5,7},{6,4},{7,5},{8,9},{9,8},{10,11... | collective-permute-start | bytes 196616 | tf_op jit(solution)/shard_map/ppermute | solution.py:274
  12.2 0.0 collective-permute-done.4
  12.2 1.5 %collective-permute-start.5 = (bf16[16,16,128]{2,1,0:T(8,128)(2,1)S(1)}, bf16[16,16,128]{2,1,0:T(8,128)(2,1)S(1)}, u32[]{:S(2)}, u32[]{:S(2)}) collective-permute-start(bf16[16,16,128]{2,1,0:T(8,128)(2,1)S(1)} %add_convert_fusion.5), channel_id=1, source_target_pairs={{0,2},{1,3},{2,0},{3,1},{4,6},{5,7},{6,4},{7,5},{8,9},{9,8},{10,11... | collective-permute-start | bytes 196616 | tf_op jit(solution)/shard_map/ppermute | solution.py:274
  13.7 0.8 %collective-permute-done.2 = bf16[16,16,128]{2,1,0:T(8,128)(2,1)S(1)} collective-permute-done((bf16[16,16,128]{2,1,0:T(8,128)(2,1)S(1)}, bf16[16,16,128]{2,1,0:T(8,128)(2,1)S(1)}, u32[]{:S(2)}, u32[]{:S(2)}) %collective-permute-start.2) | collective-permute-done | bytes 65568 | tf_op jit(solution)/shard_map/ppermute | solution.py:274
  14.4 3.1 %collective-permute-start.3 = (bf16[16,16,128]{2,1,0:T(8,128)(2,1)S(1)}, bf16[16,16,128]{2,1,0:T(8,128)(2,1)S(1)}, u32[]{:S(2)}, u32[]{:S(2)}) collective-permute-start(bf16[16,16,128]{2,1,0:T(8,128)(2,1)S(1)} %add_convert_fusion.6.sums0), channel_id=1, source_target_pairs={{0,4},{1,5},{2,6},{3,7},{4,0},{5,1},{6,2},{7,3},{8,10},{9,11},{10,... | collective-permute-start | bytes 196616 | tf_op jit(solution)/shard_map/ppermute | solution.py:274
  17.5 0.0 collective-permute-done.5
  17.6 1.7 %collective-permute-start.6 = (bf16[16,16,128]{2,1,0:T(8,128)(2,1)S(1)}, bf16[16,16,128]{2,1,0:T(8,128)(2,1)S(1)}, u32[]{:S(2)}, u32[]{:S(2)}) collective-permute-start(bf16[16,16,128]{2,1,0:T(8,128)(2,1)S(1)} %add_convert_fusion.4.sums2), channel_id=1, source_target_pairs={{0,4},{1,5},{2,6},{3,7},{4,0},{5,1},{6,2},{7,3},{8,10},{9,11},{10,... | collective-permute-start | bytes 196616 | tf_op jit(solution)/shard_map/ppermute | solution.py:274
  19.2 0.7 %collective-permute-done.3.sums1 = bf16[16,16,128]{2,1,0:T(8,128)(2,1)S(1)} collective-permute-done((bf16[16,16,128]{2,1,0:T(8,128)(2,1)S(1)}, bf16[16,16,128]{2,1,0:T(8,128)(2,1)S(1)}, u32[]{:S(2)}, u32[]{:S(2)}) %collective-permute-start.3) | collective-permute-done | bytes 65568 | tf_op jit(solution)/shard_map/ppermute | solution.py:274
  19.9 2.9 %collective-permute-done.6.sums3 = bf16[16,16,128]{2,1,0:T(8,128)(2,1)S(1)} collective-permute-done((bf16[16,16,128]{2,1,0:T(8,128)(2,1)S(1)}, bf16[16,16,128]{2,1,0:T(8,128)(2,1)S(1)}, u32[]{:S(2)}, u32[]{:S(2)}) %collective-permute-start.6) | collective-permute-done | bytes 65568 | tf_op jit(solution)/shard_map/ppermute | solution.py:274
  22.8 1.4 %shard_map.148 = (f32[64,8,128]{2,1,0:T(8,128)S(1)}, f32[9,8,128]{2,1,0:T(8,128)S(1)}) custom-call(s32[1,1,128]{2,1,0:T(1,128)S(1)} %copy-done.4, s32[1,1,128]{2,1,0:T(1,128)S(1)} %copy-done.5, s32[1,1]{1,0:T(1,128)S(6)} %copy.16.cnt, bf16[128,128,128]{2,1,0:T(8,128)(2,1)S(1)} %bitcast.2, bf16[16,16,128]{2,1,0:T(8,128)(2,1)S(1)} %add_convert_fusion.6.sums0, ...), custom_call_target="tpu_custom_call" | custom-call | tf_op jit(solution)/shard_map/pallas_call | solution.py:333
  24.2 0.1 collective-permute-start.7
  24.3 1.2 %collective-permute-done.7.other = f32[9,8,128]{2,1,0:T(8,128)S(1)} collective-permute-done((f32[9,8,128]{2,1,0:T(8,128)S(1)}, f32[9,8,128]{2,1,0:T(8,128)S(1)}, u32[]{:S(2)}, u32[]{:S(2)}) %collective-permute-start.7) | collective-permute-done | bytes 36896 | tf_op jit(solution)/shard_map/ppermute | solution.py:263
  25.5 1.8 %shard_map.149 = (bf16[17,16,128]{2,1,0:T(8,128)(2,1)S(1)}, bf16[16,16,128]{2,1,0:T(8,128)(2,1)S(1)}, f32[8,8,128]{2,1,0:T(8,128)S(1)}, f32[8,128]{1,0:T(8,128)S(1)}) custom-call(s32[1,1,128]{2,1,0:T(1,128)S(1)} %copy-done.4, s32[1,1,128]{2,1,0:T(1,128)S(1)} %copy-done.5, s32[1,1]{1,0:T(1,128)S(6)} %copy.16.cnt, bf16[128,128,128]{2,1,0:T(8,128)(2,1)S(1)} %bitcast.3, ...), custom_call_target="tpu_custom_call" | custom-call | tf_op jit(solution)/shard_map/pallas_call | solution.py:339
  27.3 1.6 %collective-permute-start.8 = (bf16[17,16,128]{2,1,0:T(8,128)(2,1)S(1)}, bf16[17,16,128]{2,1,0:T(8,128)(2,1)S(1)}, u32[]{:S(2)}, u32[]{:S(2)}) collective-permute-start(bf16[17,16,128]{2,1,0:T(8,128)(2,1)S(1)} %get-tuple-element.24), channel_id=1, source_target_pairs={{0,1},{1,0},{2,3},{3,2},{4,5},{5,4},{6,7},{7,6},{8,12},{9,13},{10,... | collective-permute-start | bytes 208904 | tf_op jit(solution)/shard_map/ppermute | solution.py:274
  28.9 0.5 collective-permute-start.11
  29.4 2.3 %collective-permute-done.8 = bf16[17,16,128]{2,1,0:T(8,128)(2,1)S(1)} collective-permute-done((bf16[17,16,128]{2,1,0:T(8,128)(2,1)S(1)}, bf16[17,16,128]{2,1,0:T(8,128)(2,1)S(1)}, u32[]{:S(2)}, u32[]{:S(2)}) %collective-permute-start.8) | collective-permute-done | bytes 69664 | tf_op jit(solution)/shard_map/ppermute | solution.py:274
  31.7 1.6 %collective-permute-start.9 = (bf16[17,16,128]{2,1,0:T(8,128)(2,1)S(1)}, bf16[17,16,128]{2,1,0:T(8,128)(2,1)S(1)}, u32[]{:S(2)}, u32[]{:S(2)}) collective-permute-start(bf16[17,16,128]{2,1,0:T(8,128)(2,1)S(1)} %add_convert_fusion.1), channel_id=1, source_target_pairs={{0,2},{1,3},{2,0},{3,1},{4,6},{5,7},{6,4},{7,5},{8,9},{9,8},{10,11... | collective-permute-start | bytes 208904 | tf_op jit(solution)/shard_map/ppermute | solution.py:274
  33.3 0.0 collective-permute-done.11
  33.4 1.4 %collective-permute-start.12 = (bf16[16,16,128]{2,1,0:T(8,128)(2,1)S(1)}, bf16[16,16,128]{2,1,0:T(8,128)(2,1)S(1)}, u32[]{:S(2)}, u32[]{:S(2)}) collective-permute-start(bf16[16,16,128]{2,1,0:T(8,128)(2,1)S(1)} %add_convert_fusion.3), channel_id=1, source_target_pairs={{0,2},{1,3},{2,0},{3,1},{4,6},{5,7},{6,4},{7,5},{8,9},{9,8},{10,11... | collective-permute-start | bytes 196616 | tf_op jit(solution)/shard_map/ppermute | solution.py:274
  34.8 1.3 %collective-permute-done.9 = bf16[17,16,128]{2,1,0:T(8,128)(2,1)S(1)} collective-permute-done((bf16[17,16,128]{2,1,0:T(8,128)(2,1)S(1)}, bf16[17,16,128]{2,1,0:T(8,128)(2,1)S(1)}, u32[]{:S(2)}, u32[]{:S(2)}) %collective-permute-start.9) | collective-permute-done | bytes 69664 | tf_op jit(solution)/shard_map/ppermute | solution.py:274
  36.1 1.8 %collective-permute-start.10 = (bf16[17,16,128]{2,1,0:T(8,128)(2,1)S(1)}, bf16[17,16,128]{2,1,0:T(8,128)(2,1)S(1)}, u32[]{:S(2)}, u32[]{:S(2)}) collective-permute-start(bf16[17,16,128]{2,1,0:T(8,128)(2,1)S(1)} %add_convert_fusion.sums0), channel_id=1, source_target_pairs={{0,4},{1,5},{2,6},{3,7},{4,0},{5,1},{6,2},{7,3},{8,10},{9,11},{10,... | collective-permute-start | bytes 208904 | tf_op jit(solution)/shard_map/ppermute | solution.py:274
  37.9 0.1 collective-permute-done.12
  38.0 1.9 %collective-permute-start.13 = (bf16[16,16,128]{2,1,0:T(8,128)(2,1)S(1)}, bf16[16,16,128]{2,1,0:T(8,128)(2,1)S(1)}, u32[]{:S(2)}, u32[]{:S(2)}) collective-permute-start(bf16[16,16,128]{2,1,0:T(8,128)(2,1)S(1)} %add_convert_fusion.2.sums2), channel_id=1, source_target_pairs={{0,4},{1,5},{2,6},{3,7},{4,0},{5,1},{6,2},{7,3},{8,10},{9,11},{10,... | collective-permute-start | bytes 196616 | tf_op jit(solution)/shard_map/ppermute | solution.py:274
  39.9 3.6 %collective-permute-done.13.sums3 = bf16[16,16,128]{2,1,0:T(8,128)(2,1)S(1)} collective-permute-done((bf16[16,16,128]{2,1,0:T(8,128)(2,1)S(1)}, bf16[16,16,128]{2,1,0:T(8,128)(2,1)S(1)}, u32[]{:S(2)}, u32[]{:S(2)}) %collective-permute-start.13) | collective-permute-done | bytes 65568 | tf_op jit(solution)/shard_map/ppermute | solution.py:274
  43.5 0.0 collective-permute-done.10.sums1
  43.5 1.5 %shard_map.150 = (f32[9,8,128]{2,1,0:T(8,128)S(1)}, f32[8,8,128]{2,1,0:T(8,128)S(1)}, f32[8,128]{1,0:T(8,128)S(1)}) custom-call(s32[1,1,128]{2,1,0:T(1,128)S(1)} %copy-done.4, s32[1,1,128]{2,1,0:T(1,128)S(1)} %copy-done.5, s32[1,1]{1,0:T(1,128)S(6)} %copy.16.cnt, bf16[128,128,128]{2,1,0:T(8,128)(2,1)S(1)} %bitcast.4, ...), custom_call_target="tpu_custom_call" | custom-call | tf_op jit(solution)/shard_map/pallas_call | solution.py:346
  45.0 0.1 collective-permute-start.14
  45.1 1.2 %collective-permute-done.14.other = f32[9,8,128]{2,1,0:T(8,128)S(1)} collective-permute-done((f32[9,8,128]{2,1,0:T(8,128)S(1)}, f32[9,8,128]{2,1,0:T(8,128)S(1)}, u32[]{:S(2)}, u32[]{:S(2)}) %collective-permute-start.14) | collective-permute-done | bytes 36896 | tf_op jit(solution)/shard_map/ppermute | solution.py:263
  46.3 0.1 shard_map.151
  46.4 1.3 %collective-permute-start.15 = (f32[8,128]{1,0:T(8,128)S(1)}, f32[8,128]{1,0:T(8,128)S(1)}, u32[]{:S(2)}, u32[]{:S(2)}) collective-permute-start(f32[8,128]{1,0:T(8,128)S(1)} %get-tuple-element.31), channel_id=1, source_target_pairs={{0,9},{1,8},{2,11},{3,10},{4,13},{5,12},{6,15},{7,14},{8,1},{9,0},... | collective-permute-start | bytes 12296 | tf_op jit(solution)/shard_map/ppermute | solution.py:291
  47.7 1.8 %collective-permute-done.15 = f32[8,128]{1,0:T(8,128)S(1)} collective-permute-done((f32[8,128]{1,0:T(8,128)S(1)}, f32[8,128]{1,0:T(8,128)S(1)}, u32[]{:S(2)}, u32[]{:S(2)}) %collective-permute-start.15) | collective-permute-done | bytes 4128 | tf_op jit(solution)/shard_map/ppermute | solution.py:291
  49.4 1.4 %collective-permute-start.16 = (f32[8,128]{1,0:T(8,128)S(1)}, f32[8,128]{1,0:T(8,128)S(1)}, u32[]{:S(2)}, u32[]{:S(2)}) collective-permute-start(f32[8,128]{1,0:T(8,128)S(1)} %add.41), channel_id=1, source_target_pairs={{0,10},{1,11},{2,8},{3,9},{4,14},{5,15},{6,12},{7,13},{8,2},{9,3},... | collective-permute-start | bytes 12296 | tf_op jit(solution)/shard_map/ppermute | solution.py:291
  50.8 1.7 %collective-permute-done.16 = f32[8,128]{1,0:T(8,128)S(1)} collective-permute-done((f32[8,128]{1,0:T(8,128)S(1)}, f32[8,128]{1,0:T(8,128)S(1)}, u32[]{:S(2)}, u32[]{:S(2)}) %collective-permute-start.16) | collective-permute-done | bytes 4128 | tf_op jit(solution)/shard_map/ppermute | solution.py:291
  52.5 1.5 %collective-permute-start.17 = (f32[8,128]{1,0:T(8,128)S(1)}, f32[8,128]{1,0:T(8,128)S(1)}, u32[]{:S(2)}, u32[]{:S(2)}) collective-permute-start(f32[8,128]{1,0:T(8,128)S(1)} %add.42), channel_id=1, source_target_pairs={{0,12},{1,13},{2,14},{3,15},{4,8},{5,9},{6,10},{7,11},{8,4},{9,5},... | collective-permute-start | bytes 12296 | tf_op jit(solution)/shard_map/ppermute | solution.py:291
  53.9 2.5 %collective-permute-done.17 = f32[8,128]{1,0:T(8,128)S(1)} collective-permute-done((f32[8,128]{1,0:T(8,128)S(1)}, f32[8,128]{1,0:T(8,128)S(1)}, u32[]{:S(2)}, u32[]{:S(2)}) %collective-permute-start.17) | collective-permute-done | bytes 4128 | tf_op jit(solution)/shard_map/ppermute | solution.py:291
  56.4 0.0 copy-done.3
  56.4 1.2 %shard_map.152 = (f32[8,1024]{1,0:T(8,128)}, f32[8,512]{1,0:T(8,128)}, f32[8,512]{1,0:T(8,128)}, f32[8,512]{1,0:T(8,128)}, f32[3,8]{1,0:T(4,128)}) custom-call(f32[8]{0:T(128)S(1)} %copy-done.6, f32[8]{0:T(128)S(1)} %copy-done.7, f32[8,128]{1,0:T(8,128)S(1)} %add.43.sq, f32[8,8,128]{2,1,0:T(8,128)S(1)} %get-tuple-element.29.v_old.v1, ...), custom_call_target="tpu_custom_call" | custom-call | tf_op jit(solution)/shard_map/pallas_call | solution.py:359
  (26 shorter events, 0.2 us)
Async XLA Ops:
  0.6 2.3 %copy-start.5 = (s32[1,1,128]{2,1,0:T(1,128)S(1)}, s32[1,1,128]{2,1,0:T(1,128)}, u32[]{:S(2)}) copy-start(s32[1,1,128]{2,1,0:T(1,128)} %cls_ref.7) | copy-start | bytes 1540
  0.6 2.3 %copy-start.4 = (s32[1,1,128]{2,1,0:T(1,128)S(1)}, s32[1,1,128]{2,1,0:T(1,128)}, u32[]{:S(2)}) copy-start(s32[1,1,128]{2,1,0:T(1,128)} %rws_ref.7) | copy-start | bytes 1540
  0.7 2.3 %copy-start.8 = (f32[8]{0:T(128)S(1)}, f32[8]{0:T(128)}, u32[]{:S(2)}) copy-start(f32[8]{0:T(128)} %alpha_ref.1) | copy-start | bytes 100
  0.7 2.3 %copy-start.1 = (f32[8,1024]{1,0:T(8,128)S(1)}, f32[8,1024]{1,0:T(8,128)}, u32[]{:S(2)}) copy-start(f32[8,1024]{1,0:T(8,128)} %u_piece.1) | copy-start | bytes 98308
  0.7 2.3 %copy-start = (bf16[1,1,128,128,128]{4,3,2,1,0:T(8,128)(2,1)S(1)}, bf16[1,1,128,128,128]{4,3,2,1,0:T(8,128)(2,1)}, u32[]{:S(2)}) copy-start(bf16[1,1,128,128,128]{4,3,2,1,0:T(8,128)(2,1)} %param.11) | copy-start | bytes 12582916
  0.7 0.9 %copy-start.9 = (f32[8,512]{1,0:T(8,128)S(1)}, f32[8,512]{1,0:T(8,128)}, u32[]{:S(2)}) copy-start(f32[8,512]{1,0:T(8,128)} %own_hbm.1) | copy-start | bytes 49156
  1.6 1.4 %collective-permute-start = (f32[8,512]{1,0:T(8,128)S(1)}, f32[8,512]{1,0:T(8,128)S(1)}, u32[]{:S(2)}, u32[]{:S(2)}) collective-permute-start(f32[8,512]{1,0:T(8,128)S(1)} %shard_map.146.own), channel_id=1, source_target_pairs={{0,8},{8,0},{1,9},{9,1},{2,10},{10,2},{3,11},{11,3},{4,12},{12,4},... | collective-permute-start | bytes 49160 | tf_op jit(solution)/shard_map/ppermute | solution.py:263
  4.8 5.2 %collective-permute-start.1 = (bf16[16,16,128]{2,1,0:T(8,128)(2,1)S(1)}, bf16[16,16,128]{2,1,0:T(8,128)(2,1)S(1)}, u32[]{:S(2)}, u32[]{:S(2)}) collective-permute-start(bf16[16,16,128]{2,1,0:T(8,128)(2,1)S(1)} %get-tuple-element.20), channel_id=1, source_target_pairs={{0,1},{1,0},{2,3},{3,2},{4,5},{5,4},{6,7},{7,6},{8,12},{9,13},{10,... | collective-permute-start | bytes 196616 | tf_op jit(solution)/shard_map/ppermute | solution.py:274
  7.7 4.4 %collective-permute-start.4 = (bf16[16,16,128]{2,1,0:T(8,128)(2,1)S(1)}, bf16[16,16,128]{2,1,0:T(8,128)(2,1)S(1)}, u32[]{:S(2)}, u32[]{:S(2)}) collective-permute-start(bf16[16,16,128]{2,1,0:T(8,128)(2,1)S(1)} %get-tuple-element.21), channel_id=1, source_target_pairs={{0,1},{1,0},{2,3},{3,2},{4,5},{5,4},{6,7},{7,6},{8,12},{9,13},{10,... | collective-permute-start | bytes 196616 | tf_op jit(solution)/shard_map/ppermute | solution.py:274
  10.0 4.4 %collective-permute-start.2 = (bf16[16,16,128]{2,1,0:T(8,128)(2,1)S(1)}, bf16[16,16,128]{2,1,0:T(8,128)(2,1)S(1)}, u32[]{:S(2)}, u32[]{:S(2)}) collective-permute-start(bf16[16,16,128]{2,1,0:T(8,128)(2,1)S(1)} %add_convert_fusion.7), channel_id=1, source_target_pairs={{0,2},{1,3},{2,0},{3,1},{4,6},{5,7},{6,4},{7,5},{8,9},{9,8},{10,11... | collective-permute-start | bytes 196616 | tf_op jit(solution)/shard_map/ppermute | solution.py:274
  12.2 5.3 %collective-permute-start.5 = (bf16[16,16,128]{2,1,0:T(8,128)(2,1)S(1)}, bf16[16,16,128]{2,1,0:T(8,128)(2,1)S(1)}, u32[]{:S(2)}, u32[]{:S(2)}) collective-permute-start(bf16[16,16,128]{2,1,0:T(8,128)(2,1)S(1)} %add_convert_fusion.5), channel_id=1, source_target_pairs={{0,2},{1,3},{2,0},{3,1},{4,6},{5,7},{6,4},{7,5},{8,9},{9,8},{10,11... | collective-permute-start | bytes 196616 | tf_op jit(solution)/shard_map/ppermute | solution.py:274
  14.4 5.4 %collective-permute-start.3 = (bf16[16,16,128]{2,1,0:T(8,128)(2,1)S(1)}, bf16[16,16,128]{2,1,0:T(8,128)(2,1)S(1)}, u32[]{:S(2)}, u32[]{:S(2)}) collective-permute-start(bf16[16,16,128]{2,1,0:T(8,128)(2,1)S(1)} %add_convert_fusion.6.sums0), channel_id=1, source_target_pairs={{0,4},{1,5},{2,6},{3,7},{4,0},{5,1},{6,2},{7,3},{8,10},{9,11},{10,... | collective-permute-start | bytes 196616 | tf_op jit(solution)/shard_map/ppermute | solution.py:274
  17.6 5.2 %collective-permute-start.6 = (bf16[16,16,128]{2,1,0:T(8,128)(2,1)S(1)}, bf16[16,16,128]{2,1,0:T(8,128)(2,1)S(1)}, u32[]{:S(2)}, u32[]{:S(2)}) collective-permute-start(bf16[16,16,128]{2,1,0:T(8,128)(2,1)S(1)} %add_convert_fusion.4.sums2), channel_id=1, source_target_pairs={{0,4},{1,5},{2,6},{3,7},{4,0},{5,1},{6,2},{7,3},{8,10},{9,11},{10,... | collective-permute-start | bytes 196616 | tf_op jit(solution)/shard_map/ppermute | solution.py:274
  24.2 1.3 %collective-permute-start.7 = (f32[9,8,128]{2,1,0:T(8,128)S(1)}, f32[9,8,128]{2,1,0:T(8,128)S(1)}, u32[]{:S(2)}, u32[]{:S(2)}) collective-permute-start(f32[9,8,128]{2,1,0:T(8,128)S(1)} %get-tuple-element.22.own), channel_id=1, source_target_pairs={{0,8},{8,0},{1,9},{9,1},{2,10},{10,2},{3,11},{11,3},{4,12},{12,4},... | collective-permute-start | bytes 110600 | tf_op jit(solution)/shard_map/ppermute | solution.py:263
  25.5 30.9 %copy-start.2 = (f32[8,512]{1,0:T(8,128)S(1)}, f32[8,512]{1,0:T(8,128)}, u32[]{:S(2)}) copy-start(f32[8,512]{1,0:T(8,128)} %x_in.1) | copy-start | bytes 49156
  25.5 30.9 %copy-start.3 = (f32[8,512]{1,0:T(8,128)S(1)}, f32[8,512]{1,0:T(8,128)}, u32[]{:S(2)}) copy-start(f32[8,512]{1,0:T(8,128)} %w_in.1) | copy-start | bytes 49156
  25.5 30.9 %copy-start.6 = (f32[8]{0:T(128)S(1)}, f32[8]{0:T(128)}, u32[]{:S(2)}) copy-start(f32[8]{0:T(128)} %phibar_in.1) | copy-start | bytes 100
  25.5 30.9 %copy-start.7 = (f32[8]{0:T(128)S(1)}, f32[8]{0:T(128)}, u32[]{:S(2)}) copy-start(f32[8]{0:T(128)} %rhobar_in.1) | copy-start | bytes 100
  27.3 4.4 %collective-permute-start.8 = (bf16[17,16,128]{2,1,0:T(8,128)(2,1)S(1)}, bf16[17,16,128]{2,1,0:T(8,128)(2,1)S(1)}, u32[]{:S(2)}, u32[]{:S(2)}) collective-permute-start(bf16[17,16,128]{2,1,0:T(8,128)(2,1)S(1)} %get-tuple-element.24), channel_id=1, source_target_pairs={{0,1},{1,0},{2,3},{3,2},{4,5},{5,4},{6,7},{7,6},{8,12},{9,13},{10,... | collective-permute-start | bytes 208904 | tf_op jit(solution)/shard_map/ppermute | solution.py:274
  28.9 4.5 %collective-permute-start.11 = (bf16[16,16,128]{2,1,0:T(8,128)(2,1)S(1)}, bf16[16,16,128]{2,1,0:T(8,128)(2,1)S(1)}, u32[]{:S(2)}, u32[]{:S(2)}) collective-permute-start(bf16[16,16,128]{2,1,0:T(8,128)(2,1)S(1)} %get-tuple-element.25), channel_id=1, source_target_pairs={{0,1},{1,0},{2,3},{3,2},{4,5},{5,4},{6,7},{7,6},{8,12},{9,13},{10,... | collective-permute-start | bytes 196616 | tf_op jit(solution)/shard_map/ppermute | solution.py:274
  31.7 4.4 %collective-permute-start.9 = (bf16[17,16,128]{2,1,0:T(8,128)(2,1)S(1)}, bf16[17,16,128]{2,1,0:T(8,128)(2,1)S(1)}, u32[]{:S(2)}, u32[]{:S(2)}) collective-permute-start(bf16[17,16,128]{2,1,0:T(8,128)(2,1)S(1)} %add_convert_fusion.1), channel_id=1, source_target_pairs={{0,2},{1,3},{2,0},{3,1},{4,6},{5,7},{6,4},{7,5},{8,9},{9,8},{10,11... | collective-permute-start | bytes 208904 | tf_op jit(solution)/shard_map/ppermute | solution.py:274
  33.4 4.6 %collective-permute-start.12 = (bf16[16,16,128]{2,1,0:T(8,128)(2,1)S(1)}, bf16[16,16,128]{2,1,0:T(8,128)(2,1)S(1)}, u32[]{:S(2)}, u32[]{:S(2)}) collective-permute-start(bf16[16,16,128]{2,1,0:T(8,128)(2,1)S(1)} %add_convert_fusion.3), channel_id=1, source_target_pairs={{0,2},{1,3},{2,0},{3,1},{4,6},{5,7},{6,4},{7,5},{8,9},{9,8},{10,11... | collective-permute-start | bytes 196616 | tf_op jit(solution)/shard_map/ppermute | solution.py:274
  36.1 7.4 %collective-permute-start.10 = (bf16[17,16,128]{2,1,0:T(8,128)(2,1)S(1)}, bf16[17,16,128]{2,1,0:T(8,128)(2,1)S(1)}, u32[]{:S(2)}, u32[]{:S(2)}) collective-permute-start(bf16[17,16,128]{2,1,0:T(8,128)(2,1)S(1)} %add_convert_fusion.sums0), channel_id=1, source_target_pairs={{0,4},{1,5},{2,6},{3,7},{4,0},{5,1},{6,2},{7,3},{8,10},{9,11},{10,... | collective-permute-start | bytes 208904 | tf_op jit(solution)/shard_map/ppermute | solution.py:274
  38.0 5.5 %collective-permute-start.13 = (bf16[16,16,128]{2,1,0:T(8,128)(2,1)S(1)}, bf16[16,16,128]{2,1,0:T(8,128)(2,1)S(1)}, u32[]{:S(2)}, u32[]{:S(2)}) collective-permute-start(bf16[16,16,128]{2,1,0:T(8,128)(2,1)S(1)} %add_convert_fusion.2.sums2), channel_id=1, source_target_pairs={{0,4},{1,5},{2,6},{3,7},{4,0},{5,1},{6,2},{7,3},{8,10},{9,11},{10,... | collective-permute-start | bytes 196616 | tf_op jit(solution)/shard_map/ppermute | solution.py:274
  45.0 1.3 %collective-permute-start.14 = (f32[9,8,128]{2,1,0:T(8,128)S(1)}, f32[9,8,128]{2,1,0:T(8,128)S(1)}, u32[]{:S(2)}, u32[]{:S(2)}) collective-permute-start(f32[9,8,128]{2,1,0:T(8,128)S(1)} %get-tuple-element.28.own), channel_id=1, source_target_pairs={{0,8},{8,0},{1,9},{9,1},{2,10},{10,2},{3,11},{11,3},{4,12},{12,4},... | collective-permute-start | bytes 110600 | tf_op jit(solution)/shard_map/ppermute | solution.py:263
  46.4 3.0 %collective-permute-start.15 = (f32[8,128]{1,0:T(8,128)S(1)}, f32[8,128]{1,0:T(8,128)S(1)}, u32[]{:S(2)}, u32[]{:S(2)}) collective-permute-start(f32[8,128]{1,0:T(8,128)S(1)} %get-tuple-element.31), channel_id=1, source_target_pairs={{0,9},{1,8},{2,11},{3,10},{4,13},{5,12},{6,15},{7,14},{8,1},{9,0},... | collective-permute-start | bytes 12296 | tf_op jit(solution)/shard_map/ppermute | solution.py:291
  49.4 3.0 %collective-permute-start.16 = (f32[8,128]{1,0:T(8,128)S(1)}, f32[8,128]{1,0:T(8,128)S(1)}, u32[]{:S(2)}, u32[]{:S(2)}) collective-permute-start(f32[8,128]{1,0:T(8,128)S(1)} %add.41), channel_id=1, source_target_pairs={{0,10},{1,11},{2,8},{3,9},{4,14},{5,15},{6,12},{7,13},{8,2},{9,3},... | collective-permute-start | bytes 12296 | tf_op jit(solution)/shard_map/ppermute | solution.py:291
  52.5 3.9 %collective-permute-start.17 = (f32[8,128]{1,0:T(8,128)S(1)}, f32[8,128]{1,0:T(8,128)S(1)}, u32[]{:S(2)}, u32[]{:S(2)}) collective-permute-start(f32[8,128]{1,0:T(8,128)S(1)} %add.42), channel_id=1, source_target_pairs={{0,12},{1,13},{2,14},{3,15},{4,8},{5,9},{6,10},{7,11},{8,4},{9,5},... | collective-permute-start | bytes 12296 | tf_op jit(solution)/shard_map/ppermute | solution.py:291

commit v7 on v6

--- a/solution.py
+++ b/solution.py
@@ -43,28 +43,52 @@
     return jnp.where(count > k, prod, 0.0)
 
 
-def forward(blk, rws, cls, cnt, v_ref, acc_ref):
+def low_lanes():
+    return lax.broadcasted_iota(jnp.int32, (8, 128), 1) < 64
+
+
+def forward(part, blk, rws, cls, cnt, v_ref, acc_ref):
+    low = low_lanes()
     count = jnp.broadcast_to(cnt[...], (8, 128))
+    even, odd = jnp.where(low, count, 0), jnp.where(low, 0, count)
     acc_ref[...] = jnp.zeros_like(acc_ref)
     for k in range(0, blk.shape[0], 2):
         pair = jnp.concatenate([v_ref[cls[0, 0, k]], v_ref[cls[0, 0, k + 1]]], axis=0)
-        a = blk[k : k + 2].reshape(256, 128)
+        a = blk[k : k + 2, 64 * part : 64 * part + 64].reshape(128, 128)
         prod = lax.dot_general(
             pair.astype(BF16), a, (((1,), (1,)), ((), ())), preferred_element_type=F32
         )
-        acc_ref[rws[0, 0, k]] += used(count, k, prod[:8, :128])
-        acc_ref[rws[0, 0, k + 1]] += used(count, k + 1, prod[8:, 128:])
-
-
-def backward(blk, rws, cls, cnt, u_ref, acc_ref):
+        acc_ref[rws[0, 0, k]] += used(even, k, prod[:8])
+        acc_ref[rws[0, 0, k + 1]] += used(odd, k + 1, prod[8:])
+
+
+def store_pairs(acc_ref, out):
+    low = low_lanes()
+    for t in range(acc_ref.shape[0] // 4):
+        rows = []
+        for r in (4 * t, 4 * t + 2):
+            x, y = acc_ref[r], acc_ref[r + 1]
+            rows.append(jnp.where(low, x + pltpu.roll(x, 64, 1), y + pltpu.roll(y, 64, 1)))
+        out[t] = jnp.concatenate(rows, axis=0).astype(BF16)
+
+
+def spread(upd, even, odd):
+    low = low_lanes()
+    for p in range(upd.shape[0]):
+        x = upd[p]
+        y = pltpu.roll(x, 64, 1)
+        even[2 * p] = jnp.where(low, x, 0.0)
+        even[2 * p + 1] = jnp.where(low, y, 0.0)
+        odd[2 * p] = jnp.where(low, 0.0, y)
+        odd[2 * p + 1] = jnp.where(low, 0.0, x)
+
+
+def backward(part, blk, rws, cls, cnt, even, odd, acc_ref):
     count = jnp.broadcast_to(cnt[...], (8, 128))
-    acc_ref[...] = jnp.zeros_like(acc_ref)
-    zero = jnp.zeros((8, 128), F32)
     for k in range(0, blk.shape[0], 2):
-        u0 = jnp.concatenate([u_ref[rws[0, 0, k]], zero], axis=0).astype(BF16)
-        u1 = jnp.concatenate([zero, u_ref[rws[0, 0, k + 1]]], axis=0).astype(BF16)
-        a = blk[k : k + 2].reshape(256, 128)
-        prod = jnp.dot(jnp.concatenate([u0, u1], axis=1), a, preferred_element_type=F32)
+        pair = jnp.concatenate([even[rws[0, 0, k]], odd[rws[0, 0, k + 1]]], axis=0)
+        a = blk[k : k + 2, 64 * part : 64 * part + 64].reshape(128, 128)
+        prod = jnp.dot(pair.astype(BF16), a, preferred_element_type=F32)
         acc_ref[cls[0, 0, k]] += used(count, k, prod[:8])
         acc_ref[cls[0, 0, k + 1]] += used(count, k + 1, prod[8:])
 
@@ -82,17 +106,10 @@
 
 
 def squares(ref, blocks):
-    total = jnp.zeros((8, 128), F32)
+    totals = [jnp.zeros((8, 128), F32)] * 4
     for b in range(blocks):
-        total = total + ref[b] * ref[b]
-    return lane_sum(total)
-
-
-def store_pairs(acc_ref, outs):
-    half = acc_ref.shape[0] // 4
-    for b in range(2 * half):
-        pair = jnp.concatenate([acc_ref[2 * b], acc_ref[2 * b + 1]], axis=0)
-        outs[b // half][b % half] = pair.astype(BF16)
+        totals[b % 4] = totals[b % 4] + ref[b] * ref[b]
+    return lane_sum((totals[0] + totals[1]) + (totals[2] + totals[3]))
 
 
 def place_halves(own, other, out_ref):
@@ -109,49 +126,43 @@
     copy.wait()
 
 
-def first_forward(
-    rws_ref, cls_ref, cnt, blk, alpha_ref, own, other, u_piece,
-    out0, out1, v_out,
+def first_sums(part, acc, alpha_ref, u_piece):
+    pieces = u_piece.shape[1] // 128
+    base = lax.axis_index("col") * pieces
+    a = column(alpha_ref)
+    mine = low_lanes() if part == 0 else jnp.logical_not(low_lanes())
+    for b in range(pieces):
+        acc[base + b] -= jnp.where(mine, a * u_piece[:, b * 128 : (b + 1) * 128], 0.0)
+
+
+def first_forward_0(
+    rws_ref, cls_ref, cnt, blk, alpha_ref, u_piece, own, other,
+    out, v_out,
     rws, cls, sems, alpha, acc,
 ):
     copies = lists((rws_ref, rws), (cls_ref, cls), (alpha_ref, alpha), sems=sems)
     place_halves(own, other, v_out)
     for c in copies:
         c.wait()
-    forward(blk, rws, cls, cnt, v_out, acc)
-    pieces = u_piece.shape[1] // 128
-    base = lax.axis_index("col") * pieces
-    a = column(alpha)
-    for b in range(pieces):
-        acc[base + b] -= a * u_piece[:, b * 128 : (b + 1) * 128]
-    store_pairs(acc, (out0, out1))
-
-
-def pair_sums(pairs, a0, a1, b0, b1):
-    half = pairs // 2
-    for b in range(pairs):
-        one, two = (a0, a1) if b < half else (b0, b1)
-        yield one[b % half].astype(F32) + two[b % half].astype(F32)
-
-
-def first_backward(rws_ref, cls_ref, cnt, blk, sums0, sums1, sums2, sums3, upd, message, rws, cls, sems, acc):
-    copies = lists((rws_ref, rws), (cls_ref, cls), sems=sems)
-    blocks = upd.shape[0]
-    for b, s in enumerate(pair_sums(blocks // 2, sums0, sums1, sums2, sums3)):
-        upd[2 * b] = s[:8]
-        upd[2 * b + 1] = s[8:]
-    cells = acc.shape[0]
-    message[cells] = squares(upd, blocks)
-    for c in copies:
-        c.wait()
-    backward(blk, rws, cls, cnt, upd, acc)
-    message[:cells] = acc[...]
-
-
-def next_forward(
+    forward(0, blk, rws, cls, cnt, v_out, acc)
+    first_sums(0, acc, alpha, u_piece)
+    store_pairs(acc, out)
+
+
+def first_forward_1(
+    rws_ref, cls_ref, cnt, blk, alpha_ref, u_piece, v, out, rws, cls, sems, alpha, acc
+):
+    for c in lists((rws_ref, rws), (cls_ref, cls), (alpha_ref, alpha), sems=sems):
+        c.wait()
+    forward(1, blk, rws, cls, cnt, v, acc)
+    first_sums(1, acc, alpha, u_piece)
+    store_pairs(acc, out)
+
+
+def next_forward_0(
     total_rays,
     rws_ref, cls_ref, cnt, blk, own, other, v_old,
-    out0, out1, vupd, beta_out,
+    out, vupd, beta_out,
     rws, cls, sems, acc,
 ):
     copies = lists((rws_ref, rws), (cls_ref, cls), sems=sems)
@@ -161,43 +172,102 @@
     inv = 1.0 / beta
     for b in range(cells):
         vupd[b] = (own[b] + other[b]) * inv - beta * v_old[b]
-    rays = acc.shape[0]
     sq = squares(vupd, cells)
     lanes = lax.broadcasted_iota(jnp.int32, (8, 128), 1)
     sq = jnp.where(lanes == lax.axis_index("col"), sq, 0.0)
     high = sq.astype(BF16).astype(F32)
-    out0[rays // 4] = jnp.concatenate([high, sq - high], axis=0).astype(BF16)
-    for c in copies:
-        c.wait()
-    forward(blk, rws, cls, cnt, vupd, acc)
-    store_pairs(acc, (out0, out1))
-
-
-def next_backward(
-    total_cells, pieces,
-    rws_ref, cls_ref, cnt, blk, sums0, sums1, sums2, sums3, old, beta,
+    out[out.shape[0] - 1] = jnp.concatenate([high, sq - high], axis=0).astype(BF16)
+    for c in copies:
+        c.wait()
+    forward(0, blk, rws, cls, cnt, vupd, acc)
+    store_pairs(acc, out)
+
+
+def next_forward_1(rws_ref, cls_ref, cnt, blk, vupd, out, rws, cls, sems, acc):
+    for c in lists((rws_ref, rws), (cls_ref, cls), sems=sems):
+        c.wait()
+    forward(1, blk, rws, cls, cnt, vupd, acc)
+    store_pairs(acc, out)
+
+
+def new_rays(sum0, sum1, upd, inv=None, ratio=None, old=None):
+    for t in range(upd.shape[0] // 2):
+        s = sum0[t].astype(F32) + sum1[t].astype(F32)
+        for i in range(2):
+            x = s[8 * i : 8 * i + 8]
+            upd[2 * t + i] = x if old is None else x * inv - ratio * old[2 * t + i]
+
+
+def begin(cells, message, upd, even, odd):
+    message[:cells] = jnp.zeros((cells, 8, 128), F32)
+    message[cells] = squares(upd, upd.shape[0])
+    spread(upd, even, odd)
+
+
+def go_on(cells, before, message, upd, even, odd):
+    message[:cells] = before[:cells]
+    message[cells] = before[cells] + squares(upd, upd.shape[0])
+    spread(upd, even, odd)
+
+
+def first_backward_0(
+    cells, rws_ref, cls_ref, cnt, blk, sum0, sum1, upd, message, rws, cls, sems, even, odd
+):
+    copies = lists((rws_ref, rws), (cls_ref, cls), sems=sems)
+    new_rays(sum0, sum1, upd)
+    begin(cells, message, upd, even, odd)
+    for c in copies:
+        c.wait()
+    backward(0, blk, rws, cls, cnt, even, odd, message)
+
+
+def first_backward_1(
+    cells, rws_ref, cls_ref, cnt, blk, sum0, sum1, before, upd, message, rws, cls, sems, even, odd
+):
+    copies = lists((rws_ref, rws), (cls_ref, cls), sems=sems)
+    new_rays(sum0, sum1, upd)
+    go_on(cells, before, message, upd, even, odd)
+    for c in copies:
+        c.wait()
+    backward(1, blk, rws, cls, cnt, even, odd, message)
+
+
+def next_backward_0(
+    cells, total_cells,
+    rws_ref, cls_ref, cnt, blk, sum0, sum1, old, beta,
     message, u_piece, alpha_out,
-    rws, cls, sems, upd, acc,
+    rws, cls, sems, even, odd, upd,
 ):
     copies = lists((rws_ref, rws), (cls_ref, cls), sems=sems)
-    blocks = upd.shape[0]
-    tail = sums0[blocks // 4].astype(F32) + sums1[blocks // 4].astype(F32)
+    last = sum0.shape[0] - 1
+    tail = sum0[last].astype(F32) + sum1[last].astype(F32)
     alpha = jnp.sqrt(lane_sum(tail[:8] + tail[8:]) / total_cells + EPS)
     alpha_out[...] = alpha
-    inv = 1.0 / alpha
-    ratio = alpha / beta[...]
-    for b, s in enumerate(pair_sums(blocks // 2, sums0, sums1, sums2, sums3)):
-        upd[2 * b] = s[:8] * inv - ratio * old[2 * b]
-        upd[2 * b + 1] = s[8:] * inv - ratio * old[2 * b + 1]
-    cells = acc.shape[0]
-    message[cells] = squares(upd, blocks)
-    base = lax.axis_index("col") * pieces
-    for b in range(pieces):
-        u_piece[b] = upd[base + b]
-    for c in copies:
-        c.wait()
-    backward(blk, rws, cls, cnt, upd, acc)
-    message[:cells] = acc[...]
+    new_rays(sum0, sum1, upd, 1.0 / alpha, alpha / beta[...], old)
+    begin(cells, message, upd, even, odd)
+    base = lax.axis_index("col") * u_piece.shape[0]
+    for b in range(u_piece.shape[0]):
+        u_piece[b] = even[base + b]
+    for c in copies:
+        c.wait()
+    backward(0, blk, rws, cls, cnt, even, odd, message)
+
+
+def next_backward_1(
+    cells,
+    rws_ref, cls_ref, cnt, blk, sum0, sum1, old, beta, alpha, before, u_low,
+    message, u_piece,
+    rws, cls, sems, even, odd, upd,
+):
+    copies = lists((rws_ref, rws), (cls_ref, cls), sems=sems)
+    new_rays(sum0, sum1, upd, 1.0 / alpha[...], alpha[...] / beta[...], old)
+    go_on(cells, before, message, upd, even, odd)
+    base = lax.axis_index("col") * u_piece.shape[0]
+    for b in range(u_piece.shape[0]):
+        u_piece[b] = u_low[b] + odd[base + b]
+    for c in copies:
+        c.wait()
+    backward(1, blk, rws, cls, cnt, even, odd, message)
 
 
 def last_cells(total_rays, own, other, v_old, alpha, sq, vupd, beta_out):
@@ -311,7 +381,18 @@
         pltpu.SemaphoreType.DMA((3,)),
     ]
     ray_acc = pltpu.VMEM((rays, 8, 128), F32)
-    cell_acc = pltpu.VMEM((cells, 8, 128), F32)
+    half_upd = shape(rays // 2, 8, 128)
+    half_rays = shape(rays // 4, 16, 128, dtype=BF16)
+    with_tail = shape(rays // 4 + 1, 16, 128, dtype=BF16)
+    group, tile = shape(cells, 8, 128), shape(8, 128)
+    sent = shape(cells + 1, 8, 128)
+    piece = shape(pieces, 8, 128)
+    flops = 2 * blocks.shape[2] * 64 * 128 * 8
+    cost = pl.CostEstimate(flops=flops, bytes_accessed=2**21, transcendentals=0)
+
+    def product(kernel, out_shape, args, *scratch):
+        return call(kernel, out_shape, [VMEM] * len(args), listed + list(scratch), cost)(*args)
+
     own = call(
         load,
         shape(*v_cells.shape),
@@ -322,33 +403,52 @@
     v_other = other_core(own)
     blk = blocks.reshape(blocks.shape[2:])
     operator = (*where, blk)
-    half_rays = shape(rays // 4, 16, 128, dtype=BF16)
-    *part, v0 = call(
-        first_forward,
-        (half_rays, half_rays, shape(cells, 8, 128)),
-        [VMEM] * 8,
-        listed + [pltpu.SMEM(alpha.shape, F32), ray_acc],
-    )(*operator, alpha, own, v_other, u_rays)
-    sums = column_sum(part)
-    upd1, message = call(
-        first_backward,
-        (shape(rays, 8, 128), shape(cells + 1, 8, 128)),
-        [VMEM] * 8,
-        listed + [cell_acc],
-    )(*operator, *sums)
-    *part, v1, beta1 = call(
-        functools.partial(next_forward, total_rays),
-        (shape(rays // 4 + 1, 16, 128, dtype=BF16), half_rays, shape(cells, 8, 128), shape(8, 128)),
-        [VMEM] * 7,
-        listed + [ray_acc],
-    )(*operator, message, other_core(message), v0)
-    sums = column_sum(part)
-    message, u_piece, alpha1 = call(
-        functools.partial(next_backward, total_cells, pieces),
-        (shape(cells + 1, 8, 128), shape(pieces, 8, 128), shape(8, 128)),
-        [VMEM] * 10,
-        listed + [pltpu.VMEM((rays, 8, 128), F32), cell_acc],
-    )(*operator, *sums, upd1, beta1)
+    first = (*operator, alpha, u_rays)
+    alpha_copy = pltpu.SMEM(alpha.shape, F32)
+    part0, v0 = product(
+        first_forward_0, (half_rays, group), (*first, own, v_other), alpha_copy, ray_acc
+    )
+    part1 = product(first_forward_1, half_rays, (*first, v0), alpha_copy, ray_acc)
+    sums = column_sum((part0, part1))
+    upd0, message = product(
+        functools.partial(first_backward_0, cells),
+        (half_upd, sent),
+        (*operator, *sums[:2]),
+        ray_acc,
+        ray_acc,
+    )
+    upd1, message = product(
+        functools.partial(first_backward_1, cells),
+        (half_upd, sent),
+        (*operator, *sums[2:], message),
+        ray_acc,
+        ray_acc,
+    )
+    part0, v1, beta1 = product(
+        functools.partial(next_forward_0, total_rays),
+        (with_tail, group, tile),
+        (*operator, message, other_core(message), v0),
+        ray_acc,
+    )
+    part1 = product(next_forward_1, half_rays, (*operator, v1), ray_acc)
+    sums = column_sum((part0, part1))
+    upd_copy = pltpu.VMEM((rays // 2, 8, 128), F32)
+    message, u_low, alpha1 = product(
+        functools.partial(next_backward_0, cells, total_cells),
+        (sent, piece, tile),
+        (*operator, *sums[:2], upd0, beta1),
+        ray_acc,
+        ray_acc,
+        upd_copy,
+    )
+    message, u_piece = product(
+        functools.partial(next_backward_1, cells),
+        (sent, piece),
+        (*operator, *sums[2:], upd1, beta1, alpha1, message, u_low),
+        ray_acc,
+        ray_acc,
+        upd_copy,
+    )
     sq, v2, beta2 = call(
         functools.partial(last_cells, total_rays),
         (shape(8, 128), shape(cells, 8, 128), shape(8, 128)),

time: 57.9 us -> 61.3 us (1.059)
  waiting for transfers between devices: 22.2 us -> 14.3 us
  Pallas kernels: 7.88 us -> 14.5 us
  starting transfers between devices: 25 us -> 29.6 us
    pallas_call x4 -> x8, Pallas kernels: 6.55 us -> 13.2 us  [product(): call(kernel, out_shape, [VMEM] * len(args), listed + list(scratch), cost)]
    ppermute x12, waiting for transfers between devices: 13.7 us -> 7.73 us  [column_sum(): lax.ppermute(x, ('row', 'col'), [(j, j ^ first[i]) for j in range(n)] + [...]
    ppermute x3, starting transfers between devices: 4.09 us -> 7.27 us  [last_sum(): x = x + lax.ppermute(x, ('row', 'col'), pairs)]
    ppermute x3, waiting for transfers between devices: 5.91 us -> 3.99 us  [last_sum(): x = x + lax.ppermute(x, ('row', 'col'), pairs)]
    ppermute x12, starting transfers between devices: 20.2 us -> 21.7 us  [column_sum(): lax.ppermute(x, ('row', 'col'), [(j, j ^ first[i]) for j in range(n)] + [...]
  transfers between devices with their start and end apart: 18 -> 18, of which waited for: 14 -> 16; matrix products, arithmetic and copies ran while one was open for 0% -> 0% of each run, Pallas kernels for 0% -> 11%
where the time goes in v7:
time: 61.3 us; the launch traced here: 61 us
  starting transfers between devices  29.6 us (48%)
  Pallas kernels  14.5 us (24%)
  waiting for transfers between devices  14.3 us (23%)
  between operations  1.5 us (2%)
  local copies, waits for them, and re-layouts  0.9 us (1%)
    ppermute x12, starting transfers between devices, column_sum(): lax.ppermute(x, ('row', 'col'), [(j, j ^ first[i]) for j in range(n)] + [...  21.7 us
    pallas_call x8, Pallas kernels, product(): call(kernel, out_shape, [VMEM] * len(args), listed + list(scratch), cost)  13.2 us
    ppermute x12, waiting for transfers between devices, column_sum(): lax.ppermute(x, ('row', 'col'), [(j, j ^ first[i]) for j in range(n)] + [...  7.73 us
    ppermute x3, starting transfers between devices, last_sum(): x = x + lax.ppermute(x, ('row', 'col'), pairs)  7.27 us
    ppermute x3, waiting for transfers between devices, last_sum(): x = x + lax.ppermute(x, ('row', 'col'), pairs)  3.99 us
    ppermute x3, waiting for transfers between devices, other_core(): return lax.ppermute(x, 'row', [(0, 1), (1, 0)])  2.59 us
  transfers between devices with their start and end apart: 18, of which 16 were waited for; matrix products, arithmetic and copies ran while one was open for 0% of the time, Pallas kernels for 11%

profile of v7, /device:TPU:0, one launch (start us, length us, event | category | flops | bytes accessed | tf_op | source)
XLA Modules:
  0.0 61.0 jit_solution(2598062927312411193)
XLA Ops:
  0.6 0.0 copy-start
  0.7 0.9 %copy-done.9 = f32[8,512]{1,0:T(8,128)S(1)} copy-done((f32[8,512]{1,0:T(8,128)S(1)}, f32[8,512]{1,0:T(8,128)}, u32[]{:S(2)}) %copy-start.9) | copy-done | bytes 16408
  1.6 0.5 collective-permute-start
  2.7 0.2 collective-permute-done.other
  3.0 1.9 %shard_map.147 = (bf16[16,16,128]{2,1,0:T(8,128)(2,1)S(1)}, f32[8,8,128]{2,1,0:T(8,128)S(1)}) custom-call(s32[1,1,128]{2,1,0:T(1,128)S(1)} %copy-done.2, s32[1,1,128]{2,1,0:T(1,128)S(1)} %copy-done.3, s32[1,1]{1,0:T(1,128)S(6)} %copy.16.cnt, bf16[128,128,128]{2,1,0:T(8,128)(2,1)S(1)} %bitcast.1, f32[8]{0:T(128)S(1)} %copy-done.6, f32[8,1024]{1,0:T(8,128)S(1)} %copy-done.1, ...), custom_call_target="tpu_custom_call" | custom-call | flops 16777216 | bytes 2097152 | tf_op jit(solution)/shard_map/pallas_call | solution.py:394
  4.9 2.9 %collective-permute-start.4 = (bf16[16,16,128]{2,1,0:T(8,128)(2,1)S(1)}, bf16[16,16,128]{2,1,0:T(8,128)(2,1)S(1)}, u32[]{:S(2)}, u32[]{:S(2)}) collective-permute-start(bf16[16,16,128]{2,1,0:T(8,128)(2,1)S(1)} %get-tuple-element.23), channel_id=1, source_target_pairs={{0,1},{1,0},{2,3},{3,2},{4,5},{5,4},{6,7},{7,6},{8,12},{9,13},{10,... | collective-permute-start | bytes 196616 | tf_op jit(solution)/shard_map/ppermute | solution.py:344
  7.8 1.9 %shard_map.148 = bf16[16,16,128]{2,1,0:T(8,128)(2,1)S(1)} custom-call(s32[1,1,128]{2,1,0:T(1,128)S(1)} %copy-done.2, s32[1,1,128]{2,1,0:T(1,128)S(1)} %copy-done.3, s32[1,1]{1,0:T(1,128)S(6)} %copy.16.cnt, bf16[128,128,128]{2,1,0:T(8,128)(2,1)S(1)} %bitcast.2, f32[8]{0:T(128)S(1)} %copy-done.6, f32[8,1024]{1,0:T(8,128)S(1)} %copy-done.1, ...), custom_call_target="tpu_custom_call" | custom-call | flops 16777216 | bytes 2097152 | tf_op jit(solution)/shard_map/pallas_call | solution.py:394
  9.8 0.1 collective-permute-start.1
  9.8 0.2 collective-permute-done.4
  10.1 2.2 %collective-permute-start.5 = (bf16[16,16,128]{2,1,0:T(8,128)(2,1)S(1)}, bf16[16,16,128]{2,1,0:T(8,128)(2,1)S(1)}, u32[]{:S(2)}, u32[]{:S(2)}) collective-permute-start(bf16[16,16,128]{2,1,0:T(8,128)(2,1)S(1)} %add_convert_fusion.5), channel_id=1, source_target_pairs={{0,2},{1,3},{2,0},{3,1},{4,6},{5,7},{6,4},{7,5},{8,9},{9,8},{10,11... | collective-permute-start | bytes 196616 | tf_op jit(solution)/shard_map/ppermute | solution.py:344
  12.2 2.4 %collective-permute-done.1 = bf16[16,16,128]{2,1,0:T(8,128)(2,1)S(1)} collective-permute-done((bf16[16,16,128]{2,1,0:T(8,128)(2,1)S(1)}, bf16[16,16,128]{2,1,0:T(8,128)(2,1)S(1)}, u32[]{:S(2)}, u32[]{:S(2)}) %collective-permute-start.1) | collective-permute-done | bytes 65568 | tf_op jit(solution)/shard_map/ppermute | solution.py:344
  14.7 1.6 %collective-permute-start.2 = (bf16[16,16,128]{2,1,0:T(8,128)(2,1)S(1)}, bf16[16,16,128]{2,1,0:T(8,128)(2,1)S(1)}, u32[]{:S(2)}, u32[]{:S(2)}) collective-permute-start(bf16[16,16,128]{2,1,0:T(8,128)(2,1)S(1)} %add_convert_fusion.7), channel_id=1, source_target_pairs={{0,2},{1,3},{2,0},{3,1},{4,6},{5,7},{6,4},{7,5},{8,9},{9,8},{10,11... | collective-permute-start | bytes 196616 | tf_op jit(solution)/shard_map/ppermute | solution.py:344
  16.3 0.0 collective-permute-done.5
  16.3 2.5 %collective-permute-start.6 = (bf16[16,16,128]{2,1,0:T(8,128)(2,1)S(1)}, bf16[16,16,128]{2,1,0:T(8,128)(2,1)S(1)}, u32[]{:S(2)}, u32[]{:S(2)}) collective-permute-start(bf16[16,16,128]{2,1,0:T(8,128)(2,1)S(1)} %add_convert_fusion.4.sum0), channel_id=1, source_target_pairs={{0,4},{1,5},{2,6},{3,7},{4,0},{5,1},{6,2},{7,3},{8,10},{9,11},{10,... | collective-permute-start | bytes 196616 | tf_op jit(solution)/shard_map/ppermute | solution.py:344
  18.8 0.3 collective-permute-done.2
  19.2 2.5 %collective-permute-start.3 = (bf16[16,16,128]{2,1,0:T(8,128)(2,1)S(1)}, bf16[16,16,128]{2,1,0:T(8,128)(2,1)S(1)}, u32[]{:S(2)}, u32[]{:S(2)}) collective-permute-start(bf16[16,16,128]{2,1,0:T(8,128)(2,1)S(1)} %add_convert_fusion.6.sum0), channel_id=1, source_target_pairs={{0,4},{1,5},{2,6},{3,7},{4,0},{5,1},{6,2},{7,3},{8,10},{9,11},{10,... | collective-permute-start | bytes 196616 | tf_op jit(solution)/shard_map/ppermute | solution.py:344
  21.7 0.4 collective-permute-done.6.sum1
  22.0 1.3 %shard_map.149 = (f32[32,8,128]{2,1,0:T(8,128)S(1)}, f32[9,8,128]{2,1,0:T(8,128)S(1)}) custom-call(s32[1,1,128]{2,1,0:T(1,128)S(1)} %copy-done.2, s32[1,1,128]{2,1,0:T(1,128)S(1)} %copy-done.3, s32[1,1]{1,0:T(1,128)S(6)} %copy.16.cnt, bf16[128,128,128]{2,1,0:T(8,128)(2,1)S(1)} %bitcast.3, bf16[16,16,128]{2,1,0:T(8,128)(2,1)S(1)} %add_convert_fusion.4.sum0, ...), custom_call_target="tpu_custom_call" | custom-call | flops 16777216 | bytes 2097152 | tf_op jit(solution)/shard_map/pallas_call | solution.py:394
  23.4 1.0 %collective-permute-done.3.sum1 = bf16[16,16,128]{2,1,0:T(8,128)(2,1)S(1)} collective-permute-done((bf16[16,16,128]{2,1,0:T(8,128)(2,1)S(1)}, bf16[16,16,128]{2,1,0:T(8,128)(2,1)S(1)}, u32[]{:S(2)}, u32[]{:S(2)}) %collective-permute-start.3) | collective-permute-done | bytes 65568 | tf_op jit(solution)/shard_map/ppermute | solution.py:344
  24.4 1.3 %shard_map.150 = (f32[32,8,128]{2,1,0:T(8,128)S(1)}, f32[9,8,128]{2,1,0:T(8,128)S(1)}) custom-call(s32[1,1,128]{2,1,0:T(1,128)S(1)} %copy-done.2, s32[1,1,128]{2,1,0:T(1,128)S(1)} %copy-done.3, s32[1,1]{1,0:T(1,128)S(6)} %copy.16.cnt, bf16[128,128,128]{2,1,0:T(8,128)(2,1)S(1)} %bitcast.4, bf16[16,16,128]{2,1,0:T(8,128)(2,1)S(1)} %add_convert_fusion.6.sum0, ...), custom_call_target="tpu_custom_call" | custom-call | flops 16777216 | bytes 2097152 | tf_op jit(solution)/shard_map/pallas_call | solution.py:394
  25.8 0.1 collective-permute-start.7
  25.8 1.2 %collective-permute-done.7.other = f32[9,8,128]{2,1,0:T(8,128)S(1)} collective-permute-done((f32[9,8,128]{2,1,0:T(8,128)S(1)}, f32[9,8,128]{2,1,0:T(8,128)S(1)}, u32[]{:S(2)}, u32[]{:S(2)}) %collective-permute-start.7) | collective-permute-done | bytes 36896 | tf_op jit(solution)/shard_map/ppermute | solution.py:333
  27.0 1.9 %shard_map.151 = (bf16[17,16,128]{2,1,0:T(8,128)(2,1)S(1)}, f32[8,8,128]{2,1,0:T(8,128)S(1)}, f32[8,128]{1,0:T(8,128)S(1)}) custom-call(s32[1,1,128]{2,1,0:T(1,128)S(1)} %copy-done.2, s32[1,1,128]{2,1,0:T(1,128)S(1)} %copy-done.3, s32[1,1]{1,0:T(1,128)S(6)} %copy.16.cnt, bf16[128,128,128]{2,1,0:T(8,128)(2,1)S(1)} %bitcast.5, ...), custom_call_target="tpu_custom_call" | custom-call | flops 16777216 | bytes 2097152 | tf_op jit(solution)/shard_map/pallas_call | solution.py:394
  29.0 0.1 collective-permute-start.11
  29.1 1.9 %shard_map.152 = bf16[16,16,128]{2,1,0:T(8,128)(2,1)S(1)} custom-call(s32[1,1,128]{2,1,0:T(1,128)S(1)} %copy-done.2, s32[1,1,128]{2,1,0:T(1,128)S(1)} %copy-done.3, s32[1,1]{1,0:T(1,128)S(6)} %copy.16.cnt, bf16[128,128,128]{2,1,0:T(8,128)(2,1)S(1)} %bitcast.6, f32[8,8,128]{2,1,0:T(8,128)S(1)} %get-tuple-element.26.vupd.v_old.v1), custom_call_target="tpu_custom_call" | custom-call | flops 16777216 | bytes 2097152 | tf_op jit(solution)/shard_map/pallas_call | solution.py:394
  31.0 2.1 %collective-permute-start.8 = (bf16[16,16,128]{2,1,0:T(8,128)(2,1)S(1)}, bf16[16,16,128]{2,1,0:T(8,128)(2,1)S(1)}, u32[]{:S(2)}, u32[]{:S(2)}) collective-permute-start(bf16[16,16,128]{2,1,0:T(8,128)(2,1)S(1)} %shard_map.152), channel_id=1, source_target_pairs={{0,1},{1,0},{2,3},{3,2},{4,5},{5,4},{6,7},{7,6},{8,12},{9,13},{10,... | collective-permute-start | bytes 196616 | tf_op jit(solution)/shard_map/ppermute | solution.py:344
  33.1 0.3 collective-permute-done.11
  33.4 1.7 %collective-permute-start.12 = (bf16[17,16,128]{2,1,0:T(8,128)(2,1)S(1)}, bf16[17,16,128]{2,1,0:T(8,128)(2,1)S(1)}, u32[]{:S(2)}, u32[]{:S(2)}) collective-permute-start(bf16[17,16,128]{2,1,0:T(8,128)(2,1)S(1)} %add_convert_fusion.1), channel_id=1, source_target_pairs={{0,2},{1,3},{2,0},{3,1},{4,6},{5,7},{6,4},{7,5},{8,9},{9,8},{10,11... | collective-permute-start | bytes 208904 | tf_op jit(solution)/shard_map/ppermute | solution.py:344
  35.1 0.5 collective-permute-done.8
  35.6 1.5 %collective-permute-start.9 = (bf16[16,16,128]{2,1,0:T(8,128)(2,1)S(1)}, bf16[16,16,128]{2,1,0:T(8,128)(2,1)S(1)}, u32[]{:S(2)}, u32[]{:S(2)}) collective-permute-start(bf16[16,16,128]{2,1,0:T(8,128)(2,1)S(1)} %add_convert_fusion.3), channel_id=1, source_target_pairs={{0,2},{1,3},{2,0},{3,1},{4,6},{5,7},{6,4},{7,5},{8,9},{9,8},{10,11... | collective-permute-start | bytes 196616 | tf_op jit(solution)/shard_map/ppermute | solution.py:344
  37.0 1.3 %collective-permute-done.12 = bf16[17,16,128]{2,1,0:T(8,128)(2,1)S(1)} collective-permute-done((bf16[17,16,128]{2,1,0:T(8,128)(2,1)S(1)}, bf16[17,16,128]{2,1,0:T(8,128)(2,1)S(1)}, u32[]{:S(2)}, u32[]{:S(2)}) %collective-permute-start.12) | collective-permute-done | bytes 69664 | tf_op jit(solution)/shard_map/ppermute | solution.py:344
  38.3 2.2 %collective-permute-start.13 = (bf16[17,16,128]{2,1,0:T(8,128)(2,1)S(1)}, bf16[17,16,128]{2,1,0:T(8,128)(2,1)S(1)}, u32[]{:S(2)}, u32[]{:S(2)}) collective-permute-start(bf16[17,16,128]{2,1,0:T(8,128)(2,1)S(1)} %add_convert_fusion.sum0), channel_id=1, source_target_pairs={{0,4},{1,5},{2,6},{3,7},{4,0},{5,1},{6,2},{7,3},{8,10},{9,11},{10,... | collective-permute-start | bytes 208904 | tf_op jit(solution)/shard_map/ppermute | solution.py:344
  40.5 0.0 collective-permute-done.9
  40.6 2.4 %collective-permute-start.10 = (bf16[16,16,128]{2,1,0:T(8,128)(2,1)S(1)}, bf16[16,16,128]{2,1,0:T(8,128)(2,1)S(1)}, u32[]{:S(2)}, u32[]{:S(2)}) collective-permute-start(bf16[16,16,128]{2,1,0:T(8,128)(2,1)S(1)} %add_convert_fusion.2.sum0), channel_id=1, source_target_pairs={{0,4},{1,5},{2,6},{3,7},{4,0},{5,1},{6,2},{7,3},{8,10},{9,11},{10,... | collective-permute-start | bytes 196616 | tf_op jit(solution)/shard_map/ppermute | solution.py:344
  43.0 1.1 %collective-permute-done.13.sum1 = bf16[17,16,128]{2,1,0:T(8,128)(2,1)S(1)} collective-permute-done((bf16[17,16,128]{2,1,0:T(8,128)(2,1)S(1)}, bf16[17,16,128]{2,1,0:T(8,128)(2,1)S(1)}, u32[]{:S(2)}, u32[]{:S(2)}) %collective-permute-start.13) | collective-permute-done | bytes 69664 | tf_op jit(solution)/shard_map/ppermute | solution.py:344
  44.0 1.5 %shard_map.153 = (f32[9,8,128]{2,1,0:T(8,128)S(1)}, f32[8,8,128]{2,1,0:T(8,128)S(1)}, f32[8,128]{1,0:T(8,128)S(1)}) custom-call(s32[1,1,128]{2,1,0:T(1,128)S(1)} %copy-done.2, s32[1,1,128]{2,1,0:T(1,128)S(1)} %copy-done.3, s32[1,1]{1,0:T(1,128)S(6)} %copy.16.cnt, bf16[128,128,128]{2,1,0:T(8,128)(2,1)S(1)} %bitcast.7, ...), custom_call_target="tpu_custom_call" | custom-call | flops 16777216 | bytes 2097152 | tf_op jit(solution)/shard_map/pallas_call | solution.py:394
  45.5 0.3 collective-permute-done.10.sum1
  45.8 1.3 %shard_map.154 = (f32[9,8,128]{2,1,0:T(8,128)S(1)}, f32[8,8,128]{2,1,0:T(8,128)S(1)}) custom-call(s32[1,1,128]{2,1,0:T(1,128)S(1)} %copy-done.2, s32[1,1,128]{2,1,0:T(1,128)S(1)} %copy-done.3, s32[1,1]{1,0:T(1,128)S(6)} %copy.16.cnt, bf16[128,128,128]{2,1,0:T(8,128)(2,1)S(1)} %bitcast.8, bf16[16,16,128]{2,1,0:T(8,128)(2,1)S(1)} %add_convert_fusion.2.sum0, ...), custom_call_target="tpu_custom_call" | custom-call | flops 16777216 | bytes 2097152 | tf_op jit(solution)/shard_map/pallas_call | solution.py:394
  47.1 0.1 collective-permute-start.14
  47.2 1.2 %collective-permute-done.14.other = f32[9,8,128]{2,1,0:T(8,128)S(1)} collective-permute-done((f32[9,8,128]{2,1,0:T(8,128)S(1)}, f32[9,8,128]{2,1,0:T(8,128)S(1)}, u32[]{:S(2)}, u32[]{:S(2)}) %collective-permute-start.14) | collective-permute-done | bytes 36896 | tf_op jit(solution)/shard_map/ppermute | solution.py:333
  48.4 0.1 shard_map.155
  48.5 2.2 %collective-permute-start.15 = (f32[8,128]{1,0:T(8,128)S(1)}, f32[8,128]{1,0:T(8,128)S(1)}, u32[]{:S(2)}, u32[]{:S(2)}) collective-permute-start(f32[8,128]{1,0:T(8,128)S(1)} %get-tuple-element.35), channel_id=1, source_target_pairs={{0,9},{1,8},{2,11},{3,10},{4,13},{5,12},{6,15},{7,14},{8,1},{9,0},... | collective-permute-start | bytes 12296 | tf_op jit(solution)/shard_map/ppermute | solution.py:361
  50.7 1.3 %collective-permute-done.15 = f32[8,128]{1,0:T(8,128)S(1)} collective-permute-done((f32[8,128]{1,0:T(8,128)S(1)}, f32[8,128]{1,0:T(8,128)S(1)}, u32[]{:S(2)}, u32[]{:S(2)}) %collective-permute-start.15) | collective-permute-done | bytes 4128 | tf_op jit(solution)/shard_map/ppermute | solution.py:361
  52.1 2.4 %collective-permute-start.16 = (f32[8,128]{1,0:T(8,128)S(1)}, f32[8,128]{1,0:T(8,128)S(1)}, u32[]{:S(2)}, u32[]{:S(2)}) collective-permute-start(f32[8,128]{1,0:T(8,128)S(1)} %add.41), channel_id=1, source_target_pairs={{0,10},{1,11},{2,8},{3,9},{4,14},{5,15},{6,12},{7,13},{8,2},{9,3},... | collective-permute-start | bytes 12296 | tf_op jit(solution)/shard_map/ppermute | solution.py:361
  54.4 1.3 %collective-permute-done.16 = f32[8,128]{1,0:T(8,128)S(1)} collective-permute-done((f32[8,128]{1,0:T(8,128)S(1)}, f32[8,128]{1,0:T(8,128)S(1)}, u32[]{:S(2)}, u32[]{:S(2)}) %collective-permute-start.16) | collective-permute-done | bytes 4128 | tf_op jit(solution)/shard_map/ppermute | solution.py:361
  55.8 2.7 %collective-permute-start.17 = (f32[8,128]{1,0:T(8,128)S(1)}, f32[8,128]{1,0:T(8,128)S(1)}, u32[]{:S(2)}, u32[]{:S(2)}) collective-permute-start(f32[8,128]{1,0:T(8,128)S(1)} %add.42), channel_id=1, source_target_pairs={{0,12},{1,13},{2,14},{3,15},{4,8},{5,9},{6,10},{7,11},{8,4},{9,5},... | collective-permute-start | bytes 12296 | tf_op jit(solution)/shard_map/ppermute | solution.py:361
  58.4 1.3 %collective-permute-done.17 = f32[8,128]{1,0:T(8,128)S(1)} collective-permute-done((f32[8,128]{1,0:T(8,128)S(1)}, f32[8,128]{1,0:T(8,128)S(1)}, u32[]{:S(2)}, u32[]{:S(2)}) %collective-permute-start.17) | collective-permute-done | bytes 4128 | tf_op jit(solution)/shard_map/ppermute | solution.py:361
  59.8 1.2 %shard_map.156 = (f32[8,1024]{1,0:T(8,128)}, f32[8,512]{1,0:T(8,128)}, f32[8,512]{1,0:T(8,128)}, f32[8,512]{1,0:T(8,128)}, f32[3,8]{1,0:T(4,128)}) custom-call(f32[8]{0:T(128)S(1)} %copy-done.7, f32[8]{0:T(128)S(1)} %copy-done.8, f32[8,128]{1,0:T(8,128)S(1)} %add.43.sq, f32[8,8,128]{2,1,0:T(8,128)S(1)} %get-tuple-element.26.vupd.v_old.v1, ...), custom_call_target="tpu_custom_call" | custom-call | tf_op jit(solution)/shard_map/pallas_call | solution.py:459
  (30 shorter events, 0.2 us)
Async XLA Ops:
  0.6 2.3 %copy-start = (bf16[1,1,128,128,128]{4,3,2,1,0:T(8,128)(2,1)S(1)}, bf16[1,1,128,128,128]{4,3,2,1,0:T(8,128)(2,1)}, u32[]{:S(2)}) copy-start(bf16[1,1,128,128,128]{4,3,2,1,0:T(8,128)(2,1)} %param.11) | copy-start | bytes 12582916
  0.6 2.3 %copy-start.2 = (s32[1,1,128]{2,1,0:T(1,128)S(1)}, s32[1,1,128]{2,1,0:T(1,128)}, u32[]{:S(2)}) copy-start(s32[1,1,128]{2,1,0:T(1,128)} %rws_ref.15) | copy-start | bytes 1540
  0.7 2.3 %copy-start.3 = (s32[1,1,128]{2,1,0:T(1,128)S(1)}, s32[1,1,128]{2,1,0:T(1,128)}, u32[]{:S(2)}) copy-start(s32[1,1,128]{2,1,0:T(1,128)} %cls_ref.15) | copy-start | bytes 1540
  0.7 2.3 %copy-start.1 = (f32[8,1024]{1,0:T(8,128)S(1)}, f32[8,1024]{1,0:T(8,128)}, u32[]{:S(2)}) copy-start(f32[8,1024]{1,0:T(8,128)} %u_piece.3) | copy-start | bytes 98308
  0.7 2.3 %copy-start.6 = (f32[8]{0:T(128)S(1)}, f32[8]{0:T(128)}, u32[]{:S(2)}) copy-start(f32[8]{0:T(128)} %alpha_ref.3) | copy-start | bytes 100
  0.7 0.9 %copy-start.9 = (f32[8,512]{1,0:T(8,128)S(1)}, f32[8,512]{1,0:T(8,128)}, u32[]{:S(2)}) copy-start(f32[8,512]{1,0:T(8,128)} %own_hbm.1) | copy-start | bytes 49156
  1.6 1.4 %collective-permute-start = (f32[8,512]{1,0:T(8,128)S(1)}, f32[8,512]{1,0:T(8,128)S(1)}, u32[]{:S(2)}, u32[]{:S(2)}) collective-permute-start(f32[8,512]{1,0:T(8,128)S(1)} %shard_map.146.own), channel_id=1, source_target_pairs={{0,8},{8,0},{1,9},{9,1},{2,10},{10,2},{3,11},{11,3},{4,12},{12,4},... | collective-permute-start | bytes 49160 | tf_op jit(solution)/shard_map/ppermute | solution.py:333
  4.9 5.1 %collective-permute-start.4 = (bf16[16,16,128]{2,1,0:T(8,128)(2,1)S(1)}, bf16[16,16,128]{2,1,0:T(8,128)(2,1)S(1)}, u32[]{:S(2)}, u32[]{:S(2)}) collective-permute-start(bf16[16,16,128]{2,1,0:T(8,128)(2,1)S(1)} %get-tuple-element.23), channel_id=1, source_target_pairs={{0,1},{1,0},{2,3},{3,2},{4,5},{5,4},{6,7},{7,6},{8,12},{9,13},{10,... | collective-permute-start | bytes 196616 | tf_op jit(solution)/shard_map/ppermute | solution.py:344
  9.8 4.9 %collective-permute-start.1 = (bf16[16,16,128]{2,1,0:T(8,128)(2,1)S(1)}, bf16[16,16,128]{2,1,0:T(8,128)(2,1)S(1)}, u32[]{:S(2)}, u32[]{:S(2)}) collective-permute-start(bf16[16,16,128]{2,1,0:T(8,128)(2,1)S(1)} %shard_map.148), channel_id=1, source_target_pairs={{0,1},{1,0},{2,3},{3,2},{4,5},{5,4},{6,7},{7,6},{8,12},{9,13},{10,... | collective-permute-start | bytes 196616 | tf_op jit(solution)/shard_map/ppermute | solution.py:344
  10.1 6.2 %collective-permute-start.5 = (bf16[16,16,128]{2,1,0:T(8,128)(2,1)S(1)}, bf16[16,16,128]{2,1,0:T(8,128)(2,1)S(1)}, u32[]{:S(2)}, u32[]{:S(2)}) collective-permute-start(bf16[16,16,128]{2,1,0:T(8,128)(2,1)S(1)} %add_convert_fusion.5), channel_id=1, source_target_pairs={{0,2},{1,3},{2,0},{3,1},{4,6},{5,7},{6,4},{7,5},{8,9},{9,8},{10,11... | collective-permute-start | bytes 196616 | tf_op jit(solution)/shard_map/ppermute | solution.py:344
  14.7 4.5 %collective-permute-start.2 = (bf16[16,16,128]{2,1,0:T(8,128)(2,1)S(1)}, bf16[16,16,128]{2,1,0:T(8,128)(2,1)S(1)}, u32[]{:S(2)}, u32[]{:S(2)}) collective-permute-start(bf16[16,16,128]{2,1,0:T(8,128)(2,1)S(1)} %add_convert_fusion.7), channel_id=1, source_target_pairs={{0,2},{1,3},{2,0},{3,1},{4,6},{5,7},{6,4},{7,5},{8,9},{9,8},{10,11... | collective-permute-start | bytes 196616 | tf_op jit(solution)/shard_map/ppermute | solution.py:344
  16.3 5.7 %collective-permute-start.6 = (bf16[16,16,128]{2,1,0:T(8,128)(2,1)S(1)}, bf16[16,16,128]{2,1,0:T(8,128)(2,1)S(1)}, u32[]{:S(2)}, u32[]{:S(2)}) collective-permute-start(bf16[16,16,128]{2,1,0:T(8,128)(2,1)S(1)} %add_convert_fusion.4.sum0), channel_id=1, source_target_pairs={{0,4},{1,5},{2,6},{3,7},{4,0},{5,1},{6,2},{7,3},{8,10},{9,11},{10,... | collective-permute-start | bytes 196616 | tf_op jit(solution)/shard_map/ppermute | solution.py:344
  19.2 5.2 %collective-permute-start.3 = (bf16[16,16,128]{2,1,0:T(8,128)(2,1)S(1)}, bf16[16,16,128]{2,1,0:T(8,128)(2,1)S(1)}, u32[]{:S(2)}, u32[]{:S(2)}) collective-permute-start(bf16[16,16,128]{2,1,0:T(8,128)(2,1)S(1)} %add_convert_fusion.6.sum0), channel_id=1, source_target_pairs={{0,4},{1,5},{2,6},{3,7},{4,0},{5,1},{6,2},{7,3},{8,10},{9,11},{10,... | collective-permute-start | bytes 196616 | tf_op jit(solution)/shard_map/ppermute | solution.py:344
  25.8 1.3 %collective-permute-start.7 = (f32[9,8,128]{2,1,0:T(8,128)S(1)}, f32[9,8,128]{2,1,0:T(8,128)S(1)}, u32[]{:S(2)}, u32[]{:S(2)}) collective-permute-start(f32[9,8,128]{2,1,0:T(8,128)S(1)} %get-tuple-element.25.own), channel_id=1, source_target_pairs={{0,8},{8,0},{1,9},{9,1},{2,10},{10,2},{3,11},{11,3},{4,12},{12,4},... | collective-permute-start | bytes 110600 | tf_op jit(solution)/shard_map/ppermute | solution.py:333
  29.0 4.4 %collective-permute-start.11 = (bf16[17,16,128]{2,1,0:T(8,128)(2,1)S(1)}, bf16[17,16,128]{2,1,0:T(8,128)(2,1)S(1)}, u32[]{:S(2)}, u32[]{:S(2)}) collective-permute-start(bf16[17,16,128]{2,1,0:T(8,128)(2,1)S(1)} %get-tuple-element.29), channel_id=1, source_target_pairs={{0,1},{1,0},{2,3},{3,2},{4,5},{5,4},{6,7},{7,6},{8,12},{9,13},{10,... | collective-permute-start | bytes 208904 | tf_op jit(solution)/shard_map/ppermute | solution.py:344
  31.0 4.5 %collective-permute-start.8 = (bf16[16,16,128]{2,1,0:T(8,128)(2,1)S(1)}, bf16[16,16,128]{2,1,0:T(8,128)(2,1)S(1)}, u32[]{:S(2)}, u32[]{:S(2)}) collective-permute-start(bf16[16,16,128]{2,1,0:T(8,128)(2,1)S(1)} %shard_map.152), channel_id=1, source_target_pairs={{0,1},{1,0},{2,3},{3,2},{4,5},{5,4},{6,7},{7,6},{8,12},{9,13},{10,... | collective-permute-start | bytes 196616 | tf_op jit(solution)/shard_map/ppermute | solution.py:344
  33.4 4.9 %collective-permute-start.12 = (bf16[17,16,128]{2,1,0:T(8,128)(2,1)S(1)}, bf16[17,16,128]{2,1,0:T(8,128)(2,1)S(1)}, u32[]{:S(2)}, u32[]{:S(2)}) collective-permute-start(bf16[17,16,128]{2,1,0:T(8,128)(2,1)S(1)} %add_convert_fusion.1), channel_id=1, source_target_pairs={{0,2},{1,3},{2,0},{3,1},{4,6},{5,7},{6,4},{7,5},{8,9},{9,8},{10,11... | collective-permute-start | bytes 208904 | tf_op jit(solution)/shard_map/ppermute | solution.py:344
  35.6 5.0 %collective-permute-start.9 = (bf16[16,16,128]{2,1,0:T(8,128)(2,1)S(1)}, bf16[16,16,128]{2,1,0:T(8,128)(2,1)S(1)}, u32[]{:S(2)}, u32[]{:S(2)}) collective-permute-start(bf16[16,16,128]{2,1,0:T(8,128)(2,1)S(1)} %add_convert_fusion.3), channel_id=1, source_target_pairs={{0,2},{1,3},{2,0},{3,1},{4,6},{5,7},{6,4},{7,5},{8,9},{9,8},{10,11... | collective-permute-start | bytes 196616 | tf_op jit(solution)/shard_map/ppermute | solution.py:344
  38.3 5.7 %collective-permute-start.13 = (bf16[17,16,128]{2,1,0:T(8,128)(2,1)S(1)}, bf16[17,16,128]{2,1,0:T(8,128)(2,1)S(1)}, u32[]{:S(2)}, u32[]{:S(2)}) collective-permute-start(bf16[17,16,128]{2,1,0:T(8,128)(2,1)S(1)} %add_convert_fusion.sum0), channel_id=1, source_target_pairs={{0,4},{1,5},{2,6},{3,7},{4,0},{5,1},{6,2},{7,3},{8,10},{9,11},{10,... | collective-permute-start | bytes 208904 | tf_op jit(solution)/shard_map/ppermute | solution.py:344
  40.6 5.2 %collective-permute-start.10 = (bf16[16,16,128]{2,1,0:T(8,128)(2,1)S(1)}, bf16[16,16,128]{2,1,0:T(8,128)(2,1)S(1)}, u32[]{:S(2)}, u32[]{:S(2)}) collective-permute-start(bf16[16,16,128]{2,1,0:T(8,128)(2,1)S(1)} %add_convert_fusion.2.sum0), channel_id=1, source_target_pairs={{0,4},{1,5},{2,6},{3,7},{4,0},{5,1},{6,2},{7,3},{8,10},{9,11},{10,... | collective-permute-start | bytes 196616 | tf_op jit(solution)/shard_map/ppermute | solution.py:344
  44.0 15.7 %copy-start.4 = (f32[8,512]{1,0:T(8,128)S(1)}, f32[8,512]{1,0:T(8,128)}, u32[]{:S(2)}) copy-start(f32[8,512]{1,0:T(8,128)} %x_in.1) | copy-start | bytes 49156
  44.0 15.7 %copy-start.5 = (f32[8,512]{1,0:T(8,128)S(1)}, f32[8,512]{1,0:T(8,128)}, u32[]{:S(2)}) copy-start(f32[8,512]{1,0:T(8,128)} %w_in.1) | copy-start | bytes 49156
  44.0 15.7 %copy-start.7 = (f32[8]{0:T(128)S(1)}, f32[8]{0:T(128)}, u32[]{:S(2)}) copy-start(f32[8]{0:T(128)} %phibar_in.1) | copy-start | bytes 100
  44.0 15.7 %copy-start.8 = (f32[8]{0:T(128)S(1)}, f32[8]{0:T(128)}, u32[]{:S(2)}) copy-start(f32[8]{0:T(128)} %rhobar_in.1) | copy-start | bytes 100
  47.1 1.3 %collective-permute-start.14 = (f32[9,8,128]{2,1,0:T(8,128)S(1)}, f32[9,8,128]{2,1,0:T(8,128)S(1)}, u32[]{:S(2)}, u32[]{:S(2)}) collective-permute-start(f32[9,8,128]{2,1,0:T(8,128)S(1)} %get-tuple-element.34.own), channel_id=1, source_target_pairs={{0,8},{8,0},{1,9},{9,1},{2,10},{10,2},{3,11},{11,3},{4,12},{12,4},... | collective-permute-start | bytes 110600 | tf_op jit(solution)/shard_map/ppermute | solution.py:333
  48.5 3.5 %collective-permute-start.15 = (f32[8,128]{1,0:T(8,128)S(1)}, f32[8,128]{1,0:T(8,128)S(1)}, u32[]{:S(2)}, u32[]{:S(2)}) collective-permute-start(f32[8,128]{1,0:T(8,128)S(1)} %get-tuple-element.35), channel_id=1, source_target_pairs={{0,9},{1,8},{2,11},{3,10},{4,13},{5,12},{6,15},{7,14},{8,1},{9,0},... | collective-permute-start | bytes 12296 | tf_op jit(solution)/shard_map/ppermute | solution.py:361
  52.1 3.7 %collective-permute-start.16 = (f32[8,128]{1,0:T(8,128)S(1)}, f32[8,128]{1,0:T(8,128)S(1)}, u32[]{:S(2)}, u32[]{:S(2)}) collective-permute-start(f32[8,128]{1,0:T(8,128)S(1)} %add.41), channel_id=1, source_target_pairs={{0,10},{1,11},{2,8},{3,9},{4,14},{5,15},{6,12},{7,13},{8,2},{9,3},... | collective-permute-start | bytes 12296 | tf_op jit(solution)/shard_map/ppermute | solution.py:361
  55.8 4.0 %collective-permute-start.17 = (f32[8,128]{1,0:T(8,128)S(1)}, f32[8,128]{1,0:T(8,128)S(1)}, u32[]{:S(2)}, u32[]{:S(2)}) collective-permute-start(f32[8,128]{1,0:T(8,128)S(1)} %add.42), channel_id=1, source_target_pairs={{0,12},{1,13},{2,14},{3,15},{4,8},{5,9},{6,10},{7,11},{8,4},{9,5},... | collective-permute-start | bytes 12296 | tf_op jit(solution)/shard_map/ppermute | solution.py:361

commit v8 on v6

--- a/solution.py
+++ b/solution.py
@@ -56,17 +56,20 @@
         acc_ref[rws[0, 0, k + 1]] += used(count, k + 1, prod[8:, 128:])
 
 
-def backward(blk, rws, cls, cnt, u_ref, acc_ref):
+def backward(blk, rws, cls, cnt, u_ref, accs, out):
     count = jnp.broadcast_to(cnt[...], (8, 128))
-    acc_ref[...] = jnp.zeros_like(acc_ref)
+    for acc in accs:
+        acc[...] = jnp.zeros_like(acc)
     zero = jnp.zeros((8, 128), F32)
     for k in range(0, blk.shape[0], 2):
         u0 = jnp.concatenate([u_ref[rws[0, 0, k]], zero], axis=0).astype(BF16)
         u1 = jnp.concatenate([zero, u_ref[rws[0, 0, k + 1]]], axis=0).astype(BF16)
         a = blk[k : k + 2].reshape(256, 128)
         prod = jnp.dot(jnp.concatenate([u0, u1], axis=1), a, preferred_element_type=F32)
-        acc_ref[cls[0, 0, k]] += used(count, k, prod[:8])
-        acc_ref[cls[0, 0, k + 1]] += used(count, k + 1, prod[8:])
+        accs[k % len(accs)][cls[0, 0, k]] += used(count, k, prod[:8])
+        accs[(k + 1) % len(accs)][cls[0, 0, k + 1]] += used(count, k + 1, prod[8:])
+    for c in range(accs[0].shape[0]):
+        out[c] = functools.reduce(jnp.add, [acc[c] for acc in accs])
 
 
 def column(ref):
@@ -82,10 +85,10 @@
 
 
 def squares(ref, blocks):
-    total = jnp.zeros((8, 128), F32)
+    totals = [jnp.zeros((8, 128), F32)] * 4
     for b in range(blocks):
-        total = total + ref[b] * ref[b]
-    return lane_sum(total)
+        totals[b % 4] = totals[b % 4] + ref[b] * ref[b]
+    return lane_sum((totals[0] + totals[1]) + (totals[2] + totals[3]))
 
 
 def store_pairs(acc_ref, outs):
@@ -134,18 +137,17 @@
         yield one[b % half].astype(F32) + two[b % half].astype(F32)
 
 
-def first_backward(rws_ref, cls_ref, cnt, blk, sums0, sums1, sums2, sums3, upd, message, rws, cls, sems, acc):
+def first_backward(rws_ref, cls_ref, cnt, blk, sums0, sums1, sums2, sums3, upd, message, rws, cls, sems, *accs):
     copies = lists((rws_ref, rws), (cls_ref, cls), sems=sems)
     blocks = upd.shape[0]
     for b, s in enumerate(pair_sums(blocks // 2, sums0, sums1, sums2, sums3)):
         upd[2 * b] = s[:8]
         upd[2 * b + 1] = s[8:]
-    cells = acc.shape[0]
+    cells = message.shape[0] - 1
     message[cells] = squares(upd, blocks)
     for c in copies:
         c.wait()
-    backward(blk, rws, cls, cnt, upd, acc)
-    message[:cells] = acc[...]
+    backward(blk, rws, cls, cnt, upd, accs, message)
 
 
 def next_forward(
@@ -177,7 +179,7 @@
     total_cells, pieces,
     rws_ref, cls_ref, cnt, blk, sums0, sums1, sums2, sums3, old, beta,
     message, u_piece, alpha_out,
-    rws, cls, sems, upd, acc,
+    rws, cls, sems, upd, *accs,
 ):
     copies = lists((rws_ref, rws), (cls_ref, cls), sems=sems)
     blocks = upd.shape[0]
@@ -189,15 +191,14 @@
     for b, s in enumerate(pair_sums(blocks // 2, sums0, sums1, sums2, sums3)):
         upd[2 * b] = s[:8] * inv - ratio * old[2 * b]
         upd[2 * b + 1] = s[8:] * inv - ratio * old[2 * b + 1]
-    cells = acc.shape[0]
+    cells = message.shape[0] - 1
     message[cells] = squares(upd, blocks)
     base = lax.axis_index("col") * pieces
     for b in range(pieces):
         u_piece[b] = upd[base + b]
     for c in copies:
         c.wait()
-    backward(blk, rws, cls, cnt, upd, acc)
-    message[:cells] = acc[...]
+    backward(blk, rws, cls, cnt, upd, accs, message)
 
 
 def last_cells(total_rays, own, other, v_old, alpha, sq, vupd, beta_out):
@@ -211,50 +212,45 @@
     sq[...] = squares(vupd, cells)
 
 
-def finish(
-    total_cells,
-    phibar_in,
-    rhobar_in,
-    sq,
-    v1,
-    v2,
-    u_piece,
-    x_in,
-    w_in,
-    beta1,
-    alpha1,
-    beta2,
-    u_out,
-    v_out,
-    x_out,
-    w_out,
-    scalars,
-):
-    alpha2 = jnp.sqrt(sq[...] / total_cells + EPS)
-    phibar, rhobar = column(phibar_in), column(rhobar_in)
-    steps = []
-    for beta, alpha in ((beta1[...], alpha1[...]), (beta2[...], alpha2)):
-        rho = jnp.sqrt(rhobar * rhobar + beta * beta)
-        cosine, sine = rhobar / rho, beta / rho
-        steps.append((cosine * phibar / rho, sine * alpha / rho, 1.0 / alpha))
-        rhobar = -cosine * alpha
-        phibar = sine * phibar
+def settle(
+    phibar_in, rhobar_in, v1, u_piece, x_in, w_in, beta1, alpha1, beta2,
+    u_out, x_out, w_mid, factors,
+):
+    phibar, rhobar, beta, alpha = column(phibar_in), column(rhobar_in), beta1[...], alpha1[...]
+    rho = jnp.sqrt(rhobar * rhobar + beta * beta)
+    cosine, sine = rhobar / rho, beta / rho
+    along, back, inv = cosine * phibar / rho, sine * alpha / rho, 1.0 / alpha
+    rhobar, phibar = -cosine * alpha, sine * phibar
+    beta = beta2[...]
+    rho = jnp.sqrt(rhobar * rhobar + beta * beta)
+    cosine, sine = rhobar / rho, beta / rho
+    along2 = cosine * phibar / rho
+    factors[0], factors[1], factors[2] = sine / rho, -cosine, sine * phibar
     half = x_in.shape[1] // 128
     base = lax.axis_index("row") * half
     for b in range(half):
         at = slice(b * 128, (b + 1) * 128)
-        x, w = x_in[:, at], w_in[:, at]
-        for (along, back, inv), vupd in zip(steps, (v1, v2)):
-            v = vupd[base + b] * inv
-            x = x + along * w
-            w = v - back * w
-        v_out[:, at], x_out[:, at], w_out[:, at] = v, x, w
-    inv = 1.0 / beta2[...]
+        w_old = w_in[:, at]
+        w = v1[base + b] * inv - back * w_old
+        x_out[:, at] = x_in[:, at] + along * w_old + along2 * w
+        w_mid[:, at] = w
+    inv = 1.0 / beta
     for b in range(u_piece.shape[0]):
         u_out[:, b * 128 : (b + 1) * 128] = u_piece[b] * inv
+
+
+def finish(total_cells, sq, v2, w_mid, factors, v_out, w_out, scalars):
+    alpha = jnp.sqrt(sq[...] / total_cells + EPS)
+    inv, back = 1.0 / alpha, factors[0] * alpha
+    half = v_out.shape[1] // 128
+    base = lax.axis_index("row") * half
+    for b in range(half):
+        at = slice(b * 128, (b + 1) * 128)
+        v = v2[base + b] * inv
+        v_out[:, at], w_out[:, at] = v, v - back * w_mid[:, at]
     rows = lax.broadcasted_iota(jnp.int32, (8, 128), 0)
     lanes = lax.broadcasted_iota(jnp.int32, (8, 128), 1)
-    for i, value in enumerate((alpha2, phibar, rhobar)):
+    for i, value in enumerate((alpha, factors[2], factors[1] * alpha)):
         line = jnp.sum(jnp.where(rows == lanes, value, 0.0), axis=0, keepdims=True)
         scalars[i : i + 1, :] = line[:, :8]
 
@@ -311,7 +307,7 @@
         pltpu.SemaphoreType.DMA((3,)),
     ]
     ray_acc = pltpu.VMEM((rays, 8, 128), F32)
-    cell_acc = pltpu.VMEM((cells, 8, 128), F32)
+    cell_accs = [pltpu.VMEM((cells, 8, 128), F32)] * 4
     own = call(
         load,
         shape(*v_cells.shape),
@@ -334,7 +330,7 @@
         first_backward,
         (shape(rays, 8, 128), shape(cells + 1, 8, 128)),
         [VMEM] * 8,
-        listed + [cell_acc],
+        listed + cell_accs,
     )(*operator, *sums)
     *part, v1, beta1 = call(
         functools.partial(next_forward, total_rays),
@@ -347,7 +343,7 @@
         functools.partial(next_backward, total_cells, pieces),
         (shape(cells + 1, 8, 128), shape(pieces, 8, 128), shape(8, 128)),
         [VMEM] * 10,
-        listed + [pltpu.VMEM((rays, 8, 128), F32), cell_acc],
+        listed + [pltpu.VMEM((rays, 8, 128), F32)] + cell_accs,
     )(*operator, *sums, upd1, beta1)
     sq, v2, beta2 = call(
         functools.partial(last_cells, total_rays),
@@ -356,11 +352,17 @@
     )(message, other_core(message), v1, alpha1)
     sq = last_sum(sq)
     flat = shape(*v_cells.shape)
-    return call(
-        functools.partial(finish, total_cells),
-        (shape(*u_rays.shape), flat, flat, flat, shape(3, 8)),
-        [SMEM] * 2 + [VMEM] * 9,
-    )(phibar, rhobar, sq, v1, v2, u_piece, x_cells, w_cells, beta1, alpha1, beta2)
+    u, x, w_mid, factors = call(
+        settle,
+        (shape(*u_rays.shape), flat, flat, shape(3, 8, 128)),
+        [SMEM] * 2 + [VMEM] * 7,
+        (),
+        pl.CostEstimate(flops=10**6, bytes_accessed=3 * 10**6, transcendentals=0),
+    )(phibar, rhobar, v1, u_piece, x_cells, w_cells, beta1, alpha1, beta2)
+    v, w, scalars = call(
+        functools.partial(finish, total_cells), (flat, flat, shape(3, 8)), [VMEM] * 4
+    )(sq, v2, w_mid, factors)
+    return u, v, x, w, scalars
 
 
 def solution(mesh):

time: 57.9 us -> 57.1 us (0.986)
  waiting for transfers between devices: 22.2 us -> 21.2 us
    ppermute x3, waiting for transfers between devices: 5.91 us -> 4.79 us  [last_sum(): x = x + lax.ppermute(x, ('row', 'col'), pairs)]
    pallas_call x1 -> x2, Pallas kernels: 1.21 us -> 1.84 us  [the longest x1 1.2 us: body(): call(settle, (shape(*u_rays.shape), flat, flat, shape(3, 8, 128)), [SMEM]...]
  transfers between devices with their start and end apart: 18 -> 18, of which waited for: 14 -> 14; matrix products, arithmetic and copies ran while one was open for 0% -> 0% of each run, Pallas kernels for 0% -> 2%
where the time goes in v8:
time: 57.1 us; the launch traced here: 56.9 us
  starting transfers between devices  24.9 us (44%)
  waiting for transfers between devices  21.2 us (37%)
  Pallas kernels  8.26 us (14%)
  between operations  1.46 us (3%)
  local copies, waits for them, and re-layouts  0.9 us (2%)
    ppermute x12, starting transfers between devices, column_sum(): lax.ppermute(x, ('row', 'col'), [(j, j ^ first[i]) for j in range(n)] + [...  20.2 us
    ppermute x12, waiting for transfers between devices, column_sum(): lax.ppermute(x, ('row', 'col'), [(j, j ^ first[i]) for j in range(n)] + [...  13.8 us
    ppermute x3, waiting for transfers between devices, last_sum(): x = x + lax.ppermute(x, ('row', 'col'), pairs)  4.79 us
    ppermute x3, starting transfers between devices, last_sum(): x = x + lax.ppermute(x, ('row', 'col'), pairs)  4 us
    ppermute x3, waiting for transfers between devices, other_core(): return lax.ppermute(x, 'row', [(0, 1), (1, 0)])  2.59 us
    pallas_call x1, Pallas kernels, body(): call(first_forward, (half_rays, half_rays, shape(cells, 8, 128)), [VMEM]...  1.83 us
    pallas_call x1, Pallas kernels, body(): call(functools.partial(next_forward, total_rays), (shape(rays // 4 + 1, 1...  1.81 us
    pallas_call x1, Pallas kernels, body(): call(functools.partial(next_backward, total_cells, pieces), (shape(cells...  1.39 us
  transfers between devices with their start and end apart: 18, of which 14 were waited for; matrix products, arithmetic and copies ran while one was open for 0% of the time, Pallas kernels for 2%

profile of v8, /device:TPU:0, one launch (start us, length us, event | category | flops | bytes accessed | tf_op | source)
XLA Modules:
  0.0 56.9 jit_solution(1992484202136899601)
XLA Ops:
  0.6 0.0 copy-start.5
  0.7 0.9 %copy-done.9 = f32[8,512]{1,0:T(8,128)S(1)} copy-done((f32[8,512]{1,0:T(8,128)S(1)}, f32[8,512]{1,0:T(8,128)}, u32[]{:S(2)}) %copy-start.9) | copy-done | bytes 16408
  1.6 0.5 collective-permute-start
  2.7 0.2 collective-permute-done.other
  2.9 0.0 copy-done.4
  2.9 0.0 copy-done.1
  3.0 1.8 %shard_map.147 = (bf16[16,16,128]{2,1,0:T(8,128)(2,1)S(1)}, bf16[16,16,128]{2,1,0:T(8,128)(2,1)S(1)}, f32[8,8,128]{2,1,0:T(8,128)S(1)}) custom-call(s32[1,1,128]{2,1,0:T(1,128)S(1)} %copy-done.4, s32[1,1,128]{2,1,0:T(1,128)S(1)} %copy-done.5, s32[1,1]{1,0:T(1,128)S(6)} %copy.16.cnt, bf16[128,128,128]{2,1,0:T(8,128)(2,1)S(1)} %bitcast.1, f32[8]{0:T(128)S(1)} %copy-done.8, ...), custom_call_target="tpu_custom_call" | custom-call | tf_op jit(solution)/shard_map/pallas_call | solution.py:322
  4.8 3.0 %collective-permute-start.1 = (bf16[16,16,128]{2,1,0:T(8,128)(2,1)S(1)}, bf16[16,16,128]{2,1,0:T(8,128)(2,1)S(1)}, u32[]{:S(2)}, u32[]{:S(2)}) collective-permute-start(bf16[16,16,128]{2,1,0:T(8,128)(2,1)S(1)} %get-tuple-element.27), channel_id=1, source_target_pairs={{0,1},{1,0},{2,3},{3,2},{4,5},{5,4},{6,7},{7,6},{8,12},{9,13},{10,... | collective-permute-start | bytes 196616 | tf_op jit(solution)/shard_map/ppermute | solution.py:270
  7.7 0.1 collective-permute-start.4
  7.8 2.2 %collective-permute-done.1 = bf16[16,16,128]{2,1,0:T(8,128)(2,1)S(1)} collective-permute-done((bf16[16,16,128]{2,1,0:T(8,128)(2,1)S(1)}, bf16[16,16,128]{2,1,0:T(8,128)(2,1)S(1)}, u32[]{:S(2)}, u32[]{:S(2)}) %collective-permute-start.1) | collective-permute-done | bytes 65568 | tf_op jit(solution)/shard_map/ppermute | solution.py:270
  10.0 2.2 %collective-permute-start.2 = (bf16[16,16,128]{2,1,0:T(8,128)(2,1)S(1)}, bf16[16,16,128]{2,1,0:T(8,128)(2,1)S(1)}, u32[]{:S(2)}, u32[]{:S(2)}) collective-permute-start(bf16[16,16,128]{2,1,0:T(8,128)(2,1)S(1)} %add_convert_fusion.7), channel_id=1, source_target_pairs={{0,2},{1,3},{2,0},{3,1},{4,6},{5,7},{6,4},{7,5},{8,9},{9,8},{10,11... | collective-permute-start | bytes 196616 | tf_op jit(solution)/shard_map/ppermute | solution.py:270
  12.2 0.0 collective-permute-done.4
  12.2 1.5 %collective-permute-start.5 = (bf16[16,16,128]{2,1,0:T(8,128)(2,1)S(1)}, bf16[16,16,128]{2,1,0:T(8,128)(2,1)S(1)}, u32[]{:S(2)}, u32[]{:S(2)}) collective-permute-start(bf16[16,16,128]{2,1,0:T(8,128)(2,1)S(1)} %add_convert_fusion.5), channel_id=1, source_target_pairs={{0,2},{1,3},{2,0},{3,1},{4,6},{5,7},{6,4},{7,5},{8,9},{9,8},{10,11... | collective-permute-start | bytes 196616 | tf_op jit(solution)/shard_map/ppermute | solution.py:270
  13.7 0.8 %collective-permute-done.2 = bf16[16,16,128]{2,1,0:T(8,128)(2,1)S(1)} collective-permute-done((bf16[16,16,128]{2,1,0:T(8,128)(2,1)S(1)}, bf16[16,16,128]{2,1,0:T(8,128)(2,1)S(1)}, u32[]{:S(2)}, u32[]{:S(2)}) %collective-permute-start.2) | collective-permute-done | bytes 65568 | tf_op jit(solution)/shard_map/ppermute | solution.py:270
  14.5 3.1 %collective-permute-start.3 = (bf16[16,16,128]{2,1,0:T(8,128)(2,1)S(1)}, bf16[16,16,128]{2,1,0:T(8,128)(2,1)S(1)}, u32[]{:S(2)}, u32[]{:S(2)}) collective-permute-start(bf16[16,16,128]{2,1,0:T(8,128)(2,1)S(1)} %add_convert_fusion.6.sums0), channel_id=1, source_target_pairs={{0,4},{1,5},{2,6},{3,7},{4,0},{5,1},{6,2},{7,3},{8,10},{9,11},{10,... | collective-permute-start | bytes 196616 | tf_op jit(solution)/shard_map/ppermute | solution.py:270
  17.5 0.0 collective-permute-done.5
  17.6 1.6 %collective-permute-start.6 = (bf16[16,16,128]{2,1,0:T(8,128)(2,1)S(1)}, bf16[16,16,128]{2,1,0:T(8,128)(2,1)S(1)}, u32[]{:S(2)}, u32[]{:S(2)}) collective-permute-start(bf16[16,16,128]{2,1,0:T(8,128)(2,1)S(1)} %add_convert_fusion.4.sums2), channel_id=1, source_target_pairs={{0,4},{1,5},{2,6},{3,7},{4,0},{5,1},{6,2},{7,3},{8,10},{9,11},{10,... | collective-permute-start | bytes 196616 | tf_op jit(solution)/shard_map/ppermute | solution.py:270
  19.2 0.7 %collective-permute-done.3.sums1 = bf16[16,16,128]{2,1,0:T(8,128)(2,1)S(1)} collective-permute-done((bf16[16,16,128]{2,1,0:T(8,128)(2,1)S(1)}, bf16[16,16,128]{2,1,0:T(8,128)(2,1)S(1)}, u32[]{:S(2)}, u32[]{:S(2)}) %collective-permute-start.3) | collective-permute-done | bytes 65568 | tf_op jit(solution)/shard_map/ppermute | solution.py:270
  19.9 2.9 %collective-permute-done.6.sums3 = bf16[16,16,128]{2,1,0:T(8,128)(2,1)S(1)} collective-permute-done((bf16[16,16,128]{2,1,0:T(8,128)(2,1)S(1)}, bf16[16,16,128]{2,1,0:T(8,128)(2,1)S(1)}, u32[]{:S(2)}, u32[]{:S(2)}) %collective-permute-start.6) | collective-permute-done | bytes 65568 | tf_op jit(solution)/shard_map/ppermute | solution.py:270
  22.8 1.3 %shard_map.148 = (f32[64,8,128]{2,1,0:T(8,128)S(1)}, f32[9,8,128]{2,1,0:T(8,128)S(1)}) custom-call(s32[1,1,128]{2,1,0:T(1,128)S(1)} %copy-done.4, s32[1,1,128]{2,1,0:T(1,128)S(1)} %copy-done.5, s32[1,1]{1,0:T(1,128)S(6)} %copy.16.cnt, bf16[128,128,128]{2,1,0:T(8,128)(2,1)S(1)} %bitcast.2, bf16[16,16,128]{2,1,0:T(8,128)(2,1)S(1)} %add_convert_fusion.6.sums0, ...), custom_call_target="tpu_custom_call" | custom-call | tf_op jit(solution)/shard_map/pallas_call | solution.py:329
  24.1 0.1 collective-permute-start.7
  24.2 1.2 %collective-permute-done.7.other = f32[9,8,128]{2,1,0:T(8,128)S(1)} collective-permute-done((f32[9,8,128]{2,1,0:T(8,128)S(1)}, f32[9,8,128]{2,1,0:T(8,128)S(1)}, u32[]{:S(2)}, u32[]{:S(2)}) %collective-permute-start.7) | collective-permute-done | bytes 36896 | tf_op jit(solution)/shard_map/ppermute | solution.py:259
  25.4 1.8 %shard_map.149 = (bf16[17,16,128]{2,1,0:T(8,128)(2,1)S(1)}, bf16[16,16,128]{2,1,0:T(8,128)(2,1)S(1)}, f32[8,8,128]{2,1,0:T(8,128)S(1)}, f32[8,128]{1,0:T(8,128)S(1)}) custom-call(s32[1,1,128]{2,1,0:T(1,128)S(1)} %copy-done.4, s32[1,1,128]{2,1,0:T(1,128)S(1)} %copy-done.5, s32[1,1]{1,0:T(1,128)S(6)} %copy.16.cnt, bf16[128,128,128]{2,1,0:T(8,128)(2,1)S(1)} %bitcast.3, ...), custom_call_target="tpu_custom_call" | custom-call | tf_op jit(solution)/shard_map/pallas_call | solution.py:335
  27.2 1.6 %collective-permute-start.8 = (bf16[17,16,128]{2,1,0:T(8,128)(2,1)S(1)}, bf16[17,16,128]{2,1,0:T(8,128)(2,1)S(1)}, u32[]{:S(2)}, u32[]{:S(2)}) collective-permute-start(bf16[17,16,128]{2,1,0:T(8,128)(2,1)S(1)} %get-tuple-element.32), channel_id=1, source_target_pairs={{0,1},{1,0},{2,3},{3,2},{4,5},{5,4},{6,7},{7,6},{8,12},{9,13},{10,... | collective-permute-start | bytes 208904 | tf_op jit(solution)/shard_map/ppermute | solution.py:270
  28.8 0.5 collective-permute-start.11
  29.3 2.3 %collective-permute-done.8 = bf16[17,16,128]{2,1,0:T(8,128)(2,1)S(1)} collective-permute-done((bf16[17,16,128]{2,1,0:T(8,128)(2,1)S(1)}, bf16[17,16,128]{2,1,0:T(8,128)(2,1)S(1)}, u32[]{:S(2)}, u32[]{:S(2)}) %collective-permute-start.8) | collective-permute-done | bytes 69664 | tf_op jit(solution)/shard_map/ppermute | solution.py:270
  31.6 1.6 %collective-permute-start.9 = (bf16[17,16,128]{2,1,0:T(8,128)(2,1)S(1)}, bf16[17,16,128]{2,1,0:T(8,128)(2,1)S(1)}, u32[]{:S(2)}, u32[]{:S(2)}) collective-permute-start(bf16[17,16,128]{2,1,0:T(8,128)(2,1)S(1)} %add_convert_fusion.1), channel_id=1, source_target_pairs={{0,2},{1,3},{2,0},{3,1},{4,6},{5,7},{6,4},{7,5},{8,9},{9,8},{10,11... | collective-permute-start | bytes 208904 | tf_op jit(solution)/shard_map/ppermute | solution.py:270
  33.3 0.0 collective-permute-done.11
  33.3 1.4 %collective-permute-start.12 = (bf16[16,16,128]{2,1,0:T(8,128)(2,1)S(1)}, bf16[16,16,128]{2,1,0:T(8,128)(2,1)S(1)}, u32[]{:S(2)}, u32[]{:S(2)}) collective-permute-start(bf16[16,16,128]{2,1,0:T(8,128)(2,1)S(1)} %add_convert_fusion.3), channel_id=1, source_target_pairs={{0,2},{1,3},{2,0},{3,1},{4,6},{5,7},{6,4},{7,5},{8,9},{9,8},{10,11... | collective-permute-start | bytes 196616 | tf_op jit(solution)/shard_map/ppermute | solution.py:270
  34.7 1.3 %collective-permute-done.9 = bf16[17,16,128]{2,1,0:T(8,128)(2,1)S(1)} collective-permute-done((bf16[17,16,128]{2,1,0:T(8,128)(2,1)S(1)}, bf16[17,16,128]{2,1,0:T(8,128)(2,1)S(1)}, u32[]{:S(2)}, u32[]{:S(2)}) %collective-permute-start.9) | collective-permute-done | bytes 69664 | tf_op jit(solution)/shard_map/ppermute | solution.py:270
  36.0 1.8 %collective-permute-start.10 = (bf16[17,16,128]{2,1,0:T(8,128)(2,1)S(1)}, bf16[17,16,128]{2,1,0:T(8,128)(2,1)S(1)}, u32[]{:S(2)}, u32[]{:S(2)}) collective-permute-start(bf16[17,16,128]{2,1,0:T(8,128)(2,1)S(1)} %add_convert_fusion.sums0), channel_id=1, source_target_pairs={{0,4},{1,5},{2,6},{3,7},{4,0},{5,1},{6,2},{7,3},{8,10},{9,11},{10,... | collective-permute-start | bytes 208904 | tf_op jit(solution)/shard_map/ppermute | solution.py:270
  37.8 0.1 collective-permute-done.12
  37.9 1.9 %collective-permute-start.13 = (bf16[16,16,128]{2,1,0:T(8,128)(2,1)S(1)}, bf16[16,16,128]{2,1,0:T(8,128)(2,1)S(1)}, u32[]{:S(2)}, u32[]{:S(2)}) collective-permute-start(bf16[16,16,128]{2,1,0:T(8,128)(2,1)S(1)} %add_convert_fusion.2.sums2), channel_id=1, source_target_pairs={{0,4},{1,5},{2,6},{3,7},{4,0},{5,1},{6,2},{7,3},{8,10},{9,11},{10,... | collective-permute-start | bytes 196616 | tf_op jit(solution)/shard_map/ppermute | solution.py:270
  39.8 3.6 %collective-permute-done.13.sums3 = bf16[16,16,128]{2,1,0:T(8,128)(2,1)S(1)} collective-permute-done((bf16[16,16,128]{2,1,0:T(8,128)(2,1)S(1)}, bf16[16,16,128]{2,1,0:T(8,128)(2,1)S(1)}, u32[]{:S(2)}, u32[]{:S(2)}) %collective-permute-start.13) | collective-permute-done | bytes 65568 | tf_op jit(solution)/shard_map/ppermute | solution.py:270
  43.4 0.0 collective-permute-done.10.sums1
  43.4 1.4 %shard_map.150 = (f32[9,8,128]{2,1,0:T(8,128)S(1)}, f32[8,8,128]{2,1,0:T(8,128)S(1)}, f32[8,128]{1,0:T(8,128)S(1)}) custom-call(s32[1,1,128]{2,1,0:T(1,128)S(1)} %copy-done.4, s32[1,1,128]{2,1,0:T(1,128)S(1)} %copy-done.5, s32[1,1]{1,0:T(1,128)S(6)} %copy.16.cnt, bf16[128,128,128]{2,1,0:T(8,128)(2,1)S(1)} %bitcast.4, ...), custom_call_target="tpu_custom_call" | custom-call | tf_op jit(solution)/shard_map/pallas_call | solution.py:342
  44.8 0.1 collective-permute-start.14
  44.9 1.2 %collective-permute-done.14.other = f32[9,8,128]{2,1,0:T(8,128)S(1)} collective-permute-done((f32[9,8,128]{2,1,0:T(8,128)S(1)}, f32[9,8,128]{2,1,0:T(8,128)S(1)}, u32[]{:S(2)}, u32[]{:S(2)}) %collective-permute-start.14) | collective-permute-done | bytes 36896 | tf_op jit(solution)/shard_map/ppermute | solution.py:259
  46.1 0.1 shard_map.151
  46.2 1.3 %collective-permute-start.15 = (f32[8,128]{1,0:T(8,128)S(1)}, f32[8,128]{1,0:T(8,128)S(1)}, u32[]{:S(2)}, u32[]{:S(2)}) collective-permute-start(f32[8,128]{1,0:T(8,128)S(1)} %get-tuple-element.41), channel_id=1, source_target_pairs={{0,9},{1,8},{2,11},{3,10},{4,13},{5,12},{6,15},{7,14},{8,1},{9,0},... | collective-permute-start | bytes 12296 | tf_op jit(solution)/shard_map/ppermute | solution.py:287
  47.5 1.8 %collective-permute-done.15 = f32[8,128]{1,0:T(8,128)S(1)} collective-permute-done((f32[8,128]{1,0:T(8,128)S(1)}, f32[8,128]{1,0:T(8,128)S(1)}, u32[]{:S(2)}, u32[]{:S(2)}) %collective-permute-start.15) | collective-permute-done | bytes 4128 | tf_op jit(solution)/shard_map/ppermute | solution.py:287
  49.3 1.3 %collective-permute-start.16 = (f32[8,128]{1,0:T(8,128)S(1)}, f32[8,128]{1,0:T(8,128)S(1)}, u32[]{:S(2)}, u32[]{:S(2)}) collective-permute-start(f32[8,128]{1,0:T(8,128)S(1)} %add.41), channel_id=1, source_target_pairs={{0,10},{1,11},{2,8},{3,9},{4,14},{5,15},{6,12},{7,13},{8,2},{9,3},... | collective-permute-start | bytes 12296 | tf_op jit(solution)/shard_map/ppermute | solution.py:287
  50.6 1.7 %collective-permute-done.16 = f32[8,128]{1,0:T(8,128)S(1)} collective-permute-done((f32[8,128]{1,0:T(8,128)S(1)}, f32[8,128]{1,0:T(8,128)S(1)}, u32[]{:S(2)}, u32[]{:S(2)}) %collective-permute-start.16) | collective-permute-done | bytes 4128 | tf_op jit(solution)/shard_map/ppermute | solution.py:287
  52.3 1.4 %collective-permute-start.17 = (f32[8,128]{1,0:T(8,128)S(1)}, f32[8,128]{1,0:T(8,128)S(1)}, u32[]{:S(2)}, u32[]{:S(2)}) collective-permute-start(f32[8,128]{1,0:T(8,128)S(1)} %add.42), channel_id=1, source_target_pairs={{0,12},{1,13},{2,14},{3,15},{4,8},{5,9},{6,10},{7,11},{8,4},{9,5},... | collective-permute-start | bytes 12296 | tf_op jit(solution)/shard_map/ppermute | solution.py:287
  53.7 0.0 copy-done.2
  53.7 1.2 %shard_map.152 = (f32[8,1024]{1,0:T(8,128)}, f32[8,512]{1,0:T(8,128)}, f32[8,512]{1,0:T(8,128)S(1)}, f32[3,8,128]{2,1,0:T(8,128)S(1)}) custom-call(f32[8]{0:T(128)S(1)} %copy-done.6, f32[8]{0:T(128)S(1)} %copy-done.7, f32[8,8,128]{2,1,0:T(8,128)S(1)} %get-tuple-element.31.v_old.v1, f32[8,8,128]{2,1,0:T(8,128)S(1)} %get-tuple-element.36.u_piece, ...), custom_call_target="tpu_custom_call" | custom-call | flops 1000000 | bytes 3000000 | tf_op jit(solution)/shard_map/pallas_call | solution.py:355
  54.9 1.3 %collective-permute-done.17 = f32[8,128]{1,0:T(8,128)S(1)} collective-permute-done((f32[8,128]{1,0:T(8,128)S(1)}, f32[8,128]{1,0:T(8,128)S(1)}, u32[]{:S(2)}, u32[]{:S(2)}) %collective-permute-start.17) | collective-permute-done | bytes 4128 | tf_op jit(solution)/shard_map/ppermute | solution.py:287
  56.2 0.6 %shard_map.153 = (f32[8,512]{1,0:T(8,128)}, f32[8,512]{1,0:T(8,128)}, f32[3,8]{1,0:T(4,128)}) custom-call(f32[8,128]{1,0:T(8,128)S(1)} %add.43.sq, f32[8,8,128]{2,1,0:T(8,128)S(1)} %get-tuple-element.42.v2, f32[8,512]{1,0:T(8,128)S(1)} %get-tuple-element.43.w_mid, f32[3,8,128]{2,1,0:T(8,128)S(1)} %get-tuple-element.44.factors), custom_call_target="tpu_custom_call" | custom-call | tf_op jit(solution)/shard_map/pallas_call | solution.py:362
  (27 shorter events, 0.2 us)
Async XLA Ops:
  0.6 2.3 %copy-start.5 = (s32[1,1,128]{2,1,0:T(1,128)S(1)}, s32[1,1,128]{2,1,0:T(1,128)}, u32[]{:S(2)}) copy-start(s32[1,1,128]{2,1,0:T(1,128)} %cls_ref.7) | copy-start | bytes 1540
  0.6 2.3 %copy-start.4 = (s32[1,1,128]{2,1,0:T(1,128)S(1)}, s32[1,1,128]{2,1,0:T(1,128)}, u32[]{:S(2)}) copy-start(s32[1,1,128]{2,1,0:T(1,128)} %rws_ref.7) | copy-start | bytes 1540
  0.7 2.3 %copy-start.8 = (f32[8]{0:T(128)S(1)}, f32[8]{0:T(128)}, u32[]{:S(2)}) copy-start(f32[8]{0:T(128)} %alpha_ref.1) | copy-start | bytes 100
  0.7 2.3 %copy-start.1 = (f32[8,1024]{1,0:T(8,128)S(1)}, f32[8,1024]{1,0:T(8,128)}, u32[]{:S(2)}) copy-start(f32[8,1024]{1,0:T(8,128)} %u_piece.1) | copy-start | bytes 98308
  0.7 2.3 %copy-start = (bf16[1,1,128,128,128]{4,3,2,1,0:T(8,128)(2,1)S(1)}, bf16[1,1,128,128,128]{4,3,2,1,0:T(8,128)(2,1)}, u32[]{:S(2)}) copy-start(bf16[1,1,128,128,128]{4,3,2,1,0:T(8,128)(2,1)} %param.11) | copy-start | bytes 12582916
  0.7 0.9 %copy-start.9 = (f32[8,512]{1,0:T(8,128)S(1)}, f32[8,512]{1,0:T(8,128)}, u32[]{:S(2)}) copy-start(f32[8,512]{1,0:T(8,128)} %own_hbm.1) | copy-start | bytes 49156
  1.6 1.4 %collective-permute-start = (f32[8,512]{1,0:T(8,128)S(1)}, f32[8,512]{1,0:T(8,128)S(1)}, u32[]{:S(2)}, u32[]{:S(2)}) collective-permute-start(f32[8,512]{1,0:T(8,128)S(1)} %shard_map.146.own), channel_id=1, source_target_pairs={{0,8},{8,0},{1,9},{9,1},{2,10},{10,2},{3,11},{11,3},{4,12},{12,4},... | collective-permute-start | bytes 49160 | tf_op jit(solution)/shard_map/ppermute | solution.py:259
  4.8 5.2 %collective-permute-start.1 = (bf16[16,16,128]{2,1,0:T(8,128)(2,1)S(1)}, bf16[16,16,128]{2,1,0:T(8,128)(2,1)S(1)}, u32[]{:S(2)}, u32[]{:S(2)}) collective-permute-start(bf16[16,16,128]{2,1,0:T(8,128)(2,1)S(1)} %get-tuple-element.27), channel_id=1, source_target_pairs={{0,1},{1,0},{2,3},{3,2},{4,5},{5,4},{6,7},{7,6},{8,12},{9,13},{10,... | collective-permute-start | bytes 196616 | tf_op jit(solution)/shard_map/ppermute | solution.py:270
  7.7 4.4 %collective-permute-start.4 = (bf16[16,16,128]{2,1,0:T(8,128)(2,1)S(1)}, bf16[16,16,128]{2,1,0:T(8,128)(2,1)S(1)}, u32[]{:S(2)}, u32[]{:S(2)}) collective-permute-start(bf16[16,16,128]{2,1,0:T(8,128)(2,1)S(1)} %get-tuple-element.28), channel_id=1, source_target_pairs={{0,1},{1,0},{2,3},{3,2},{4,5},{5,4},{6,7},{7,6},{8,12},{9,13},{10,... | collective-permute-start | bytes 196616 | tf_op jit(solution)/shard_map/ppermute | solution.py:270
  10.0 4.4 %collective-permute-start.2 = (bf16[16,16,128]{2,1,0:T(8,128)(2,1)S(1)}, bf16[16,16,128]{2,1,0:T(8,128)(2,1)S(1)}, u32[]{:S(2)}, u32[]{:S(2)}) collective-permute-start(bf16[16,16,128]{2,1,0:T(8,128)(2,1)S(1)} %add_convert_fusion.7), channel_id=1, source_target_pairs={{0,2},{1,3},{2,0},{3,1},{4,6},{5,7},{6,4},{7,5},{8,9},{9,8},{10,11... | collective-permute-start | bytes 196616 | tf_op jit(solution)/shard_map/ppermute | solution.py:270
  12.2 5.3 %collective-permute-start.5 = (bf16[16,16,128]{2,1,0:T(8,128)(2,1)S(1)}, bf16[16,16,128]{2,1,0:T(8,128)(2,1)S(1)}, u32[]{:S(2)}, u32[]{:S(2)}) collective-permute-start(bf16[16,16,128]{2,1,0:T(8,128)(2,1)S(1)} %add_convert_fusion.5), channel_id=1, source_target_pairs={{0,2},{1,3},{2,0},{3,1},{4,6},{5,7},{6,4},{7,5},{8,9},{9,8},{10,11... | collective-permute-start | bytes 196616 | tf_op jit(solution)/shard_map/ppermute | solution.py:270
  14.5 5.4 %collective-permute-start.3 = (bf16[16,16,128]{2,1,0:T(8,128)(2,1)S(1)}, bf16[16,16,128]{2,1,0:T(8,128)(2,1)S(1)}, u32[]{:S(2)}, u32[]{:S(2)}) collective-permute-start(bf16[16,16,128]{2,1,0:T(8,128)(2,1)S(1)} %add_convert_fusion.6.sums0), channel_id=1, source_target_pairs={{0,4},{1,5},{2,6},{3,7},{4,0},{5,1},{6,2},{7,3},{8,10},{9,11},{10,... | collective-permute-start | bytes 196616 | tf_op jit(solution)/shard_map/ppermute | solution.py:270
  17.6 5.2 %collective-permute-start.6 = (bf16[16,16,128]{2,1,0:T(8,128)(2,1)S(1)}, bf16[16,16,128]{2,1,0:T(8,128)(2,1)S(1)}, u32[]{:S(2)}, u32[]{:S(2)}) collective-permute-start(bf16[16,16,128]{2,1,0:T(8,128)(2,1)S(1)} %add_convert_fusion.4.sums2), channel_id=1, source_target_pairs={{0,4},{1,5},{2,6},{3,7},{4,0},{5,1},{6,2},{7,3},{8,10},{9,11},{10,... | collective-permute-start | bytes 196616 | tf_op jit(solution)/shard_map/ppermute | solution.py:270
  24.1 1.3 %collective-permute-start.7 = (f32[9,8,128]{2,1,0:T(8,128)S(1)}, f32[9,8,128]{2,1,0:T(8,128)S(1)}, u32[]{:S(2)}, u32[]{:S(2)}) collective-permute-start(f32[9,8,128]{2,1,0:T(8,128)S(1)} %get-tuple-element.29.own), channel_id=1, source_target_pairs={{0,8},{8,0},{1,9},{9,1},{2,10},{10,2},{3,11},{11,3},{4,12},{12,4},... | collective-permute-start | bytes 110600 | tf_op jit(solution)/shard_map/ppermute | solution.py:259
  25.4 28.3 %copy-start.2 = (f32[8,512]{1,0:T(8,128)S(1)}, f32[8,512]{1,0:T(8,128)}, u32[]{:S(2)}) copy-start(f32[8,512]{1,0:T(8,128)} %x_in.1) | copy-start | bytes 49156
  25.4 28.3 %copy-start.3 = (f32[8,512]{1,0:T(8,128)S(1)}, f32[8,512]{1,0:T(8,128)}, u32[]{:S(2)}) copy-start(f32[8,512]{1,0:T(8,128)} %w_in.1) | copy-start | bytes 49156
  25.4 28.3 %copy-start.6 = (f32[8]{0:T(128)S(1)}, f32[8]{0:T(128)}, u32[]{:S(2)}) copy-start(f32[8]{0:T(128)} %phibar_in.1) | copy-start | bytes 100
  25.4 28.3 %copy-start.7 = (f32[8]{0:T(128)S(1)}, f32[8]{0:T(128)}, u32[]{:S(2)}) copy-start(f32[8]{0:T(128)} %rhobar_in.1) | copy-start | bytes 100
  27.2 4.4 %collective-permute-start.8 = (bf16[17,16,128]{2,1,0:T(8,128)(2,1)S(1)}, bf16[17,16,128]{2,1,0:T(8,128)(2,1)S(1)}, u32[]{:S(2)}, u32[]{:S(2)}) collective-permute-start(bf16[17,16,128]{2,1,0:T(8,128)(2,1)S(1)} %get-tuple-element.32), channel_id=1, source_target_pairs={{0,1},{1,0},{2,3},{3,2},{4,5},{5,4},{6,7},{7,6},{8,12},{9,13},{10,... | collective-permute-start | bytes 208904 | tf_op jit(solution)/shard_map/ppermute | solution.py:270
  28.8 4.5 %collective-permute-start.11 = (bf16[16,16,128]{2,1,0:T(8,128)(2,1)S(1)}, bf16[16,16,128]{2,1,0:T(8,128)(2,1)S(1)}, u32[]{:S(2)}, u32[]{:S(2)}) collective-permute-start(bf16[16,16,128]{2,1,0:T(8,128)(2,1)S(1)} %get-tuple-element.33), channel_id=1, source_target_pairs={{0,1},{1,0},{2,3},{3,2},{4,5},{5,4},{6,7},{7,6},{8,12},{9,13},{10,... | collective-permute-start | bytes 196616 | tf_op jit(solution)/shard_map/ppermute | solution.py:270
  31.6 4.4 %collective-permute-start.9 = (bf16[17,16,128]{2,1,0:T(8,128)(2,1)S(1)}, bf16[17,16,128]{2,1,0:T(8,128)(2,1)S(1)}, u32[]{:S(2)}, u32[]{:S(2)}) collective-permute-start(bf16[17,16,128]{2,1,0:T(8,128)(2,1)S(1)} %add_convert_fusion.1), channel_id=1, source_target_pairs={{0,2},{1,3},{2,0},{3,1},{4,6},{5,7},{6,4},{7,5},{8,9},{9,8},{10,11... | collective-permute-start | bytes 208904 | tf_op jit(solution)/shard_map/ppermute | solution.py:270
  33.3 4.6 %collective-permute-start.12 = (bf16[16,16,128]{2,1,0:T(8,128)(2,1)S(1)}, bf16[16,16,128]{2,1,0:T(8,128)(2,1)S(1)}, u32[]{:S(2)}, u32[]{:S(2)}) collective-permute-start(bf16[16,16,128]{2,1,0:T(8,128)(2,1)S(1)} %add_convert_fusion.3), channel_id=1, source_target_pairs={{0,2},{1,3},{2,0},{3,1},{4,6},{5,7},{6,4},{7,5},{8,9},{9,8},{10,11... | collective-permute-start | bytes 196616 | tf_op jit(solution)/shard_map/ppermute | solution.py:270
  36.0 7.4 %collective-permute-start.10 = (bf16[17,16,128]{2,1,0:T(8,128)(2,1)S(1)}, bf16[17,16,128]{2,1,0:T(8,128)(2,1)S(1)}, u32[]{:S(2)}, u32[]{:S(2)}) collective-permute-start(bf16[17,16,128]{2,1,0:T(8,128)(2,1)S(1)} %add_convert_fusion.sums0), channel_id=1, source_target_pairs={{0,4},{1,5},{2,6},{3,7},{4,0},{5,1},{6,2},{7,3},{8,10},{9,11},{10,... | collective-permute-start | bytes 208904 | tf_op jit(solution)/shard_map/ppermute | solution.py:270
  37.9 5.5 %collective-permute-start.13 = (bf16[16,16,128]{2,1,0:T(8,128)(2,1)S(1)}, bf16[16,16,128]{2,1,0:T(8,128)(2,1)S(1)}, u32[]{:S(2)}, u32[]{:S(2)}) collective-permute-start(bf16[16,16,128]{2,1,0:T(8,128)(2,1)S(1)} %add_convert_fusion.2.sums2), channel_id=1, source_target_pairs={{0,4},{1,5},{2,6},{3,7},{4,0},{5,1},{6,2},{7,3},{8,10},{9,11},{10,... | collective-permute-start | bytes 196616 | tf_op jit(solution)/shard_map/ppermute | solution.py:270
  44.8 1.3 %collective-permute-start.14 = (f32[9,8,128]{2,1,0:T(8,128)S(1)}, f32[9,8,128]{2,1,0:T(8,128)S(1)}, u32[]{:S(2)}, u32[]{:S(2)}) collective-permute-start(f32[9,8,128]{2,1,0:T(8,128)S(1)} %get-tuple-element.38.own), channel_id=1, source_target_pairs={{0,8},{8,0},{1,9},{9,1},{2,10},{10,2},{3,11},{11,3},{4,12},{12,4},... | collective-permute-start | bytes 110600 | tf_op jit(solution)/shard_map/ppermute | solution.py:259
  46.2 3.0 %collective-permute-start.15 = (f32[8,128]{1,0:T(8,128)S(1)}, f32[8,128]{1,0:T(8,128)S(1)}, u32[]{:S(2)}, u32[]{:S(2)}) collective-permute-start(f32[8,128]{1,0:T(8,128)S(1)} %get-tuple-element.41), channel_id=1, source_target_pairs={{0,9},{1,8},{2,11},{3,10},{4,13},{5,12},{6,15},{7,14},{8,1},{9,0},... | collective-permute-start | bytes 12296 | tf_op jit(solution)/shard_map/ppermute | solution.py:287
  49.3 3.0 %collective-permute-start.16 = (f32[8,128]{1,0:T(8,128)S(1)}, f32[8,128]{1,0:T(8,128)S(1)}, u32[]{:S(2)}, u32[]{:S(2)}) collective-permute-start(f32[8,128]{1,0:T(8,128)S(1)} %add.41), channel_id=1, source_target_pairs={{0,10},{1,11},{2,8},{3,9},{4,14},{5,15},{6,12},{7,13},{8,2},{9,3},... | collective-permute-start | bytes 12296 | tf_op jit(solution)/shard_map/ppermute | solution.py:287
  52.3 3.9 %collective-permute-start.17 = (f32[8,128]{1,0:T(8,128)S(1)}, f32[8,128]{1,0:T(8,128)S(1)}, u32[]{:S(2)}, u32[]{:S(2)}) collective-permute-start(f32[8,128]{1,0:T(8,128)S(1)} %add.42), channel_id=1, source_target_pairs={{0,12},{1,13},{2,14},{3,15},{4,8},{5,9},{6,10},{7,11},{8,4},{9,5},... | collective-permute-start | bytes 12296 | tf_op jit(solution)/shard_map/ppermute | solution.py:287

commit v9 on v8

--- a/solution.py
+++ b/solution.py
@@ -9,6 +9,7 @@
 
 ITERS = 2
 EPS = 1e-6
+CUT = 16
 F32 = jnp.float32
 BF16 = jnp.bfloat16
 SMEM = pl.BlockSpec(memory_space=pltpu.SMEM)
@@ -43,15 +44,19 @@
     return jnp.where(count > k, prod, 0.0)
 
 
-def forward(blk, rws, cls, cnt, v_ref, acc_ref):
+def forward(blk, rws, cls, cnt, v_ref, acc_ref, turned=False):
     count = jnp.broadcast_to(cnt[...], (8, 128))
     acc_ref[...] = jnp.zeros_like(acc_ref)
     for k in range(0, blk.shape[0], 2):
         pair = jnp.concatenate([v_ref[cls[0, 0, k]], v_ref[cls[0, 0, k + 1]]], axis=0)
-        a = blk[k : k + 2].reshape(256, 128)
-        prod = lax.dot_general(
-            pair.astype(BF16), a, (((1,), (1,)), ((), ())), preferred_element_type=F32
-        )
+        if turned:
+            a = jnp.concatenate([blk[k], blk[k + 1]], axis=1)
+            prod = jnp.dot(pair.astype(BF16), a, preferred_element_type=F32)
+        else:
+            a = blk[k : k + 2].reshape(256, 128)
+            prod = lax.dot_general(
+                pair.astype(BF16), a, (((1,), (1,)), ((), ())), preferred_element_type=F32
+            )
         acc_ref[rws[0, 0, k]] += used(count, k, prod[:8, :128])
         acc_ref[rws[0, 0, k + 1]] += used(count, k + 1, prod[8:, 128:])
 
@@ -91,11 +96,15 @@
     return lane_sum((totals[0] + totals[1]) + (totals[2] + totals[3]))
 
 
+def first_part(pairs):
+    return pairs * CUT // 32
+
+
 def store_pairs(acc_ref, outs):
-    half = acc_ref.shape[0] // 4
-    for b in range(2 * half):
+    cut = first_part(acc_ref.shape[0] // 2)
+    for b in range(acc_ref.shape[0] // 2):
         pair = jnp.concatenate([acc_ref[2 * b], acc_ref[2 * b + 1]], axis=0)
-        outs[b // half][b % half] = pair.astype(BF16)
+        outs[int(b >= cut)][b - cut * int(b >= cut)] = pair.astype(BF16)
 
 
 def place_halves(own, other, out_ref):
@@ -110,6 +119,11 @@
     copy = pltpu.make_async_copy(own_hbm, own, sem)
     copy.start()
     copy.wait()
+
+
+def turn(blk, out):
+    for k in range(blk.shape[0]):
+        out[k] = blk[k].T
 
 
 def first_forward(
@@ -131,10 +145,10 @@
 
 
 def pair_sums(pairs, a0, a1, b0, b1):
-    half = pairs // 2
+    cut = first_part(pairs)
     for b in range(pairs):
-        one, two = (a0, a1) if b < half else (b0, b1)
-        yield one[b % half].astype(F32) + two[b % half].astype(F32)
+        one, two, at = (a0, a1, b) if b < cut else (b0, b1, b - cut)
+        yield one[at].astype(F32) + two[at].astype(F32)
 
 
 def first_backward(rws_ref, cls_ref, cnt, blk, sums0, sums1, sums2, sums3, upd, message, rws, cls, sems, *accs):
@@ -168,10 +182,10 @@
     lanes = lax.broadcasted_iota(jnp.int32, (8, 128), 1)
     sq = jnp.where(lanes == lax.axis_index("col"), sq, 0.0)
     high = sq.astype(BF16).astype(F32)
-    out0[rays // 4] = jnp.concatenate([high, sq - high], axis=0).astype(BF16)
+    out0[out0.shape[0] - 1] = jnp.concatenate([high, sq - high], axis=0).astype(BF16)
     for c in copies:
         c.wait()
-    forward(blk, rws, cls, cnt, vupd, acc)
+    forward(blk, rws, cls, cnt, vupd, acc, turned=True)
     store_pairs(acc, (out0, out1))
 
 
@@ -183,7 +197,7 @@
 ):
     copies = lists((rws_ref, rws), (cls_ref, cls), sems=sems)
     blocks = upd.shape[0]
-    tail = sums0[blocks // 4].astype(F32) + sums1[blocks // 4].astype(F32)
+    tail = sums0[sums0.shape[0] - 1].astype(F32) + sums1[sums1.shape[0] - 1].astype(F32)
     alpha = jnp.sqrt(lane_sum(tail[:8] + tail[8:]) / total_cells + EPS)
     alpha_out[...] = alpha
     inv = 1.0 / alpha
@@ -259,13 +273,15 @@
     return lax.ppermute(x, "row", [(0, 1), (1, 0)])
 
 
-def column_sum(halves):
+def column_sum(halves, held=None):
     n = lax.axis_size("col")
     steps = [1 << i for i in range((n - 1).bit_length())]
     turned = steps[-1:] + steps[:-1]
     orders = ((steps, turned), (steps, turned))
     xs = list(halves)
     for i in range(len(steps)):
+        if held is not None and i == len(steps) - 1:
+            xs[1], held = lax.optimization_barrier((xs[1], held))
         ys = [
             lax.ppermute(
                 x,
@@ -275,7 +291,7 @@
             for x, (first, second) in zip(xs, orders)
         ]
         if i == len(steps) - 1:
-            return xs[0], ys[0], xs[1], ys[1]
+            return (xs[0], ys[0], xs[1], ys[1]), held
         xs = [(x.astype(F32) + y.astype(F32)).astype(BF16) for x, y in zip(xs, ys)]
 
 
@@ -318,14 +334,24 @@
     v_other = other_core(own)
     blk = blocks.reshape(blocks.shape[2:])
     operator = (*where, blk)
-    half_rays = shape(rays // 4, 16, 128, dtype=BF16)
+    cut = first_part(rays // 2)
+    rest = shape(rays // 2 - cut, 16, 128, dtype=BF16)
     *part, v0 = call(
         first_forward,
-        (half_rays, half_rays, shape(cells, 8, 128)),
+        (shape(cut, 16, 128, dtype=BF16), rest, shape(cells, 8, 128)),
         [VMEM] * 8,
         listed + [pltpu.SMEM(alpha.shape, F32), ray_acc],
     )(*operator, alpha, own, v_other, u_rays)
-    sums = column_sum(part)
+    sums, held = column_sum(part, blk)
+    turned = call(
+        turn,
+        shape(*blk.shape, dtype=BF16),
+        [VMEM],
+        (),
+        pl.CostEstimate(flops=10**6, bytes_accessed=4 * 10**6, transcendentals=0),
+    )(held)
+    blk, turned = lax.optimization_barrier((blk, turned))
+    operator = (*where, blk)
     upd1, message = call(
         first_backward,
         (shape(rays, 8, 128), shape(cells + 1, 8, 128)),
@@ -334,11 +360,11 @@
     )(*operator, *sums)
     *part, v1, beta1 = call(
         functools.partial(next_forward, total_rays),
-        (shape(rays // 4 + 1, 16, 128, dtype=BF16), half_rays, shape(cells, 8, 128), shape(8, 128)),
+        (shape(cut + 1, 16, 128, dtype=BF16), rest, shape(cells, 8, 128), shape(8, 128)),
         [VMEM] * 7,
         listed + [ray_acc],
-    )(*operator, message, other_core(message), v0)
-    sums = column_sum(part)
+    )(*where, turned, message, other_core(message), v0)
+    sums, _ = column_sum(part)
     message, u_piece, alpha1 = call(
         functools.partial(next_backward, total_cells, pieces),
         (shape(cells + 1, 8, 128), shape(pieces, 8, 128), shape(8, 128)),

time: 57.1 us -> 56.7 us (level)
  waiting for transfers between devices: 21.2 us -> 17.9 us
  Pallas kernels: 8.26 us -> 11.1 us
    ppermute x12, waiting for transfers between devices: 13.8 us -> 10.5 us  [column_sum(): lax.ppermute(x, ('row', 'col'), [(j, j ^ first[i]) for j in range(n)] + [...]
    pallas_call x2 -> x3, Pallas kernels: 3.64 us -> 6.51 us  [the longest x1 3.32 us: body(): call(turn, shape(*blk.shape, dtype=BF16), [VMEM], (), pl.CostEstimate(flo...]
  transfers between devices with their start and end apart: 18 -> 18, of which waited for: 14 -> 13; matrix products, arithmetic and copies ran while one was open for 0% -> 0% of each run, Pallas kernels for 2% -> 8%
where the time goes in v9:
time: 56.7 us; the launch traced here: 56.4 us
  starting transfers between devices  24.9 us (44%)
  waiting for transfers between devices  17.9 us (32%)
  Pallas kernels  11.1 us (20%)
  between operations  1.49 us (3%)
  local copies, waits for them, and re-layouts  0.9 us (2%)
    ppermute x12, starting transfers between devices, column_sum(): lax.ppermute(x, ('row', 'col'), [(j, j ^ first[i]) for j in range(n)] + [...  20.2 us
    ppermute x12, waiting for transfers between devices, column_sum(): lax.ppermute(x, ('row', 'col'), [(j, j ^ first[i]) for j in range(n)] + [...  10.5 us
    ppermute x3, waiting for transfers between devices, last_sum(): x = x + lax.ppermute(x, ('row', 'col'), pairs)  4.78 us
    ppermute x3, starting transfers between devices, last_sum(): x = x + lax.ppermute(x, ('row', 'col'), pairs)  4.01 us
    pallas_call x1, Pallas kernels, body(): call(turn, shape(*blk.shape, dtype=BF16), [VMEM], (), pl.CostEstimate(flo...  3.32 us
    ppermute x3, waiting for transfers between devices, other_core(): return lax.ppermute(x, 'row', [(0, 1), (1, 0)])  2.59 us
    pallas_call x1, Pallas kernels, body(): call(first_forward, (shape(cut, 16, 128, dtype=BF16), rest, shape(cells,...  1.83 us
    pallas_call x1, Pallas kernels, body(): call(functools.partial(next_backward, total_cells, pieces), (shape(cells...  1.4 us
  transfers between devices with their start and end apart: 18, of which 13 were waited for; matrix products, arithmetic and copies ran while one was open for 0% of the time, Pallas kernels for 8%

profile of v9, /device:TPU:0, one launch (start us, length us, event | category | flops | bytes accessed | tf_op | source)
XLA Modules:
  0.0 56.4 jit_solution(2804035289616060773)
XLA Ops:
  0.7 0.0 copy-start
  0.7 0.9 %copy-done.10 = f32[8,512]{1,0:T(8,128)S(1)} copy-done((f32[8,512]{1,0:T(8,128)S(1)}, f32[8,512]{1,0:T(8,128)}, u32[]{:S(2)}) %copy-start.10) | copy-done | bytes 16408
  1.6 0.5 collective-permute-start
  2.7 0.2 collective-permute-done.other
  2.9 0.0 copy-done.9
  3.0 1.8 %shard_map.147 = (bf16[16,16,128]{2,1,0:T(8,128)(2,1)S(1)}, bf16[16,16,128]{2,1,0:T(8,128)(2,1)S(1)}, f32[8,8,128]{2,1,0:T(8,128)S(1)}) custom-call(s32[1,1,128]{2,1,0:T(1,128)S(1)} %copy-done.5, s32[1,1,128]{2,1,0:T(1,128)S(1)} %copy-done.6, s32[1,1]{1,0:T(1,128)S(6)} %copy.16.cnt, bf16[128,128,128]{2,1,0:T(8,128)(2,1)S(1)} %bitcast.2, f32[8]{0:T(128)S(1)} %copy-done.9, ...), custom_call_target="tpu_custom_call" | custom-call | tf_op jit(solution)/shard_map/pallas_call | solution.py:339
  4.8 2.9 %collective-permute-start.1 = (bf16[16,16,128]{2,1,0:T(8,128)(2,1)S(1)}, bf16[16,16,128]{2,1,0:T(8,128)(2,1)S(1)}, u32[]{:S(2)}, u32[]{:S(2)}) collective-permute-start(bf16[16,16,128]{2,1,0:T(8,128)(2,1)S(1)} %get-tuple-element.31), channel_id=1, source_target_pairs={{0,1},{1,0},{2,3},{3,2},{4,5},{5,4},{6,7},{7,6},{8,12},{9,13},{10,... | collective-permute-start | bytes 196616 | tf_op jit(solution)/shard_map/ppermute | solution.py:286
  7.7 0.1 collective-permute-start.3
  7.8 2.2 %collective-permute-done.1 = bf16[16,16,128]{2,1,0:T(8,128)(2,1)S(1)} collective-permute-done((bf16[16,16,128]{2,1,0:T(8,128)(2,1)S(1)}, bf16[16,16,128]{2,1,0:T(8,128)(2,1)S(1)}, u32[]{:S(2)}, u32[]{:S(2)}) %collective-permute-start.1) | collective-permute-done | bytes 65568 | tf_op jit(solution)/shard_map/ppermute | solution.py:286
  10.0 2.2 %collective-permute-start.2 = (bf16[16,16,128]{2,1,0:T(8,128)(2,1)S(1)}, bf16[16,16,128]{2,1,0:T(8,128)(2,1)S(1)}, u32[]{:S(2)}, u32[]{:S(2)}) collective-permute-start(bf16[16,16,128]{2,1,0:T(8,128)(2,1)S(1)} %add_convert_fusion.7), channel_id=1, source_target_pairs={{0,2},{1,3},{2,0},{3,1},{4,6},{5,7},{6,4},{7,5},{8,9},{9,8},{10,11... | collective-permute-start | bytes 196616 | tf_op jit(solution)/shard_map/ppermute | solution.py:286
  12.2 0.0 collective-permute-done.3
  12.2 1.5 %collective-permute-start.4 = (bf16[16,16,128]{2,1,0:T(8,128)(2,1)S(1)}, bf16[16,16,128]{2,1,0:T(8,128)(2,1)S(1)}, u32[]{:S(2)}, u32[]{:S(2)}) collective-permute-start(bf16[16,16,128]{2,1,0:T(8,128)(2,1)S(1)} %add_convert_fusion.5), channel_id=1, source_target_pairs={{0,2},{1,3},{2,0},{3,1},{4,6},{5,7},{6,4},{7,5},{8,9},{9,8},{10,11... | collective-permute-start | bytes 196616 | tf_op jit(solution)/shard_map/ppermute | solution.py:286
  13.7 0.7 %collective-permute-done.2 = bf16[16,16,128]{2,1,0:T(8,128)(2,1)S(1)} collective-permute-done((bf16[16,16,128]{2,1,0:T(8,128)(2,1)S(1)}, bf16[16,16,128]{2,1,0:T(8,128)(2,1)S(1)}, u32[]{:S(2)}, u32[]{:S(2)}) %collective-permute-start.2) | collective-permute-done | bytes 65568 | tf_op jit(solution)/shard_map/ppermute | solution.py:286
  14.4 3.1 %collective-permute-start.6 = (bf16[16,16,128]{2,1,0:T(8,128)(2,1)S(1)}, bf16[16,16,128]{2,1,0:T(8,128)(2,1)S(1)}, u32[]{:S(2)}, u32[]{:S(2)}) collective-permute-start(bf16[16,16,128]{2,1,0:T(8,128)(2,1)S(1)} %add_convert_fusion.6.sums2), channel_id=1, source_target_pairs={{0,4},{1,5},{2,6},{3,7},{4,0},{5,1},{6,2},{7,3},{8,10},{9,11},{10,... | collective-permute-start | bytes 196616 | tf_op jit(solution)/shard_map/ppermute | solution.py:286
  17.5 0.0 collective-permute-done.4
  17.6 0.0 copy-start.1
  17.6 1.6 %collective-permute-start.5 = (bf16[16,16,128]{2,1,0:T(8,128)(2,1)S(1)}, bf16[16,16,128]{2,1,0:T(8,128)(2,1)S(1)}, u32[]{:S(2)}, u32[]{:S(2)}) collective-permute-start(bf16[16,16,128]{2,1,0:T(8,128)(2,1)S(1)} %add_convert_fusion.4.sums0), channel_id=1, source_target_pairs={{0,4},{1,5},{2,6},{3,7},{4,0},{5,1},{6,2},{7,3},{8,10},{9,11},{10,... | collective-permute-start | bytes 196616 | tf_op jit(solution)/shard_map/ppermute | solution.py:286
  19.2 3.3 %shard_map.148.blk = bf16[128,128,128]{2,1,0:T(8,128)(2,1)S(1)} custom-call(bf16[128,128,128]{2,1,0:T(8,128)(2,1)} %bitcast.1), custom_call_target="tpu_custom_call" | custom-call | flops 1000000 | bytes 4000000 | tf_op jit(solution)/shard_map/pallas_call | solution.py:346
  22.5 0.0 collective-permute-done.6.sums3
  22.6 0.3 collective-permute-done.5.sums1
  22.8 1.3 %shard_map.149 = (f32[64,8,128]{2,1,0:T(8,128)S(1)}, f32[9,8,128]{2,1,0:T(8,128)S(1)}) custom-call(s32[1,1,128]{2,1,0:T(1,128)S(1)} %copy-done.5, s32[1,1,128]{2,1,0:T(1,128)S(1)} %copy-done.6, s32[1,1]{1,0:T(1,128)S(6)} %copy.16.cnt, bf16[128,128,128]{2,1,0:T(8,128)(2,1)S(1)} %bitcast.3, bf16[16,16,128]{2,1,0:T(8,128)(2,1)S(1)} %add_convert_fusion.4.sums0, ...), custom_call_target="tpu_custom_call" | custom-call | tf_op jit(solution)/shard_map/pallas_call | solution.py:355
  24.1 0.1 collective-permute-start.7
  24.2 1.2 %collective-permute-done.7.other = f32[9,8,128]{2,1,0:T(8,128)S(1)} collective-permute-done((f32[9,8,128]{2,1,0:T(8,128)S(1)}, f32[9,8,128]{2,1,0:T(8,128)S(1)}, u32[]{:S(2)}, u32[]{:S(2)}) %collective-permute-start.7) | collective-permute-done | bytes 36896 | tf_op jit(solution)/shard_map/ppermute | solution.py:273
  25.4 1.4 %shard_map.150 = (bf16[17,16,128]{2,1,0:T(8,128)(2,1)S(1)}, bf16[16,16,128]{2,1,0:T(8,128)(2,1)S(1)}, f32[8,8,128]{2,1,0:T(8,128)S(1)}, f32[8,128]{1,0:T(8,128)S(1)}) custom-call(s32[1,1,128]{2,1,0:T(1,128)S(1)} %copy-done.5, s32[1,1,128]{2,1,0:T(1,128)S(1)} %copy-done.6, s32[1,1]{1,0:T(1,128)S(6)} %copy.16.cnt, bf16[128,128,128]{2,1,0:T(8,128)(2,1)S(1)} %shard_map.148.blk, ...), custom_call_target="tpu_custom_call" | custom-call | tf_op jit(solution)/shard_map/pallas_call | solution.py:361
  26.8 1.6 %collective-permute-start.8 = (bf16[17,16,128]{2,1,0:T(8,128)(2,1)S(1)}, bf16[17,16,128]{2,1,0:T(8,128)(2,1)S(1)}, u32[]{:S(2)}, u32[]{:S(2)}) collective-permute-start(bf16[17,16,128]{2,1,0:T(8,128)(2,1)S(1)} %get-tuple-element.40), channel_id=1, source_target_pairs={{0,1},{1,0},{2,3},{3,2},{4,5},{5,4},{6,7},{7,6},{8,12},{9,13},{10,... | collective-permute-start | bytes 208904 | tf_op jit(solution)/shard_map/ppermute | solution.py:286
  28.3 0.5 collective-permute-start.11
  28.9 2.3 %collective-permute-done.8 = bf16[17,16,128]{2,1,0:T(8,128)(2,1)S(1)} collective-permute-done((bf16[17,16,128]{2,1,0:T(8,128)(2,1)S(1)}, bf16[17,16,128]{2,1,0:T(8,128)(2,1)S(1)}, u32[]{:S(2)}, u32[]{:S(2)}) %collective-permute-start.8) | collective-permute-done | bytes 69664 | tf_op jit(solution)/shard_map/ppermute | solution.py:286
  31.2 1.6 %collective-permute-start.9 = (bf16[17,16,128]{2,1,0:T(8,128)(2,1)S(1)}, bf16[17,16,128]{2,1,0:T(8,128)(2,1)S(1)}, u32[]{:S(2)}, u32[]{:S(2)}) collective-permute-start(bf16[17,16,128]{2,1,0:T(8,128)(2,1)S(1)} %add_convert_fusion.1), channel_id=1, source_target_pairs={{0,2},{1,3},{2,0},{3,1},{4,6},{5,7},{6,4},{7,5},{8,9},{9,8},{10,11... | collective-permute-start | bytes 208904 | tf_op jit(solution)/shard_map/ppermute | solution.py:286
  32.8 0.0 collective-permute-done.11
  32.8 1.4 %collective-permute-start.12 = (bf16[16,16,128]{2,1,0:T(8,128)(2,1)S(1)}, bf16[16,16,128]{2,1,0:T(8,128)(2,1)S(1)}, u32[]{:S(2)}, u32[]{:S(2)}) collective-permute-start(bf16[16,16,128]{2,1,0:T(8,128)(2,1)S(1)} %add_convert_fusion.3), channel_id=1, source_target_pairs={{0,2},{1,3},{2,0},{3,1},{4,6},{5,7},{6,4},{7,5},{8,9},{9,8},{10,11... | collective-permute-start | bytes 196616 | tf_op jit(solution)/shard_map/ppermute | solution.py:286
  34.3 1.3 %collective-permute-done.9 = bf16[17,16,128]{2,1,0:T(8,128)(2,1)S(1)} collective-permute-done((bf16[17,16,128]{2,1,0:T(8,128)(2,1)S(1)}, bf16[17,16,128]{2,1,0:T(8,128)(2,1)S(1)}, u32[]{:S(2)}, u32[]{:S(2)}) %collective-permute-start.9) | collective-permute-done | bytes 69664 | tf_op jit(solution)/shard_map/ppermute | solution.py:286
  35.6 1.8 %collective-permute-start.10 = (bf16[17,16,128]{2,1,0:T(8,128)(2,1)S(1)}, bf16[17,16,128]{2,1,0:T(8,128)(2,1)S(1)}, u32[]{:S(2)}, u32[]{:S(2)}) collective-permute-start(bf16[17,16,128]{2,1,0:T(8,128)(2,1)S(1)} %add_convert_fusion.sums0), channel_id=1, source_target_pairs={{0,4},{1,5},{2,6},{3,7},{4,0},{5,1},{6,2},{7,3},{8,10},{9,11},{10,... | collective-permute-start | bytes 208904 | tf_op jit(solution)/shard_map/ppermute | solution.py:286
  37.3 0.1 collective-permute-done.12
  37.5 1.9 %collective-permute-start.13 = (bf16[16,16,128]{2,1,0:T(8,128)(2,1)S(1)}, bf16[16,16,128]{2,1,0:T(8,128)(2,1)S(1)}, u32[]{:S(2)}, u32[]{:S(2)}) collective-permute-start(bf16[16,16,128]{2,1,0:T(8,128)(2,1)S(1)} %add_convert_fusion.2.sums2), channel_id=1, source_target_pairs={{0,4},{1,5},{2,6},{3,7},{4,0},{5,1},{6,2},{7,3},{8,10},{9,11},{10,... | collective-permute-start | bytes 196616 | tf_op jit(solution)/shard_map/ppermute | solution.py:286
  39.4 3.6 %collective-permute-done.13.sums3 = bf16[16,16,128]{2,1,0:T(8,128)(2,1)S(1)} collective-permute-done((bf16[16,16,128]{2,1,0:T(8,128)(2,1)S(1)}, bf16[16,16,128]{2,1,0:T(8,128)(2,1)S(1)}, u32[]{:S(2)}, u32[]{:S(2)}) %collective-permute-start.13) | collective-permute-done | bytes 65568 | tf_op jit(solution)/shard_map/ppermute | solution.py:286
  43.0 0.0 collective-permute-done.10.sums1
  43.0 1.4 %shard_map.151 = (f32[9,8,128]{2,1,0:T(8,128)S(1)}, f32[8,8,128]{2,1,0:T(8,128)S(1)}, f32[8,128]{1,0:T(8,128)S(1)}) custom-call(s32[1,1,128]{2,1,0:T(1,128)S(1)} %copy-done.5, s32[1,1,128]{2,1,0:T(1,128)S(1)} %copy-done.6, s32[1,1]{1,0:T(1,128)S(6)} %copy.16.cnt, bf16[128,128,128]{2,1,0:T(8,128)(2,1)S(1)} %bitcast.4, ...), custom_call_target="tpu_custom_call" | custom-call | tf_op jit(solution)/shard_map/pallas_call | solution.py:368
  44.4 0.1 collective-permute-start.14
  44.5 1.2 %collective-permute-done.14.other = f32[9,8,128]{2,1,0:T(8,128)S(1)} collective-permute-done((f32[9,8,128]{2,1,0:T(8,128)S(1)}, f32[9,8,128]{2,1,0:T(8,128)S(1)}, u32[]{:S(2)}, u32[]{:S(2)}) %collective-permute-start.14) | collective-permute-done | bytes 36896 | tf_op jit(solution)/shard_map/ppermute | solution.py:273
  45.7 0.1 shard_map.152
  45.8 1.3 %collective-permute-start.15 = (f32[8,128]{1,0:T(8,128)S(1)}, f32[8,128]{1,0:T(8,128)S(1)}, u32[]{:S(2)}, u32[]{:S(2)}) collective-permute-start(f32[8,128]{1,0:T(8,128)S(1)} %get-tuple-element.49), channel_id=1, source_target_pairs={{0,9},{1,8},{2,11},{3,10},{4,13},{5,12},{6,15},{7,14},{8,1},{9,0},... | collective-permute-start | bytes 12296 | tf_op jit(solution)/shard_map/ppermute | solution.py:303
  47.1 1.8 %collective-permute-done.15 = f32[8,128]{1,0:T(8,128)S(1)} collective-permute-done((f32[8,128]{1,0:T(8,128)S(1)}, f32[8,128]{1,0:T(8,128)S(1)}, u32[]{:S(2)}, u32[]{:S(2)}) %collective-permute-start.15) | collective-permute-done | bytes 4128 | tf_op jit(solution)/shard_map/ppermute | solution.py:303
  48.8 1.3 %collective-permute-start.16 = (f32[8,128]{1,0:T(8,128)S(1)}, f32[8,128]{1,0:T(8,128)S(1)}, u32[]{:S(2)}, u32[]{:S(2)}) collective-permute-start(f32[8,128]{1,0:T(8,128)S(1)} %add.41), channel_id=1, source_target_pairs={{0,10},{1,11},{2,8},{3,9},{4,14},{5,15},{6,12},{7,13},{8,2},{9,3},... | collective-permute-start | bytes 12296 | tf_op jit(solution)/shard_map/ppermute | solution.py:303
  50.2 1.7 %collective-permute-done.16 = f32[8,128]{1,0:T(8,128)S(1)} collective-permute-done((f32[8,128]{1,0:T(8,128)S(1)}, f32[8,128]{1,0:T(8,128)S(1)}, u32[]{:S(2)}, u32[]{:S(2)}) %collective-permute-start.16) | collective-permute-done | bytes 4128 | tf_op jit(solution)/shard_map/ppermute | solution.py:303
  51.9 1.4 %collective-permute-start.17 = (f32[8,128]{1,0:T(8,128)S(1)}, f32[8,128]{1,0:T(8,128)S(1)}, u32[]{:S(2)}, u32[]{:S(2)}) collective-permute-start(f32[8,128]{1,0:T(8,128)S(1)} %add.42), channel_id=1, source_target_pairs={{0,12},{1,13},{2,14},{3,15},{4,8},{5,9},{6,10},{7,11},{8,4},{9,5},... | collective-permute-start | bytes 12296 | tf_op jit(solution)/shard_map/ppermute | solution.py:303
  53.3 1.2 %shard_map.153 = (f32[8,1024]{1,0:T(8,128)}, f32[8,512]{1,0:T(8,128)}, f32[8,512]{1,0:T(8,128)S(1)}, f32[3,8,128]{2,1,0:T(8,128)S(1)}) custom-call(f32[8]{0:T(128)S(1)} %copy-done.7, f32[8]{0:T(128)S(1)} %copy-done.8, f32[8,8,128]{2,1,0:T(8,128)S(1)} %get-tuple-element.39.v_old.v1, f32[8,8,128]{2,1,0:T(8,128)S(1)} %get-tuple-element.44.u_piece, ...), custom_call_target="tpu_custom_call" | custom-call | flops 1000000 | bytes 3000000 | tf_op jit(solution)/shard_map/pallas_call | solution.py:381
  54.5 1.3 %collective-permute-done.17 = f32[8,128]{1,0:T(8,128)S(1)} collective-permute-done((f32[8,128]{1,0:T(8,128)S(1)}, f32[8,128]{1,0:T(8,128)S(1)}, u32[]{:S(2)}, u32[]{:S(2)}) %collective-permute-start.17) | collective-permute-done | bytes 4128 | tf_op jit(solution)/shard_map/ppermute | solution.py:303
  55.8 0.6 %shard_map.154 = (f32[8,512]{1,0:T(8,128)}, f32[8,512]{1,0:T(8,128)}, f32[3,8]{1,0:T(4,128)}) custom-call(f32[8,128]{1,0:T(8,128)S(1)} %add.43.sq, f32[8,8,128]{2,1,0:T(8,128)S(1)} %get-tuple-element.50.v2, f32[8,512]{1,0:T(8,128)S(1)} %get-tuple-element.51.w_mid, f32[3,8,128]{2,1,0:T(8,128)S(1)} %get-tuple-element.52.factors), custom_call_target="tpu_custom_call" | custom-call | tf_op jit(solution)/shard_map/pallas_call | solution.py:388
  (30 shorter events, 0.2 us)
Async XLA Ops:
  0.6 2.3 %copy-start.6 = (s32[1,1,128]{2,1,0:T(1,128)S(1)}, s32[1,1,128]{2,1,0:T(1,128)}, u32[]{:S(2)}) copy-start(s32[1,1,128]{2,1,0:T(1,128)} %cls_ref.7) | copy-start | bytes 1540
  0.6 2.3 %copy-start.5 = (s32[1,1,128]{2,1,0:T(1,128)S(1)}, s32[1,1,128]{2,1,0:T(1,128)}, u32[]{:S(2)}) copy-start(s32[1,1,128]{2,1,0:T(1,128)} %rws_ref.7) | copy-start | bytes 1540
  0.7 2.3 %copy-start.9 = (f32[8]{0:T(128)S(1)}, f32[8]{0:T(128)}, u32[]{:S(2)}) copy-start(f32[8]{0:T(128)} %alpha_ref.1) | copy-start | bytes 100
  0.7 2.3 %copy-start.2 = (f32[8,1024]{1,0:T(8,128)S(1)}, f32[8,1024]{1,0:T(8,128)}, u32[]{:S(2)}) copy-start(f32[8,1024]{1,0:T(8,128)} %u_piece.1) | copy-start | bytes 98308
  0.7 2.3 %copy-start = (bf16[1,1,128,128,128]{4,3,2,1,0:T(8,128)(2,1)S(1)}, bf16[1,1,128,128,128]{4,3,2,1,0:T(8,128)(2,1)}, u32[]{:S(2)}) copy-start(bf16[1,1,128,128,128]{4,3,2,1,0:T(8,128)(2,1)} %param.11) | copy-start | bytes 12582916
  0.7 0.9 %copy-start.10 = (f32[8,512]{1,0:T(8,128)S(1)}, f32[8,512]{1,0:T(8,128)}, u32[]{:S(2)}) copy-start(f32[8,512]{1,0:T(8,128)} %own_hbm.1) | copy-start | bytes 49156
  1.6 1.4 %collective-permute-start = (f32[8,512]{1,0:T(8,128)S(1)}, f32[8,512]{1,0:T(8,128)S(1)}, u32[]{:S(2)}, u32[]{:S(2)}) collective-permute-start(f32[8,512]{1,0:T(8,128)S(1)} %shard_map.146.own), channel_id=1, source_target_pairs={{0,8},{8,0},{1,9},{9,1},{2,10},{10,2},{3,11},{11,3},{4,12},{12,4},... | collective-permute-start | bytes 49160 | tf_op jit(solution)/shard_map/ppermute | solution.py:273
  4.8 5.2 %collective-permute-start.1 = (bf16[16,16,128]{2,1,0:T(8,128)(2,1)S(1)}, bf16[16,16,128]{2,1,0:T(8,128)(2,1)S(1)}, u32[]{:S(2)}, u32[]{:S(2)}) collective-permute-start(bf16[16,16,128]{2,1,0:T(8,128)(2,1)S(1)} %get-tuple-element.31), channel_id=1, source_target_pairs={{0,1},{1,0},{2,3},{3,2},{4,5},{5,4},{6,7},{7,6},{8,12},{9,13},{10,... | collective-permute-start | bytes 196616 | tf_op jit(solution)/shard_map/ppermute | solution.py:286
  7.7 4.4 %collective-permute-start.3 = (bf16[16,16,128]{2,1,0:T(8,128)(2,1)S(1)}, bf16[16,16,128]{2,1,0:T(8,128)(2,1)S(1)}, u32[]{:S(2)}, u32[]{:S(2)}) collective-permute-start(bf16[16,16,128]{2,1,0:T(8,128)(2,1)S(1)} %get-tuple-element.35), channel_id=1, source_target_pairs={{0,1},{1,0},{2,3},{3,2},{4,5},{5,4},{6,7},{7,6},{8,12},{9,13},{10,... | collective-permute-start | bytes 196616 | tf_op jit(solution)/shard_map/ppermute | solution.py:286
  10.0 4.4 %collective-permute-start.2 = (bf16[16,16,128]{2,1,0:T(8,128)(2,1)S(1)}, bf16[16,16,128]{2,1,0:T(8,128)(2,1)S(1)}, u32[]{:S(2)}, u32[]{:S(2)}) collective-permute-start(bf16[16,16,128]{2,1,0:T(8,128)(2,1)S(1)} %add_convert_fusion.7), channel_id=1, source_target_pairs={{0,2},{1,3},{2,0},{3,1},{4,6},{5,7},{6,4},{7,5},{8,9},{9,8},{10,11... | collective-permute-start | bytes 196616 | tf_op jit(solution)/shard_map/ppermute | solution.py:286
  12.2 5.3 %collective-permute-start.4 = (bf16[16,16,128]{2,1,0:T(8,128)(2,1)S(1)}, bf16[16,16,128]{2,1,0:T(8,128)(2,1)S(1)}, u32[]{:S(2)}, u32[]{:S(2)}) collective-permute-start(bf16[16,16,128]{2,1,0:T(8,128)(2,1)S(1)} %add_convert_fusion.5), channel_id=1, source_target_pairs={{0,2},{1,3},{2,0},{3,1},{4,6},{5,7},{6,4},{7,5},{8,9},{9,8},{10,11... | collective-permute-start | bytes 196616 | tf_op jit(solution)/shard_map/ppermute | solution.py:286
  14.4 8.1 %collective-permute-start.6 = (bf16[16,16,128]{2,1,0:T(8,128)(2,1)S(1)}, bf16[16,16,128]{2,1,0:T(8,128)(2,1)S(1)}, u32[]{:S(2)}, u32[]{:S(2)}) collective-permute-start(bf16[16,16,128]{2,1,0:T(8,128)(2,1)S(1)} %add_convert_fusion.6.sums2), channel_id=1, source_target_pairs={{0,4},{1,5},{2,6},{3,7},{4,0},{5,1},{6,2},{7,3},{8,10},{9,11},{10,... | collective-permute-start | bytes 196616 | tf_op jit(solution)/shard_map/ppermute | solution.py:286
  17.6 5.2 %copy-start.1 = (bf16[1,1,128,128,128]{4,3,2,1,0:T(8,128)(2,1)S(1)}, bf16[1,1,128,128,128]{4,3,2,1,0:T(8,128)(2,1)}, u32[]{:S(2)}) copy-start(bf16[1,1,128,128,128]{4,3,2,1,0:T(8,128)(2,1)} %param.11) | copy-start | bytes 12582916
  17.6 5.2 %collective-permute-start.5 = (bf16[16,16,128]{2,1,0:T(8,128)(2,1)S(1)}, bf16[16,16,128]{2,1,0:T(8,128)(2,1)S(1)}, u32[]{:S(2)}, u32[]{:S(2)}) collective-permute-start(bf16[16,16,128]{2,1,0:T(8,128)(2,1)S(1)} %add_convert_fusion.4.sums0), channel_id=1, source_target_pairs={{0,4},{1,5},{2,6},{3,7},{4,0},{5,1},{6,2},{7,3},{8,10},{9,11},{10,... | collective-permute-start | bytes 196616 | tf_op jit(solution)/shard_map/ppermute | solution.py:286
  24.1 1.3 %collective-permute-start.7 = (f32[9,8,128]{2,1,0:T(8,128)S(1)}, f32[9,8,128]{2,1,0:T(8,128)S(1)}, u32[]{:S(2)}, u32[]{:S(2)}) collective-permute-start(f32[9,8,128]{2,1,0:T(8,128)S(1)} %get-tuple-element.37.own), channel_id=1, source_target_pairs={{0,8},{8,0},{1,9},{9,1},{2,10},{10,2},{3,11},{11,3},{4,12},{12,4},... | collective-permute-start | bytes 110600 | tf_op jit(solution)/shard_map/ppermute | solution.py:273
  25.4 27.9 %copy-start.3 = (f32[8,512]{1,0:T(8,128)S(1)}, f32[8,512]{1,0:T(8,128)}, u32[]{:S(2)}) copy-start(f32[8,512]{1,0:T(8,128)} %x_in.1) | copy-start | bytes 49156
  25.4 27.9 %copy-start.4 = (f32[8,512]{1,0:T(8,128)S(1)}, f32[8,512]{1,0:T(8,128)}, u32[]{:S(2)}) copy-start(f32[8,512]{1,0:T(8,128)} %w_in.1) | copy-start | bytes 49156
  25.4 27.9 %copy-start.7 = (f32[8]{0:T(128)S(1)}, f32[8]{0:T(128)}, u32[]{:S(2)}) copy-start(f32[8]{0:T(128)} %phibar_in.1) | copy-start | bytes 100
  25.4 27.9 %copy-start.8 = (f32[8]{0:T(128)S(1)}, f32[8]{0:T(128)}, u32[]{:S(2)}) copy-start(f32[8]{0:T(128)} %rhobar_in.1) | copy-start | bytes 100
  26.8 4.4 %collective-permute-start.8 = (bf16[17,16,128]{2,1,0:T(8,128)(2,1)S(1)}, bf16[17,16,128]{2,1,0:T(8,128)(2,1)S(1)}, u32[]{:S(2)}, u32[]{:S(2)}) collective-permute-start(bf16[17,16,128]{2,1,0:T(8,128)(2,1)S(1)} %get-tuple-element.40), channel_id=1, source_target_pairs={{0,1},{1,0},{2,3},{3,2},{4,5},{5,4},{6,7},{7,6},{8,12},{9,13},{10,... | collective-permute-start | bytes 208904 | tf_op jit(solution)/shard_map/ppermute | solution.py:286
  28.3 4.5 %collective-permute-start.11 = (bf16[16,16,128]{2,1,0:T(8,128)(2,1)S(1)}, bf16[16,16,128]{2,1,0:T(8,128)(2,1)S(1)}, u32[]{:S(2)}, u32[]{:S(2)}) collective-permute-start(bf16[16,16,128]{2,1,0:T(8,128)(2,1)S(1)} %get-tuple-element.41), channel_id=1, source_target_pairs={{0,1},{1,0},{2,3},{3,2},{4,5},{5,4},{6,7},{7,6},{8,12},{9,13},{10,... | collective-permute-start | bytes 196616 | tf_op jit(solution)/shard_map/ppermute | solution.py:286
  31.2 4.4 %collective-permute-start.9 = (bf16[17,16,128]{2,1,0:T(8,128)(2,1)S(1)}, bf16[17,16,128]{2,1,0:T(8,128)(2,1)S(1)}, u32[]{:S(2)}, u32[]{:S(2)}) collective-permute-start(bf16[17,16,128]{2,1,0:T(8,128)(2,1)S(1)} %add_convert_fusion.1), channel_id=1, source_target_pairs={{0,2},{1,3},{2,0},{3,1},{4,6},{5,7},{6,4},{7,5},{8,9},{9,8},{10,11... | collective-permute-start | bytes 208904 | tf_op jit(solution)/shard_map/ppermute | solution.py:286
  32.8 4.6 %collective-permute-start.12 = (bf16[16,16,128]{2,1,0:T(8,128)(2,1)S(1)}, bf16[16,16,128]{2,1,0:T(8,128)(2,1)S(1)}, u32[]{:S(2)}, u32[]{:S(2)}) collective-permute-start(bf16[16,16,128]{2,1,0:T(8,128)(2,1)S(1)} %add_convert_fusion.3), channel_id=1, source_target_pairs={{0,2},{1,3},{2,0},{3,1},{4,6},{5,7},{6,4},{7,5},{8,9},{9,8},{10,11... | collective-permute-start | bytes 196616 | tf_op jit(solution)/shard_map/ppermute | solution.py:286
  35.6 7.4 %collective-permute-start.10 = (bf16[17,16,128]{2,1,0:T(8,128)(2,1)S(1)}, bf16[17,16,128]{2,1,0:T(8,128)(2,1)S(1)}, u32[]{:S(2)}, u32[]{:S(2)}) collective-permute-start(bf16[17,16,128]{2,1,0:T(8,128)(2,1)S(1)} %add_convert_fusion.sums0), channel_id=1, source_target_pairs={{0,4},{1,5},{2,6},{3,7},{4,0},{5,1},{6,2},{7,3},{8,10},{9,11},{10,... | collective-permute-start | bytes 208904 | tf_op jit(solution)/shard_map/ppermute | solution.py:286
  37.5 5.5 %collective-permute-start.13 = (bf16[16,16,128]{2,1,0:T(8,128)(2,1)S(1)}, bf16[16,16,128]{2,1,0:T(8,128)(2,1)S(1)}, u32[]{:S(2)}, u32[]{:S(2)}) collective-permute-start(bf16[16,16,128]{2,1,0:T(8,128)(2,1)S(1)} %add_convert_fusion.2.sums2), channel_id=1, source_target_pairs={{0,4},{1,5},{2,6},{3,7},{4,0},{5,1},{6,2},{7,3},{8,10},{9,11},{10,... | collective-permute-start | bytes 196616 | tf_op jit(solution)/shard_map/ppermute | solution.py:286
  44.4 1.3 %collective-permute-start.14 = (f32[9,8,128]{2,1,0:T(8,128)S(1)}, f32[9,8,128]{2,1,0:T(8,128)S(1)}, u32[]{:S(2)}, u32[]{:S(2)}) collective-permute-start(f32[9,8,128]{2,1,0:T(8,128)S(1)} %get-tuple-element.46.own), channel_id=1, source_target_pairs={{0,8},{8,0},{1,9},{9,1},{2,10},{10,2},{3,11},{11,3},{4,12},{12,4},... | collective-permute-start | bytes 110600 | tf_op jit(solution)/shard_map/ppermute | solution.py:273
  45.8 3.0 %collective-permute-start.15 = (f32[8,128]{1,0:T(8,128)S(1)}, f32[8,128]{1,0:T(8,128)S(1)}, u32[]{:S(2)}, u32[]{:S(2)}) collective-permute-start(f32[8,128]{1,0:T(8,128)S(1)} %get-tuple-element.49), channel_id=1, source_target_pairs={{0,9},{1,8},{2,11},{3,10},{4,13},{5,12},{6,15},{7,14},{8,1},{9,0},... | collective-permute-start | bytes 12296 | tf_op jit(solution)/shard_map/ppermute | solution.py:303
  48.8 3.0 %collective-permute-start.16 = (f32[8,128]{1,0:T(8,128)S(1)}, f32[8,128]{1,0:T(8,128)S(1)}, u32[]{:S(2)}, u32[]{:S(2)}) collective-permute-start(f32[8,128]{1,0:T(8,128)S(1)} %add.41), channel_id=1, source_target_pairs={{0,10},{1,11},{2,8},{3,9},{4,14},{5,15},{6,12},{7,13},{8,2},{9,3},... | collective-permute-start | bytes 12296 | tf_op jit(solution)/shard_map/ppermute | solution.py:303
  51.9 3.9 %collective-permute-start.17 = (f32[8,128]{1,0:T(8,128)S(1)}, f32[8,128]{1,0:T(8,128)S(1)}, u32[]{:S(2)}, u32[]{:S(2)}) collective-permute-start(f32[8,128]{1,0:T(8,128)S(1)} %add.42), channel_id=1, source_target_pairs={{0,12},{1,13},{2,14},{3,15},{4,8},{5,9},{6,10},{7,11},{8,4},{9,5},... | collective-permute-start | bytes 12296 | tf_op jit(solution)/shard_map/ppermute | solution.py:303

commit v10 on v8

--- a/solution.py
+++ b/solution.py
@@ -262,8 +262,11 @@
 def column_sum(halves):
     n = lax.axis_size("col")
     steps = [1 << i for i in range((n - 1).bit_length())]
-    turned = steps[-1:] + steps[:-1]
-    orders = ((steps, turned), (steps, turned))
+    back = steps[::-1]
+    orders = (
+        (steps[1::-1] + steps[2:], back),
+        (steps[:-2] + back[:2], back),
+    )
     xs = list(halves)
     for i in range(len(steps)):
         ys = [

time: 57.1 us -> 56.5 us (0.989)
  waiting for transfers between devices: 21.2 us -> 16.6 us
  starting transfers between devices: 24.9 us -> 28.8 us
    ppermute x12, waiting for transfers between devices: 13.8 us -> 10.2 us  [column_sum(): lax.ppermute(x, ('row', 'col'), [(j, j ^ first[i]) for j in range(n)] + [...]
    ppermute x12, starting transfers between devices: 20.2 us -> 23.2 us  [column_sum(): lax.ppermute(x, ('row', 'col'), [(j, j ^ first[i]) for j in range(n)] + [...]
    ppermute x3, starting transfers between devices: 4 us -> 4.96 us  [last_sum(): x = x + lax.ppermute(x, ('row', 'col'), pairs)]
    ppermute x3, waiting for transfers between devices: 4.79 us -> 3.88 us  [last_sum(): x = x + lax.ppermute(x, ('row', 'col'), pairs)]
  transfers between devices with their start and end apart: 18 -> 18, of which waited for: 14 -> 15; matrix products, arithmetic and copies ran while one was open for 0% -> 0% of each run, Pallas kernels for 2% -> 2%
where the time goes in v10:
time: 56.5 us; the launch traced here: 56.3 us
  starting transfers between devices  28.8 us (51%)
  waiting for transfers between devices  16.6 us (29%)
  Pallas kernels  8.28 us (15%)
  between operations  1.46 us (3%)
  local copies, waits for them, and re-layouts  0.9 us (2%)
    ppermute x12, starting transfers between devices, column_sum(): lax.ppermute(x, ('row', 'col'), [(j, j ^ first[i]) for j in range(n)] + [...  23.2 us
    ppermute x12, waiting for transfers between devices, column_sum(): lax.ppermute(x, ('row', 'col'), [(j, j ^ first[i]) for j in range(n)] + [...  10.2 us
    ppermute x3, starting transfers between devices, last_sum(): x = x + lax.ppermute(x, ('row', 'col'), pairs)  4.96 us
    ppermute x3, waiting for transfers between devices, last_sum(): x = x + lax.ppermute(x, ('row', 'col'), pairs)  3.88 us
    ppermute x3, waiting for transfers between devices, other_core(): return lax.ppermute(x, 'row', [(0, 1), (1, 0)])  2.59 us
    pallas_call x1, Pallas kernels, body(): call(first_forward, (half_rays, half_rays, shape(cells, 8, 128)), [VMEM]...  1.83 us
    pallas_call x1, Pallas kernels, body(): call(functools.partial(next_forward, total_rays), (shape(rays // 4 + 1, 1...  1.82 us
    pallas_call x1, Pallas kernels, body(): call(functools.partial(next_backward, total_cells, pieces), (shape(cells...  1.4 us
  transfers between devices with their start and end apart: 18, of which 15 were waited for; matrix products, arithmetic and copies ran while one was open for 0% of the time, Pallas kernels for 2%

profile of v10, /device:TPU:0, one launch (start us, length us, event | category | flops | bytes accessed | tf_op | source)
XLA Modules:
  0.0 56.3 jit_solution(9688802350281697432)
XLA Ops:
  0.6 0.0 copy-start.5
  0.6 0.0 copy-start.4
  0.7 0.0 copy-start.8
  0.7 0.0 copy-start.1
  0.7 0.9 %copy-done.9 = f32[8,512]{1,0:T(8,128)S(1)} copy-done((f32[8,512]{1,0:T(8,128)S(1)}, f32[8,512]{1,0:T(8,128)}, u32[]{:S(2)}) %copy-start.9) | copy-done | bytes 16408
  1.6 0.5 collective-permute-start
  2.7 0.2 collective-permute-done.other
  3.0 1.8 %shard_map.147 = (bf16[16,16,128]{2,1,0:T(8,128)(2,1)S(1)}, bf16[16,16,128]{2,1,0:T(8,128)(2,1)S(1)}, f32[8,8,128]{2,1,0:T(8,128)S(1)}) custom-call(s32[1,1,128]{2,1,0:T(1,128)S(1)} %copy-done.4, s32[1,1,128]{2,1,0:T(1,128)S(1)} %copy-done.5, s32[1,1]{1,0:T(1,128)S(6)} %copy.16.cnt, bf16[128,128,128]{2,1,0:T(8,128)(2,1)S(1)} %bitcast.1, f32[8]{0:T(128)S(1)} %copy-done.8, ...), custom_call_target="tpu_custom_call" | custom-call | tf_op jit(solution)/shard_map/pallas_call | solution.py:325
  4.8 3.0 %collective-permute-start.1 = (bf16[16,16,128]{2,1,0:T(8,128)(2,1)S(1)}, bf16[16,16,128]{2,1,0:T(8,128)(2,1)S(1)}, u32[]{:S(2)}, u32[]{:S(2)}) collective-permute-start(bf16[16,16,128]{2,1,0:T(8,128)(2,1)S(1)} %get-tuple-element.27), channel_id=1, source_target_pairs={{0,2},{1,3},{2,0},{3,1},{4,6},{5,7},{6,4},{7,5},{8,12},{9,13},{10,... | collective-permute-start | bytes 196616 | tf_op jit(solution)/shard_map/ppermute | solution.py:273
  7.8 1.5 %collective-permute-start.4 = (bf16[16,16,128]{2,1,0:T(8,128)(2,1)S(1)}, bf16[16,16,128]{2,1,0:T(8,128)(2,1)S(1)}, u32[]{:S(2)}, u32[]{:S(2)}) collective-permute-start(bf16[16,16,128]{2,1,0:T(8,128)(2,1)S(1)} %get-tuple-element.28), channel_id=1, source_target_pairs={{0,1},{1,0},{2,3},{3,2},{4,5},{5,4},{6,7},{7,6},{8,12},{9,13},{10,... | collective-permute-start | bytes 196616 | tf_op jit(solution)/shard_map/ppermute | solution.py:273
  9.3 1.4 %collective-permute-done.1 = bf16[16,16,128]{2,1,0:T(8,128)(2,1)S(1)} collective-permute-done((bf16[16,16,128]{2,1,0:T(8,128)(2,1)S(1)}, bf16[16,16,128]{2,1,0:T(8,128)(2,1)S(1)}, u32[]{:S(2)}, u32[]{:S(2)}) %collective-permute-start.1) | collective-permute-done | bytes 65568 | tf_op jit(solution)/shard_map/ppermute | solution.py:273
  10.8 2.0 %collective-permute-start.2 = (bf16[16,16,128]{2,1,0:T(8,128)(2,1)S(1)}, bf16[16,16,128]{2,1,0:T(8,128)(2,1)S(1)}, u32[]{:S(2)}, u32[]{:S(2)}) collective-permute-start(bf16[16,16,128]{2,1,0:T(8,128)(2,1)S(1)} %add_convert_fusion.7), channel_id=1, source_target_pairs={{0,1},{1,0},{2,3},{3,2},{4,5},{5,4},{6,7},{7,6},{8,10},{9,11},{10,... | collective-permute-start | bytes 196616 | tf_op jit(solution)/shard_map/ppermute | solution.py:273
  12.8 0.0 collective-permute-done.4
  12.8 1.9 %collective-permute-start.5 = (bf16[16,16,128]{2,1,0:T(8,128)(2,1)S(1)}, bf16[16,16,128]{2,1,0:T(8,128)(2,1)S(1)}, u32[]{:S(2)}, u32[]{:S(2)}) collective-permute-start(bf16[16,16,128]{2,1,0:T(8,128)(2,1)S(1)} %add_convert_fusion.5), channel_id=1, source_target_pairs={{0,4},{1,5},{2,6},{3,7},{4,0},{5,1},{6,2},{7,3},{8,10},{9,11},{10,... | collective-permute-start | bytes 196616 | tf_op jit(solution)/shard_map/ppermute | solution.py:273
  14.8 0.3 collective-permute-done.2
  15.2 2.4 %collective-permute-start.3 = (bf16[16,16,128]{2,1,0:T(8,128)(2,1)S(1)}, bf16[16,16,128]{2,1,0:T(8,128)(2,1)S(1)}, u32[]{:S(2)}, u32[]{:S(2)}) collective-permute-start(bf16[16,16,128]{2,1,0:T(8,128)(2,1)S(1)} %add_convert_fusion.6.sums0), channel_id=1, source_target_pairs={{0,4},{1,5},{2,6},{3,7},{4,0},{5,1},{6,2},{7,3},{8,9},{9,8},{10,11... | collective-permute-start | bytes 196616 | tf_op jit(solution)/shard_map/ppermute | solution.py:273
  17.6 0.5 collective-permute-done.5
  18.1 1.8 %collective-permute-start.6 = (bf16[16,16,128]{2,1,0:T(8,128)(2,1)S(1)}, bf16[16,16,128]{2,1,0:T(8,128)(2,1)S(1)}, u32[]{:S(2)}, u32[]{:S(2)}) collective-permute-start(bf16[16,16,128]{2,1,0:T(8,128)(2,1)S(1)} %add_convert_fusion.4.sums2), channel_id=1, source_target_pairs={{0,2},{1,3},{2,0},{3,1},{4,6},{5,7},{6,4},{7,5},{8,9},{9,8},{10,11... | collective-permute-start | bytes 196616 | tf_op jit(solution)/shard_map/ppermute | solution.py:273
  19.9 0.5 collective-permute-done.3.sums1
  20.4 2.0 %collective-permute-done.6.sums3 = bf16[16,16,128]{2,1,0:T(8,128)(2,1)S(1)} collective-permute-done((bf16[16,16,128]{2,1,0:T(8,128)(2,1)S(1)}, bf16[16,16,128]{2,1,0:T(8,128)(2,1)S(1)}, u32[]{:S(2)}, u32[]{:S(2)}) %collective-permute-start.6) | collective-permute-done | bytes 65568 | tf_op jit(solution)/shard_map/ppermute | solution.py:273
  22.4 1.3 %shard_map.148 = (f32[64,8,128]{2,1,0:T(8,128)S(1)}, f32[9,8,128]{2,1,0:T(8,128)S(1)}) custom-call(s32[1,1,128]{2,1,0:T(1,128)S(1)} %copy-done.4, s32[1,1,128]{2,1,0:T(1,128)S(1)} %copy-done.5, s32[1,1]{1,0:T(1,128)S(6)} %copy.16.cnt, bf16[128,128,128]{2,1,0:T(8,128)(2,1)S(1)} %bitcast.2, bf16[16,16,128]{2,1,0:T(8,128)(2,1)S(1)} %add_convert_fusion.6.sums0, ...), custom_call_target="tpu_custom_call" | custom-call | tf_op jit(solution)/shard_map/pallas_call | solution.py:332
  23.7 0.1 collective-permute-start.7
  23.8 1.2 %collective-permute-done.7.other = f32[9,8,128]{2,1,0:T(8,128)S(1)} collective-permute-done((f32[9,8,128]{2,1,0:T(8,128)S(1)}, f32[9,8,128]{2,1,0:T(8,128)S(1)}, u32[]{:S(2)}, u32[]{:S(2)}) %collective-permute-start.7) | collective-permute-done | bytes 36896 | tf_op jit(solution)/shard_map/ppermute | solution.py:259
  25.0 1.8 %shard_map.149 = (bf16[17,16,128]{2,1,0:T(8,128)(2,1)S(1)}, bf16[16,16,128]{2,1,0:T(8,128)(2,1)S(1)}, f32[8,8,128]{2,1,0:T(8,128)S(1)}, f32[8,128]{1,0:T(8,128)S(1)}) custom-call(s32[1,1,128]{2,1,0:T(1,128)S(1)} %copy-done.4, s32[1,1,128]{2,1,0:T(1,128)S(1)} %copy-done.5, s32[1,1]{1,0:T(1,128)S(6)} %copy.16.cnt, bf16[128,128,128]{2,1,0:T(8,128)(2,1)S(1)} %bitcast.3, ...), custom_call_target="tpu_custom_call" | custom-call | tf_op jit(solution)/shard_map/pallas_call | solution.py:338
  26.8 1.8 %collective-permute-start.8 = (bf16[17,16,128]{2,1,0:T(8,128)(2,1)S(1)}, bf16[17,16,128]{2,1,0:T(8,128)(2,1)S(1)}, u32[]{:S(2)}, u32[]{:S(2)}) collective-permute-start(bf16[17,16,128]{2,1,0:T(8,128)(2,1)S(1)} %get-tuple-element.32), channel_id=1, source_target_pairs={{0,2},{1,3},{2,0},{3,1},{4,6},{5,7},{6,4},{7,5},{8,12},{9,13},{10,... | collective-permute-start | bytes 208904 | tf_op jit(solution)/shard_map/ppermute | solution.py:273
  28.6 1.4 %collective-permute-start.11 = (bf16[16,16,128]{2,1,0:T(8,128)(2,1)S(1)}, bf16[16,16,128]{2,1,0:T(8,128)(2,1)S(1)}, u32[]{:S(2)}, u32[]{:S(2)}) collective-permute-start(bf16[16,16,128]{2,1,0:T(8,128)(2,1)S(1)} %get-tuple-element.33), channel_id=1, source_target_pairs={{0,1},{1,0},{2,3},{3,2},{4,5},{5,4},{6,7},{7,6},{8,12},{9,13},{10,... | collective-permute-start | bytes 196616 | tf_op jit(solution)/shard_map/ppermute | solution.py:273
  30.0 1.9 %collective-permute-done.8 = bf16[17,16,128]{2,1,0:T(8,128)(2,1)S(1)} collective-permute-done((bf16[17,16,128]{2,1,0:T(8,128)(2,1)S(1)}, bf16[17,16,128]{2,1,0:T(8,128)(2,1)S(1)}, u32[]{:S(2)}, u32[]{:S(2)}) %collective-permute-start.8) | collective-permute-done | bytes 69664 | tf_op jit(solution)/shard_map/ppermute | solution.py:273
  32.0 1.2 %collective-permute-start.9 = (bf16[17,16,128]{2,1,0:T(8,128)(2,1)S(1)}, bf16[17,16,128]{2,1,0:T(8,128)(2,1)S(1)}, u32[]{:S(2)}, u32[]{:S(2)}) collective-permute-start(bf16[17,16,128]{2,1,0:T(8,128)(2,1)S(1)} %add_convert_fusion.1), channel_id=1, source_target_pairs={{0,1},{1,0},{2,3},{3,2},{4,5},{5,4},{6,7},{7,6},{8,10},{9,11},{10,... | collective-permute-start | bytes 208904 | tf_op jit(solution)/shard_map/ppermute | solution.py:273
  33.2 0.0 collective-permute-done.11
  33.2 2.2 %collective-permute-start.12 = (bf16[16,16,128]{2,1,0:T(8,128)(2,1)S(1)}, bf16[16,16,128]{2,1,0:T(8,128)(2,1)S(1)}, u32[]{:S(2)}, u32[]{:S(2)}) collective-permute-start(bf16[16,16,128]{2,1,0:T(8,128)(2,1)S(1)} %add_convert_fusion.3), channel_id=1, source_target_pairs={{0,4},{1,5},{2,6},{3,7},{4,0},{5,1},{6,2},{7,3},{8,10},{9,11},{10,... | collective-permute-start | bytes 196616 | tf_op jit(solution)/shard_map/ppermute | solution.py:273
  35.4 1.0 %collective-permute-done.9 = bf16[17,16,128]{2,1,0:T(8,128)(2,1)S(1)} collective-permute-done((bf16[17,16,128]{2,1,0:T(8,128)(2,1)S(1)}, bf16[17,16,128]{2,1,0:T(8,128)(2,1)S(1)}, u32[]{:S(2)}, u32[]{:S(2)}) %collective-permute-start.9) | collective-permute-done | bytes 69664 | tf_op jit(solution)/shard_map/ppermute | solution.py:273
  36.4 1.9 %collective-permute-start.10 = (bf16[17,16,128]{2,1,0:T(8,128)(2,1)S(1)}, bf16[17,16,128]{2,1,0:T(8,128)(2,1)S(1)}, u32[]{:S(2)}, u32[]{:S(2)}) collective-permute-start(bf16[17,16,128]{2,1,0:T(8,128)(2,1)S(1)} %add_convert_fusion.sums0), channel_id=1, source_target_pairs={{0,4},{1,5},{2,6},{3,7},{4,0},{5,1},{6,2},{7,3},{8,9},{9,8},{10,11... | collective-permute-start | bytes 208904 | tf_op jit(solution)/shard_map/ppermute | solution.py:273
  38.3 0.2 collective-permute-done.12
  38.5 2.1 %collective-permute-start.13 = (bf16[16,16,128]{2,1,0:T(8,128)(2,1)S(1)}, bf16[16,16,128]{2,1,0:T(8,128)(2,1)S(1)}, u32[]{:S(2)}, u32[]{:S(2)}) collective-permute-start(bf16[16,16,128]{2,1,0:T(8,128)(2,1)S(1)} %add_convert_fusion.2.sums2), channel_id=1, source_target_pairs={{0,2},{1,3},{2,0},{3,1},{4,6},{5,7},{6,4},{7,5},{8,9},{9,8},{10,11... | collective-permute-start | bytes 196616 | tf_op jit(solution)/shard_map/ppermute | solution.py:273
  40.5 2.3 %collective-permute-done.13.sums3 = bf16[16,16,128]{2,1,0:T(8,128)(2,1)S(1)} collective-permute-done((bf16[16,16,128]{2,1,0:T(8,128)(2,1)S(1)}, bf16[16,16,128]{2,1,0:T(8,128)(2,1)S(1)}, u32[]{:S(2)}, u32[]{:S(2)}) %collective-permute-start.13) | collective-permute-done | bytes 65568 | tf_op jit(solution)/shard_map/ppermute | solution.py:273
  42.8 0.0 collective-permute-done.10.sums1
  42.8 1.4 %shard_map.150 = (f32[9,8,128]{2,1,0:T(8,128)S(1)}, f32[8,8,128]{2,1,0:T(8,128)S(1)}, f32[8,128]{1,0:T(8,128)S(1)}) custom-call(s32[1,1,128]{2,1,0:T(1,128)S(1)} %copy-done.4, s32[1,1,128]{2,1,0:T(1,128)S(1)} %copy-done.5, s32[1,1]{1,0:T(1,128)S(6)} %copy.16.cnt, bf16[128,128,128]{2,1,0:T(8,128)(2,1)S(1)} %bitcast.4, ...), custom_call_target="tpu_custom_call" | custom-call | tf_op jit(solution)/shard_map/pallas_call | solution.py:345
  44.2 0.1 collective-permute-start.14
  44.3 1.2 %collective-permute-done.14.other = f32[9,8,128]{2,1,0:T(8,128)S(1)} collective-permute-done((f32[9,8,128]{2,1,0:T(8,128)S(1)}, f32[9,8,128]{2,1,0:T(8,128)S(1)}, u32[]{:S(2)}, u32[]{:S(2)}) %collective-permute-start.14) | collective-permute-done | bytes 36896 | tf_op jit(solution)/shard_map/ppermute | solution.py:259
  45.5 0.1 shard_map.151
  45.6 1.0 %collective-permute-start.15 = (f32[8,128]{1,0:T(8,128)S(1)}, f32[8,128]{1,0:T(8,128)S(1)}, u32[]{:S(2)}, u32[]{:S(2)}) collective-permute-start(f32[8,128]{1,0:T(8,128)S(1)} %get-tuple-element.41), channel_id=1, source_target_pairs={{0,9},{1,8},{2,11},{3,10},{4,13},{5,12},{6,15},{7,14},{8,1},{9,0},... | collective-permute-start | bytes 12296 | tf_op jit(solution)/shard_map/ppermute | solution.py:290
  46.6 2.0 %collective-permute-done.15 = f32[8,128]{1,0:T(8,128)S(1)} collective-permute-done((f32[8,128]{1,0:T(8,128)S(1)}, f32[8,128]{1,0:T(8,128)S(1)}, u32[]{:S(2)}, u32[]{:S(2)}) %collective-permute-start.15) | collective-permute-done | bytes 4128 | tf_op jit(solution)/shard_map/ppermute | solution.py:290
  48.6 1.8 %collective-permute-start.16 = (f32[8,128]{1,0:T(8,128)S(1)}, f32[8,128]{1,0:T(8,128)S(1)}, u32[]{:S(2)}, u32[]{:S(2)}) collective-permute-start(f32[8,128]{1,0:T(8,128)S(1)} %add.41), channel_id=1, source_target_pairs={{0,10},{1,11},{2,8},{3,9},{4,14},{5,15},{6,12},{7,13},{8,2},{9,3},... | collective-permute-start | bytes 12296 | tf_op jit(solution)/shard_map/ppermute | solution.py:290
  50.4 1.3 %collective-permute-done.16 = f32[8,128]{1,0:T(8,128)S(1)} collective-permute-done((f32[8,128]{1,0:T(8,128)S(1)}, f32[8,128]{1,0:T(8,128)S(1)}, u32[]{:S(2)}, u32[]{:S(2)}) %collective-permute-start.16) | collective-permute-done | bytes 4128 | tf_op jit(solution)/shard_map/ppermute | solution.py:290
  51.7 2.2 %collective-permute-start.17 = (f32[8,128]{1,0:T(8,128)S(1)}, f32[8,128]{1,0:T(8,128)S(1)}, u32[]{:S(2)}, u32[]{:S(2)}) collective-permute-start(f32[8,128]{1,0:T(8,128)S(1)} %add.42), channel_id=1, source_target_pairs={{0,12},{1,13},{2,14},{3,15},{4,8},{5,9},{6,10},{7,11},{8,4},{9,5},... | collective-permute-start | bytes 12296 | tf_op jit(solution)/shard_map/ppermute | solution.py:290
  53.9 1.2 %shard_map.152 = (f32[8,1024]{1,0:T(8,128)}, f32[8,512]{1,0:T(8,128)}, f32[8,512]{1,0:T(8,128)S(1)}, f32[3,8,128]{2,1,0:T(8,128)S(1)}) custom-call(f32[8]{0:T(128)S(1)} %copy-done.6, f32[8]{0:T(128)S(1)} %copy-done.7, f32[8,8,128]{2,1,0:T(8,128)S(1)} %get-tuple-element.31.v_old.v1, f32[8,8,128]{2,1,0:T(8,128)S(1)} %get-tuple-element.36.u_piece, ...), custom_call_target="tpu_custom_call" | custom-call | flops 1000000 | bytes 3000000 | tf_op jit(solution)/shard_map/pallas_call | solution.py:358
  55.1 0.5 collective-permute-done.17
  55.6 0.6 %shard_map.153 = (f32[8,512]{1,0:T(8,128)}, f32[8,512]{1,0:T(8,128)}, f32[3,8]{1,0:T(4,128)}) custom-call(f32[8,128]{1,0:T(8,128)S(1)} %add.43.sq, f32[8,8,128]{2,1,0:T(8,128)S(1)} %get-tuple-element.42.v2, f32[8,512]{1,0:T(8,128)S(1)} %get-tuple-element.43.w_mid, f32[3,8,128]{2,1,0:T(8,128)S(1)} %get-tuple-element.44.factors), custom_call_target="tpu_custom_call" | custom-call | tf_op jit(solution)/shard_map/pallas_call | solution.py:365
  (27 shorter events, 0.2 us)
Async XLA Ops:
  0.6 2.3 %copy-start.5 = (s32[1,1,128]{2,1,0:T(1,128)S(1)}, s32[1,1,128]{2,1,0:T(1,128)}, u32[]{:S(2)}) copy-start(s32[1,1,128]{2,1,0:T(1,128)} %cls_ref.7) | copy-start | bytes 1540
  0.6 2.3 %copy-start.4 = (s32[1,1,128]{2,1,0:T(1,128)S(1)}, s32[1,1,128]{2,1,0:T(1,128)}, u32[]{:S(2)}) copy-start(s32[1,1,128]{2,1,0:T(1,128)} %rws_ref.7) | copy-start | bytes 1540
  0.7 2.3 %copy-start.8 = (f32[8]{0:T(128)S(1)}, f32[8]{0:T(128)}, u32[]{:S(2)}) copy-start(f32[8]{0:T(128)} %alpha_ref.1) | copy-start | bytes 100
  0.7 2.3 %copy-start.1 = (f32[8,1024]{1,0:T(8,128)S(1)}, f32[8,1024]{1,0:T(8,128)}, u32[]{:S(2)}) copy-start(f32[8,1024]{1,0:T(8,128)} %u_piece.1) | copy-start | bytes 98308
  0.7 2.3 %copy-start = (bf16[1,1,128,128,128]{4,3,2,1,0:T(8,128)(2,1)S(1)}, bf16[1,1,128,128,128]{4,3,2,1,0:T(8,128)(2,1)}, u32[]{:S(2)}) copy-start(bf16[1,1,128,128,128]{4,3,2,1,0:T(8,128)(2,1)} %param.11) | copy-start | bytes 12582916
  0.7 0.9 %copy-start.9 = (f32[8,512]{1,0:T(8,128)S(1)}, f32[8,512]{1,0:T(8,128)}, u32[]{:S(2)}) copy-start(f32[8,512]{1,0:T(8,128)} %own_hbm.1) | copy-start | bytes 49156
  1.6 1.4 %collective-permute-start = (f32[8,512]{1,0:T(8,128)S(1)}, f32[8,512]{1,0:T(8,128)S(1)}, u32[]{:S(2)}, u32[]{:S(2)}) collective-permute-start(f32[8,512]{1,0:T(8,128)S(1)} %shard_map.146.own), channel_id=1, source_target_pairs={{0,8},{8,0},{1,9},{9,1},{2,10},{10,2},{3,11},{11,3},{4,12},{12,4},... | collective-permute-start | bytes 49160 | tf_op jit(solution)/shard_map/ppermute | solution.py:259
  4.8 6.0 %collective-permute-start.1 = (bf16[16,16,128]{2,1,0:T(8,128)(2,1)S(1)}, bf16[16,16,128]{2,1,0:T(8,128)(2,1)S(1)}, u32[]{:S(2)}, u32[]{:S(2)}) collective-permute-start(bf16[16,16,128]{2,1,0:T(8,128)(2,1)S(1)} %get-tuple-element.27), channel_id=1, source_target_pairs={{0,2},{1,3},{2,0},{3,1},{4,6},{5,7},{6,4},{7,5},{8,12},{9,13},{10,... | collective-permute-start | bytes 196616 | tf_op jit(solution)/shard_map/ppermute | solution.py:273
  7.8 5.0 %collective-permute-start.4 = (bf16[16,16,128]{2,1,0:T(8,128)(2,1)S(1)}, bf16[16,16,128]{2,1,0:T(8,128)(2,1)S(1)}, u32[]{:S(2)}, u32[]{:S(2)}) collective-permute-start(bf16[16,16,128]{2,1,0:T(8,128)(2,1)S(1)} %get-tuple-element.28), channel_id=1, source_target_pairs={{0,1},{1,0},{2,3},{3,2},{4,5},{5,4},{6,7},{7,6},{8,12},{9,13},{10,... | collective-permute-start | bytes 196616 | tf_op jit(solution)/shard_map/ppermute | solution.py:273
  10.8 4.3 %collective-permute-start.2 = (bf16[16,16,128]{2,1,0:T(8,128)(2,1)S(1)}, bf16[16,16,128]{2,1,0:T(8,128)(2,1)S(1)}, u32[]{:S(2)}, u32[]{:S(2)}) collective-permute-start(bf16[16,16,128]{2,1,0:T(8,128)(2,1)S(1)} %add_convert_fusion.7), channel_id=1, source_target_pairs={{0,1},{1,0},{2,3},{3,2},{4,5},{5,4},{6,7},{7,6},{8,10},{9,11},{10,... | collective-permute-start | bytes 196616 | tf_op jit(solution)/shard_map/ppermute | solution.py:273
  12.8 5.2 %collective-permute-start.5 = (bf16[16,16,128]{2,1,0:T(8,128)(2,1)S(1)}, bf16[16,16,128]{2,1,0:T(8,128)(2,1)S(1)}, u32[]{:S(2)}, u32[]{:S(2)}) collective-permute-start(bf16[16,16,128]{2,1,0:T(8,128)(2,1)S(1)} %add_convert_fusion.5), channel_id=1, source_target_pairs={{0,4},{1,5},{2,6},{3,7},{4,0},{5,1},{6,2},{7,3},{8,10},{9,11},{10,... | collective-permute-start | bytes 196616 | tf_op jit(solution)/shard_map/ppermute | solution.py:273
  15.2 5.2 %collective-permute-start.3 = (bf16[16,16,128]{2,1,0:T(8,128)(2,1)S(1)}, bf16[16,16,128]{2,1,0:T(8,128)(2,1)S(1)}, u32[]{:S(2)}, u32[]{:S(2)}) collective-permute-start(bf16[16,16,128]{2,1,0:T(8,128)(2,1)S(1)} %add_convert_fusion.6.sums0), channel_id=1, source_target_pairs={{0,4},{1,5},{2,6},{3,7},{4,0},{5,1},{6,2},{7,3},{8,9},{9,8},{10,11... | collective-permute-start | bytes 196616 | tf_op jit(solution)/shard_map/ppermute | solution.py:273
  18.1 4.3 %collective-permute-start.6 = (bf16[16,16,128]{2,1,0:T(8,128)(2,1)S(1)}, bf16[16,16,128]{2,1,0:T(8,128)(2,1)S(1)}, u32[]{:S(2)}, u32[]{:S(2)}) collective-permute-start(bf16[16,16,128]{2,1,0:T(8,128)(2,1)S(1)} %add_convert_fusion.4.sums2), channel_id=1, source_target_pairs={{0,2},{1,3},{2,0},{3,1},{4,6},{5,7},{6,4},{7,5},{8,9},{9,8},{10,11... | collective-permute-start | bytes 196616 | tf_op jit(solution)/shard_map/ppermute | solution.py:273
  23.7 1.3 %collective-permute-start.7 = (f32[9,8,128]{2,1,0:T(8,128)S(1)}, f32[9,8,128]{2,1,0:T(8,128)S(1)}, u32[]{:S(2)}, u32[]{:S(2)}) collective-permute-start(f32[9,8,128]{2,1,0:T(8,128)S(1)} %get-tuple-element.29.own), channel_id=1, source_target_pairs={{0,8},{8,0},{1,9},{9,1},{2,10},{10,2},{3,11},{11,3},{4,12},{12,4},... | collective-permute-start | bytes 110600 | tf_op jit(solution)/shard_map/ppermute | solution.py:259
  25.0 28.9 %copy-start.2 = (f32[8,512]{1,0:T(8,128)S(1)}, f32[8,512]{1,0:T(8,128)}, u32[]{:S(2)}) copy-start(f32[8,512]{1,0:T(8,128)} %x_in.1) | copy-start | bytes 49156
  25.0 28.9 %copy-start.3 = (f32[8,512]{1,0:T(8,128)S(1)}, f32[8,512]{1,0:T(8,128)}, u32[]{:S(2)}) copy-start(f32[8,512]{1,0:T(8,128)} %w_in.1) | copy-start | bytes 49156
  25.0 28.9 %copy-start.6 = (f32[8]{0:T(128)S(1)}, f32[8]{0:T(128)}, u32[]{:S(2)}) copy-start(f32[8]{0:T(128)} %phibar_in.1) | copy-start | bytes 100
  25.0 28.9 %copy-start.7 = (f32[8]{0:T(128)S(1)}, f32[8]{0:T(128)}, u32[]{:S(2)}) copy-start(f32[8]{0:T(128)} %rhobar_in.1) | copy-start | bytes 100
  26.8 5.1 %collective-permute-start.8 = (bf16[17,16,128]{2,1,0:T(8,128)(2,1)S(1)}, bf16[17,16,128]{2,1,0:T(8,128)(2,1)S(1)}, u32[]{:S(2)}, u32[]{:S(2)}) collective-permute-start(bf16[17,16,128]{2,1,0:T(8,128)(2,1)S(1)} %get-tuple-element.32), channel_id=1, source_target_pairs={{0,2},{1,3},{2,0},{3,1},{4,6},{5,7},{6,4},{7,5},{8,12},{9,13},{10,... | collective-permute-start | bytes 208904 | tf_op jit(solution)/shard_map/ppermute | solution.py:273
  28.6 4.6 %collective-permute-start.11 = (bf16[16,16,128]{2,1,0:T(8,128)(2,1)S(1)}, bf16[16,16,128]{2,1,0:T(8,128)(2,1)S(1)}, u32[]{:S(2)}, u32[]{:S(2)}) collective-permute-start(bf16[16,16,128]{2,1,0:T(8,128)(2,1)S(1)} %get-tuple-element.33), channel_id=1, source_target_pairs={{0,1},{1,0},{2,3},{3,2},{4,5},{5,4},{6,7},{7,6},{8,12},{9,13},{10,... | collective-permute-start | bytes 196616 | tf_op jit(solution)/shard_map/ppermute | solution.py:273
  32.0 4.4 %collective-permute-start.9 = (bf16[17,16,128]{2,1,0:T(8,128)(2,1)S(1)}, bf16[17,16,128]{2,1,0:T(8,128)(2,1)S(1)}, u32[]{:S(2)}, u32[]{:S(2)}) collective-permute-start(bf16[17,16,128]{2,1,0:T(8,128)(2,1)S(1)} %add_convert_fusion.1), channel_id=1, source_target_pairs={{0,1},{1,0},{2,3},{3,2},{4,5},{5,4},{6,7},{7,6},{8,10},{9,11},{10,... | collective-permute-start | bytes 208904 | tf_op jit(solution)/shard_map/ppermute | solution.py:273
  33.2 5.2 %collective-permute-start.12 = (bf16[16,16,128]{2,1,0:T(8,128)(2,1)S(1)}, bf16[16,16,128]{2,1,0:T(8,128)(2,1)S(1)}, u32[]{:S(2)}, u32[]{:S(2)}) collective-permute-start(bf16[16,16,128]{2,1,0:T(8,128)(2,1)S(1)} %add_convert_fusion.3), channel_id=1, source_target_pairs={{0,4},{1,5},{2,6},{3,7},{4,0},{5,1},{6,2},{7,3},{8,10},{9,11},{10,... | collective-permute-start | bytes 196616 | tf_op jit(solution)/shard_map/ppermute | solution.py:273
  36.4 6.4 %collective-permute-start.10 = (bf16[17,16,128]{2,1,0:T(8,128)(2,1)S(1)}, bf16[17,16,128]{2,1,0:T(8,128)(2,1)S(1)}, u32[]{:S(2)}, u32[]{:S(2)}) collective-permute-start(bf16[17,16,128]{2,1,0:T(8,128)(2,1)S(1)} %add_convert_fusion.sums0), channel_id=1, source_target_pairs={{0,4},{1,5},{2,6},{3,7},{4,0},{5,1},{6,2},{7,3},{8,9},{9,8},{10,11... | collective-permute-start | bytes 208904 | tf_op jit(solution)/shard_map/ppermute | solution.py:273
  38.5 4.3 %collective-permute-start.13 = (bf16[16,16,128]{2,1,0:T(8,128)(2,1)S(1)}, bf16[16,16,128]{2,1,0:T(8,128)(2,1)S(1)}, u32[]{:S(2)}, u32[]{:S(2)}) collective-permute-start(bf16[16,16,128]{2,1,0:T(8,128)(2,1)S(1)} %add_convert_fusion.2.sums2), channel_id=1, source_target_pairs={{0,2},{1,3},{2,0},{3,1},{4,6},{5,7},{6,4},{7,5},{8,9},{9,8},{10,11... | collective-permute-start | bytes 196616 | tf_op jit(solution)/shard_map/ppermute | solution.py:273
  44.2 1.3 %collective-permute-start.14 = (f32[9,8,128]{2,1,0:T(8,128)S(1)}, f32[9,8,128]{2,1,0:T(8,128)S(1)}, u32[]{:S(2)}, u32[]{:S(2)}) collective-permute-start(f32[9,8,128]{2,1,0:T(8,128)S(1)} %get-tuple-element.38.own), channel_id=1, source_target_pairs={{0,8},{8,0},{1,9},{9,1},{2,10},{10,2},{3,11},{11,3},{4,12},{12,4},... | collective-permute-start | bytes 110600 | tf_op jit(solution)/shard_map/ppermute | solution.py:259
  45.6 3.0 %collective-permute-start.15 = (f32[8,128]{1,0:T(8,128)S(1)}, f32[8,128]{1,0:T(8,128)S(1)}, u32[]{:S(2)}, u32[]{:S(2)}) collective-permute-start(f32[8,128]{1,0:T(8,128)S(1)} %get-tuple-element.41), channel_id=1, source_target_pairs={{0,9},{1,8},{2,11},{3,10},{4,13},{5,12},{6,15},{7,14},{8,1},{9,0},... | collective-permute-start | bytes 12296 | tf_op jit(solution)/shard_map/ppermute | solution.py:290
  48.6 3.1 %collective-permute-start.16 = (f32[8,128]{1,0:T(8,128)S(1)}, f32[8,128]{1,0:T(8,128)S(1)}, u32[]{:S(2)}, u32[]{:S(2)}) collective-permute-start(f32[8,128]{1,0:T(8,128)S(1)} %add.41), channel_id=1, source_target_pairs={{0,10},{1,11},{2,8},{3,9},{4,14},{5,15},{6,12},{7,13},{8,2},{9,3},... | collective-permute-start | bytes 12296 | tf_op jit(solution)/shard_map/ppermute | solution.py:290
  51.7 3.9 %collective-permute-start.17 = (f32[8,128]{1,0:T(8,128)S(1)}, f32[8,128]{1,0:T(8,128)S(1)}, u32[]{:S(2)}, u32[]{:S(2)}) collective-permute-start(f32[8,128]{1,0:T(8,128)S(1)} %add.42), channel_id=1, source_target_pairs={{0,12},{1,13},{2,14},{3,15},{4,8},{5,9},{6,10},{7,11},{8,4},{9,5},... | collective-permute-start | bytes 12296 | tf_op jit(solution)/shard_map/ppermute | solution.py:290

commit v11 on v10

--- a/solution.py
+++ b/solution.py
@@ -284,11 +284,10 @@
 
 def last_sum(x):
     n = lax.axis_size("col")
-    m = 1
-    while m < n:
+    steps = [1 << i for i in range((n - 1).bit_length())]
+    for m in steps[1:] + steps[:1]:
         pairs = [(i + n * r, (i ^ m) + n * (1 - r)) for r in (0, 1) for i in range(n)]
         x = x + lax.ppermute(x, ("row", "col"), pairs)
-        m *= 2
     return x
 
 

time: 56.5 us -> 56.5 us (level)
  no operation moved by 1% of the time
where the time goes in v11:
time: 56.5 us; the launch traced here: 56.3 us
  starting transfers between devices  28.9 us (51%)
  waiting for transfers between devices  16.6 us (29%)
  Pallas kernels  8.26 us (15%)
  between operations  1.46 us (3%)
  local copies, waits for them, and re-layouts  0.9 us (2%)
    ppermute x12, starting transfers between devices, column_sum(): lax.ppermute(x, ('row', 'col'), [(j, j ^ first[i]) for j in range(n)] + [...  23.2 us
    ppermute x12, waiting for transfers between devices, column_sum(): lax.ppermute(x, ('row', 'col'), [(j, j ^ first[i]) for j in range(n)] + [...  10.1 us
    ppermute x3, starting transfers between devices, last_sum(): x = x + lax.ppermute(x, ('row', 'col'), pairs)  5.02 us
    ppermute x3, waiting for transfers between devices, last_sum(): x = x + lax.ppermute(x, ('row', 'col'), pairs)  3.84 us
    ppermute x3, waiting for transfers between devices, other_core(): return lax.ppermute(x, 'row', [(0, 1), (1, 0)])  2.59 us
    pallas_call x1, Pallas kernels, body(): call(first_forward, (half_rays, half_rays, shape(cells, 8, 128)), [VMEM]...  1.83 us
    pallas_call x1, Pallas kernels, body(): call(functools.partial(next_forward, total_rays), (shape(rays // 4 + 1, 1...  1.81 us
    pallas_call x1, Pallas kernels, body(): call(functools.partial(next_backward, total_cells, pieces), (shape(cells...  1.4 us
  transfers between devices with their start and end apart: 18, of which 15 were waited for; matrix products, arithmetic and copies ran while one was open for 0% of the time, Pallas kernels for 2%

profile of v11, /device:TPU:0, one launch (start us, length us, event | category | flops | bytes accessed | tf_op | source)
XLA Modules:
  0.0 56.3 jit_solution(3817877932752308804)
XLA Ops:
  0.6 0.0 copy-start.5
  0.6 0.0 copy-start.4
  0.7 0.0 copy-start.8
  0.7 0.0 copy-start.1
  0.7 0.9 %copy-done.9 = f32[8,512]{1,0:T(8,128)S(1)} copy-done((f32[8,512]{1,0:T(8,128)S(1)}, f32[8,512]{1,0:T(8,128)}, u32[]{:S(2)}) %copy-start.9) | copy-done | bytes 16408
  1.6 0.5 collective-permute-start
  2.7 0.2 collective-permute-done.other
  3.0 1.8 %shard_map.147 = (bf16[16,16,128]{2,1,0:T(8,128)(2,1)S(1)}, bf16[16,16,128]{2,1,0:T(8,128)(2,1)S(1)}, f32[8,8,128]{2,1,0:T(8,128)S(1)}) custom-call(s32[1,1,128]{2,1,0:T(1,128)S(1)} %copy-done.4, s32[1,1,128]{2,1,0:T(1,128)S(1)} %copy-done.5, s32[1,1]{1,0:T(1,128)S(6)} %copy.16.cnt, bf16[128,128,128]{2,1,0:T(8,128)(2,1)S(1)} %bitcast.1, f32[8]{0:T(128)S(1)} %copy-done.8, ...), custom_call_target="tpu_custom_call" | custom-call | tf_op jit(solution)/shard_map/pallas_call | solution.py:324
  4.8 3.0 %collective-permute-start.1 = (bf16[16,16,128]{2,1,0:T(8,128)(2,1)S(1)}, bf16[16,16,128]{2,1,0:T(8,128)(2,1)S(1)}, u32[]{:S(2)}, u32[]{:S(2)}) collective-permute-start(bf16[16,16,128]{2,1,0:T(8,128)(2,1)S(1)} %get-tuple-element.27), channel_id=1, source_target_pairs={{0,2},{1,3},{2,0},{3,1},{4,6},{5,7},{6,4},{7,5},{8,12},{9,13},{10,... | collective-permute-start | bytes 196616 | tf_op jit(solution)/shard_map/ppermute | solution.py:273
  7.8 1.5 %collective-permute-start.4 = (bf16[16,16,128]{2,1,0:T(8,128)(2,1)S(1)}, bf16[16,16,128]{2,1,0:T(8,128)(2,1)S(1)}, u32[]{:S(2)}, u32[]{:S(2)}) collective-permute-start(bf16[16,16,128]{2,1,0:T(8,128)(2,1)S(1)} %get-tuple-element.28), channel_id=1, source_target_pairs={{0,1},{1,0},{2,3},{3,2},{4,5},{5,4},{6,7},{7,6},{8,12},{9,13},{10,... | collective-permute-start | bytes 196616 | tf_op jit(solution)/shard_map/ppermute | solution.py:273
  9.3 1.5 %collective-permute-done.1 = bf16[16,16,128]{2,1,0:T(8,128)(2,1)S(1)} collective-permute-done((bf16[16,16,128]{2,1,0:T(8,128)(2,1)S(1)}, bf16[16,16,128]{2,1,0:T(8,128)(2,1)S(1)}, u32[]{:S(2)}, u32[]{:S(2)}) %collective-permute-start.1) | collective-permute-done | bytes 65568 | tf_op jit(solution)/shard_map/ppermute | solution.py:273
  10.8 2.0 %collective-permute-start.2 = (bf16[16,16,128]{2,1,0:T(8,128)(2,1)S(1)}, bf16[16,16,128]{2,1,0:T(8,128)(2,1)S(1)}, u32[]{:S(2)}, u32[]{:S(2)}) collective-permute-start(bf16[16,16,128]{2,1,0:T(8,128)(2,1)S(1)} %add_convert_fusion.7), channel_id=1, source_target_pairs={{0,1},{1,0},{2,3},{3,2},{4,5},{5,4},{6,7},{7,6},{8,10},{9,11},{10,... | collective-permute-start | bytes 196616 | tf_op jit(solution)/shard_map/ppermute | solution.py:273
  12.8 0.0 collective-permute-done.4
  12.8 2.0 %collective-permute-start.5 = (bf16[16,16,128]{2,1,0:T(8,128)(2,1)S(1)}, bf16[16,16,128]{2,1,0:T(8,128)(2,1)S(1)}, u32[]{:S(2)}, u32[]{:S(2)}) collective-permute-start(bf16[16,16,128]{2,1,0:T(8,128)(2,1)S(1)} %add_convert_fusion.5), channel_id=1, source_target_pairs={{0,4},{1,5},{2,6},{3,7},{4,0},{5,1},{6,2},{7,3},{8,10},{9,11},{10,... | collective-permute-start | bytes 196616 | tf_op jit(solution)/shard_map/ppermute | solution.py:273
  14.8 0.3 collective-permute-done.2
  15.2 2.4 %collective-permute-start.3 = (bf16[16,16,128]{2,1,0:T(8,128)(2,1)S(1)}, bf16[16,16,128]{2,1,0:T(8,128)(2,1)S(1)}, u32[]{:S(2)}, u32[]{:S(2)}) collective-permute-start(bf16[16,16,128]{2,1,0:T(8,128)(2,1)S(1)} %add_convert_fusion.6.sums0), channel_id=1, source_target_pairs={{0,4},{1,5},{2,6},{3,7},{4,0},{5,1},{6,2},{7,3},{8,9},{9,8},{10,11... | collective-permute-start | bytes 196616 | tf_op jit(solution)/shard_map/ppermute | solution.py:273
  17.5 0.5 collective-permute-done.5
  18.1 1.8 %collective-permute-start.6 = (bf16[16,16,128]{2,1,0:T(8,128)(2,1)S(1)}, bf16[16,16,128]{2,1,0:T(8,128)(2,1)S(1)}, u32[]{:S(2)}, u32[]{:S(2)}) collective-permute-start(bf16[16,16,128]{2,1,0:T(8,128)(2,1)S(1)} %add_convert_fusion.4.sums2), channel_id=1, source_target_pairs={{0,2},{1,3},{2,0},{3,1},{4,6},{5,7},{6,4},{7,5},{8,9},{9,8},{10,11... | collective-permute-start | bytes 196616 | tf_op jit(solution)/shard_map/ppermute | solution.py:273
  19.9 0.5 collective-permute-done.3.sums1
  20.4 2.0 %collective-permute-done.6.sums3 = bf16[16,16,128]{2,1,0:T(8,128)(2,1)S(1)} collective-permute-done((bf16[16,16,128]{2,1,0:T(8,128)(2,1)S(1)}, bf16[16,16,128]{2,1,0:T(8,128)(2,1)S(1)}, u32[]{:S(2)}, u32[]{:S(2)}) %collective-permute-start.6) | collective-permute-done | bytes 65568 | tf_op jit(solution)/shard_map/ppermute | solution.py:273
  22.4 1.3 %shard_map.148 = (f32[64,8,128]{2,1,0:T(8,128)S(1)}, f32[9,8,128]{2,1,0:T(8,128)S(1)}) custom-call(s32[1,1,128]{2,1,0:T(1,128)S(1)} %copy-done.4, s32[1,1,128]{2,1,0:T(1,128)S(1)} %copy-done.5, s32[1,1]{1,0:T(1,128)S(6)} %copy.16.cnt, bf16[128,128,128]{2,1,0:T(8,128)(2,1)S(1)} %bitcast.2, bf16[16,16,128]{2,1,0:T(8,128)(2,1)S(1)} %add_convert_fusion.6.sums0, ...), custom_call_target="tpu_custom_call" | custom-call | tf_op jit(solution)/shard_map/pallas_call | solution.py:331
  23.7 0.1 collective-permute-start.7
  23.8 1.2 %collective-permute-done.7.other = f32[9,8,128]{2,1,0:T(8,128)S(1)} collective-permute-done((f32[9,8,128]{2,1,0:T(8,128)S(1)}, f32[9,8,128]{2,1,0:T(8,128)S(1)}, u32[]{:S(2)}, u32[]{:S(2)}) %collective-permute-start.7) | collective-permute-done | bytes 36896 | tf_op jit(solution)/shard_map/ppermute | solution.py:259
  25.0 1.8 %shard_map.149 = (bf16[17,16,128]{2,1,0:T(8,128)(2,1)S(1)}, bf16[16,16,128]{2,1,0:T(8,128)(2,1)S(1)}, f32[8,8,128]{2,1,0:T(8,128)S(1)}, f32[8,128]{1,0:T(8,128)S(1)}) custom-call(s32[1,1,128]{2,1,0:T(1,128)S(1)} %copy-done.4, s32[1,1,128]{2,1,0:T(1,128)S(1)} %copy-done.5, s32[1,1]{1,0:T(1,128)S(6)} %copy.16.cnt, bf16[128,128,128]{2,1,0:T(8,128)(2,1)S(1)} %bitcast.3, ...), custom_call_target="tpu_custom_call" | custom-call | tf_op jit(solution)/shard_map/pallas_call | solution.py:337
  26.8 1.8 %collective-permute-start.8 = (bf16[17,16,128]{2,1,0:T(8,128)(2,1)S(1)}, bf16[17,16,128]{2,1,0:T(8,128)(2,1)S(1)}, u32[]{:S(2)}, u32[]{:S(2)}) collective-permute-start(bf16[17,16,128]{2,1,0:T(8,128)(2,1)S(1)} %get-tuple-element.32), channel_id=1, source_target_pairs={{0,2},{1,3},{2,0},{3,1},{4,6},{5,7},{6,4},{7,5},{8,12},{9,13},{10,... | collective-permute-start | bytes 208904 | tf_op jit(solution)/shard_map/ppermute | solution.py:273
  28.6 1.4 %collective-permute-start.11 = (bf16[16,16,128]{2,1,0:T(8,128)(2,1)S(1)}, bf16[16,16,128]{2,1,0:T(8,128)(2,1)S(1)}, u32[]{:S(2)}, u32[]{:S(2)}) collective-permute-start(bf16[16,16,128]{2,1,0:T(8,128)(2,1)S(1)} %get-tuple-element.33), channel_id=1, source_target_pairs={{0,1},{1,0},{2,3},{3,2},{4,5},{5,4},{6,7},{7,6},{8,12},{9,13},{10,... | collective-permute-start | bytes 196616 | tf_op jit(solution)/shard_map/ppermute | solution.py:273
  30.0 1.9 %collective-permute-done.8 = bf16[17,16,128]{2,1,0:T(8,128)(2,1)S(1)} collective-permute-done((bf16[17,16,128]{2,1,0:T(8,128)(2,1)S(1)}, bf16[17,16,128]{2,1,0:T(8,128)(2,1)S(1)}, u32[]{:S(2)}, u32[]{:S(2)}) %collective-permute-start.8) | collective-permute-done | bytes 69664 | tf_op jit(solution)/shard_map/ppermute | solution.py:273
  32.0 1.2 %collective-permute-start.9 = (bf16[17,16,128]{2,1,0:T(8,128)(2,1)S(1)}, bf16[17,16,128]{2,1,0:T(8,128)(2,1)S(1)}, u32[]{:S(2)}, u32[]{:S(2)}) collective-permute-start(bf16[17,16,128]{2,1,0:T(8,128)(2,1)S(1)} %add_convert_fusion.1), channel_id=1, source_target_pairs={{0,1},{1,0},{2,3},{3,2},{4,5},{5,4},{6,7},{7,6},{8,10},{9,11},{10,... | collective-permute-start | bytes 208904 | tf_op jit(solution)/shard_map/ppermute | solution.py:273
  33.2 0.0 collective-permute-done.11
  33.2 2.2 %collective-permute-start.12 = (bf16[16,16,128]{2,1,0:T(8,128)(2,1)S(1)}, bf16[16,16,128]{2,1,0:T(8,128)(2,1)S(1)}, u32[]{:S(2)}, u32[]{:S(2)}) collective-permute-start(bf16[16,16,128]{2,1,0:T(8,128)(2,1)S(1)} %add_convert_fusion.3), channel_id=1, source_target_pairs={{0,4},{1,5},{2,6},{3,7},{4,0},{5,1},{6,2},{7,3},{8,10},{9,11},{10,... | collective-permute-start | bytes 196616 | tf_op jit(solution)/shard_map/ppermute | solution.py:273
  35.4 1.0 %collective-permute-done.9 = bf16[17,16,128]{2,1,0:T(8,128)(2,1)S(1)} collective-permute-done((bf16[17,16,128]{2,1,0:T(8,128)(2,1)S(1)}, bf16[17,16,128]{2,1,0:T(8,128)(2,1)S(1)}, u32[]{:S(2)}, u32[]{:S(2)}) %collective-permute-start.9) | collective-permute-done | bytes 69664 | tf_op jit(solution)/shard_map/ppermute | solution.py:273
  36.4 1.9 %collective-permute-start.10 = (bf16[17,16,128]{2,1,0:T(8,128)(2,1)S(1)}, bf16[17,16,128]{2,1,0:T(8,128)(2,1)S(1)}, u32[]{:S(2)}, u32[]{:S(2)}) collective-permute-start(bf16[17,16,128]{2,1,0:T(8,128)(2,1)S(1)} %add_convert_fusion.sums0), channel_id=1, source_target_pairs={{0,4},{1,5},{2,6},{3,7},{4,0},{5,1},{6,2},{7,3},{8,9},{9,8},{10,11... | collective-permute-start | bytes 208904 | tf_op jit(solution)/shard_map/ppermute | solution.py:273
  38.2 0.2 collective-permute-done.12
  38.4 2.1 %collective-permute-start.13 = (bf16[16,16,128]{2,1,0:T(8,128)(2,1)S(1)}, bf16[16,16,128]{2,1,0:T(8,128)(2,1)S(1)}, u32[]{:S(2)}, u32[]{:S(2)}) collective-permute-start(bf16[16,16,128]{2,1,0:T(8,128)(2,1)S(1)} %add_convert_fusion.2.sums2), channel_id=1, source_target_pairs={{0,2},{1,3},{2,0},{3,1},{4,6},{5,7},{6,4},{7,5},{8,9},{9,8},{10,11... | collective-permute-start | bytes 196616 | tf_op jit(solution)/shard_map/ppermute | solution.py:273
  40.5 2.3 %collective-permute-done.13.sums3 = bf16[16,16,128]{2,1,0:T(8,128)(2,1)S(1)} collective-permute-done((bf16[16,16,128]{2,1,0:T(8,128)(2,1)S(1)}, bf16[16,16,128]{2,1,0:T(8,128)(2,1)S(1)}, u32[]{:S(2)}, u32[]{:S(2)}) %collective-permute-start.13) | collective-permute-done | bytes 65568 | tf_op jit(solution)/shard_map/ppermute | solution.py:273
  42.8 0.0 collective-permute-done.10.sums1
  42.8 1.4 %shard_map.150 = (f32[9,8,128]{2,1,0:T(8,128)S(1)}, f32[8,8,128]{2,1,0:T(8,128)S(1)}, f32[8,128]{1,0:T(8,128)S(1)}) custom-call(s32[1,1,128]{2,1,0:T(1,128)S(1)} %copy-done.4, s32[1,1,128]{2,1,0:T(1,128)S(1)} %copy-done.5, s32[1,1]{1,0:T(1,128)S(6)} %copy.16.cnt, bf16[128,128,128]{2,1,0:T(8,128)(2,1)S(1)} %bitcast.4, ...), custom_call_target="tpu_custom_call" | custom-call | tf_op jit(solution)/shard_map/pallas_call | solution.py:344
  44.2 0.1 collective-permute-start.14
  44.3 1.2 %collective-permute-done.14.other = f32[9,8,128]{2,1,0:T(8,128)S(1)} collective-permute-done((f32[9,8,128]{2,1,0:T(8,128)S(1)}, f32[9,8,128]{2,1,0:T(8,128)S(1)}, u32[]{:S(2)}, u32[]{:S(2)}) %collective-permute-start.14) | collective-permute-done | bytes 36896 | tf_op jit(solution)/shard_map/ppermute | solution.py:259
  45.5 0.1 shard_map.151
  45.6 1.8 %collective-permute-start.15 = (f32[8,128]{1,0:T(8,128)S(1)}, f32[8,128]{1,0:T(8,128)S(1)}, u32[]{:S(2)}, u32[]{:S(2)}) collective-permute-start(f32[8,128]{1,0:T(8,128)S(1)} %get-tuple-element.41), channel_id=1, source_target_pairs={{0,10},{1,11},{2,8},{3,9},{4,14},{5,15},{6,12},{7,13},{8,2},{9,3},... | collective-permute-start | bytes 12296 | tf_op jit(solution)/shard_map/ppermute | solution.py:290
  47.3 1.3 %collective-permute-done.15 = f32[8,128]{1,0:T(8,128)S(1)} collective-permute-done((f32[8,128]{1,0:T(8,128)S(1)}, f32[8,128]{1,0:T(8,128)S(1)}, u32[]{:S(2)}, u32[]{:S(2)}) %collective-permute-start.15) | collective-permute-done | bytes 4128 | tf_op jit(solution)/shard_map/ppermute | solution.py:290
  48.7 2.2 %collective-permute-start.16 = (f32[8,128]{1,0:T(8,128)S(1)}, f32[8,128]{1,0:T(8,128)S(1)}, u32[]{:S(2)}, u32[]{:S(2)}) collective-permute-start(f32[8,128]{1,0:T(8,128)S(1)} %add.41), channel_id=1, source_target_pairs={{0,12},{1,13},{2,14},{3,15},{4,8},{5,9},{6,10},{7,11},{8,4},{9,5},... | collective-permute-start | bytes 12296 | tf_op jit(solution)/shard_map/ppermute | solution.py:290
  50.9 1.7 %collective-permute-done.16 = f32[8,128]{1,0:T(8,128)S(1)} collective-permute-done((f32[8,128]{1,0:T(8,128)S(1)}, f32[8,128]{1,0:T(8,128)S(1)}, u32[]{:S(2)}, u32[]{:S(2)}) %collective-permute-start.16) | collective-permute-done | bytes 4128 | tf_op jit(solution)/shard_map/ppermute | solution.py:290
  52.6 1.0 %collective-permute-start.17 = (f32[8,128]{1,0:T(8,128)S(1)}, f32[8,128]{1,0:T(8,128)S(1)}, u32[]{:S(2)}, u32[]{:S(2)}) collective-permute-start(f32[8,128]{1,0:T(8,128)S(1)} %add.42), channel_id=1, source_target_pairs={{0,9},{1,8},{2,11},{3,10},{4,13},{5,12},{6,15},{7,14},{8,1},{9,0},... | collective-permute-start | bytes 12296 | tf_op jit(solution)/shard_map/ppermute | solution.py:290
  53.7 1.2 %shard_map.152 = (f32[8,1024]{1,0:T(8,128)}, f32[8,512]{1,0:T(8,128)}, f32[8,512]{1,0:T(8,128)S(1)}, f32[3,8,128]{2,1,0:T(8,128)S(1)}) custom-call(f32[8]{0:T(128)S(1)} %copy-done.6, f32[8]{0:T(128)S(1)} %copy-done.7, f32[8,8,128]{2,1,0:T(8,128)S(1)} %get-tuple-element.31.v_old.v1, f32[8,8,128]{2,1,0:T(8,128)S(1)} %get-tuple-element.36.u_piece, ...), custom_call_target="tpu_custom_call" | custom-call | flops 1000000 | bytes 3000000 | tf_op jit(solution)/shard_map/pallas_call | solution.py:357
  54.9 0.8 %collective-permute-done.17 = f32[8,128]{1,0:T(8,128)S(1)} collective-permute-done((f32[8,128]{1,0:T(8,128)S(1)}, f32[8,128]{1,0:T(8,128)S(1)}, u32[]{:S(2)}, u32[]{:S(2)}) %collective-permute-start.17) | collective-permute-done | bytes 4128 | tf_op jit(solution)/shard_map/ppermute | solution.py:290
  55.6 0.6 %shard_map.153 = (f32[8,512]{1,0:T(8,128)}, f32[8,512]{1,0:T(8,128)}, f32[3,8]{1,0:T(4,128)}) custom-call(f32[8,128]{1,0:T(8,128)S(1)} %add.43.sq, f32[8,8,128]{2,1,0:T(8,128)S(1)} %get-tuple-element.42.v2, f32[8,512]{1,0:T(8,128)S(1)} %get-tuple-element.43.w_mid, f32[3,8,128]{2,1,0:T(8,128)S(1)} %get-tuple-element.44.factors), custom_call_target="tpu_custom_call" | custom-call | tf_op jit(solution)/shard_map/pallas_call | solution.py:364
  (27 shorter events, 0.2 us)
Async XLA Ops:
  0.6 2.3 %copy-start.5 = (s32[1,1,128]{2,1,0:T(1,128)S(1)}, s32[1,1,128]{2,1,0:T(1,128)}, u32[]{:S(2)}) copy-start(s32[1,1,128]{2,1,0:T(1,128)} %cls_ref.7) | copy-start | bytes 1540
  0.6 2.3 %copy-start.4 = (s32[1,1,128]{2,1,0:T(1,128)S(1)}, s32[1,1,128]{2,1,0:T(1,128)}, u32[]{:S(2)}) copy-start(s32[1,1,128]{2,1,0:T(1,128)} %rws_ref.7) | copy-start | bytes 1540
  0.7 2.3 %copy-start.8 = (f32[8]{0:T(128)S(1)}, f32[8]{0:T(128)}, u32[]{:S(2)}) copy-start(f32[8]{0:T(128)} %alpha_ref.1) | copy-start | bytes 100
  0.7 2.3 %copy-start.1 = (f32[8,1024]{1,0:T(8,128)S(1)}, f32[8,1024]{1,0:T(8,128)}, u32[]{:S(2)}) copy-start(f32[8,1024]{1,0:T(8,128)} %u_piece.1) | copy-start | bytes 98308
  0.7 2.3 %copy-start = (bf16[1,1,128,128,128]{4,3,2,1,0:T(8,128)(2,1)S(1)}, bf16[1,1,128,128,128]{4,3,2,1,0:T(8,128)(2,1)}, u32[]{:S(2)}) copy-start(bf16[1,1,128,128,128]{4,3,2,1,0:T(8,128)(2,1)} %param.11) | copy-start | bytes 12582916
  0.7 0.9 %copy-start.9 = (f32[8,512]{1,0:T(8,128)S(1)}, f32[8,512]{1,0:T(8,128)}, u32[]{:S(2)}) copy-start(f32[8,512]{1,0:T(8,128)} %own_hbm.1) | copy-start | bytes 49156
  1.6 1.4 %collective-permute-start = (f32[8,512]{1,0:T(8,128)S(1)}, f32[8,512]{1,0:T(8,128)S(1)}, u32[]{:S(2)}, u32[]{:S(2)}) collective-permute-start(f32[8,512]{1,0:T(8,128)S(1)} %shard_map.146.own), channel_id=1, source_target_pairs={{0,8},{8,0},{1,9},{9,1},{2,10},{10,2},{3,11},{11,3},{4,12},{12,4},... | collective-permute-start | bytes 49160 | tf_op jit(solution)/shard_map/ppermute | solution.py:259
  4.8 6.0 %collective-permute-start.1 = (bf16[16,16,128]{2,1,0:T(8,128)(2,1)S(1)}, bf16[16,16,128]{2,1,0:T(8,128)(2,1)S(1)}, u32[]{:S(2)}, u32[]{:S(2)}) collective-permute-start(bf16[16,16,128]{2,1,0:T(8,128)(2,1)S(1)} %get-tuple-element.27), channel_id=1, source_target_pairs={{0,2},{1,3},{2,0},{3,1},{4,6},{5,7},{6,4},{7,5},{8,12},{9,13},{10,... | collective-permute-start | bytes 196616 | tf_op jit(solution)/shard_map/ppermute | solution.py:273
  7.8 5.0 %collective-permute-start.4 = (bf16[16,16,128]{2,1,0:T(8,128)(2,1)S(1)}, bf16[16,16,128]{2,1,0:T(8,128)(2,1)S(1)}, u32[]{:S(2)}, u32[]{:S(2)}) collective-permute-start(bf16[16,16,128]{2,1,0:T(8,128)(2,1)S(1)} %get-tuple-element.28), channel_id=1, source_target_pairs={{0,1},{1,0},{2,3},{3,2},{4,5},{5,4},{6,7},{7,6},{8,12},{9,13},{10,... | collective-permute-start | bytes 196616 | tf_op jit(solution)/shard_map/ppermute | solution.py:273
  10.8 4.3 %collective-permute-start.2 = (bf16[16,16,128]{2,1,0:T(8,128)(2,1)S(1)}, bf16[16,16,128]{2,1,0:T(8,128)(2,1)S(1)}, u32[]{:S(2)}, u32[]{:S(2)}) collective-permute-start(bf16[16,16,128]{2,1,0:T(8,128)(2,1)S(1)} %add_convert_fusion.7), channel_id=1, source_target_pairs={{0,1},{1,0},{2,3},{3,2},{4,5},{5,4},{6,7},{7,6},{8,10},{9,11},{10,... | collective-permute-start | bytes 196616 | tf_op jit(solution)/shard_map/ppermute | solution.py:273
  12.8 5.2 %collective-permute-start.5 = (bf16[16,16,128]{2,1,0:T(8,128)(2,1)S(1)}, bf16[16,16,128]{2,1,0:T(8,128)(2,1)S(1)}, u32[]{:S(2)}, u32[]{:S(2)}) collective-permute-start(bf16[16,16,128]{2,1,0:T(8,128)(2,1)S(1)} %add_convert_fusion.5), channel_id=1, source_target_pairs={{0,4},{1,5},{2,6},{3,7},{4,0},{5,1},{6,2},{7,3},{8,10},{9,11},{10,... | collective-permute-start | bytes 196616 | tf_op jit(solution)/shard_map/ppermute | solution.py:273
  15.2 5.2 %collective-permute-start.3 = (bf16[16,16,128]{2,1,0:T(8,128)(2,1)S(1)}, bf16[16,16,128]{2,1,0:T(8,128)(2,1)S(1)}, u32[]{:S(2)}, u32[]{:S(2)}) collective-permute-start(bf16[16,16,128]{2,1,0:T(8,128)(2,1)S(1)} %add_convert_fusion.6.sums0), channel_id=1, source_target_pairs={{0,4},{1,5},{2,6},{3,7},{4,0},{5,1},{6,2},{7,3},{8,9},{9,8},{10,11... | collective-permute-start | bytes 196616 | tf_op jit(solution)/shard_map/ppermute | solution.py:273
  18.1 4.3 %collective-permute-start.6 = (bf16[16,16,128]{2,1,0:T(8,128)(2,1)S(1)}, bf16[16,16,128]{2,1,0:T(8,128)(2,1)S(1)}, u32[]{:S(2)}, u32[]{:S(2)}) collective-permute-start(bf16[16,16,128]{2,1,0:T(8,128)(2,1)S(1)} %add_convert_fusion.4.sums2), channel_id=1, source_target_pairs={{0,2},{1,3},{2,0},{3,1},{4,6},{5,7},{6,4},{7,5},{8,9},{9,8},{10,11... | collective-permute-start | bytes 196616 | tf_op jit(solution)/shard_map/ppermute | solution.py:273
  23.7 1.3 %collective-permute-start.7 = (f32[9,8,128]{2,1,0:T(8,128)S(1)}, f32[9,8,128]{2,1,0:T(8,128)S(1)}, u32[]{:S(2)}, u32[]{:S(2)}) collective-permute-start(f32[9,8,128]{2,1,0:T(8,128)S(1)} %get-tuple-element.29.own), channel_id=1, source_target_pairs={{0,8},{8,0},{1,9},{9,1},{2,10},{10,2},{3,11},{11,3},{4,12},{12,4},... | collective-permute-start | bytes 110600 | tf_op jit(solution)/shard_map/ppermute | solution.py:259
  25.0 28.7 %copy-start.2 = (f32[8,512]{1,0:T(8,128)S(1)}, f32[8,512]{1,0:T(8,128)}, u32[]{:S(2)}) copy-start(f32[8,512]{1,0:T(8,128)} %x_in.1) | copy-start | bytes 49156
  25.0 28.7 %copy-start.3 = (f32[8,512]{1,0:T(8,128)S(1)}, f32[8,512]{1,0:T(8,128)}, u32[]{:S(2)}) copy-start(f32[8,512]{1,0:T(8,128)} %w_in.1) | copy-start | bytes 49156
  25.0 28.7 %copy-start.6 = (f32[8]{0:T(128)S(1)}, f32[8]{0:T(128)}, u32[]{:S(2)}) copy-start(f32[8]{0:T(128)} %phibar_in.1) | copy-start | bytes 100
  25.0 28.7 %copy-start.7 = (f32[8]{0:T(128)S(1)}, f32[8]{0:T(128)}, u32[]{:S(2)}) copy-start(f32[8]{0:T(128)} %rhobar_in.1) | copy-start | bytes 100
  26.8 5.1 %collective-permute-start.8 = (bf16[17,16,128]{2,1,0:T(8,128)(2,1)S(1)}, bf16[17,16,128]{2,1,0:T(8,128)(2,1)S(1)}, u32[]{:S(2)}, u32[]{:S(2)}) collective-permute-start(bf16[17,16,128]{2,1,0:T(8,128)(2,1)S(1)} %get-tuple-element.32), channel_id=1, source_target_pairs={{0,2},{1,3},{2,0},{3,1},{4,6},{5,7},{6,4},{7,5},{8,12},{9,13},{10,... | collective-permute-start | bytes 208904 | tf_op jit(solution)/shard_map/ppermute | solution.py:273
  28.6 4.6 %collective-permute-start.11 = (bf16[16,16,128]{2,1,0:T(8,128)(2,1)S(1)}, bf16[16,16,128]{2,1,0:T(8,128)(2,1)S(1)}, u32[]{:S(2)}, u32[]{:S(2)}) collective-permute-start(bf16[16,16,128]{2,1,0:T(8,128)(2,1)S(1)} %get-tuple-element.33), channel_id=1, source_target_pairs={{0,1},{1,0},{2,3},{3,2},{4,5},{5,4},{6,7},{7,6},{8,12},{9,13},{10,... | collective-permute-start | bytes 196616 | tf_op jit(solution)/shard_map/ppermute | solution.py:273
  32.0 4.4 %collective-permute-start.9 = (bf16[17,16,128]{2,1,0:T(8,128)(2,1)S(1)}, bf16[17,16,128]{2,1,0:T(8,128)(2,1)S(1)}, u32[]{:S(2)}, u32[]{:S(2)}) collective-permute-start(bf16[17,16,128]{2,1,0:T(8,128)(2,1)S(1)} %add_convert_fusion.1), channel_id=1, source_target_pairs={{0,1},{1,0},{2,3},{3,2},{4,5},{5,4},{6,7},{7,6},{8,10},{9,11},{10,... | collective-permute-start | bytes 208904 | tf_op jit(solution)/shard_map/ppermute | solution.py:273
  33.2 5.2 %collective-permute-start.12 = (bf16[16,16,128]{2,1,0:T(8,128)(2,1)S(1)}, bf16[16,16,128]{2,1,0:T(8,128)(2,1)S(1)}, u32[]{:S(2)}, u32[]{:S(2)}) collective-permute-start(bf16[16,16,128]{2,1,0:T(8,128)(2,1)S(1)} %add_convert_fusion.3), channel_id=1, source_target_pairs={{0,4},{1,5},{2,6},{3,7},{4,0},{5,1},{6,2},{7,3},{8,10},{9,11},{10,... | collective-permute-start | bytes 196616 | tf_op jit(solution)/shard_map/ppermute | solution.py:273
  36.4 6.4 %collective-permute-start.10 = (bf16[17,16,128]{2,1,0:T(8,128)(2,1)S(1)}, bf16[17,16,128]{2,1,0:T(8,128)(2,1)S(1)}, u32[]{:S(2)}, u32[]{:S(2)}) collective-permute-start(bf16[17,16,128]{2,1,0:T(8,128)(2,1)S(1)} %add_convert_fusion.sums0), channel_id=1, source_target_pairs={{0,4},{1,5},{2,6},{3,7},{4,0},{5,1},{6,2},{7,3},{8,9},{9,8},{10,11... | collective-permute-start | bytes 208904 | tf_op jit(solution)/shard_map/ppermute | solution.py:273
  38.4 4.3 %collective-permute-start.13 = (bf16[16,16,128]{2,1,0:T(8,128)(2,1)S(1)}, bf16[16,16,128]{2,1,0:T(8,128)(2,1)S(1)}, u32[]{:S(2)}, u32[]{:S(2)}) collective-permute-start(bf16[16,16,128]{2,1,0:T(8,128)(2,1)S(1)} %add_convert_fusion.2.sums2), channel_id=1, source_target_pairs={{0,2},{1,3},{2,0},{3,1},{4,6},{5,7},{6,4},{7,5},{8,9},{9,8},{10,11... | collective-permute-start | bytes 196616 | tf_op jit(solution)/shard_map/ppermute | solution.py:273
  44.2 1.3 %collective-permute-start.14 = (f32[9,8,128]{2,1,0:T(8,128)S(1)}, f32[9,8,128]{2,1,0:T(8,128)S(1)}, u32[]{:S(2)}, u32[]{:S(2)}) collective-permute-start(f32[9,8,128]{2,1,0:T(8,128)S(1)} %get-tuple-element.38.own), channel_id=1, source_target_pairs={{0,8},{8,0},{1,9},{9,1},{2,10},{10,2},{3,11},{11,3},{4,12},{12,4},... | collective-permute-start | bytes 110600 | tf_op jit(solution)/shard_map/ppermute | solution.py:259
  45.6 3.1 %collective-permute-start.15 = (f32[8,128]{1,0:T(8,128)S(1)}, f32[8,128]{1,0:T(8,128)S(1)}, u32[]{:S(2)}, u32[]{:S(2)}) collective-permute-start(f32[8,128]{1,0:T(8,128)S(1)} %get-tuple-element.41), channel_id=1, source_target_pairs={{0,10},{1,11},{2,8},{3,9},{4,14},{5,15},{6,12},{7,13},{8,2},{9,3},... | collective-permute-start | bytes 12296 | tf_op jit(solution)/shard_map/ppermute | solution.py:290
  48.7 3.9 %collective-permute-start.16 = (f32[8,128]{1,0:T(8,128)S(1)}, f32[8,128]{1,0:T(8,128)S(1)}, u32[]{:S(2)}, u32[]{:S(2)}) collective-permute-start(f32[8,128]{1,0:T(8,128)S(1)} %add.41), channel_id=1, source_target_pairs={{0,12},{1,13},{2,14},{3,15},{4,8},{5,9},{6,10},{7,11},{8,4},{9,5},... | collective-permute-start | bytes 12296 | tf_op jit(solution)/shard_map/ppermute | solution.py:290
  52.6 3.0 %collective-permute-start.17 = (f32[8,128]{1,0:T(8,128)S(1)}, f32[8,128]{1,0:T(8,128)S(1)}, u32[]{:S(2)}, u32[]{:S(2)}) collective-permute-start(f32[8,128]{1,0:T(8,128)S(1)} %add.42), channel_id=1, source_target_pairs={{0,9},{1,8},{2,11},{3,10},{4,13},{5,12},{6,15},{7,14},{8,1},{9,0},... | collective-permute-start | bytes 12296 | tf_op jit(solution)/shard_map/ppermute | solution.py:290
